TPU v7x, 512 devices: a whole 4x4x16 slice. The times are simulated.
512 devices in a mesh: tile: 32 (over z, core), band: 4 (over x), pos: 4 (over y).
Axes of the slice: x: 4, y: 4, z: 16, core: 2. Of those that a mesh axis runs over, the one named last changes fastest.
Arguments:
- object_planes: float32 [2, 8192, 1024], P(None, 'tile', 'band'), may hold values from -6 to 6
- probe_planes: float32 [2, 2, 256, 256], replicated, may hold values from -6 to 6
- patterns: float32 [32, 4, 4, 3, 256, 256], P('tile', 'band', 'pos'), may hold values from 0.5 to 8
- offsets: int32 [32, 4, 4, 3, 2], P('tile', 'band', 'pos'), may hold values from 0 to 255, as said below
- counts: int32 [32, 4, 4], P('tile', 'band', 'pos'), may hold values from 0 to 3, as said below
Outputs:
- object_new: float32 [2, 8192, 1024], P(None, 'tile', 'band')
- probe_new: float32 [2, 2, 256, 256], replicated
Inputs may be any that keep to these rules, and one draw needn't show every extreme that they name: `offsets`: corners lie inside their tile: rows below 256, columns below 256. Only the first counts[t, b, p] slots of a device hold positions; later slots are to be ignored. `counts`: each device holds at most 3 positions; in every tile one device along pos holds exactly 3, and the 4 devices of a tile hold exactly 8 positions together.
All inputs are finite; a program needn't handle non-finite values.
Results may differ from a plain program's by a relative error of at most 0.0003.
Values sent between devices are 32-bit elements; how exact they have to be, the bound alone decides.
No kernel may reach another device: no remote copies, remote signals or barrier semaphores. Data moves between devices by JAX's collectives and lax.ppermute only.
A program may use at most 192 MiB of HBM per device.

v0:
```python
import math

import jax
import jax.numpy as jnp
from jax import lax
from jax.sharding import PartitionSpec as P

precise = lax.Precision.HIGHEST


def shifted(block, axis, distance):
    devices = range(lax.axis_size(axis))
    route = [(i - distance, i) for i in devices if i - distance in devices]
    return lax.ppermute(block, axis, route)


def dft_tables(pixels):
    indices = jnp.arange(pixels, dtype=jnp.int32)
    phase = indices[:, None] * indices[None, :] % pixels
    angle = phase.astype(jnp.float32) * (2.0 * math.pi / pixels)
    factor = 1.0 / math.sqrt(pixels)
    return (jnp.cos(angle) * factor, jnp.sin(angle) * factor)


def transform(real_part, imag_part, cosine, sine_table, direction):
    left_real = jnp.einsum(
        "ij,nmjk->nmik", cosine, real_part, precision=precise
    ) + direction * jnp.einsum("ij,nmjk->nmik", sine_table, imag_part, precision=precise)
    left_imag = jnp.einsum(
        "ij,nmjk->nmik", cosine, imag_part, precision=precise
    ) - direction * jnp.einsum("ij,nmjk->nmik", sine_table, real_part, precision=precise)
    out_real = jnp.einsum(
        "nmij,jk->nmik", left_real, cosine, precision=precise
    ) + direction * jnp.einsum("nmij,jk->nmik", left_imag, sine_table, precision=precise)
    out_imag = jnp.einsum(
        "nmij,jk->nmik", left_imag, cosine, precision=precise
    ) - direction * jnp.einsum("nmij,jk->nmik", left_real, sine_table, precision=precise)
    return (out_real, out_imag)


def on_device(object_planes, probe_planes, patterns, offsets, counts):
    pixels = probe_planes.shape[-1]
    capacity = patterns.shape[3]
    tile_rows = object_planes.shape[1]
    tile_cols = object_planes.shape[2]
    beside_cols = shifted(object_planes, "band", -1)
    widened = jnp.concatenate([object_planes, beside_cols], axis=2)
    below_rows = shifted(widened, "tile", -1)
    extended = jnp.concatenate([widened, below_rows], axis=1)
    local_count = counts.reshape(())
    frames = patterns[0, 0, 0]
    places = offsets[0, 0, 0]
    weights = (jnp.arange(capacity, dtype=jnp.int32) < local_count).astype(jnp.float32)
    slot_total = frames.shape[0]
    zero_index = jnp.int32(0)
    patches = jnp.stack(
        [
            lax.dynamic_slice(
                extended, (zero_index, places[number, 0], places[number, 1]), (2, pixels, pixels)
            )
            for number in range(slot_total)
        ]
    )
    patch_real = patches[:, 0][:, None]
    patch_imag = patches[:, 1][:, None]
    probe_real = probe_planes[0][None]
    probe_imag = probe_planes[1][None]
    wave_real = probe_real * patch_real - probe_imag * patch_imag
    wave_imag = probe_real * patch_imag + probe_imag * patch_real
    cosine, sine_table = dft_tables(pixels)
    far_real, far_imag = transform(wave_real, wave_imag, cosine, sine_table, 1.0)
    intensity = jnp.sum(far_real * far_real + far_imag * far_imag, axis=1)
    scaling = (jnp.sqrt(frames) / jnp.sqrt(intensity + 1.0))[:, None]
    back_real, back_imag = transform(
        far_real * scaling, far_imag * scaling, cosine, sine_table, -1.0
    )
    corr_real = back_real - wave_real
    corr_imag = back_imag - wave_imag
    slot_weight = weights[:, None, None]
    object_real = slot_weight * jnp.sum(probe_real * corr_real + probe_imag * corr_imag, axis=1)
    object_imag = slot_weight * jnp.sum(probe_real * corr_imag - probe_imag * corr_real, axis=1)
    probe_power = jnp.sum(probe_planes[0] ** 2 + probe_planes[1] ** 2, axis=0)
    lighting = slot_weight * probe_power[None]
    contributions = jnp.stack([object_real, object_imag, lighting], axis=1)
    plane_count = contributions.shape[1]
    running = jnp.zeros((plane_count, tile_rows + pixels, tile_cols + pixels), jnp.float32)
    for number in range(slot_total):
        corner_at = (zero_index, places[number, 0], places[number, 1])
        previous = lax.dynamic_slice(running, corner_at, (plane_count, pixels, pixels))
        running = lax.dynamic_update_slice(running, previous + contributions[number], corner_at)
    mode_weight = weights[:, None, None, None]
    numer_real = jnp.sum(mode_weight * (patch_real * corr_real + patch_imag * corr_imag), axis=0)
    numer_imag = jnp.sum(mode_weight * (patch_real * corr_imag - patch_imag * corr_real), axis=0)
    density = jnp.sum(slot_weight * (patches[:, 0] ** 2 + patches[:, 1] ** 2), axis=0)
    from_left = shifted(running[:, :, tile_cols:], "band", 1)
    column_core = running[:, :, :tile_cols].at[:, :, :pixels].add(from_left)
    from_above = shifted(column_core[:, tile_rows:, :], "tile", 1)
    tile_core = column_core[:, :tile_rows, :].at[:, :pixels, :].add(from_above)
    tile_total = lax.psum(tile_core, "pos")
    tile_light = tile_total[2]
    object_new = object_planes + tile_total[:2] / (tile_light + 1.0)
    sum_numer, sum_density = lax.psum(
        (jnp.stack([numer_real, numer_imag]), density), ("tile", "band", "pos")
    )
    probe_new = probe_planes + sum_numer / (sum_density + 1.0)
    return (object_new, probe_new)


def solution(mesh):
    in_specs = (
        P(None, "tile", "band"),
        P(),
        P("tile", "band", "pos", None, None, None),
        P("tile", "band", "pos", None, None),
        P("tile", "band", "pos"),
    )
    out_specs = (P(None, "tile", "band"), P())
    return jax.shard_map(
        on_device, mesh=mesh, in_specs=in_specs, out_specs=out_specs, check_vma=False
    )
```

profile of v0, /device:TPU:2, one launch (start us, length us, event | category | flops | bytes accessed | tf_op | source)
XLA Modules:
  0.0 732.0 jit_solution(11217168582069033955)
XLA Ops:
  7.2 8.0 %collective-permute-start = (f32[2,256,256]{2,1,0:T(8,128)}, f32[2,256,256]{2,1,0:T(8,128)S(1)}, u32[]{:S(2)}, u32[]{:S(2)}) collective-permute-start(f32[2,256,256]{2,1,0:T(8,128)} %param.13), channel_id=1, source_target_pairs={{4,0},{8,4},{12,8},{5,1},{9,5},{13,9},{6,2},{10,6},{14,10},{7,3},{... | collective-permute-start | bytes 1572872 | tf_op jit(solution)/shard_map/ppermute | solution.py:14
  15.2 1.1 constant_dynamic-update-slice_fusion.1
  16.3 6.8 collective-permute-done
  23.2 1.3 collective-permute-start.1
  24.5 0.6 fusion.170
  37.3 1.0 fusion.63
  38.5 1.0 copy-done
  39.5 3.7 fusion.16
  43.2 3.7 fusion.31
  46.9 4.1 fusion.8
  51.0 3.6 fusion.10
  54.6 3.7 fusion.17
  58.3 3.7 fusion.30
  62.0 3.8 fusion.20
  65.9 3.8 add_reduce_fusion.1
  69.6 0.3 bitcast_multiply_fusion.2
  69.9 3.6 fusion.36
  73.5 3.8 fusion.32
  77.3 3.6 multiply_subtract_fusion
  80.9 3.6 fusion
  84.5 4.0 fusion.2
  88.6 3.6 multiply_add_fusion
  92.2 3.9 add_subtract_fusion
  96.2 6.0 multiply_reduce_fusion.1
  102.1 0.3 bitcast_multiply_fusion.1
  102.4 0.2 pad_maximum_fusion
  102.6 1.0 slice_bitcast_fusion.2
  103.6 0.7 copy-done.4
  104.3 0.4 broadcast_in_dim.2
  104.7 11.2 %dynamic_update_slice.9 = f32[3,512,512]{2,1,0:T(8,128)S(1)} dynamic-update-slice(f32[3,512,512]{2,1,0:T(8,128)S(1)} %broadcast_in_dim.2, f32[3,256,256]{2,1,0:T(8,128)} %slice_bitcast_fusion.2, s32[]{:T(128)} %constant.88.clone.1, s32[]{:T(128)S(6)} %select_n.65, s32[]{:T(128)S(6)} %select_n.66) | dynamic-update-slice | bytes 1572868 | tf_op jit(solution)/shard_map/dynamic_update_slice | solution.py:90
  115.8 2.3 fusion.39
  118.1 10.7 %dynamic_update_slice.10 = f32[3,512,512]{2,1,0:T(8,128)S(1)} dynamic-update-slice(f32[3,512,512]{2,1,0:T(8,128)S(1)} %dynamic_update_slice.9, f32[3,256,256]{2,1,0:T(8,128)} %fusion.39, s32[]{:T(128)} %constant.88.clone.1, s32[]{:T(128)S(6)} %select_n.67, s32[]{:T(128)S(6)} %select_n.68) | dynamic-update-slice | bytes 1572868 | tf_op jit(solution)/shard_map/dynamic_update_slice | solution.py:90
  128.8 2.3 fusion.38
  131.1 10.5 %dynamic_update_slice.11 = f32[3,512,512]{2,1,0:T(8,128)S(1)} dynamic-update-slice(f32[3,512,512]{2,1,0:T(8,128)S(1)} %dynamic_update_slice.10, f32[3,256,256]{2,1,0:T(8,128)} %fusion.38, s32[]{:T(128)} %constant.88.clone.1, s32[]{:T(128)S(6)} %select_n.69, s32[]{:T(128)S(6)} %select_n.70) | dynamic-update-slice | bytes 1572868 | tf_op jit(solution)/shard_map/dynamic_update_slice | solution.py:90
  141.6 0.2 slice.130
  141.8 6.5 collective-permute-start.2
  148.2 34.1 %collective-permute-done.2 = f32[3,512,256]{2,1,0:T(8,128)S(1)} collective-permute-done((f32[3,512,256]{2,1,0:T(8,128)S(1)}, f32[3,512,256]{2,1,0:T(8,128)S(1)}, u32[]{:S(2)}, u32[]{:S(2)}) %collective-permute-start.2) | collective-permute-done | bytes 1572896 | tf_op jit(solution)/shard_map/ppermute | solution.py:14
  182.3 0.3 slice_add_fusion
  182.7 3.4 collective-permute-start.3
  186.1 1.0 pad_maximum_fusion.2
  187.1 0.9 multiply_reduce_fusion.2
  188.1 2.2 slice_add_fusion.1
  190.3 471.8 %all-reduce.6.cloned.1.call-done = (f32[2,2,256,256]{3,2,1,0:T(8,128)}, f32[256,256]{1,0:T(8,128)}) async-done(((f32[2,2,256,256]{3,2,1,0:T(8,128)}, f32[256,256]{1,0:T(8,128)}), (f32[2,2,256,256]{3,2,1,0:T(8,128)}, f32[256,256]{1,0:T(8,128)})) %all-reduce.6.cloned.1.call-update) | async-done | bytes 1310736 | tf_op jit(solution)/shard_map/psum | solution.py:102
  662.1 1.0 broadcast_add_fusion
  663.1 2.4 divide_add_fusion
  665.5 56.5 %all-reduce.4.cloned.1.call-done = f32[3,256,256]{2,1,0:T(8,128)} async-done(((f32[3,256,256]{2,1,0:T(8,128)}), f32[3,256,256]{2,1,0:T(8,128)}) %all-reduce.4.cloned.1.call-update) | async-done | bytes 786448 | tf_op jit(solution)/shard_map/psum | solution.py:99
  722.0 1.0 fusion.70
  723.0 1.9 fusion.66
  (33 shorter events, 0.6 us)
Async XLA Ops:
  7.2 17.3 %copy-start.10 = (s32[1,1,1,3,2]{3,4,2,1,0:T(2,128)S(1)}, s32[1,1,1,3,2]{3,4,2,1,0:T(2,128)}, u32[]{:S(2)}) copy-start(s32[1,1,1,3,2]{3,4,2,1,0:T(2,128)} %param.16) | copy-start | bytes 76
  7.2 29.9 %copy-start.2 = (f32[2,2,256,256]{3,2,1,0:T(8,128)S(1)}, f32[2,2,256,256]{3,2,1,0:T(8,128)}, u32[]{:S(2)}) copy-start(f32[2,2,256,256]{3,2,1,0:T(8,128)} %param.14) | copy-start | bytes 3145732
  7.2 654.9 %all-reduce.6.cloned.1.call-start = ((), (), s32[]{:S(2)}) async-start(), calls=%async_computation.1 | async-start | bytes 2621440 | tf_op jit(solution)/shard_map/psum | solution.py:102
  7.2 15.9 %collective-permute-start = (f32[2,256,256]{2,1,0:T(8,128)}, f32[2,256,256]{2,1,0:T(8,128)S(1)}, u32[]{:S(2)}, u32[]{:S(2)}) collective-permute-start(f32[2,256,256]{2,1,0:T(8,128)} %param.13), channel_id=1, source_target_pairs={{4,0},{8,4},{12,8},{5,1},{9,5},{13,9},{6,2},{10,6},{14,10},{7,3},{... | collective-permute-start | bytes 1572872 | tf_op jit(solution)/shard_map/ppermute | solution.py:14
  23.2 14.1 %collective-permute-start.1 = (f32[2,256,512]{2,1,0:T(8,128)S(1)}, f32[2,256,512]{2,1,0:T(8,128)S(1)}, u32[]{:S(2)}, u32[]{:S(2)}) collective-permute-start(f32[2,256,512]{2,1,0:T(8,128)S(1)} %constant_dynamic-update-slice_fusion), channel_id=1, source_target_pairs={{16,0},{32,16},{48,32},{64,48},{80,64},{96,80},{112,96},{128,112},... | collective-permute-start | bytes 3145736 | tf_op jit(solution)/shard_map/ppermute | solution.py:14
  38.3 1.1 copy-start
  65.8 3.8 copy-start.7
  102.6 1.7 copy-start.4
  141.8 40.5 %collective-permute-start.2 = (f32[3,512,256]{2,1,0:T(8,128)S(1)}, f32[3,512,256]{2,1,0:T(8,128)S(1)}, u32[]{:S(2)}, u32[]{:S(2)}) collective-permute-start(f32[3,512,256]{2,1,0:T(8,128)S(1)} %slice.130), channel_id=1, source_target_pairs={{0,4},{4,8},{8,12},{1,5},{5,9},{9,13},{2,6},{6,10},{10,14},{3,7},{... | collective-permute-start | bytes 4718600 | tf_op jit(solution)/shard_map/ppermute | solution.py:14
  182.3 3.7 copy-start.8
  182.3 3.8 copy-start.9
  182.6 4.5 copy-start.5
  182.6 4.5 copy-start.1
  182.7 5.4 collective-permute-start.3
  188.0 475.1 %copy-start.3 = (f32[2,2,256,256]{3,2,1,0:T(8,128)S(1)}, f32[2,2,256,256]{3,2,1,0:T(8,128)}, u32[]{:S(2)}) copy-start(f32[2,2,256,256]{3,2,1,0:T(8,128)} %param.14) | copy-start | bytes 3145732
  188.0 534.0 %all-reduce.4.cloned.1.call-start = ((), (), s32[]{:S(2)}) async-start(), calls=%async_computation | async-start | bytes 1572864 | tf_op jit(solution)/shard_map/psum | solution.py:99
  663.1 59.9 %copy-start.6 = (f32[2,256,256]{2,1,0:T(8,128)S(1)}, f32[2,256,256]{2,1,0:T(8,128)}, u32[]{:S(2)}) copy-start(f32[2,256,256]{2,1,0:T(8,128)} %param.13) | copy-start | bytes 1572868
Sparse Core Ops, SparseCore 0:
  188.1 473.9 all-reduce.5
  664.5 57.5 all-reduce.3
where the time goes:
time: 743 us; the launch traced here: 732 us
  waiting for transfers between devices  569 us (77%)
  matrix products  62.2 us (8%)
  local copies, waits for them, and re-layouts  37.7 us (5%)
  between operations  26.6 us (4%)
  starting transfers between devices  19.1 us (3%)
  other arithmetic  17.1 us (2%)
    psum x1, waiting for transfers between devices, on_device(): lax.psum((jnp.stack([numer_real, numer_imag]), density), ('tile', 'band',...  472 us
    psum x1, waiting for transfers between devices, on_device(): tile_total = lax.psum(tile_core, 'pos')  56.5 us
    ppermute x4, waiting for transfers between devices, shifted(): return lax.ppermute(block, axis, route)  40.9 us
    dynamic_update_slice x3, local copies, waits for them, and re-layouts, on_device(): lax.dynamic_update_slice(running, previous + contributions[number], corne...  32.3 us
    ppermute x4, starting transfers between devices, shifted(): return lax.ppermute(block, axis, route)  19 us
  transfers between devices with their start and end apart: 6, of which 4 were waited for; matrix products, arithmetic and copies ran while one was open for 1% of the time, Pallas kernels for 0%

commit v1 on v0

v1 whole, which is shorter than its diff:
```python
import functools
import math

import jax
import jax.numpy as jnp
import ml_dtypes
import numpy as np
from jax import lax
from jax.experimental import pallas as pl
from jax.experimental.pallas import tpu as pltpu
from jax.sharding import PartitionSpec as P

S = 256
QUARTERS = 4


def tables():
    index = np.arange(S)
    angle = (index[:, None] * index[None, :] % S) * (2.0 * math.pi / S)
    cosine, sine = np.cos(angle) / 16.0, np.sin(angle) / 16.0
    left = np.block([[cosine, sine], [-sine, cosine]]).astype(np.float32)
    head = left.astype(ml_dtypes.bfloat16)
    rest = (left - head.astype(np.float32)).astype(ml_dtypes.bfloat16)
    return (head, rest, np.ascontiguousarray(head.T), np.ascontiguousarray(rest.T))


def split(value):
    head = value.astype(jnp.bfloat16)
    return head, (value - head.astype(jnp.float32)).astype(jnp.bfloat16)


def product(first, second):
    dot = functools.partial(jnp.dot, preferred_element_type=jnp.float32)
    return dot(first[0], second[0]) + dot(first[0], second[1]) + dot(first[1], second[0])


def regroup(value):
    return jnp.concatenate(
        [
            jnp.concatenate([value[:S, :S], value[S:, :S]], axis=1),
            jnp.concatenate([value[:S, S:], value[S:, S:]], axis=1),
        ],
        axis=0,
    )


def cut(block, row, column):
    block = pltpu.roll(block, lax.rem(2 * S - column, 2 * S), 1)[:, :S]
    return pltpu.roll(block, lax.rem(S + 8 - row, S + 8), 0)[:S]


def placed(value, row, column):
    value = jnp.concatenate([value, jnp.zeros((8, S), jnp.float32)], axis=0)
    value = pltpu.roll(value, row, 0)
    return pltpu.roll(jnp.concatenate([value, jnp.zeros_like(value)], axis=1), column, 1)


def slots_kernel(
    places, scalars, own, right, below, corner, probe, frames, lh, lr, rh, rr,
    top_left, bottom_left, right_half, keep, send, extended, total, terms,
):
    extended[:, :S, :S] = own[...]
    extended[:, :S, S:] = right[...]
    extended[:, S:, :S] = below[...]
    extended[:, S:, S:] = corner[...]
    total[...] = jnp.zeros_like(total)
    terms[...] = jnp.zeros_like(terms)
    blank = jnp.zeros((S, S), jnp.float32)

    def one_slot(slot, carry):
        row, column = places[slot, 0], places[slot, 1]
        inside = lax.rem(row, 8)
        band_rows = pl.ds(pl.multiple_of(row - inside, 8), S + 8)
        patch_real, patch_imag = (cut(extended[p, band_rows, :], inside, column) for p in range(2))
        real = jnp.concatenate(
            [probe[0, m] * patch_real - probe[1, m] * patch_imag for m in range(2)], axis=1
        )
        imag = jnp.concatenate(
            [probe[0, m] * patch_imag + probe[1, m] * patch_real for m in range(2)], axis=1
        )
        left_table, right_table = (lh[...], lr[...]), (rh[...], rr[...])
        wave = product(left_table, split(jnp.concatenate([real, imag], axis=0)))
        far = product(split(regroup(wave)), right_table)
        power = far * far
        power = power[:S, :S] + power[:S, S:] + power[S:, :S] + power[S:, S:]
        change = jnp.sqrt(frames[slot]) / jnp.sqrt(power + 1.0) - 1.0
        swapped = jnp.concatenate(
            [
                jnp.concatenate([far[:S, S:] * change, far[:S, :S] * change], axis=1),
                jnp.concatenate([far[S:, S:] * change, far[S:, :S] * change], axis=1),
            ],
            axis=0,
        )
        back = product(split(swapped), right_table)
        chi = product(left_table, split(regroup(back)))
        object_real, object_imag = blank, blank
        for m in range(2):
            chi_imag = chi[:S, m * S : (m + 1) * S]
            chi_real = chi[S:, m * S : (m + 1) * S]
            object_real += probe[0, m] * chi_real + probe[1, m] * chi_imag
            object_imag += probe[0, m] * chi_imag - probe[1, m] * chi_real
            terms[m] += patch_real * chi_real + patch_imag * chi_imag
            terms[2 + m] += patch_real * chi_imag - patch_imag * chi_real
        terms[4] += patch_real * patch_real + patch_imag * patch_imag
        light = jnp.zeros((S, S), jnp.float32)
        for m in range(2):
            light += probe[0, m] * probe[0, m] + probe[1, m] * probe[1, m]
        for plane, value in enumerate((object_real, object_imag, light)):
            total[plane, band_rows, :] += placed(value, inside, column)
        return carry

    lax.fori_loop(0, scalars[0], one_slot, 0)
    rows = S // QUARTERS
    for q in range(QUARTERS):
        for plane in range(3):
            at = q * rows
            top_left[q, plane] = total[plane, at : at + rows, :S]
            bottom_left[q, plane] = total[plane, S + at : S + at + rows, :S]
            right_half[0, q, plane] = total[plane, at : at + rows, S:]
            right_half[1, q, plane] = total[plane, S + at : S + at + rows, S:]
    chunks, _, height, _ = keep.shape
    core = scalars[1]
    for chunk in range(chunks):
        mine = pl.multiple_of(core * (S // 2) + chunk * height, height)
        other = pl.multiple_of((1 - core) * (S // 2) + chunk * height, height)
        for plane in range(5):
            keep[chunk, plane] = terms[plane, pl.ds(mine, height), :]
            send[chunk, plane] = terms[plane, pl.ds(other, height), :]


def run_slots(places, scalars, blocks, probe, frames, chunks):
    height = S // 2 // chunks
    f32 = jnp.float32
    quarter = (QUARTERS, 3, S // QUARTERS, S)
    vmem = pl.BlockSpec(memory_space=pltpu.VMEM)
    smem = pl.BlockSpec(memory_space=pltpu.SMEM)
    return pl.pallas_call(
        slots_kernel,
        out_shape=(
            jax.ShapeDtypeStruct(quarter, f32),
            jax.ShapeDtypeStruct(quarter, f32),
            jax.ShapeDtypeStruct((2, *quarter), f32),
            jax.ShapeDtypeStruct((chunks, 5, height, S), f32),
            jax.ShapeDtypeStruct((chunks, 5, height, S), f32),
        ),
        in_specs=[smem] * 2 + [vmem] * 10,
        out_specs=[vmem] * 5,
        scratch_shapes=[
            pltpu.VMEM((2, 2 * S, 2 * S), f32),
            pltpu.VMEM((3, 2 * S, 2 * S), f32),
            pltpu.VMEM((5, S, S), f32),
        ],
        compiler_params=pltpu.CompilerParams(vmem_limit_bytes=52 * 1024 * 1024),
        name="slots",
    )(places, scalars, *blocks, probe, frames, *(jnp.asarray(t) for t in tables()))


def shifted(block, axis, distance):
    devices = range(lax.axis_size(axis))
    route = [(i - distance, i) for i in devices if i - distance in devices]
    return lax.ppermute(block, axis, route)


def crossed(block, bit):
    devices = range(lax.axis_size("tile"))
    return lax.ppermute(block, "tile", [(i, i ^ bit) for i in devices])


def exchanged(block, axes):
    return lax.all_to_all(block, axes, 0, 0)


def on_device(object_planes, probe_planes, patterns, offsets, counts):
    core = lax.axis_index("tile") % 2
    plane = ("band", "pos")
    chunks = lax.axis_size("band") * lax.axis_size("pos")
    right = shifted(object_planes, "band", -1)
    below = shifted(object_planes, "tile", -1)
    corner = shifted(right, "tile", -1)
    scalars = jnp.stack([counts.reshape(()), core.astype(jnp.int32)])
    top, bottom, right_half, keep, send = run_slots(
        offsets[0, 0, 0], scalars, (object_planes, right, below, corner),
        probe_planes, patterns[0, 0, 0], chunks,
    )

    from_left = shifted(right_half, "band", 1)
    terms = keep + crossed(send, 1)
    from_above = shifted(bottom + from_left[1], "tile", 1)
    terms = jnp.sum(exchanged(terms, plane), axis=0)
    tile_sum = top + from_left[0] + from_above
    tile_sum = jnp.sum(exchanged(tile_sum, "pos"), axis=0)
    bit = 2
    while bit < lax.axis_size("tile"):
        terms = terms + crossed(terms, bit)
        bit *= 2

    rows = S // QUARTERS
    own_rows = lax.dynamic_slice_in_dim(object_planes, lax.axis_index("pos") * rows, rows, 1)
    own_rows = own_rows + tile_sum[:2] / (tile_sum[2] + 1.0)
    gathered = exchanged(jnp.broadcast_to(own_rows, (QUARTERS, *own_rows.shape)), "pos")
    object_new = gathered.transpose(1, 0, 2, 3).reshape(object_planes.shape)

    height = S // 2 // chunks
    place = core * (S // 2) + (lax.axis_index("band") * lax.axis_size("pos") + lax.axis_index("pos")) * height
    own_probe = lax.dynamic_slice_in_dim(probe_planes.reshape(4, S, S), place, height, 1)
    own_probe = own_probe + terms[:4] / (terms[4] + 1.0)
    mine = exchanged(jnp.broadcast_to(own_probe, (chunks, *own_probe.shape)), plane)
    other = crossed(mine, 1)
    halves = jnp.stack(
        [jnp.where(core == 0, mine, other), jnp.where(core == 0, other, mine)]
    )
    probe_new = halves.transpose(2, 0, 1, 3, 4).reshape(probe_planes.shape)
    return (object_new, probe_new)


def solution(mesh):
    in_specs = (
        P(None, "tile", "band"),
        P(),
        P("tile", "band", "pos", None, None, None),
        P("tile", "band", "pos", None, None),
        P("tile", "band", "pos"),
    )
    out_specs = (P(None, "tile", "band"), P())
    return jax.shard_map(
        on_device, mesh=mesh, in_specs=in_specs, out_specs=out_specs, check_vma=False
    )
```

time: 743 us -> 188 us (0.25)
  the two profiles are of different devices: /device:TPU:2 before, /device:TPU:64 now
where the time goes in v1:
time: 188 us; the launch traced here: 187 us
  starting transfers between devices  58.5 us (31%)
  waiting for transfers between devices  58.3 us (31%)
  blocking collectives  35.3 us (19%)
  Pallas kernels  20.4 us (11%)
  other arithmetic  7.5 us (4%)
  local copies, waits for them, and re-layouts  5.18 us (3%)
    ppermute x6, starting transfers between devices, crossed(): return lax.ppermute(block, 'tile', [(i, i ^ bit) for i in devices])  35.5 us
    all_to_all x1, blocking collectives, exchanged(): return lax.all_to_all(block, axes, 0, 0)  35.3 us
    all_to_all x3, waiting for transfers between devices, exchanged(): return lax.all_to_all(block, axes, 0, 0)  28.2 us
    pallas_call x1, Pallas kernels, run_slots(): pl.pallas_call(slots_kernel, out_shape=(jax.ShapeDtypeStruct(quarter, f32...  20.4 us
    ppermute x5, waiting for transfers between devices, shifted(): return lax.ppermute(block, axis, route)  17.7 us
    ppermute x5, starting transfers between devices, shifted(): return lax.ppermute(block, axis, route)  12.5 us
    ppermute x6, waiting for transfers between devices, crossed(): return lax.ppermute(block, 'tile', [(i, i ^ bit) for i in devices])  12.5 us
    all_to_all x3, starting transfers between devices, exchanged(): return lax.all_to_all(block, axes, 0, 0)  10.5 us
  transfers between devices with their start and end apart: 14, of which 9 were waited for; matrix products, arithmetic and copies ran while one was open for 5% of the time, Pallas kernels for 0%

profile of v1, /device:TPU:64, one launch (start us, length us, event | category | flops | bytes accessed | tf_op | source)
XLA Modules:
  0.0 186.8 jit_solution(8657227025943499548)
XLA Ops:
  0.6 1.3 collective-permute-start
  1.9 1.9 %collective-permute-start.1 = (f32[2,256,256]{2,1,0:T(8,128)}, f32[2,256,256]{2,1,0:T(8,128)S(1)}, u32[]{:S(2)}, u32[]{:S(2)}) collective-permute-start(f32[2,256,256]{2,1,0:T(8,128)} %own.1), channel_id=1, source_target_pairs={{16,0},{32,16},{48,32},{64,48},{80,64},{96,80},{112,96},{128,112},... | collective-permute-start | bytes 1572872 | tf_op jit(solution)/shard_map/ppermute | solution.py:161
  3.9 12.5 %collective-permute-done.right = f32[2,256,256]{2,1,0:T(8,128)S(1)} collective-permute-done((f32[2,256,256]{2,1,0:T(8,128)}, f32[2,256,256]{2,1,0:T(8,128)S(1)}, u32[]{:S(2)}, u32[]{:S(2)}) %collective-permute-start) | collective-permute-done | bytes 524320 | tf_op jit(solution)/shard_map/ppermute | solution.py:161
  16.4 1.9 %collective-permute-start.2 = (f32[2,256,256]{2,1,0:T(8,128)S(1)}, f32[2,256,256]{2,1,0:T(8,128)S(1)}, u32[]{:S(2)}, u32[]{:S(2)}) collective-permute-start(f32[2,256,256]{2,1,0:T(8,128)S(1)} %collective-permute-done.right), channel_id=1, source_target_pairs={{16,0},{32,16},{48,32},{64,48},{80,64},{96,80},{112,96},{128,112},... | collective-permute-start | bytes 1572872 | tf_op jit(solution)/shard_map/ppermute | solution.py:161
  19.0 0.8 copy.14.places
  19.7 0.1 pad_add_fusion.scalars
  19.8 0.0 collective-permute-done.1.below
  19.8 5.2 %collective-permute-done.2.corner = f32[2,256,256]{2,1,0:T(8,128)S(1)} collective-permute-done((f32[2,256,256]{2,1,0:T(8,128)S(1)}, f32[2,256,256]{2,1,0:T(8,128)S(1)}, u32[]{:S(2)}, u32[]{:S(2)}) %collective-permute-start.2) | collective-permute-done | bytes 524320 | tf_op jit(solution)/shard_map/ppermute | solution.py:161
  25.0 0.0 copy-start.3
  25.0 0.8 copy-done.3
  25.8 1.0 copy-done
  26.8 20.4 %slots.1 = (f32[4,3,64,256]{3,2,1,0:T(8,128)}, f32[4,3,64,256]{3,2,1,0:T(8,128)}, f32[2,4,3,64,256]{4,3,2,1,0:T(8,128)}, f32[16,5,8,256]{3,2,1,0:T(8,128)}, f32[16,5,8,256]{3,2,1,0:T(8,128)}) custom-call(s32[3,2]{1,0:T(4,128)S(1)} %copy.14.places, s32[2]{0:T(128)S(1)} %pad_add_fusion.scalars, f32[2,256,256]{2,1,0:T(8,128)S(1)} %copy-done, ...), custom_call_target="tpu_custom_call" | custom-call | tf_op jit(solution)/shard_map/slots/pallas_call | solution.py:137
  47.3 3.5 %collective-permute-start.3 = (f32[2,4,3,64,256]{4,3,2,1,0:T(8,128)}, f32[2,4,3,64,256]{4,3,2,1,0:T(8,128)S(1)}, u32[]{:S(2)}, u32[]{:S(2)}) collective-permute-start(f32[2,4,3,64,256]{4,3,2,1,0:T(8,128)} %get-tuple-element.8), channel_id=1, source_target_pairs={{0,4},{4,8},{8,12},{1,5},{5,9},{9,13},{2,6},{6,10},{10,14},{3,7},{... | collective-permute-start | bytes 4718600 | tf_op jit(solution)/shard_map/ppermute | solution.py:161
  50.8 3.8 %collective-permute-start.5 = (f32[16,5,8,256]{3,2,1,0:T(8,128)}, f32[16,5,8,256]{3,2,1,0:T(8,128)S(1)}, u32[]{:S(2)}, u32[]{:S(2)}) collective-permute-start(f32[16,5,8,256]{3,2,1,0:T(8,128)} %get-tuple-element.11), channel_id=1, source_target_pairs={{0,16},{16,0},{32,48},{48,32},{64,80},{80,64},{96,112},{112,96},{1... | collective-permute-start | bytes 1966088 | tf_op jit(solution)/shard_map/ppermute | solution.py:166
  54.6 1.9 %collective-permute-done.5 = f32[16,5,8,256]{3,2,1,0:T(8,128)S(1)} collective-permute-done((f32[16,5,8,256]{3,2,1,0:T(8,128)}, f32[16,5,8,256]{3,2,1,0:T(8,128)S(1)}, u32[]{:S(2)}, u32[]{:S(2)}) %collective-permute-start.5) | collective-permute-done | bytes 655392 | tf_op jit(solution)/shard_map/ppermute | solution.py:166
  56.5 1.2 add.71
  57.8 35.3 %all_to_all.20 = f32[16,5,8,256]{3,2,1,0:T(8,128)S(1)} all-to-all(f32[16,5,8,256]{3,2,1,0:T(8,128)S(1)} %add.71), channel_id=1, replica_groups=mesh['tile'=32,'band'=4,'pos'=4] {'band','pos'}, dimensions={0} | all-to-all | bytes 1310720 | tf_op jit(solution)/shard_map/all_to_all | solution.py:170
  93.1 5.2 %collective-permute-start.6 = (f32[5,8,256]{2,1,0:T(8,128)S(1)}, f32[5,8,256]{2,1,0:T(8,128)S(1)}, u32[]{:S(2)}, u32[]{:S(2)}) collective-permute-start(f32[5,8,256]{2,1,0:T(8,128)S(1)} %reduce_sum.19), channel_id=1, source_target_pairs={{0,32},{16,48},{32,0},{48,16},{64,96},{80,112},{96,64},{112,80},{1... | collective-permute-start | bytes 122888 | tf_op jit(solution)/shard_map/ppermute | solution.py:166
  98.4 0.0 collective-permute-done.3
  98.4 0.0 copy-done.2
  98.4 1.0 fusion
  99.4 3.9 %collective-permute-start.4 = (f32[4,3,64,256]{3,2,1,0:T(8,128)}, f32[4,3,64,256]{3,2,1,0:T(8,128)}, u32[]{:S(2)}, u32[]{:S(2)}) collective-permute-start(f32[4,3,64,256]{3,2,1,0:T(8,128)} %fusion), channel_id=1, source_target_pairs={{0,16},{16,32},{32,48},{48,64},{64,80},{80,96},{96,112},{112,128},... | collective-permute-start | bytes 2359304 | tf_op jit(solution)/shard_map/ppermute | solution.py:161
  103.3 0.0 collective-permute-done.6
  103.3 2.3 %collective-permute-start.7 = (f32[5,8,256]{2,1,0:T(8,128)S(1)}, f32[5,8,256]{2,1,0:T(8,128)S(1)}, u32[]{:S(2)}, u32[]{:S(2)}) collective-permute-start(f32[5,8,256]{2,1,0:T(8,128)S(1)} %add.72), channel_id=1, source_target_pairs={{0,64},{16,80},{32,96},{48,112},{64,0},{80,16},{96,32},{112,48},{1... | collective-permute-start | bytes 122888 | tf_op jit(solution)/shard_map/ppermute | solution.py:166
  105.6 5.0 %collective-permute-done.7 = f32[5,8,256]{2,1,0:T(8,128)S(1)} collective-permute-done((f32[5,8,256]{2,1,0:T(8,128)S(1)}, f32[5,8,256]{2,1,0:T(8,128)S(1)}, u32[]{:S(2)}, u32[]{:S(2)}) %collective-permute-start.7) | collective-permute-done | bytes 40992 | tf_op jit(solution)/shard_map/ppermute | solution.py:166
  110.6 9.1 %collective-permute-start.8 = (f32[5,8,256]{2,1,0:T(8,128)S(1)}, f32[5,8,256]{2,1,0:T(8,128)S(1)}, u32[]{:S(2)}, u32[]{:S(2)}) collective-permute-start(f32[5,8,256]{2,1,0:T(8,128)S(1)} %add.73), channel_id=1, source_target_pairs={{0,128},{16,144},{32,160},{48,176},{64,192},{80,208},{96,224},{112... | collective-permute-start | bytes 122888 | tf_op jit(solution)/shard_map/ppermute | solution.py:166
  119.7 2.1 %collective-permute-done.8 = f32[5,8,256]{2,1,0:T(8,128)S(1)} collective-permute-done((f32[5,8,256]{2,1,0:T(8,128)S(1)}, f32[5,8,256]{2,1,0:T(8,128)S(1)}, u32[]{:S(2)}, u32[]{:S(2)}) %collective-permute-start.8) | collective-permute-done | bytes 40992 | tf_op jit(solution)/shard_map/ppermute | solution.py:166
  121.8 11.9 %collective-permute-start.9 = (f32[5,8,256]{2,1,0:T(8,128)S(1)}, f32[5,8,256]{2,1,0:T(8,128)S(1)}, u32[]{:S(2)}, u32[]{:S(2)}) collective-permute-start(f32[5,8,256]{2,1,0:T(8,128)S(1)} %add.74), channel_id=1, source_target_pairs={{0,256},{16,272},{32,288},{48,304},{64,320},{80,336},{96,352},{112... | collective-permute-start | bytes 122888 | tf_op jit(solution)/shard_map/ppermute | solution.py:166
  133.8 3.4 %collective-permute-done.9 = f32[5,8,256]{2,1,0:T(8,128)S(1)} collective-permute-done((f32[5,8,256]{2,1,0:T(8,128)S(1)}, f32[5,8,256]{2,1,0:T(8,128)S(1)}, u32[]{:S(2)}, u32[]{:S(2)}) %collective-permute-start.9) | collective-permute-done | bytes 40992 | tf_op jit(solution)/shard_map/ppermute | solution.py:166
  137.2 0.8 fusion.5
  137.9 0.8 broadcast_in_dim.9
  138.8 3.6 %all-to-all-start.3 = ((f32[16,4,8,256]{3,2,1,0:T(8,128)}), f32[16,4,8,256]{3,2,1,0:T(8,128)S(1)}, u32[]{:S(2)}, u32[]{:S(2)}) async-start(f32[16,4,8,256]{3,2,1,0:T(8,128)} %broadcast_in_dim.9), calls=%async_computation.3 | async-start | bytes 1048576 | tf_op jit(solution)/shard_map/all_to_all | solution.py:170
  142.4 0.0 collective-permute-done.4
  142.4 0.0 copy-done.1
  142.4 2.2 %fusion.2 = f32[4,3,64,256]{3,2,1,0:T(8,128)} fusion(f32[4,3,64,256]{3,2,1,0:T(8,128)} %collective-permute-done.4, f32[4,3,64,256]{3,2,1,0:T(8,128)S(1)} %copy-done.1, f32[2,4,3,64,256]{4,3,2,1,0:T(8,128)S(1)} %collective-permute-done.3), kind=kLoop, calls=%fused_computation.5 | loop fusion | flops 393216 | bytes 3145728 | tf_op jit(solution)/shard_map/add | solution.py:190
  144.6 9.2 %all-to-all-done.3 = f32[16,4,8,256]{3,2,1,0:T(8,128)S(1)} async-done(((f32[16,4,8,256]{3,2,1,0:T(8,128)}), f32[16,4,8,256]{3,2,1,0:T(8,128)S(1)}, u32[]{:S(2)}, u32[]{:S(2)}) %all-to-all-start.3) | async-done | bytes 524320 | tf_op jit(solution)/shard_map/all_to_all | solution.py:170
  153.8 3.5 %all-to-all-start = ((f32[4,3,64,256]{3,2,1,0:T(8,128)}), f32[4,3,64,256]{3,2,1,0:T(8,128)S(1)}, u32[]{:S(2)}, u32[]{:S(2)}) async-start(f32[4,3,64,256]{3,2,1,0:T(8,128)} %fusion.2), calls=%async_computation | async-start | bytes 1572864 | tf_op jit(solution)/shard_map/all_to_all | solution.py:170
  157.3 3.2 %collective-permute-start.10 = (f32[16,4,8,256]{3,2,0,1:T(8,128)S(1)}, f32[16,4,8,256]{3,2,0,1:T(8,128)S(1)}, u32[]{:S(2)}, u32[]{:S(2)}) collective-permute-start(f32[16,4,8,256]{3,2,0,1:T(8,128)S(1)} %copy.17), channel_id=1, source_target_pairs={{0,16},{16,0},{32,48},{48,32},{64,80},{80,64},{96,112},{112,96},{1... | collective-permute-start | bytes 1572872 | tf_op jit(solution)/shard_map/ppermute | solution.py:166
  160.5 10.1 %all-to-all-done = f32[4,3,64,256]{3,2,1,0:T(8,128)S(1)} async-done(((f32[4,3,64,256]{3,2,1,0:T(8,128)}), f32[4,3,64,256]{3,2,1,0:T(8,128)S(1)}, u32[]{:S(2)}, u32[]{:S(2)}) %all-to-all-start) | async-done | bytes 786464 | tf_op jit(solution)/shard_map/all_to_all | solution.py:170
  170.6 0.1 reduce_sum.18
  170.7 0.9 fusion.3
  171.6 0.8 broadcast_in_dim.8
  172.5 3.5 %all-to-all-start.1 = ((f32[4,2,64,256]{3,2,1,0:T(8,128)}), f32[4,2,64,256]{3,2,1,0:T(8,128)S(1)}, u32[]{:S(2)}, u32[]{:S(2)}) async-start(f32[4,2,64,256]{3,2,1,0:T(8,128)} %broadcast_in_dim.8), calls=%async_computation.1 | async-start | bytes 1048576 | tf_op jit(solution)/shard_map/all_to_all | solution.py:170
  175.9 0.0 collective-permute-done.10
  175.9 0.1 select_bitcast_fusion.1
  176.1 1.0 pad_maximum_fusion
  177.1 8.9 %all-to-all-done.1 = f32[4,2,64,256]{3,2,1,0:T(8,128)S(1)} async-done(((f32[4,2,64,256]{3,2,1,0:T(8,128)}), f32[4,2,64,256]{3,2,1,0:T(8,128)S(1)}, u32[]{:S(2)}, u32[]{:S(2)}) %all-to-all-start.1) | async-done | bytes 524320 | tf_op jit(solution)/shard_map/all_to_all | solution.py:170
  186.0 0.8 copy.15
  (11 shorter events, 0.1 us)
Async XLA Ops:
  0.6 15.8 %collective-permute-start = (f32[2,256,256]{2,1,0:T(8,128)}, f32[2,256,256]{2,1,0:T(8,128)S(1)}, u32[]{:S(2)}, u32[]{:S(2)}) collective-permute-start(f32[2,256,256]{2,1,0:T(8,128)} %own.1), channel_id=1, source_target_pairs={{4,0},{8,4},{12,8},{5,1},{9,5},{13,9},{6,2},{10,6},{14,10},{7,3},{... | collective-permute-start | bytes 1572872 | tf_op jit(solution)/shard_map/ppermute | solution.py:161
  1.9 17.9 %collective-permute-start.1 = (f32[2,256,256]{2,1,0:T(8,128)}, f32[2,256,256]{2,1,0:T(8,128)S(1)}, u32[]{:S(2)}, u32[]{:S(2)}) collective-permute-start(f32[2,256,256]{2,1,0:T(8,128)} %own.1), channel_id=1, source_target_pairs={{16,0},{32,16},{48,32},{64,48},{80,64},{96,80},{112,96},{128,112},... | collective-permute-start | bytes 1572872 | tf_op jit(solution)/shard_map/ppermute | solution.py:161
  16.4 8.6 %collective-permute-start.2 = (f32[2,256,256]{2,1,0:T(8,128)S(1)}, f32[2,256,256]{2,1,0:T(8,128)S(1)}, u32[]{:S(2)}, u32[]{:S(2)}) collective-permute-start(f32[2,256,256]{2,1,0:T(8,128)S(1)} %collective-permute-done.right), channel_id=1, source_target_pairs={{16,0},{32,16},{48,32},{64,48},{80,64},{96,80},{112,96},{128,112},... | collective-permute-start | bytes 1572872 | tf_op jit(solution)/shard_map/ppermute | solution.py:161
  25.0 0.8 copy-start.3
  25.8 1.0 copy-start
  47.3 51.1 %collective-permute-start.3 = (f32[2,4,3,64,256]{4,3,2,1,0:T(8,128)}, f32[2,4,3,64,256]{4,3,2,1,0:T(8,128)S(1)}, u32[]{:S(2)}, u32[]{:S(2)}) collective-permute-start(f32[2,4,3,64,256]{4,3,2,1,0:T(8,128)} %get-tuple-element.8), channel_id=1, source_target_pairs={{0,4},{4,8},{8,12},{1,5},{5,9},{9,13},{2,6},{6,10},{10,14},{3,7},{... | collective-permute-start | bytes 4718600 | tf_op jit(solution)/shard_map/ppermute | solution.py:161
  50.8 5.8 %collective-permute-start.5 = (f32[16,5,8,256]{3,2,1,0:T(8,128)}, f32[16,5,8,256]{3,2,1,0:T(8,128)S(1)}, u32[]{:S(2)}, u32[]{:S(2)}) collective-permute-start(f32[16,5,8,256]{3,2,1,0:T(8,128)} %get-tuple-element.11), channel_id=1, source_target_pairs={{0,16},{16,0},{32,48},{48,32},{64,80},{80,64},{96,112},{112,96},{1... | collective-permute-start | bytes 1966088 | tf_op jit(solution)/shard_map/ppermute | solution.py:166
  56.5 41.8 %copy-start.2 = (f32[4,3,64,256]{3,2,1,0:T(8,128)S(1)}, f32[4,3,64,256]{3,2,1,0:T(8,128)}, u32[]{:S(2)}) copy-start(f32[4,3,64,256]{3,2,1,0:T(8,128)} %get-tuple-element.9) | copy-start | bytes 2359300
  93.1 10.1 %collective-permute-start.6 = (f32[5,8,256]{2,1,0:T(8,128)S(1)}, f32[5,8,256]{2,1,0:T(8,128)S(1)}, u32[]{:S(2)}, u32[]{:S(2)}) collective-permute-start(f32[5,8,256]{2,1,0:T(8,128)S(1)} %reduce_sum.19), channel_id=1, source_target_pairs={{0,32},{16,48},{32,0},{48,16},{64,96},{80,112},{96,64},{112,80},{1... | collective-permute-start | bytes 122888 | tf_op jit(solution)/shard_map/ppermute | solution.py:166
  99.4 43.0 %copy-start.1 = (f32[4,3,64,256]{3,2,1,0:T(8,128)S(1)}, f32[4,3,64,256]{3,2,1,0:T(8,128)}, u32[]{:S(2)}) copy-start(f32[4,3,64,256]{3,2,1,0:T(8,128)} %get-tuple-element.7) | copy-start | bytes 2359300
  99.4 43.0 %collective-permute-start.4 = (f32[4,3,64,256]{3,2,1,0:T(8,128)}, f32[4,3,64,256]{3,2,1,0:T(8,128)}, u32[]{:S(2)}, u32[]{:S(2)}) collective-permute-start(f32[4,3,64,256]{3,2,1,0:T(8,128)} %fusion), channel_id=1, source_target_pairs={{0,16},{16,32},{32,48},{48,64},{64,80},{80,96},{96,112},{112,128},... | collective-permute-start | bytes 2359304 | tf_op jit(solution)/shard_map/ppermute | solution.py:161
  103.3 7.3 %collective-permute-start.7 = (f32[5,8,256]{2,1,0:T(8,128)S(1)}, f32[5,8,256]{2,1,0:T(8,128)S(1)}, u32[]{:S(2)}, u32[]{:S(2)}) collective-permute-start(f32[5,8,256]{2,1,0:T(8,128)S(1)} %add.72), channel_id=1, source_target_pairs={{0,64},{16,80},{32,96},{48,112},{64,0},{80,16},{96,32},{112,48},{1... | collective-permute-start | bytes 122888 | tf_op jit(solution)/shard_map/ppermute | solution.py:166
  110.6 11.2 %collective-permute-start.8 = (f32[5,8,256]{2,1,0:T(8,128)S(1)}, f32[5,8,256]{2,1,0:T(8,128)S(1)}, u32[]{:S(2)}, u32[]{:S(2)}) collective-permute-start(f32[5,8,256]{2,1,0:T(8,128)S(1)} %add.73), channel_id=1, source_target_pairs={{0,128},{16,144},{32,160},{48,176},{64,192},{80,208},{96,224},{112... | collective-permute-start | bytes 122888 | tf_op jit(solution)/shard_map/ppermute | solution.py:166
  121.8 15.3 %collective-permute-start.9 = (f32[5,8,256]{2,1,0:T(8,128)S(1)}, f32[5,8,256]{2,1,0:T(8,128)S(1)}, u32[]{:S(2)}, u32[]{:S(2)}) collective-permute-start(f32[5,8,256]{2,1,0:T(8,128)S(1)} %add.74), channel_id=1, source_target_pairs={{0,256},{16,272},{32,288},{48,304},{64,320},{80,336},{96,352},{112... | collective-permute-start | bytes 122888 | tf_op jit(solution)/shard_map/ppermute | solution.py:166
  138.8 15.0 %all-to-all-start.3 = ((f32[16,4,8,256]{3,2,1,0:T(8,128)}), f32[16,4,8,256]{3,2,1,0:T(8,128)S(1)}, u32[]{:S(2)}, u32[]{:S(2)}) async-start(f32[16,4,8,256]{3,2,1,0:T(8,128)} %broadcast_in_dim.9), calls=%async_computation.3 | async-start | bytes 1048576 | tf_op jit(solution)/shard_map/all_to_all | solution.py:170
  153.8 16.8 %all-to-all-start = ((f32[4,3,64,256]{3,2,1,0:T(8,128)}), f32[4,3,64,256]{3,2,1,0:T(8,128)S(1)}, u32[]{:S(2)}, u32[]{:S(2)}) async-start(f32[4,3,64,256]{3,2,1,0:T(8,128)} %fusion.2), calls=%async_computation | async-start | bytes 1572864 | tf_op jit(solution)/shard_map/all_to_all | solution.py:170
  157.3 18.6 %collective-permute-start.10 = (f32[16,4,8,256]{3,2,0,1:T(8,128)S(1)}, f32[16,4,8,256]{3,2,0,1:T(8,128)S(1)}, u32[]{:S(2)}, u32[]{:S(2)}) collective-permute-start(f32[16,4,8,256]{3,2,0,1:T(8,128)S(1)} %copy.17), channel_id=1, source_target_pairs={{0,16},{16,0},{32,48},{48,32},{64,80},{80,64},{96,112},{112,96},{1... | collective-permute-start | bytes 1572872 | tf_op jit(solution)/shard_map/ppermute | solution.py:166
  172.5 13.5 %all-to-all-start.1 = ((f32[4,2,64,256]{3,2,1,0:T(8,128)}), f32[4,2,64,256]{3,2,1,0:T(8,128)S(1)}, u32[]{:S(2)}, u32[]{:S(2)}) async-start(f32[4,2,64,256]{3,2,1,0:T(8,128)} %broadcast_in_dim.8), calls=%async_computation.1 | async-start | bytes 1048576 | tf_op jit(solution)/shard_map/all_to_all | solution.py:170

commit v2 on v1

v2 whole, which is shorter than its diff:
```python
import functools
import math

import jax
import jax.numpy as jnp
import ml_dtypes
import numpy as np
from jax import lax
from jax.experimental import pallas as pl
from jax.experimental.pallas import tpu as pltpu
from jax.sharding import PartitionSpec as P

S = 256
QUARTERS = 4


def tables():
    index = np.arange(S)
    angle = (index[:, None] * index[None, :] % S) * (2.0 * math.pi / S)
    cosine, sine = np.cos(angle) / 16.0, np.sin(angle) / 16.0
    left = np.block([[cosine, sine], [-sine, cosine]]).astype(np.float32)
    head = left.astype(ml_dtypes.bfloat16)
    rest = (left - head.astype(np.float32)).astype(ml_dtypes.bfloat16)
    return (head, rest, np.ascontiguousarray(head.T), np.ascontiguousarray(rest.T))


def split(value):
    head = value.astype(jnp.bfloat16)
    return head, (value - head.astype(jnp.float32)).astype(jnp.bfloat16)


def product(first, second):
    dot = functools.partial(jnp.dot, preferred_element_type=jnp.float32)
    return dot(first[0], second[0]) + dot(first[0], second[1]) + dot(first[1], second[0])


def regroup(value):
    return jnp.concatenate(
        [
            jnp.concatenate([value[:S, :S], value[S:, :S]], axis=1),
            jnp.concatenate([value[:S, S:], value[S:, S:]], axis=1),
        ],
        axis=0,
    )


def cut(block, row, column):
    height = block.shape[0]
    lane = lax.broadcasted_iota(jnp.int32, (height, 128), 1)
    turned = [pltpu.roll(block[:, k * 128 : k * 128 + 128], 128 - column, 1) for k in range(3)]
    block = jnp.concatenate(
        [jnp.where(lane < 128 - column, turned[k], turned[k + 1]) for k in range(2)], axis=1
    )
    turned = pltpu.roll(block.reshape(height // 8, 8, S), 8 - row, 1)
    within = lax.broadcasted_iota(jnp.int32, (height // 8 - 1, 8, S), 1)
    return jnp.where(within < 8 - row, turned[:-1], turned[1:]).reshape(height - 8, S)


def placed(value, row, column):
    turned = pltpu.roll(value.reshape(S // 8, 8, S), row, 1)
    gap = jnp.zeros((1, 8, S), jnp.float32)
    within = lax.broadcasted_iota(jnp.int32, (S // 8 + 1, 8, S), 1)
    value = jnp.where(
        within < row, jnp.concatenate([gap, turned], axis=0), jnp.concatenate([turned, gap], axis=0)
    ).reshape(S + 8, S)
    lane = lax.broadcasted_iota(jnp.int32, (S + 8, 128), 1)
    turned = [pltpu.roll(value[:, k * 128 : k * 128 + 128], column, 1) for k in range(2)]
    return jnp.concatenate(
        [
            jnp.where(lane < column, 0.0, turned[0]),
            jnp.where(lane < column, turned[0], turned[1]),
            jnp.where(lane < column, turned[1], 0.0),
        ],
        axis=1,
    )


def slots_kernel(
    places, scalars, own, right, below, corner_a, corner_b, probe, frames, lh, lr, rh, rr, after,
    left_half, right_half, keep, send, extended, total, terms,
):
    extended[:, :S, :S] = own[...]
    extended[:, :S, S:] = right[...]
    extended[:, S:, :S] = below[...]
    extended[:, S:, S:] = corner_a[...] + corner_b[...]
    total[...] = jnp.zeros_like(total)
    terms[...] = jnp.zeros_like(terms)
    blank = jnp.zeros((S, S), jnp.float32)

    def one_slot(slot, carry):
        row, column = places[slot, 0], places[slot, 1]
        inside = lax.rem(row, 8)
        band_rows = pl.ds(pl.multiple_of(row - inside, 8), S + 8)
        fine = lax.rem(column, 128)
        band_columns = pl.ds(pl.multiple_of(column - fine, 128), 384)
        patch_real, patch_imag = (cut(extended[p, band_rows, band_columns], inside, fine) for p in range(2))
        left_table, right_table = (lh[...], lr[...]), (rh[...], rr[...])
        RC = 256
        wave = []
        for m in range(2):
            real = probe[0, m] * patch_real - probe[1, m] * patch_imag
            imag = probe[0, m] * patch_imag + probe[1, m] * patch_real
            wave.append(product(left_table, split(jnp.concatenate([real, imag], axis=0))))
        back = [[], []]
        for at in range(0, S, RC):
            part = slice(at, at + RC)
            far = [
                jnp.concatenate([wave[m][at : at + RC], wave[m][S + at : S + at + RC]], axis=1)
                for m in range(2)
            ]
            far = product(split(jnp.concatenate(far, axis=0)), right_table)
            power = far[:RC] * far[:RC] + far[RC:] * far[RC:]
            power = power[:, :S] + power[:, S:]
            change = jnp.sqrt(frames[slot, part]) / jnp.sqrt(power + 1.0) - 1.0
            change = jnp.concatenate([change, change], axis=0)
            swapped = jnp.concatenate([far[:, S:] * change, far[:, :S] * change], axis=1)
            chunk = product(split(swapped), right_table)
            for m in range(2):
                back[m].append(chunk[m * RC : m * RC + RC])
        object_real, object_imag = blank, blank
        for m in range(2):
            whole = jnp.concatenate([c[:, :S] for c in back[m]] + [c[:, S:] for c in back[m]], axis=0)
            chi = product(left_table, split(whole))
            chi_imag, chi_real = chi[:S], chi[S:]
            object_real += probe[0, m] * chi_real + probe[1, m] * chi_imag
            object_imag += probe[0, m] * chi_imag - probe[1, m] * chi_real
            terms[m] += patch_real * chi_real + patch_imag * chi_imag
            terms[2 + m] += patch_real * chi_imag - patch_imag * chi_real
        terms[4] += patch_real * patch_real + patch_imag * patch_imag
        for plane, value in enumerate((object_real, object_imag)):
            total[plane, band_rows, band_columns] += placed(value, inside, fine)
        return carry

    lax.fori_loop(0, scalars[0], one_slot, 0)
    left_half[...] = total[:, :, :S]
    right_half[...] = total[:, :, S:]
    chunks, _, height, _ = keep.shape
    core = scalars[1]
    for chunk in range(chunks):
        mine = pl.multiple_of(core * (S // 2) + chunk * height, height)
        other = pl.multiple_of((1 - core) * (S // 2) + chunk * height, height)
        for plane in range(5):
            keep[chunk, plane] = terms[plane, pl.ds(mine, height), :]
            send[chunk, plane] = terms[plane, pl.ds(other, height), :]


def run_slots(places, scalars, blocks, probe, frames, chunks, after):
    height = S // 2 // chunks
    f32 = jnp.float32
    vmem = pl.BlockSpec(memory_space=pltpu.VMEM)
    smem = pl.BlockSpec(memory_space=pltpu.SMEM)
    return pl.pallas_call(
        slots_kernel,
        out_shape=(
            jax.ShapeDtypeStruct((2, 2 * S, S), f32),
            jax.ShapeDtypeStruct((2, 2 * S, S), f32),
            jax.ShapeDtypeStruct((chunks, 5, height, S), f32),
            jax.ShapeDtypeStruct((chunks, 5, height, S), f32),
        ),
        in_specs=[smem] * 2 + [vmem] * 11 + [pl.BlockSpec(memory_space=pl.ANY)],
        out_specs=[vmem] * 4,
        scratch_shapes=[
            pltpu.VMEM((2, 2 * S, 2 * S), f32),
            pltpu.VMEM((2, 2 * S, 2 * S), f32),
            pltpu.VMEM((5, S, S), f32),
        ],
        compiler_params=pltpu.CompilerParams(vmem_limit_bytes=54 * 1024 * 1024),
        name="slots",
    )(places, scalars, *blocks, probe, frames, *(jnp.asarray(t) for t in tables()), after)


def light_kernel(gathered, scalars, probe, light, padded):
    power = jnp.zeros((S, S), jnp.float32)
    for m in range(2):
        power += probe[0, m] * probe[0, m] + probe[1, m] * probe[1, m]
    padded[...] = jnp.zeros_like(padded)
    padded[S : 2 * S, S : 2 * S] = power
    rows = S // QUARTERS
    band, quarter = scalars[2], scalars[3]
    posts = QUARTERS

    def one_device(number, sum_so_far):
        above, left, post = number // (2 * posts), (number // posts) % 2, number % posts
        source = jnp.maximum(band - left, 0) * posts + post
        live = jnp.where(band >= left, gathered[above, source, 6], 0)

        def one_position(slot, sum_so_far):
            first_row = S + quarter * rows + above * S - gathered[above, source, 2 * slot]
            first_column = S + left * S - gathered[above, source, 2 * slot + 1]
            inside, fine = lax.rem(first_row, 8), lax.rem(first_column, 128)
            block = padded[
                pl.ds(pl.multiple_of(first_row - inside, 8), rows + 8),
                pl.ds(pl.multiple_of(first_column - fine, 128), 384),
            ]
            return sum_so_far + cut(block, inside, fine)

        return lax.fori_loop(0, live, one_position, sum_so_far)

    light[...] = lax.fori_loop(0, 4 * posts, one_device, jnp.zeros((rows, S), jnp.float32))


def run_light(gathered, scalars, probe):
    vmem = pl.BlockSpec(memory_space=pltpu.VMEM)
    smem = pl.BlockSpec(memory_space=pltpu.SMEM)
    return pl.pallas_call(
        light_kernel,
        out_shape=jax.ShapeDtypeStruct((S // QUARTERS, S), jnp.float32),
        in_specs=[smem, smem, vmem],
        out_specs=vmem,
        scratch_shapes=[pltpu.VMEM((3 * S + 8, 3 * S + 128), jnp.float32)],
        compiler_params=pltpu.CompilerParams(vmem_limit_bytes=54 * 1024 * 1024),
        name="light",
    )(gathered, scalars, probe)


def shifted(block, axis, distance):
    devices = range(lax.axis_size(axis))
    route = [(i - distance, i) for i in devices if i - distance in devices]
    return lax.ppermute(block, axis, route)


def crossed(block, bit):
    devices = range(lax.axis_size("tile"))
    return lax.ppermute(block, "tile", [(i, i ^ bit) for i in devices])


def exchanged(block, axes):
    return lax.all_to_all(block, axes, 0, 0)


def shared(block, axes):
    return exchanged(jnp.broadcast_to(block, (lax.axis_size(axes), *block.shape)), axes)


def corners(right, below):
    tiles, bands = lax.axis_size("tile"), lax.axis_size("band")
    across = [(t * bands + b, t * bands + b - 1) for t in range(1, tiles, 2) for b in range(1, bands)]
    beside = [(t, t - 1) for t in range(1, tiles, 2)]
    return lax.ppermute(below, ("tile", "band"), across), lax.ppermute(right, "tile", beside)


def sum_along_z(block):
    bit, tiles = 2, lax.axis_size("tile")
    while bit < tiles:
        if 4 * bit <= tiles:
            one, two, three = (crossed(block, bit * k) for k in (1, 2, 3))
            block = (block + one) + (two + three)
            bit *= 4
        else:
            block = block + crossed(block, bit)
            bit *= 2
    return block


def on_device(object_planes, probe_planes, patterns, offsets, counts):
    core = lax.axis_index("tile") % 2
    band, post = lax.axis_index("band"), lax.axis_index("pos")
    bands, posts = lax.axis_size("band"), lax.axis_size("pos")
    plane = ("band", "pos")
    chunks = bands * posts
    right = shifted(object_planes, "band", -1)
    below = shifted(object_planes, "tile", -1)
    card = jnp.concatenate([offsets.reshape(6), counts.reshape(1), jnp.zeros(1, jnp.int32)])
    cards = shared(jnp.pad(card[None], ((0, 7), (0, 120))), plane)
    cards_above = shifted(cards, "tile", 1)
    corner_a, corner_b = corners(right, below)
    scalars = jnp.stack([counts.reshape(()), core, band, post])
    light = run_light(jnp.stack([cards[:, 0, :8], cards_above[:, 0, :8]]), scalars, probe_planes)
    left_half, right_half, keep, send = run_slots(
        offsets[0, 0, 0], scalars, (object_planes, right, below, corner_a, corner_b),
        probe_planes, patterns[0, 0, 0], chunks, light,
    )

    from_left = shifted(right_half, "band", 1)
    terms = keep + crossed(send, 1)
    terms = jnp.sum(exchanged(terms.reshape(posts, bands, *terms.shape[1:]), "pos"), axis=0)
    terms = jnp.sum(exchanged(terms, "band"), axis=0)
    merged = left_half + from_left
    from_above = shifted(merged[:, S:], "tile", 1)
    terms = sum_along_z(terms)

    rows = S // QUARTERS
    tile_sum = (merged[:, :S] + from_above).reshape(2, QUARTERS, rows, S).transpose(1, 0, 2, 3)
    tile_sum = jnp.sum(exchanged(tile_sum, "pos"), axis=0)
    own_rows = lax.dynamic_slice_in_dim(object_planes, post * rows, rows, 1)
    own_rows = own_rows + tile_sum / (light + 1.0)
    object_new = shared(own_rows, "pos").transpose(1, 0, 2, 3).reshape(object_planes.shape)

    height = S // 2 // chunks
    place = core * (S // 2) + (post * bands + band) * height
    own_probe = lax.dynamic_slice_in_dim(probe_planes.reshape(4, S, S), place, height, 1)
    own_probe = own_probe + terms[:4] / (terms[4] + 1.0)
    mine = shared(own_probe, plane)
    other = crossed(mine, 1)
    halves = jnp.stack(
        [jnp.where(core == 0, mine, other), jnp.where(core == 0, other, mine)]
    )
    halves = halves.reshape(2, bands, posts, 4, height, S).transpose(3, 0, 2, 1, 4, 5)
    probe_new = halves.reshape(probe_planes.shape)
    return (object_new, probe_new)


def solution(mesh):
    in_specs = (
        P(None, "tile", "band"),
        P(),
        P("tile", "band", "pos", None, None, None),
        P("tile", "band", "pos", None, None),
        P("tile", "band", "pos"),
    )
    out_specs = (P(None, "tile", "band"), P())
    return jax.shard_map(
        on_device, mesh=mesh, in_specs=in_specs, out_specs=out_specs, check_vma=False
    )
```

time: 188 us -> 179 us (0.952)
  starting transfers between devices: 58.5 us -> 75.5 us
  waiting for transfers between devices: 58.3 us -> 45.1 us
  Pallas kernels: 20.4 us -> 13.8 us
  blocking collectives: 35.3 us -> 29.8 us
  other arithmetic: 7.5 us -> 4.69 us
  local copies, waits for them, and re-layouts: 5.18 us -> 7.35 us
    ppermute x5, waiting for transfers between devices: 17.7 us -> 6.45 us  [shifted(): return lax.ppermute(block, axis, route)]
    all_to_all x3 -> x4, starting transfers between devices: 10.5 us -> 21.4 us  [exchanged(): return lax.all_to_all(block, axes, 0, 0)]
    ppermute x6 -> x8, starting transfers between devices: 35.5 us -> 43.4 us  [crossed(): return lax.ppermute(block, 'tile', [(i, i ^ bit) for i in devices])]
    pallas_call x1 -> x2, Pallas kernels: 20.4 us -> 13.8 us  [the longest x1 9.53 us: run_slots(): pl.pallas_call(slots_kernel, out_shape=(jax.ShapeDtypeStruct((2, 2 * S, S...]
    all_to_all x1 -> x2, blocking collectives: 35.3 us -> 29.8 us  [exchanged(): return lax.all_to_all(block, axes, 0, 0)]
    ppermute x6 -> x8, waiting for transfers between devices: 12.5 us -> 8.12 us  [crossed(): return lax.ppermute(block, 'tile', [(i, i ^ bit) for i in devices])]
    ppermute x5, starting transfers between devices: 12.5 us -> 8.66 us  [shifted(): return lax.ppermute(block, axis, route)]
    add x7 -> x6, other arithmetic: 4.16 us -> 1.18 us  [the longest x2 0.95 us: on_device(): own_rows = own_rows + tile_sum / (light + 1.0)]
  transfers between devices with their start and end apart: 14 -> 19, of which waited for: 9 -> 9; matrix products, arithmetic and copies ran while one was open for 5% -> 5% of each run, Pallas kernels for 0% -> 2%
where the time goes in v2:
time: 179 us; the launch traced here: 178 us
  starting transfers between devices  75.5 us (42%)
  waiting for transfers between devices  45.1 us (25%)
  blocking collectives  29.8 us (17%)
  Pallas kernels  13.8 us (8%)
  local copies, waits for them, and re-layouts  7.35 us (4%)
  other arithmetic  4.69 us (3%)
    ppermute x8, starting transfers between devices, crossed(): return lax.ppermute(block, 'tile', [(i, i ^ bit) for i in devices])  43.4 us
    all_to_all x4, waiting for transfers between devices, exchanged(): return lax.all_to_all(block, axes, 0, 0)  30.5 us
    all_to_all x2, blocking collectives, exchanged(): return lax.all_to_all(block, axes, 0, 0)  29.8 us
    all_to_all x4, starting transfers between devices, exchanged(): return lax.all_to_all(block, axes, 0, 0)  21.4 us
    pallas_call x1, Pallas kernels, run_slots(): pl.pallas_call(slots_kernel, out_shape=(jax.ShapeDtypeStruct((2, 2 * S, S...  9.53 us
    ppermute x5, starting transfers between devices, shifted(): return lax.ppermute(block, axis, route)  8.66 us
    ppermute x8, waiting for transfers between devices, crossed(): return lax.ppermute(block, 'tile', [(i, i ^ bit) for i in devices])  8.12 us
    ppermute x5, waiting for transfers between devices, shifted(): return lax.ppermute(block, axis, route)  6.45 us
  transfers between devices with their start and end apart: 19, of which 9 were waited for; matrix products, arithmetic and copies ran while one was open for 5% of the time, Pallas kernels for 2%

profile of v2, /device:TPU:64, one launch (start us, length us, event | category | flops | bytes accessed | tf_op | source)
XLA Modules:
  0.0 177.9 jit_solution(2140301042438971637)
XLA Ops:
  0.6 1.9 %collective-permute-start.1 = (f32[2,256,256]{2,1,0:T(8,128)}, f32[2,256,256]{2,1,0:T(8,128)S(1)}, u32[]{:S(2)}, u32[]{:S(2)}) collective-permute-start(f32[2,256,256]{2,1,0:T(8,128)} %own.1), channel_id=1, source_target_pairs={{16,0},{32,16},{48,32},{64,48},{80,64},{96,80},{112,96},{128,112},... | collective-permute-start | bytes 1572872 | tf_op jit(solution)/shard_map/ppermute | solution.py:219
  2.6 1.3 collective-permute-start
  4.8 0.6 broadcast_in_dim.15
  5.4 8.2 %all-to-all-start = ((s32[16,8,128]{2,1,0:T(8,128)}), s32[16,8,128]{2,1,0:T(8,128)S(1)}, u32[]{:S(2)}, u32[]{:S(2)}) async-start(s32[16,8,128]{2,1,0:T(8,128)} %broadcast_in_dim.15), calls=%async_computation | async-start | bytes 131072 | tf_op jit(solution)/shard_map/all_to_all | solution.py:228
  13.7 0.7 copy.46.places
  14.4 0.6 pad_add_fusion.1.scalars
  15.0 7.2 %all-to-all-done = s32[16,8,128]{2,1,0:T(8,128)S(1)} async-done(((s32[16,8,128]{2,1,0:T(8,128)}), s32[16,8,128]{2,1,0:T(8,128)S(1)}, u32[]{:S(2)}, u32[]{:S(2)}) %all-to-all-start) | async-done | bytes 65568 | tf_op jit(solution)/shard_map/all_to_all | solution.py:228
  22.2 0.2 copy.42
  22.4 1.9 %collective-permute-start.4 = (s32[16,8,128]{0,2,1:T(8,128)S(1)}, s32[16,8,128]{0,2,1:T(8,128)S(1)}, u32[]{:S(2)}, u32[]{:S(2)}) collective-permute-start(s32[16,8,128]{0,2,1:T(8,128)S(1)} %copy.42), channel_id=1, source_target_pairs={{0,16},{16,32},{32,48},{48,64},{64,80},{80,96},{96,112},{112,128},... | collective-permute-start | bytes 196616 | tf_op jit(solution)/shard_map/ppermute | solution.py:219
  24.3 0.7 collective-permute-start.2
  25.0 1.3 collective-permute-start.3
  26.4 6.4 %collective-permute-done.4 = s32[16,8,128]{0,2,1:T(8,128)S(1)} collective-permute-done((s32[16,8,128]{0,2,1:T(8,128)S(1)}, s32[16,8,128]{0,2,1:T(8,128)S(1)}, u32[]{:S(2)}, u32[]{:S(2)}) %collective-permute-start.4) | collective-permute-done | bytes 65568 | tf_op jit(solution)/shard_map/ppermute | solution.py:219
  32.9 0.6 pad_add_fusion.gathered
  33.6 4.3 %light.1.after = f32[64,256]{1,0:T(8,128)} custom-call(s32[2,16,8]{2,1,0:T(8,128)} %pad_add_fusion.gathered, s32[4]{0:T(128)} %pad_add_fusion.1.scalars, f32[2,2,256,256]{3,2,1,0:T(8,128)} %probe.3), custom_call_target="tpu_custom_call" | custom-call | tf_op jit(solution)/shard_map/light/pallas_call | solution.py:205
  37.9 0.8 copy-done.4
  38.7 0.2 copy-done.5
  38.9 9.5 %slots.1 = (f32[2,512,256]{2,1,0:T(8,128)}, f32[2,512,256]{2,1,0:T(8,128)}, f32[16,5,8,256]{3,2,1,0:T(8,128)}, f32[16,5,8,256]{3,2,1,0:T(8,128)}) custom-call(s32[3,2]{1,0:T(4,128)} %copy.46.places, s32[4]{0:T(128)} %pad_add_fusion.1.scalars, f32[2,256,256]{2,1,0:T(8,128)} %own.1, f32[2,256,256]{2,1,0:T(8,128)} %copy-done.3, f32[2,256,256]{2,1,0:T(8,128)} %copy-done.2, ...), custom_call_target="tpu_custom_call" | custom-call | tf_op jit(solution)/shard_map/slots/pallas_call | solution.py:152
  48.4 10.3 %collective-permute-start.7 = (f32[16,5,8,256]{3,2,1,0:T(8,128)}, f32[16,5,8,256]{3,2,1,0:T(8,128)S(1)}, u32[]{:S(2)}, u32[]{:S(2)}) collective-permute-start(f32[16,5,8,256]{3,2,1,0:T(8,128)} %get-tuple-element.9), channel_id=1, source_target_pairs={{0,16},{16,0},{32,48},{48,32},{64,80},{80,64},{96,112},{112,96},{1... | collective-permute-start | bytes 1966088 | tf_op jit(solution)/shard_map/ppermute | solution.py:224
  58.7 1.6 collective-permute-start.5
  60.3 0.3 collective-permute-done.7
  60.6 1.2 add.74
  61.8 18.4 %all_to_all.30 = f32[4,4,5,8,256]{4,3,2,1,0:T(8,128)S(1)} all-to-all(f32[4,4,5,8,256]{4,3,2,1,0:T(8,128)S(1)} %bitcast.31), channel_id=1, replica_groups=mesh['tile'=32,'band'=4,'pos'=4] {'pos'}, dimensions={0} | all-to-all | bytes 1310720 | tf_op jit(solution)/shard_map/all_to_all | solution.py:228
  80.3 11.4 %all_to_all.31 = f32[4,5,8,256]{3,2,1,0:T(8,128)S(1)} all-to-all(f32[4,5,8,256]{3,2,1,0:T(8,128)S(1)} %reduce_sum.28), channel_id=1, replica_groups=mesh['tile'=32,'band'=4,'pos'=4] {'band'}, dimensions={0} | all-to-all | bytes 327680 | tf_op jit(solution)/shard_map/all_to_all | solution.py:228
  91.7 1.9 %collective-permute-start.10 = (f32[5,8,256]{2,1,0:T(8,128)S(1)}, f32[5,8,256]{2,1,0:T(8,128)S(1)}, u32[]{:S(2)}, u32[]{:S(2)}) collective-permute-start(f32[5,8,256]{2,1,0:T(8,128)S(1)} %reduce_sum.29), channel_id=1, source_target_pairs={{0,96},{16,112},{32,64},{48,80},{64,32},{80,48},{96,0},{112,16},{1... | collective-permute-start | bytes 122888 | tf_op jit(solution)/shard_map/ppermute | solution.py:224
  93.6 4.1 %collective-permute-start.8 = (f32[5,8,256]{2,1,0:T(8,128)S(1)}, f32[5,8,256]{2,1,0:T(8,128)S(1)}, u32[]{:S(2)}, u32[]{:S(2)}) collective-permute-start(f32[5,8,256]{2,1,0:T(8,128)S(1)} %reduce_sum.29), channel_id=1, source_target_pairs={{0,32},{16,48},{32,0},{48,16},{64,96},{80,112},{96,64},{112,80},{1... | collective-permute-start | bytes 122888 | tf_op jit(solution)/shard_map/ppermute | solution.py:224
  97.7 4.3 %collective-permute-start.9 = (f32[5,8,256]{2,1,0:T(8,128)S(1)}, f32[5,8,256]{2,1,0:T(8,128)S(1)}, u32[]{:S(2)}, u32[]{:S(2)}) collective-permute-start(f32[5,8,256]{2,1,0:T(8,128)S(1)} %reduce_sum.29), channel_id=1, source_target_pairs={{0,64},{16,80},{32,96},{48,112},{64,0},{80,16},{96,32},{112,48},{1... | collective-permute-start | bytes 122888 | tf_op jit(solution)/shard_map/ppermute | solution.py:224
  102.0 2.6 %collective-permute-done.9 = f32[5,8,256]{2,1,0:T(8,128)S(1)} collective-permute-done((f32[5,8,256]{2,1,0:T(8,128)S(1)}, f32[5,8,256]{2,1,0:T(8,128)S(1)}, u32[]{:S(2)}, u32[]{:S(2)}) %collective-permute-start.9) | collective-permute-done | bytes 40992 | tf_op jit(solution)/shard_map/ppermute | solution.py:224
  104.6 9.6 %collective-permute-start.11 = (f32[5,8,256]{2,1,0:T(8,128)S(1)}, f32[5,8,256]{2,1,0:T(8,128)S(1)}, u32[]{:S(2)}, u32[]{:S(2)}) collective-permute-start(f32[5,8,256]{2,1,0:T(8,128)S(1)} %add_add_fusion.1), channel_id=1, source_target_pairs={{0,128},{16,144},{32,160},{48,176},{64,192},{80,208},{96,224},{112... | collective-permute-start | bytes 122888 | tf_op jit(solution)/shard_map/ppermute | solution.py:224
  114.2 8.8 %collective-permute-start.12 = (f32[5,8,256]{2,1,0:T(8,128)S(1)}, f32[5,8,256]{2,1,0:T(8,128)S(1)}, u32[]{:S(2)}, u32[]{:S(2)}) collective-permute-start(f32[5,8,256]{2,1,0:T(8,128)S(1)} %add_add_fusion.1), channel_id=1, source_target_pairs={{0,256},{16,272},{32,288},{48,304},{64,320},{80,336},{96,352},{112... | collective-permute-start | bytes 122888 | tf_op jit(solution)/shard_map/ppermute | solution.py:224
  123.0 2.5 %collective-permute-start.13 = (f32[5,8,256]{2,1,0:T(8,128)S(1)}, f32[5,8,256]{2,1,0:T(8,128)S(1)}, u32[]{:S(2)}, u32[]{:S(2)}) collective-permute-start(f32[5,8,256]{2,1,0:T(8,128)S(1)} %add_add_fusion.1), channel_id=1, source_target_pairs={{0,384},{16,400},{32,416},{48,432},{64,448},{80,464},{96,480},{112... | collective-permute-start | bytes 122888 | tf_op jit(solution)/shard_map/ppermute | solution.py:224
  125.6 0.1 add.66
  125.8 1.9 %collective-permute-start.6 = (f32[2,256,256]{2,1,0:T(8,128)S(1)}, f32[2,256,256]{2,1,0:T(8,128)S(1)}, u32[]{:S(2)}, u32[]{:S(2)}) collective-permute-start(f32[2,256,256]{2,1,0:T(8,128)S(1)} %slice.27), channel_id=1, source_target_pairs={{0,16},{16,32},{32,48},{48,64},{64,80},{80,96},{96,112},{112,128},... | collective-permute-start | bytes 1572872 | tf_op jit(solution)/shard_map/ppermute | solution.py:219
  127.7 1.2 collective-permute-done.12
  128.9 4.0 %collective-permute-done.13 = f32[5,8,256]{2,1,0:T(8,128)S(1)} collective-permute-done((f32[5,8,256]{2,1,0:T(8,128)S(1)}, f32[5,8,256]{2,1,0:T(8,128)S(1)}, u32[]{:S(2)}, u32[]{:S(2)}) %collective-permute-start.13) | collective-permute-done | bytes 40992 | tf_op jit(solution)/shard_map/ppermute | solution.py:224
  132.9 0.8 fusion
  133.7 0.8 broadcast_in_dim.17
  134.6 6.1 %all-to-all-start.5 = ((f32[16,4,8,256]{3,2,1,0:T(8,128)}), f32[16,4,8,256]{3,2,1,0:T(8,128)S(1)}, u32[]{:S(2)}, u32[]{:S(2)}) async-start(f32[16,4,8,256]{3,2,1,0:T(8,128)} %broadcast_in_dim.17), calls=%async_computation.5 | async-start | bytes 1048576 | tf_op jit(solution)/shard_map/all_to_all | solution.py:228
  140.7 0.8 copy.51
  141.5 9.2 %all-to-all-done.5 = f32[16,4,8,256]{3,2,1,0:T(8,128)S(1)} async-done(((f32[16,4,8,256]{3,2,1,0:T(8,128)}), f32[16,4,8,256]{3,2,1,0:T(8,128)S(1)}, u32[]{:S(2)}, u32[]{:S(2)}) %all-to-all-start.5) | async-done | bytes 524320 | tf_op jit(solution)/shard_map/all_to_all | solution.py:228
  150.7 3.6 %all-to-all-start.1 = ((f32[4,2,64,256]{3,2,1,0:T(8,128)}), f32[4,2,64,256]{3,2,1,0:T(8,128)S(1)}, u32[]{:S(2)}, u32[]{:S(2)}) async-start(f32[4,2,64,256]{3,2,1,0:T(8,128)} %bitcast.27), calls=%async_computation.1 | async-start | bytes 1048576 | tf_op jit(solution)/shard_map/all_to_all | solution.py:228
  154.3 1.9 %collective-permute-start.14 = (f32[16,4,8,256]{3,2,1,0:T(8,128)S(1)}, f32[16,4,8,256]{3,2,1,0:T(8,128)S(1)}, u32[]{:S(2)}, u32[]{:S(2)}) collective-permute-start(f32[16,4,8,256]{3,2,1,0:T(8,128)S(1)} %all-to-all-done.5), channel_id=1, source_target_pairs={{0,16},{16,0},{32,48},{48,32},{64,80},{80,64},{96,112},{112,96},{1... | collective-permute-start | bytes 1572872 | tf_op jit(solution)/shard_map/ppermute | solution.py:224
  156.3 6.1 %all-to-all-done.1 = f32[4,2,64,256]{3,2,1,0:T(8,128)S(1)} async-done(((f32[4,2,64,256]{3,2,1,0:T(8,128)}), f32[4,2,64,256]{3,2,1,0:T(8,128)S(1)}, u32[]{:S(2)}, u32[]{:S(2)}) %all-to-all-start.1) | async-done | bytes 524320 | tf_op jit(solution)/shard_map/all_to_all | solution.py:228
  162.4 0.9 divide_add_fusion
  163.3 0.8 broadcast_in_dim.16
  164.2 3.5 %all-to-all-start.2 = ((f32[4,2,64,256]{3,2,1,0:T(8,128)}), f32[4,2,64,256]{3,2,1,0:T(8,128)S(1)}, u32[]{:S(2)}, u32[]{:S(2)}) async-start(f32[4,2,64,256]{3,2,1,0:T(8,128)} %broadcast_in_dim.16), calls=%async_computation.2 | async-start | bytes 1048576 | tf_op jit(solution)/shard_map/all_to_all | solution.py:228
  167.7 8.0 %all-to-all-done.2 = f32[4,2,64,256]{3,2,1,0:T(8,128)S(1)} async-done(((f32[4,2,64,256]{3,2,1,0:T(8,128)}), f32[4,2,64,256]{3,2,1,0:T(8,128)S(1)}, u32[]{:S(2)}, u32[]{:S(2)}) %all-to-all-start.2) | async-done | bytes 524320 | tf_op jit(solution)/shard_map/all_to_all | solution.py:228
  175.7 0.8 copy.48
  176.8 1.1 copy.49
  (41 shorter events, 0.9 us)
Async XLA Ops:
  0.6 3.9 %copy-start.6 = (s32[1,1,1,3,2]{3,4,2,1,0:T(2,128)S(1)}, s32[1,1,1,3,2]{3,4,2,1,0:T(2,128)}, u32[]{:S(2)}) copy-start(s32[1,1,1,3,2]{3,4,2,1,0:T(2,128)} %param.12) | copy-start | bytes 76
  0.6 23.7 %collective-permute-start.1 = (f32[2,256,256]{2,1,0:T(8,128)}, f32[2,256,256]{2,1,0:T(8,128)S(1)}, u32[]{:S(2)}, u32[]{:S(2)}) collective-permute-start(f32[2,256,256]{2,1,0:T(8,128)} %own.1), channel_id=1, source_target_pairs={{16,0},{32,16},{48,32},{64,48},{80,64},{96,80},{112,96},{128,112},... | collective-permute-start | bytes 1572872 | tf_op jit(solution)/shard_map/ppermute | solution.py:219
  2.6 22.4 %collective-permute-start = (f32[2,256,256]{2,1,0:T(8,128)}, f32[2,256,256]{2,1,0:T(8,128)S(1)}, u32[]{:S(2)}, u32[]{:S(2)}) collective-permute-start(f32[2,256,256]{2,1,0:T(8,128)} %own.1), channel_id=1, source_target_pairs={{4,0},{8,4},{12,8},{5,1},{9,5},{13,9},{6,2},{10,6},{14,10},{7,3},{... | collective-permute-start | bytes 1572872 | tf_op jit(solution)/shard_map/ppermute | solution.py:219
  5.4 16.7 %all-to-all-start = ((s32[16,8,128]{2,1,0:T(8,128)}), s32[16,8,128]{2,1,0:T(8,128)S(1)}, u32[]{:S(2)}, u32[]{:S(2)}) async-start(s32[16,8,128]{2,1,0:T(8,128)} %broadcast_in_dim.15), calls=%async_computation | async-start | bytes 131072 | tf_op jit(solution)/shard_map/all_to_all | solution.py:228
  22.4 10.5 %collective-permute-start.4 = (s32[16,8,128]{0,2,1:T(8,128)S(1)}, s32[16,8,128]{0,2,1:T(8,128)S(1)}, u32[]{:S(2)}, u32[]{:S(2)}) collective-permute-start(s32[16,8,128]{0,2,1:T(8,128)S(1)} %copy.42), channel_id=1, source_target_pairs={{0,16},{16,32},{32,48},{48,64},{64,80},{80,96},{96,112},{112,128},... | collective-permute-start | bytes 196616 | tf_op jit(solution)/shard_map/ppermute | solution.py:219
  24.3 13.6 %copy-start.2 = (f32[2,256,256]{2,1,0:T(8,128)}, f32[2,256,256]{2,1,0:T(8,128)S(1)}, u32[]{:S(2)}) copy-start(f32[2,256,256]{2,1,0:T(8,128)S(1)} %collective-permute-done.1.below) | copy-start | bytes 1572868
  24.3 13.5 %collective-permute-start.2 = (f32[2,256,256]{2,1,0:T(8,128)S(1)}, f32[2,256,256]{2,1,0:T(8,128)S(1)}, u32[]{:S(2)}, u32[]{:S(2)}) collective-permute-start(f32[2,256,256]{2,1,0:T(8,128)S(1)} %collective-permute-done.1.below), channel_id=1, source_target_pairs={{20,16},{24,20},{28,24},{52,48},{56,52},{60,56},{84,80},{88,84},{9... | collective-permute-start | bytes 1572872 | tf_op jit(solution)/shard_map/ppermute | solution.py:239
  25.0 12.8 %copy-start.3 = (f32[2,256,256]{2,1,0:T(8,128)}, f32[2,256,256]{2,1,0:T(8,128)S(1)}, u32[]{:S(2)}) copy-start(f32[2,256,256]{2,1,0:T(8,128)S(1)} %collective-permute-done.right) | copy-start | bytes 1572868
  25.0 12.8 %collective-permute-start.3 = (f32[2,256,256]{2,1,0:T(8,128)S(1)}, f32[2,256,256]{2,1,0:T(8,128)S(1)}, u32[]{:S(2)}, u32[]{:S(2)}) collective-permute-start(f32[2,256,256]{2,1,0:T(8,128)S(1)} %collective-permute-done.right), channel_id=1, source_target_pairs={{16,0},{48,32},{80,64},{112,96},{144,128},{176,160},{208,192},{240... | collective-permute-start | bytes 1572872 | tf_op jit(solution)/shard_map/ppermute | solution.py:239
  37.9 0.8 copy-start.4
  37.9 1.0 copy-start.5
  48.4 12.3 %collective-permute-start.7 = (f32[16,5,8,256]{3,2,1,0:T(8,128)}, f32[16,5,8,256]{3,2,1,0:T(8,128)S(1)}, u32[]{:S(2)}, u32[]{:S(2)}) collective-permute-start(f32[16,5,8,256]{3,2,1,0:T(8,128)} %get-tuple-element.9), channel_id=1, source_target_pairs={{0,16},{16,0},{32,48},{48,32},{64,80},{80,64},{96,112},{112,96},{1... | collective-permute-start | bytes 1966088 | tf_op jit(solution)/shard_map/ppermute | solution.py:224
  58.7 66.8 %collective-permute-start.5 = (f32[2,512,256]{2,1,0:T(8,128)}, f32[2,512,256]{2,1,0:T(8,128)S(1)}, u32[]{:S(2)}, u32[]{:S(2)}) collective-permute-start(f32[2,512,256]{2,1,0:T(8,128)} %get-tuple-element.7), channel_id=1, source_target_pairs={{0,4},{4,8},{8,12},{1,5},{5,9},{9,13},{2,6},{6,10},{10,14},{3,7},{... | collective-permute-start | bytes 3145736 | tf_op jit(solution)/shard_map/ppermute | solution.py:219
  80.2 45.3 %copy-start = (f32[2,512,256]{2,1,0:T(8,128)S(1)}, f32[2,512,256]{2,1,0:T(8,128)}, u32[]{:S(2)}) copy-start(f32[2,512,256]{2,1,0:T(8,128)} %get-tuple-element.6) | copy-start | bytes 3145732
  91.7 10.3 %collective-permute-start.10 = (f32[5,8,256]{2,1,0:T(8,128)S(1)}, f32[5,8,256]{2,1,0:T(8,128)S(1)}, u32[]{:S(2)}, u32[]{:S(2)}) collective-permute-start(f32[5,8,256]{2,1,0:T(8,128)S(1)} %reduce_sum.29), channel_id=1, source_target_pairs={{0,96},{16,112},{32,64},{48,80},{64,32},{80,48},{96,0},{112,16},{1... | collective-permute-start | bytes 122888 | tf_op jit(solution)/shard_map/ppermute | solution.py:224
  93.6 8.4 %collective-permute-start.8 = (f32[5,8,256]{2,1,0:T(8,128)S(1)}, f32[5,8,256]{2,1,0:T(8,128)S(1)}, u32[]{:S(2)}, u32[]{:S(2)}) collective-permute-start(f32[5,8,256]{2,1,0:T(8,128)S(1)} %reduce_sum.29), channel_id=1, source_target_pairs={{0,32},{16,48},{32,0},{48,16},{64,96},{80,112},{96,64},{112,80},{1... | collective-permute-start | bytes 122888 | tf_op jit(solution)/shard_map/ppermute | solution.py:224
  97.7 6.9 %collective-permute-start.9 = (f32[5,8,256]{2,1,0:T(8,128)S(1)}, f32[5,8,256]{2,1,0:T(8,128)S(1)}, u32[]{:S(2)}, u32[]{:S(2)}) collective-permute-start(f32[5,8,256]{2,1,0:T(8,128)S(1)} %reduce_sum.29), channel_id=1, source_target_pairs={{0,64},{16,80},{32,96},{48,112},{64,0},{80,16},{96,32},{112,48},{1... | collective-permute-start | bytes 122888 | tf_op jit(solution)/shard_map/ppermute | solution.py:224
  104.6 23.1 %collective-permute-start.11 = (f32[5,8,256]{2,1,0:T(8,128)S(1)}, f32[5,8,256]{2,1,0:T(8,128)S(1)}, u32[]{:S(2)}, u32[]{:S(2)}) collective-permute-start(f32[5,8,256]{2,1,0:T(8,128)S(1)} %add_add_fusion.1), channel_id=1, source_target_pairs={{0,128},{16,144},{32,160},{48,176},{64,192},{80,208},{96,224},{112... | collective-permute-start | bytes 122888 | tf_op jit(solution)/shard_map/ppermute | solution.py:224
  114.2 14.6 %collective-permute-start.12 = (f32[5,8,256]{2,1,0:T(8,128)S(1)}, f32[5,8,256]{2,1,0:T(8,128)S(1)}, u32[]{:S(2)}, u32[]{:S(2)}) collective-permute-start(f32[5,8,256]{2,1,0:T(8,128)S(1)} %add_add_fusion.1), channel_id=1, source_target_pairs={{0,256},{16,272},{32,288},{48,304},{64,320},{80,336},{96,352},{112... | collective-permute-start | bytes 122888 | tf_op jit(solution)/shard_map/ppermute | solution.py:224
  123.0 9.9 %collective-permute-start.13 = (f32[5,8,256]{2,1,0:T(8,128)S(1)}, f32[5,8,256]{2,1,0:T(8,128)S(1)}, u32[]{:S(2)}, u32[]{:S(2)}) collective-permute-start(f32[5,8,256]{2,1,0:T(8,128)S(1)} %add_add_fusion.1), channel_id=1, source_target_pairs={{0,384},{16,400},{32,416},{48,432},{64,448},{80,464},{96,480},{112... | collective-permute-start | bytes 122888 | tf_op jit(solution)/shard_map/ppermute | solution.py:224
  125.8 14.9 %collective-permute-start.6 = (f32[2,256,256]{2,1,0:T(8,128)S(1)}, f32[2,256,256]{2,1,0:T(8,128)S(1)}, u32[]{:S(2)}, u32[]{:S(2)}) collective-permute-start(f32[2,256,256]{2,1,0:T(8,128)S(1)} %slice.27), channel_id=1, source_target_pairs={{0,16},{16,32},{32,48},{48,64},{64,80},{80,96},{96,112},{112,128},... | collective-permute-start | bytes 1572872 | tf_op jit(solution)/shard_map/ppermute | solution.py:219
  134.6 16.2 %all-to-all-start.5 = ((f32[16,4,8,256]{3,2,1,0:T(8,128)}), f32[16,4,8,256]{3,2,1,0:T(8,128)S(1)}, u32[]{:S(2)}, u32[]{:S(2)}) async-start(f32[16,4,8,256]{3,2,1,0:T(8,128)} %broadcast_in_dim.17), calls=%async_computation.5 | async-start | bytes 1048576 | tf_op jit(solution)/shard_map/all_to_all | solution.py:228
  150.7 3.6 %copy-start.1 = (f32[64,256]{1,0:T(8,128)S(1)}, f32[64,256]{1,0:T(8,128)}, u32[]{:S(2)}) copy-start(f32[64,256]{1,0:T(8,128)} %light.1.after) | copy-start | bytes 196612
  150.7 11.7 %all-to-all-start.1 = ((f32[4,2,64,256]{3,2,1,0:T(8,128)}), f32[4,2,64,256]{3,2,1,0:T(8,128)S(1)}, u32[]{:S(2)}, u32[]{:S(2)}) async-start(f32[4,2,64,256]{3,2,1,0:T(8,128)} %bitcast.27), calls=%async_computation.1 | async-start | bytes 1048576 | tf_op jit(solution)/shard_map/all_to_all | solution.py:228
  154.3 22.2 %collective-permute-start.14 = (f32[16,4,8,256]{3,2,1,0:T(8,128)S(1)}, f32[16,4,8,256]{3,2,1,0:T(8,128)S(1)}, u32[]{:S(2)}, u32[]{:S(2)}) collective-permute-start(f32[16,4,8,256]{3,2,1,0:T(8,128)S(1)} %all-to-all-done.5), channel_id=1, source_target_pairs={{0,16},{16,0},{32,48},{48,32},{64,80},{80,64},{96,112},{112,96},{1... | collective-permute-start | bytes 1572872 | tf_op jit(solution)/shard_map/ppermute | solution.py:224
  164.2 11.5 %all-to-all-start.2 = ((f32[4,2,64,256]{3,2,1,0:T(8,128)}), f32[4,2,64,256]{3,2,1,0:T(8,128)S(1)}, u32[]{:S(2)}, u32[]{:S(2)}) async-start(f32[4,2,64,256]{3,2,1,0:T(8,128)} %broadcast_in_dim.16), calls=%async_computation.2 | async-start | bytes 1048576 | tf_op jit(solution)/shard_map/all_to_all | solution.py:228

commit v3 on v2

v3 whole, which is shorter than its diff:
```python
import functools
import math

import jax
import jax.numpy as jnp
import ml_dtypes
import numpy as np
from jax import lax
from jax.experimental import pallas as pl
from jax.experimental.pallas import tpu as pltpu
from jax.sharding import PartitionSpec as P

S = 256
QUARTERS = 4
COUNT = 6
TILE = ("z_high", "z_low", "core")


def tables():
    index = np.arange(S)
    angle = (index[:, None] * index[None, :] % S) * (2.0 * math.pi / S)
    cosine, sine = np.cos(angle) / 16.0, np.sin(angle) / 16.0
    left = np.block([[cosine, sine], [-sine, cosine]]).astype(np.float32)
    head = left.astype(ml_dtypes.bfloat16)
    rest = (left - head.astype(np.float32)).astype(ml_dtypes.bfloat16)
    return (head, rest, np.ascontiguousarray(head.T), np.ascontiguousarray(rest.T))


def split(value):
    head = value.astype(jnp.bfloat16)
    return head, (value - head.astype(jnp.float32)).astype(jnp.bfloat16)


def product(first, second):
    dot = functools.partial(jnp.dot, preferred_element_type=jnp.float32)
    return dot(first[0], second[0]) + dot(first[0], second[1]) + dot(first[1], second[0])


def regroup(value):
    return jnp.concatenate(
        [
            jnp.concatenate([value[:S, :S], value[S:, :S]], axis=1),
            jnp.concatenate([value[:S, S:], value[S:, S:]], axis=1),
        ],
        axis=0,
    )


def cut(block, row, column):
    height = block.shape[0]
    lane = lax.broadcasted_iota(jnp.int32, (height, 128), 1)
    turned = [pltpu.roll(block[:, k * 128 : k * 128 + 128], 128 - column, 1) for k in range(3)]
    block = jnp.concatenate(
        [jnp.where(lane < 128 - column, turned[k], turned[k + 1]) for k in range(2)], axis=1
    )
    turned = pltpu.roll(block.reshape(height // 8, 8, S), 8 - row, 1)
    within = lax.broadcasted_iota(jnp.int32, (height // 8 - 1, 8, S), 1)
    return jnp.where(within < 8 - row, turned[:-1], turned[1:]).reshape(height - 8, S)


def placed(value, row, column):
    turned = pltpu.roll(value.reshape(S // 8, 8, S), row, 1)
    gap = jnp.zeros((1, 8, S), jnp.float32)
    within = lax.broadcasted_iota(jnp.int32, (S // 8 + 1, 8, S), 1)
    value = jnp.where(
        within < row, jnp.concatenate([gap, turned], axis=0), jnp.concatenate([turned, gap], axis=0)
    ).reshape(S + 8, S)
    lane = lax.broadcasted_iota(jnp.int32, (S + 8, 128), 1)
    turned = [pltpu.roll(value[:, k * 128 : k * 128 + 128], column, 1) for k in range(2)]
    return jnp.concatenate(
        [
            jnp.where(lane < column, 0.0, turned[0]),
            jnp.where(lane < column, turned[0], turned[1]),
            jnp.where(lane < column, turned[1], 0.0),
        ],
        axis=1,
    )


def slots_kernel(
    card, own, right, below, corner_a, corner_b, probe, frames, lh, lr, rh, rr, after,
    top_left, top_right, bottom, keep, send, extended, total, terms,
):
    extended[:, :S, :S] = own[...]
    extended[:, :S, S:] = right[...]
    extended[:, S:, :S] = below[...]
    extended[:, S:, S:] = corner_a[...] + corner_b[...]
    total[...] = jnp.zeros_like(total)
    terms[...] = jnp.zeros_like(terms)
    blank = jnp.zeros((S, S), jnp.float32)

    def one_slot(slot, carry):
        row, column = card[0, 2 * slot], card[0, 2 * slot + 1]
        inside = lax.rem(row, 8)
        band_rows = pl.ds(pl.multiple_of(row - inside, 8), S + 8)
        fine = lax.rem(column, 128)
        band_columns = pl.ds(pl.multiple_of(column - fine, 128), 384)
        patch_real, patch_imag = (cut(extended[p, band_rows, band_columns], inside, fine) for p in range(2))
        left_table, right_table = (lh[...], lr[...]), (rh[...], rr[...])
        RC = 256
        wave = []
        for m in range(2):
            real = probe[0, m] * patch_real - probe[1, m] * patch_imag
            imag = probe[0, m] * patch_imag + probe[1, m] * patch_real
            wave.append(product(left_table, split(jnp.concatenate([real, imag], axis=0))))
        back = [[], []]
        for at in range(0, S, RC):
            part = slice(at, at + RC)
            far = [
                jnp.concatenate([wave[m][at : at + RC], wave[m][S + at : S + at + RC]], axis=1)
                for m in range(2)
            ]
            far = product(split(jnp.concatenate(far, axis=0)), right_table)
            power = far[:RC] * far[:RC] + far[RC:] * far[RC:]
            power = power[:, :S] + power[:, S:]
            change = jnp.sqrt(frames[slot, part]) / jnp.sqrt(power + 1.0) - 1.0
            change = jnp.concatenate([change, change], axis=0)
            swapped = jnp.concatenate([far[:, S:] * change, far[:, :S] * change], axis=1)
            chunk = product(split(swapped), right_table)
            for m in range(2):
                back[m].append(chunk[m * RC : m * RC + RC])
        object_real, object_imag = blank, blank
        for m in range(2):
            whole = jnp.concatenate([c[:, :S] for c in back[m]] + [c[:, S:] for c in back[m]], axis=0)
            chi = product(left_table, split(whole))
            chi_imag, chi_real = chi[:S], chi[S:]
            object_real += probe[0, m] * chi_real + probe[1, m] * chi_imag
            object_imag += probe[0, m] * chi_imag - probe[1, m] * chi_real
            terms[m] += patch_real * chi_real + patch_imag * chi_imag
            terms[2 + m] += patch_real * chi_imag - patch_imag * chi_real
        terms[4] += patch_real * patch_real + patch_imag * patch_imag
        for plane, value in enumerate((object_real, object_imag)):
            total[plane, band_rows, band_columns] += placed(value, inside, fine)
        return carry

    lax.fori_loop(0, card[0, COUNT], one_slot, 0)
    rows = S // QUARTERS
    for q in range(QUARTERS):
        upper, lower = slice(q * rows, (q + 1) * rows), slice(S + q * rows, S + (q + 1) * rows)
        top_left[q] = total[:, upper, :S]
        top_right[q] = total[:, upper, S:]
        bottom[0, q] = total[:, lower, :S]
        bottom[1, q] = total[:, lower, S:]
    chunks, _, height, _ = keep.shape
    core = lax.axis_index("core")
    for chunk in range(chunks):
        mine = pl.multiple_of(core * (S // 2) + chunk * height, height)
        other = pl.multiple_of((1 - core) * (S // 2) + chunk * height, height)
        for plane in range(5):
            keep[chunk, plane] = terms[plane, pl.ds(mine, height), :]
            send[chunk, plane] = terms[plane, pl.ds(other, height), :]


def run_slots(card, blocks, probe, frames, chunks, after):
    height = S // 2 // chunks
    f32 = jnp.float32
    quarter = (QUARTERS, 2, S // QUARTERS, S)
    vmem = pl.BlockSpec(memory_space=pltpu.VMEM)
    return pl.pallas_call(
        slots_kernel,
        out_shape=(
            jax.ShapeDtypeStruct(quarter, f32),
            jax.ShapeDtypeStruct(quarter, f32),
            jax.ShapeDtypeStruct((2, *quarter), f32),
            jax.ShapeDtypeStruct((chunks, 5, height, S), f32),
            jax.ShapeDtypeStruct((chunks, 5, height, S), f32),
        ),
        in_specs=[
            pl.BlockSpec(memory_space=pltpu.SMEM), *[vmem] * 11, pl.BlockSpec(memory_space=pl.ANY)
        ],
        out_specs=[vmem] * 5,
        scratch_shapes=[
            pltpu.VMEM((2, 2 * S, 2 * S), f32),
            pltpu.VMEM((2, 2 * S, 2 * S), f32),
            pltpu.VMEM((5, S, S), f32),
        ],
        compiler_params=pltpu.CompilerParams(vmem_limit_bytes=54 * 1024 * 1024),
        name="slots",
    )(card, *blocks, probe, frames, *(jnp.asarray(t) for t in tables()), after)


def light_kernel(cards, probe, light, padded):
    power = jnp.zeros((S, S), jnp.float32)
    for m in range(2):
        power += probe[0, m] * probe[0, m] + probe[1, m] * probe[1, m]
    padded[...] = jnp.zeros_like(padded)
    padded[S : 2 * S, S : 2 * S] = power
    rows = S // QUARTERS
    first = S + lax.axis_index("pos") * rows
    sum_so_far = jnp.zeros((rows, S), jnp.float32)
    for post in range(QUARTERS):
        for tile in range(4):
            above, left = tile // 2, tile % 2

            def one_position(slot, sum_so_far):
                first_row = first + above * S - cards[post, tile, 2 * slot]
                first_column = S + left * S - cards[post, tile, 2 * slot + 1]
                inside, fine = lax.rem(first_row, 8), lax.rem(first_column, 128)
                block = padded[
                    pl.ds(pl.multiple_of(first_row - inside, 8), rows + 8),
                    pl.ds(pl.multiple_of(first_column - fine, 128), 384),
                ]
                return sum_so_far + cut(block, inside, fine)

            sum_so_far = lax.fori_loop(0, cards[post, tile, COUNT], one_position, sum_so_far)
    light[...] = sum_so_far


def run_light(cards, probe):
    vmem = pl.BlockSpec(memory_space=pltpu.VMEM)
    return pl.pallas_call(
        light_kernel,
        out_shape=jax.ShapeDtypeStruct((S // QUARTERS, S), jnp.float32),
        in_specs=[pl.BlockSpec(memory_space=pltpu.SMEM), vmem],
        out_specs=vmem,
        scratch_shapes=[pltpu.VMEM((3 * S + 8, 3 * S + 128), jnp.float32)],
        compiler_params=pltpu.CompilerParams(vmem_limit_bytes=54 * 1024 * 1024),
        name="light",
    )(cards, probe)


def moved(block, tiles_by, bands_by):
    tiles, bands = lax.axis_size(TILE), lax.axis_size("band")
    route = [
        (t * bands + b, (t + tiles_by) * bands + b + bands_by)
        for t in range(tiles)
        for b in range(bands)
        if t + tiles_by in range(tiles) and b + bands_by in range(bands)
    ]
    return lax.ppermute(block, (*TILE, "band"), route)


def across_cores(block):
    return lax.ppermute(block, "core", [(0, 1), (1, 0)])


def across_posts(block, bits):
    return lax.ppermute(block, "pos", [(p, p ^ bits) for p in range(QUARTERS)])


def exchanged(block, axes):
    return lax.all_to_all(block, axes, 0, 0)


def shared(block, axes):
    return exchanged(jnp.broadcast_to(block, (lax.axis_size(axes), *block.shape)), axes)


def corners(right, below):
    tiles, bands = lax.axis_size(TILE), lax.axis_size("band")
    across = [(t * bands + b, t * bands + b - 1) for t in range(1, tiles, 2) for b in range(1, bands)]
    return lax.ppermute(below, (*TILE, "band"), across), lax.ppermute(right, "core", [(1, 0)])


def on_device(object_planes, probe_planes, patterns, offsets, counts):
    core, band, post = (lax.axis_index(name) for name in ("core", "band", "pos"))
    bands, posts = lax.axis_size("band"), lax.axis_size("pos")
    plane = ("band", "pos")
    chunks = bands * posts
    right = moved(object_planes, 0, -1)
    below = moved(object_planes, -1, 0)
    card = jnp.pad(jnp.concatenate([offsets.reshape(6), counts.reshape(1)])[None], ((0, 0), (0, 121)))
    cards = [card, moved(card, 0, 1), moved(card, 1, 0), moved(card, 1, 1)]
    right, below, cards = lax.optimization_barrier((right, below, cards))
    corner_a, corner_b = corners(right, below)
    cards = shared(jnp.concatenate([*cards, jnp.zeros((4, 128), jnp.int32)]), "pos")
    top_left, top_right, bottom, keep, send = run_slots(
        card, (object_planes, right, below, corner_a, corner_b),
        probe_planes, patterns[0, 0, 0], chunks, cards,
    )

    from_above = moved(bottom, 1, 0)
    terms = keep + across_cores(send)
    terms = jnp.sum(exchanged(terms, plane), axis=0)
    terms, from_above = lax.optimization_barrier((terms, from_above))
    from_left = moved(top_right + from_above[1], 0, 1)
    terms = jnp.sum(shared(terms, "z_low"), axis=0)
    light = run_light(cards, probe_planes)
    terms, from_left, light = lax.optimization_barrier((terms, from_left, light))
    tile_sum = top_left + from_above[0] + from_left
    pieces = [lax.dynamic_index_in_dim(tile_sum, post ^ k, 0, keepdims=False) for k in range(QUARTERS)]
    pieces = [pieces[0], *(across_posts(pieces[k], k) for k in range(1, QUARTERS))]
    terms = jnp.sum(shared(terms, "z_high"), axis=0)

    rows = S // QUARTERS
    own_rows = lax.dynamic_slice_in_dim(object_planes, post * rows, rows, 1)
    own_rows = own_rows + sum(pieces[1:], pieces[0]) / (light + 1.0)
    object_new = jnp.zeros_like(object_planes)
    for k in range(QUARTERS):
        piece = across_posts(own_rows, k) if k else own_rows
        object_new = lax.dynamic_update_slice_in_dim(object_new, piece, (post ^ k) * rows, 1)

    height = S // 2 // chunks
    place = core * (S // 2) + (band * posts + post) * height
    own_probe = lax.dynamic_slice_in_dim(probe_planes.reshape(4, S, S), place, height, 1)
    own_probe = own_probe + terms[:4] / (terms[4] + 1.0)
    mine = shared(own_probe, plane).transpose(1, 0, 2, 3).reshape(4, S // 2, S)
    probe_new = jnp.zeros((4, S, S), jnp.float32)
    for half, at in ((mine, core), (across_cores(mine), 1 - core)):
        probe_new = lax.dynamic_update_slice_in_dim(probe_new, half, at * (S // 2), 1)
    return (object_new, probe_new.reshape(probe_planes.shape))


def solution(mesh):
    tiles, bands, posts = mesh.devices.shape
    low = min(4, tiles // 2)
    devices = mesh.devices.reshape(tiles // 2 // low, low, 2, bands, posts)
    mesh = jax.sharding.Mesh(devices, (*TILE, "band", "pos"))
    in_specs = (
        P(None, TILE, "band"),
        P(),
        P(TILE, "band", "pos", None, None, None),
        P(TILE, "band", "pos", None, None),
        P(TILE, "band", "pos"),
    )
    out_specs = (P(None, TILE, "band"), P())
    return jax.shard_map(
        on_device, mesh=mesh, in_specs=in_specs, out_specs=out_specs, check_vma=False
    )
```

time: 179 us -> 147 us (0.82)
  the two profiles are of different devices: /device:TPU:64 before, /device:TPU:2 now
where the time goes in v3:
time: 147 us; the launch traced here: 146 us
  starting transfers between devices  80.7 us (55%)
  blocking collectives  26.8 us (18%)
  Pallas kernels  13.5 us (9%)
  waiting for transfers between devices  12.8 us (9%)
  local copies, waits for them, and re-layouts  7.05 us (5%)
  other arithmetic  3.25 us (2%)
  between operations  1.73 us (1%)
    all_to_all x2, blocking collectives, exchanged(): return lax.all_to_all(block, axes, 0, 0)  26.8 us
    all_to_all x3, starting transfers between devices, exchanged(): return lax.all_to_all(block, axes, 0, 0)  23.5 us
    ppermute x6, starting transfers between devices, across_posts(): return lax.ppermute(block, 'pos', [(p, p ^ bits) for p in range(QUARTERS)])  20.8 us
    ppermute x7, starting transfers between devices, moved(): return lax.ppermute(block, (*TILE, 'band'), route)  20 us
    ppermute x2, starting transfers between devices, across_cores(): return lax.ppermute(block, 'core', [(0, 1), (1, 0)])  14.4 us
    pallas_call x1, Pallas kernels, run_slots(): pl.pallas_call(slots_kernel, out_shape=(jax.ShapeDtypeStruct(quarter, f32...  9.55 us
    all_to_all x3, waiting for transfers between devices, exchanged(): return lax.all_to_all(block, axes, 0, 0)  7.92 us
    unnamed x21, local copies, waits for them, and re-layouts  4.4 us
  transfers between devices with their start and end apart: 20, of which 4 were waited for; matrix products, arithmetic and copies ran while one was open for 4% of the time, Pallas kernels for 3%

profile of v3, /device:TPU:2, one launch (start us, length us, event | category | flops | bytes accessed | tf_op | source)
XLA Modules:
  0.0 145.8 jit_solution(2972135056469967293)
XLA Ops:
  0.6 7.8 %collective-permute-start = (f32[2,256,256]{2,1,0:T(8,128)}, f32[2,256,256]{2,1,0:T(8,128)S(1)}, u32[]{:S(2)}, u32[]{:S(2)}) collective-permute-start(f32[2,256,256]{2,1,0:T(8,128)} %own.1), channel_id=1, source_target_pairs={{4,0},{8,4},{12,8},{20,16},{24,20},{28,24},{36,32},{40,36},{44,40}... | collective-permute-start | bytes 1572872 | tf_op jit(solution)/shard_map/ppermute | solution.py:230
  8.5 1.3 collective-permute-start.1
  9.8 0.8 copy.16
  10.5 0.1 reshape.20
  11.3 0.1 add_bitcast_fusion
  11.3 1.9 %collective-permute-start.2 = (s32[1,128]{1,0:T(1,128)S(1)}, s32[1,128]{1,0:T(1,128)S(1)}, u32[]{:S(2)}, u32[]{:S(2)}) collective-permute-start(s32[1,128]{1,0:T(1,128)S(1)} %pad.4.card), channel_id=1, source_target_pairs={{0,4},{4,8},{8,12},{16,20},{20,24},{24,28},{32,36},{36,40},{40,44}... | collective-permute-start | bytes 1544 | tf_op jit(solution)/shard_map/ppermute | solution.py:230
  13.3 3.0 %collective-permute-start.3 = (s32[1,128]{1,0:T(1,128)S(1)}, s32[1,128]{1,0:T(1,128)S(1)}, u32[]{:S(2)}, u32[]{:S(2)}) collective-permute-start(s32[1,128]{1,0:T(1,128)S(1)} %pad.4.card), channel_id=1, source_target_pairs={{0,16},{4,20},{8,24},{12,28},{16,32},{20,36},{24,40},{28,44},{32,4... | collective-permute-start | bytes 1544 | tf_op jit(solution)/shard_map/ppermute | solution.py:230
  16.3 1.3 collective-permute-start.4
  17.6 0.0 collective-permute-done.2
  17.6 1.3 collective-permute-done.4
  18.9 0.7 collective-permute-start.5
  19.6 1.3 collective-permute-start.6
  20.9 9.1 %all_to_all.25.after.cards = s32[4,8,128]{2,1,0:T(8,128)} all-to-all(s32[4,8,128]{2,1,0:T(8,128)S(1)} %broadcast_in_dim.29), channel_id=1, replica_groups=mesh['z_high'=4,'z_low'=4,'core'=2,'band'=4,'pos'=4] {'pos'}, dimensions={0} | all-to-all | bytes 32768 | tf_op jit(solution)/shard_map/all_to_all | solution.py:242
  30.1 0.8 copy-done.6
  30.9 0.2 copy-done.7
  31.1 9.5 %slots.1 = (f32[4,2,64,256]{3,2,1,0:T(8,128)}, f32[4,2,64,256]{3,2,1,0:T(8,128)}, f32[2,4,2,64,256]{4,3,2,1,0:T(8,128)}, f32[16,5,8,256]{3,2,1,0:T(8,128)}, f32[16,5,8,256]{3,2,1,0:T(8,128)}) custom-call(s32[1,128]{1,0:T(1,128)} %copy-done.9, f32[2,256,256]{2,1,0:T(8,128)} %own.1, f32[2,256,256]{2,1,0:T(8,128)} %copy-done.4, f32[2,256,256]{2,1,0:T(8,128)} %copy-done.5, ...), custom_call_target="tpu_custom_call" | custom-call | tf_op jit(solution)/shard_map/slots/pallas_call | solution.py:159
  40.6 12.5 %collective-permute-start.7 = (f32[16,5,8,256]{3,2,1,0:T(8,128)}, f32[16,5,8,256]{3,2,1,0:T(8,128)S(1)}, u32[]{:S(2)}, u32[]{:S(2)}) collective-permute-start(f32[16,5,8,256]{3,2,1,0:T(8,128)} %get-tuple-element.26), channel_id=1, source_target_pairs={{0,16},{16,0},{1,17},{17,1},{2,18},{18,2},{3,19},{19,3},{4,20},{20... | collective-permute-start | bytes 1966088 | tf_op jit(solution)/shard_map/ppermute | solution.py:234
  53.1 2.0 %collective-permute-start.8 = (f32[2,4,2,64,256]{4,3,2,1,0:T(8,128)}, f32[2,4,2,64,256]{4,3,2,1,0:T(8,128)S(1)}, u32[]{:S(2)}, u32[]{:S(2)}) collective-permute-start(f32[2,4,2,64,256]{4,3,2,1,0:T(8,128)} %get-tuple-element.27), channel_id=1, source_target_pairs={{0,16},{4,20},{8,24},{12,28},{16,32},{20,36},{24,40},{28,44},{32,4... | collective-permute-start | bytes 3145736 | tf_op jit(solution)/shard_map/ppermute | solution.py:230
  55.1 1.2 add.84
  56.3 17.7 %all_to_all.26 = f32[16,5,8,256]{3,2,1,0:T(8,128)S(1)} all-to-all(f32[16,5,8,256]{3,2,1,0:T(8,128)S(1)} %add.84), channel_id=1, replica_groups=mesh['z_high'=4,'z_low'=4,'core'=2,'band'=4,'pos'=4] {'band','pos'}, dimensions={0} | all-to-all | bytes 1310720 | tf_op jit(solution)/shard_map/all_to_all | solution.py:242
  74.1 1.0 copy-done.1
  75.0 0.1 bitcast_add_fusion
  75.1 2.7 %collective-permute-start.9 = (f32[4,2,64,256]{3,2,1,0:T(8,128)S(1)}, f32[4,2,64,256]{3,2,1,0:T(8,128)S(1)}, u32[]{:S(2)}, u32[]{:S(2)}) collective-permute-start(f32[4,2,64,256]{3,2,1,0:T(8,128)S(1)} %bitcast_add_fusion), channel_id=1, source_target_pairs={{0,4},{4,8},{8,12},{16,20},{20,24},{24,28},{32,36},{36,40},{40,44}... | collective-permute-start | bytes 1572872 | tf_op jit(solution)/shard_map/ppermute | solution.py:230
  77.8 0.7 broadcast_in_dim.30
  78.5 5.4 %all-to-all-start.2 = ((f32[4,5,8,256]{3,2,1,0:T(8,128)}), f32[4,5,8,256]{3,2,1,0:T(8,128)S(1)}, u32[]{:S(2)}, u32[]{:S(2)}) async-start(f32[4,5,8,256]{3,2,1,0:T(8,128)} %broadcast_in_dim.30), calls=%async_computation.2 | async-start | bytes 327680 | tf_op jit(solution)/shard_map/all_to_all | solution.py:242
  83.9 3.9 %light.1 = f32[64,256]{1,0:T(8,128)} custom-call(s32[4,8,128]{2,1,0:T(8,128)} %all_to_all.25.after.cards, f32[2,2,256,256]{3,2,1,0:T(8,128)} %probe.3), custom_call_target="tpu_custom_call" | custom-call | tf_op jit(solution)/shard_map/light/pallas_call | solution.py:211
  87.8 3.1 %all-to-all-done.2 = f32[4,5,8,256]{3,2,1,0:T(8,128)S(1)} async-done(((f32[4,5,8,256]{3,2,1,0:T(8,128)}), f32[4,5,8,256]{3,2,1,0:T(8,128)S(1)}, u32[]{:S(2)}, u32[]{:S(2)}) %all-to-all-start.2) | async-done | bytes 163872 | tf_op jit(solution)/shard_map/all_to_all | solution.py:242
  90.9 0.7 broadcast_in_dim.32
  91.6 12.1 %all-to-all-start.3 = ((f32[4,5,8,256]{3,2,1,0:T(8,128)}), f32[4,5,8,256]{3,2,1,0:T(8,128)S(1)}, u32[]{:S(2)}, u32[]{:S(2)}) async-start(f32[4,5,8,256]{3,2,1,0:T(8,128)} %broadcast_in_dim.32), calls=%async_computation.3 | async-start | bytes 327680 | tf_op jit(solution)/shard_map/all_to_all | solution.py:242
  103.7 0.1 fusion
  103.9 2.3 %collective-permute-start.10 = (f32[2,64,256]{2,1,0:T(8,128)S(1)}, f32[2,64,256]{2,1,0:T(8,128)S(1)}, u32[]{:S(2)}, u32[]{:S(2)}) collective-permute-start(f32[2,64,256]{2,1,0:T(8,128)S(1)} %get-tuple-element.36), channel_id=1, source_target_pairs={{0,1},{1,0},{2,3},{3,2},{4,5},{5,4},{6,7},{7,6},{8,9},{9,8},{10,11... | collective-permute-start | bytes 393224 | tf_op jit(solution)/shard_map/ppermute | solution.py:238
  106.1 4.2 %collective-permute-start.11 = (f32[2,64,256]{2,1,0:T(8,128)S(1)}, f32[2,64,256]{2,1,0:T(8,128)S(1)}, u32[]{:S(2)}, u32[]{:S(2)}) collective-permute-start(f32[2,64,256]{2,1,0:T(8,128)S(1)} %get-tuple-element.38), channel_id=1, source_target_pairs={{0,2},{1,3},{2,0},{3,1},{4,6},{5,7},{6,4},{7,5},{8,10},{9,11},{10,... | collective-permute-start | bytes 393224 | tf_op jit(solution)/shard_map/ppermute | solution.py:238
  110.3 4.0 %collective-permute-start.12 = (f32[2,64,256]{2,1,0:T(8,128)S(1)}, f32[2,64,256]{2,1,0:T(8,128)S(1)}, u32[]{:S(2)}, u32[]{:S(2)}) collective-permute-start(f32[2,64,256]{2,1,0:T(8,128)S(1)} %get-tuple-element.37), channel_id=1, source_target_pairs={{0,3},{1,2},{2,1},{3,0},{4,7},{5,6},{6,5},{7,4},{8,11},{9,10},{10,... | collective-permute-start | bytes 393224 | tf_op jit(solution)/shard_map/ppermute | solution.py:238
  114.3 4.8 %all-to-all-done.3 = f32[4,5,8,256]{3,2,1,0:T(8,128)S(1)} async-done(((f32[4,5,8,256]{3,2,1,0:T(8,128)}), f32[4,5,8,256]{3,2,1,0:T(8,128)S(1)}, u32[]{:S(2)}, u32[]{:S(2)}) %all-to-all-start.3) | async-done | bytes 163872 | tf_op jit(solution)/shard_map/all_to_all | solution.py:242
  119.2 0.8 fusion.5
  119.9 0.8 broadcast_in_dim.33
  120.8 5.9 %all-to-all-start.4 = ((f32[16,4,8,256]{3,2,1,0:T(8,128)}), f32[16,4,8,256]{3,2,1,0:T(8,128)S(1)}, u32[]{:S(2)}, u32[]{:S(2)}) async-start(f32[16,4,8,256]{3,2,1,0:T(8,128)} %broadcast_in_dim.33), calls=%async_computation.4 | async-start | bytes 1048576 | tf_op jit(solution)/shard_map/all_to_all | solution.py:242
  126.8 1.0 constant_dynamic-update-slice_fusion.5
  127.8 3.4 %collective-permute-start.13 = (f32[2,64,256]{2,1,0:T(8,128)S(1)}, f32[2,64,256]{2,1,0:T(8,128)S(1)}, u32[]{:S(2)}, u32[]{:S(2)}) collective-permute-start(f32[2,64,256]{2,1,0:T(8,128)S(1)} %get-tuple-element.35), channel_id=1, source_target_pairs={{0,1},{1,0},{2,3},{3,2},{4,5},{5,4},{6,7},{7,6},{8,9},{9,8},{10,11... | collective-permute-start | bytes 393224 | tf_op jit(solution)/shard_map/ppermute | solution.py:238
  131.2 4.6 %collective-permute-start.14 = (f32[2,64,256]{2,1,0:T(8,128)S(1)}, f32[2,64,256]{2,1,0:T(8,128)S(1)}, u32[]{:S(2)}, u32[]{:S(2)}) collective-permute-start(f32[2,64,256]{2,1,0:T(8,128)S(1)} %get-tuple-element.35), channel_id=1, source_target_pairs={{0,2},{1,3},{2,0},{3,1},{4,6},{5,7},{6,4},{7,5},{8,10},{9,11},{10,... | collective-permute-start | bytes 393224 | tf_op jit(solution)/shard_map/ppermute | solution.py:238
  135.8 2.5 %collective-permute-start.15 = (f32[2,64,256]{2,1,0:T(8,128)S(1)}, f32[2,64,256]{2,1,0:T(8,128)S(1)}, u32[]{:S(2)}, u32[]{:S(2)}) collective-permute-start(f32[2,64,256]{2,1,0:T(8,128)S(1)} %get-tuple-element.35), channel_id=1, source_target_pairs={{0,3},{1,2},{2,1},{3,0},{4,7},{5,6},{6,5},{7,4},{8,11},{9,10},{10,... | collective-permute-start | bytes 393224 | tf_op jit(solution)/shard_map/ppermute | solution.py:238
  138.3 1.9 %collective-permute-start.16 = (f32[4,128,256]{2,1,0:T(8,128)S(1)}, f32[4,128,256]{2,1,0:T(8,128)S(1)}, u32[]{:S(2)}, u32[]{:S(2)}) collective-permute-start(f32[4,128,256]{2,1,0:T(8,128)S(1)} %bitcast.42), channel_id=1, source_target_pairs={{0,16},{16,0},{1,17},{17,1},{2,18},{18,2},{3,19},{19,3},{4,20},{20... | collective-permute-start | bytes 1572872 | tf_op jit(solution)/shard_map/ppermute | solution.py:234
  140.3 3.5 %collective-permute-done.15 = f32[2,64,256]{2,1,0:T(8,128)S(1)} collective-permute-done((f32[2,64,256]{2,1,0:T(8,128)S(1)}, f32[2,64,256]{2,1,0:T(8,128)S(1)}, u32[]{:S(2)}, u32[]{:S(2)}) %collective-permute-start.15) | collective-permute-done | bytes 131104 | tf_op jit(solution)/shard_map/ppermute | solution.py:238
  143.9 0.0 copy-start.2
  143.9 0.1 broadcast_in_dim.31
  144.0 0.7 copy-done.2
  144.8 0.0 copy-start
  144.8 1.0 copy-done
  (45 shorter events, 0.4 us)
Async XLA Ops:
  0.6 18.3 %collective-permute-start = (f32[2,256,256]{2,1,0:T(8,128)}, f32[2,256,256]{2,1,0:T(8,128)S(1)}, u32[]{:S(2)}, u32[]{:S(2)}) collective-permute-start(f32[2,256,256]{2,1,0:T(8,128)} %own.1), channel_id=1, source_target_pairs={{4,0},{8,4},{12,8},{20,16},{24,20},{28,24},{36,32},{40,36},{44,40}... | collective-permute-start | bytes 1572872 | tf_op jit(solution)/shard_map/ppermute | solution.py:230
  8.5 10.4 %collective-permute-start.1 = (f32[2,256,256]{2,1,0:T(8,128)}, f32[2,256,256]{2,1,0:T(8,128)S(1)}, u32[]{:S(2)}, u32[]{:S(2)}) collective-permute-start(f32[2,256,256]{2,1,0:T(8,128)} %own.1), channel_id=1, source_target_pairs={{16,0},{20,4},{24,8},{28,12},{32,16},{36,20},{40,24},{44,28},{48,3... | collective-permute-start | bytes 1572872 | tf_op jit(solution)/shard_map/ppermute | solution.py:230
  11.3 9.6 %copy-start.9 = (s32[1,128]{1,0:T(1,128)}, s32[1,128]{1,0:T(1,128)S(1)}, u32[]{:S(2)}) copy-start(s32[1,128]{1,0:T(1,128)S(1)} %pad.4.card) | copy-start | bytes 1540
  11.3 6.3 %collective-permute-start.2 = (s32[1,128]{1,0:T(1,128)S(1)}, s32[1,128]{1,0:T(1,128)S(1)}, u32[]{:S(2)}, u32[]{:S(2)}) collective-permute-start(s32[1,128]{1,0:T(1,128)S(1)} %pad.4.card), channel_id=1, source_target_pairs={{0,4},{4,8},{8,12},{16,20},{20,24},{24,28},{32,36},{36,40},{40,44}... | collective-permute-start | bytes 1544 | tf_op jit(solution)/shard_map/ppermute | solution.py:230
  13.3 4.4 %collective-permute-start.3 = (s32[1,128]{1,0:T(1,128)S(1)}, s32[1,128]{1,0:T(1,128)S(1)}, u32[]{:S(2)}, u32[]{:S(2)}) collective-permute-start(s32[1,128]{1,0:T(1,128)S(1)} %pad.4.card), channel_id=1, source_target_pairs={{0,16},{4,20},{8,24},{12,28},{16,32},{20,36},{24,40},{28,44},{32,4... | collective-permute-start | bytes 1544 | tf_op jit(solution)/shard_map/ppermute | solution.py:230
  16.3 2.6 %collective-permute-start.4 = (s32[1,128]{1,0:T(1,128)S(1)}, s32[1,128]{1,0:T(1,128)S(1)}, u32[]{:S(2)}, u32[]{:S(2)}) collective-permute-start(s32[1,128]{1,0:T(1,128)S(1)} %pad.4.card), channel_id=1, source_target_pairs={{0,20},{4,24},{8,28},{16,36},{20,40},{24,44},{32,52},{36,56},{40,6... | collective-permute-start | bytes 1544 | tf_op jit(solution)/shard_map/ppermute | solution.py:230
  18.9 11.2 %copy-start.4 = (f32[2,256,256]{2,1,0:T(8,128)}, f32[2,256,256]{2,1,0:T(8,128)S(1)}, u32[]{:S(2)}) copy-start(f32[2,256,256]{2,1,0:T(8,128)S(1)} %collective-permute-done.right) | copy-start | bytes 1572868
  18.9 11.2 %copy-start.5 = (f32[2,256,256]{2,1,0:T(8,128)}, f32[2,256,256]{2,1,0:T(8,128)S(1)}, u32[]{:S(2)}) copy-start(f32[2,256,256]{2,1,0:T(8,128)S(1)} %collective-permute-done.1.below) | copy-start | bytes 1572868
  18.9 11.2 %collective-permute-start.5 = (f32[2,256,256]{2,1,0:T(8,128)S(1)}, f32[2,256,256]{2,1,0:T(8,128)S(1)}, u32[]{:S(2)}, u32[]{:S(2)}) collective-permute-start(f32[2,256,256]{2,1,0:T(8,128)S(1)} %collective-permute-done.1.below), channel_id=1, source_target_pairs={{20,16},{24,20},{28,24},{52,48},{56,52},{60,56},{84,80},{88,84},{9... | collective-permute-start | bytes 1572872 | tf_op jit(solution)/shard_map/ppermute | solution.py:252
  19.6 10.5 %collective-permute-start.6 = (f32[2,256,256]{2,1,0:T(8,128)S(1)}, f32[2,256,256]{2,1,0:T(8,128)S(1)}, u32[]{:S(2)}, u32[]{:S(2)}) collective-permute-start(f32[2,256,256]{2,1,0:T(8,128)S(1)} %collective-permute-done.right), channel_id=1, source_target_pairs={{16,0},{17,1},{18,2},{19,3},{20,4},{21,5},{22,6},{23,7},{24,8},{25... | collective-permute-start | bytes 1572872 | tf_op jit(solution)/shard_map/ppermute | solution.py:252
  30.1 0.8 copy-start.6
  30.1 1.0 copy-start.7
  40.6 14.5 %collective-permute-start.7 = (f32[16,5,8,256]{3,2,1,0:T(8,128)}, f32[16,5,8,256]{3,2,1,0:T(8,128)S(1)}, u32[]{:S(2)}, u32[]{:S(2)}) collective-permute-start(f32[16,5,8,256]{3,2,1,0:T(8,128)} %get-tuple-element.26), channel_id=1, source_target_pairs={{0,16},{16,0},{1,17},{17,1},{2,18},{18,2},{3,19},{19,3},{4,20},{20... | collective-permute-start | bytes 1966088 | tf_op jit(solution)/shard_map/ppermute | solution.py:234
  53.1 20.9 %collective-permute-start.8 = (f32[2,4,2,64,256]{4,3,2,1,0:T(8,128)}, f32[2,4,2,64,256]{4,3,2,1,0:T(8,128)S(1)}, u32[]{:S(2)}, u32[]{:S(2)}) collective-permute-start(f32[2,4,2,64,256]{4,3,2,1,0:T(8,128)} %get-tuple-element.27), channel_id=1, source_target_pairs={{0,16},{4,20},{8,24},{12,28},{16,32},{20,36},{24,40},{28,44},{32,4... | collective-permute-start | bytes 3145736 | tf_op jit(solution)/shard_map/ppermute | solution.py:230
  74.0 1.0 copy-start.1
  75.1 15.8 %collective-permute-start.9 = (f32[4,2,64,256]{3,2,1,0:T(8,128)S(1)}, f32[4,2,64,256]{3,2,1,0:T(8,128)S(1)}, u32[]{:S(2)}, u32[]{:S(2)}) collective-permute-start(f32[4,2,64,256]{3,2,1,0:T(8,128)S(1)} %bitcast_add_fusion), channel_id=1, source_target_pairs={{0,4},{4,8},{8,12},{16,20},{20,24},{24,28},{32,36},{36,40},{40,44}... | collective-permute-start | bytes 1572872 | tf_op jit(solution)/shard_map/ppermute | solution.py:230
  78.5 12.4 %all-to-all-start.2 = ((f32[4,5,8,256]{3,2,1,0:T(8,128)}), f32[4,5,8,256]{3,2,1,0:T(8,128)S(1)}, u32[]{:S(2)}, u32[]{:S(2)}) async-start(f32[4,5,8,256]{3,2,1,0:T(8,128)} %broadcast_in_dim.30), calls=%async_computation.2 | async-start | bytes 327680 | tf_op jit(solution)/shard_map/all_to_all | solution.py:242
  87.8 15.9 %copy-start.3 = (f32[4,2,64,256]{3,2,1,0:T(8,128)S(1)}, f32[4,2,64,256]{3,2,1,0:T(8,128)}, u32[]{:S(2)}) copy-start(f32[4,2,64,256]{3,2,1,0:T(8,128)} %get-tuple-element.24) | copy-start | bytes 1572868
  91.6 27.6 %all-to-all-start.3 = ((f32[4,5,8,256]{3,2,1,0:T(8,128)}), f32[4,5,8,256]{3,2,1,0:T(8,128)S(1)}, u32[]{:S(2)}, u32[]{:S(2)}) async-start(f32[4,5,8,256]{3,2,1,0:T(8,128)} %broadcast_in_dim.32), calls=%async_computation.3 | async-start | bytes 327680 | tf_op jit(solution)/shard_map/all_to_all | solution.py:242
  103.9 22.9 %collective-permute-start.10 = (f32[2,64,256]{2,1,0:T(8,128)S(1)}, f32[2,64,256]{2,1,0:T(8,128)S(1)}, u32[]{:S(2)}, u32[]{:S(2)}) collective-permute-start(f32[2,64,256]{2,1,0:T(8,128)S(1)} %get-tuple-element.36), channel_id=1, source_target_pairs={{0,1},{1,0},{2,3},{3,2},{4,5},{5,4},{6,7},{7,6},{8,9},{9,8},{10,11... | collective-permute-start | bytes 393224 | tf_op jit(solution)/shard_map/ppermute | solution.py:238
  106.1 20.6 %collective-permute-start.11 = (f32[2,64,256]{2,1,0:T(8,128)S(1)}, f32[2,64,256]{2,1,0:T(8,128)S(1)}, u32[]{:S(2)}, u32[]{:S(2)}) collective-permute-start(f32[2,64,256]{2,1,0:T(8,128)S(1)} %get-tuple-element.38), channel_id=1, source_target_pairs={{0,2},{1,3},{2,0},{3,1},{4,6},{5,7},{6,4},{7,5},{8,10},{9,11},{10,... | collective-permute-start | bytes 393224 | tf_op jit(solution)/shard_map/ppermute | solution.py:238
  110.3 16.5 %collective-permute-start.12 = (f32[2,64,256]{2,1,0:T(8,128)S(1)}, f32[2,64,256]{2,1,0:T(8,128)S(1)}, u32[]{:S(2)}, u32[]{:S(2)}) collective-permute-start(f32[2,64,256]{2,1,0:T(8,128)S(1)} %get-tuple-element.37), channel_id=1, source_target_pairs={{0,3},{1,2},{2,1},{3,0},{4,7},{5,6},{6,5},{7,4},{8,11},{9,10},{10,... | collective-permute-start | bytes 393224 | tf_op jit(solution)/shard_map/ppermute | solution.py:238
  120.8 5.9 %copy-start.8 = (f32[64,256]{1,0:T(8,128)S(1)}, f32[64,256]{1,0:T(8,128)}, u32[]{:S(2)}) copy-start(f32[64,256]{1,0:T(8,128)} %light.1) | copy-start | bytes 196612
  120.8 17.5 %all-to-all-start.4 = ((f32[16,4,8,256]{3,2,1,0:T(8,128)}), f32[16,4,8,256]{3,2,1,0:T(8,128)S(1)}, u32[]{:S(2)}, u32[]{:S(2)}) async-start(f32[16,4,8,256]{3,2,1,0:T(8,128)} %broadcast_in_dim.33), calls=%async_computation.4 | async-start | bytes 1048576 | tf_op jit(solution)/shard_map/all_to_all | solution.py:242
  127.8 12.5 %collective-permute-start.13 = (f32[2,64,256]{2,1,0:T(8,128)S(1)}, f32[2,64,256]{2,1,0:T(8,128)S(1)}, u32[]{:S(2)}, u32[]{:S(2)}) collective-permute-start(f32[2,64,256]{2,1,0:T(8,128)S(1)} %get-tuple-element.35), channel_id=1, source_target_pairs={{0,1},{1,0},{2,3},{3,2},{4,5},{5,4},{6,7},{7,6},{8,9},{9,8},{10,11... | collective-permute-start | bytes 393224 | tf_op jit(solution)/shard_map/ppermute | solution.py:238
  131.2 9.1 %collective-permute-start.14 = (f32[2,64,256]{2,1,0:T(8,128)S(1)}, f32[2,64,256]{2,1,0:T(8,128)S(1)}, u32[]{:S(2)}, u32[]{:S(2)}) collective-permute-start(f32[2,64,256]{2,1,0:T(8,128)S(1)} %get-tuple-element.35), channel_id=1, source_target_pairs={{0,2},{1,3},{2,0},{3,1},{4,6},{5,7},{6,4},{7,5},{8,10},{9,11},{10,... | collective-permute-start | bytes 393224 | tf_op jit(solution)/shard_map/ppermute | solution.py:238
  135.8 8.1 %collective-permute-start.15 = (f32[2,64,256]{2,1,0:T(8,128)S(1)}, f32[2,64,256]{2,1,0:T(8,128)S(1)}, u32[]{:S(2)}, u32[]{:S(2)}) collective-permute-start(f32[2,64,256]{2,1,0:T(8,128)S(1)} %get-tuple-element.35), channel_id=1, source_target_pairs={{0,3},{1,2},{2,1},{3,0},{4,7},{5,6},{6,5},{7,4},{8,11},{9,10},{10,... | collective-permute-start | bytes 393224 | tf_op jit(solution)/shard_map/ppermute | solution.py:238
  138.3 6.4 %collective-permute-start.16 = (f32[4,128,256]{2,1,0:T(8,128)S(1)}, f32[4,128,256]{2,1,0:T(8,128)S(1)}, u32[]{:S(2)}, u32[]{:S(2)}) collective-permute-start(f32[4,128,256]{2,1,0:T(8,128)S(1)} %bitcast.42), channel_id=1, source_target_pairs={{0,16},{16,0},{1,17},{17,1},{2,18},{18,2},{3,19},{19,3},{4,20},{20... | collective-permute-start | bytes 1572872 | tf_op jit(solution)/shard_map/ppermute | solution.py:234
  143.9 0.8 copy-start.2
  144.8 1.0 copy-start

commit v4 on v3

--- a/solution.py
+++ b/solution.py
@@ -179,44 +179,39 @@
     )(card, *blocks, probe, frames, *(jnp.asarray(t) for t in tables()), after)
 
 
-def light_kernel(cards, probe, light, padded):
+def light_kernel(card, probe, top_left, top_right, bottom, total):
     power = jnp.zeros((S, S), jnp.float32)
     for m in range(2):
         power += probe[0, m] * probe[0, m] + probe[1, m] * probe[1, m]
-    padded[...] = jnp.zeros_like(padded)
-    padded[S : 2 * S, S : 2 * S] = power
-    rows = S // QUARTERS
-    first = S + lax.axis_index("pos") * rows
-    sum_so_far = jnp.zeros((rows, S), jnp.float32)
-    for post in range(QUARTERS):
-        for tile in range(4):
-            above, left = tile // 2, tile % 2
-
-            def one_position(slot, sum_so_far):
-                first_row = first + above * S - cards[post, tile, 2 * slot]
-                first_column = S + left * S - cards[post, tile, 2 * slot + 1]
-                inside, fine = lax.rem(first_row, 8), lax.rem(first_column, 128)
-                block = padded[
-                    pl.ds(pl.multiple_of(first_row - inside, 8), rows + 8),
-                    pl.ds(pl.multiple_of(first_column - fine, 128), 384),
-                ]
-                return sum_so_far + cut(block, inside, fine)
-
-            sum_so_far = lax.fori_loop(0, cards[post, tile, COUNT], one_position, sum_so_far)
-    light[...] = sum_so_far
-
-
-def run_light(cards, probe):
+    total[...] = jnp.zeros_like(total)
+
+    def one_slot(slot, carry):
+        row, column = card[0, 2 * slot], card[0, 2 * slot + 1]
+        inside, fine = lax.rem(row, 8), lax.rem(column, 128)
+        band_rows = pl.ds(pl.multiple_of(row - inside, 8), S + 8)
+        band_columns = pl.ds(pl.multiple_of(column - fine, 128), 384)
+        total[band_rows, band_columns] += placed(power, inside, fine)
+        return carry
+
+    lax.fori_loop(0, card[0, COUNT], one_slot, 0)
+    top_left[...] = total[:S, :S]
+    top_right[...] = total[:S, S:]
+    bottom[0] = total[S:, :S]
+    bottom[1] = total[S:, S:]
+
+
+def run_light(card, probe):
     vmem = pl.BlockSpec(memory_space=pltpu.VMEM)
+    tile = jax.ShapeDtypeStruct((S, S), jnp.float32)
     return pl.pallas_call(
         light_kernel,
-        out_shape=jax.ShapeDtypeStruct((S // QUARTERS, S), jnp.float32),
+        out_shape=(tile, tile, jax.ShapeDtypeStruct((2, S, S), jnp.float32)),
         in_specs=[pl.BlockSpec(memory_space=pltpu.SMEM), vmem],
-        out_specs=vmem,
-        scratch_shapes=[pltpu.VMEM((3 * S + 8, 3 * S + 128), jnp.float32)],
+        out_specs=[vmem] * 3,
+        scratch_shapes=[pltpu.VMEM((2 * S, 2 * S), jnp.float32)],
         compiler_params=pltpu.CompilerParams(vmem_limit_bytes=54 * 1024 * 1024),
         name="light",
-    )(cards, probe)
+    )(card, probe)
 
 
 def moved(block, tiles_by, bands_by):
@@ -260,31 +255,31 @@
     right = moved(object_planes, 0, -1)
     below = moved(object_planes, -1, 0)
     card = jnp.pad(jnp.concatenate([offsets.reshape(6), counts.reshape(1)])[None], ((0, 0), (0, 121)))
-    cards = [card, moved(card, 0, 1), moved(card, 1, 0), moved(card, 1, 1)]
-    right, below, cards = lax.optimization_barrier((right, below, cards))
+    light, light_right, light_bottom = run_light(card, probe_planes)
+    right, below, light_bottom = lax.optimization_barrier((right, below, light_bottom))
+    light_above = moved(light_bottom, 1, 0)
     corner_a, corner_b = corners(right, below)
-    cards = shared(jnp.concatenate([*cards, jnp.zeros((4, 128), jnp.int32)]), "pos")
+    light_left = moved(light_right + light_above[1], 0, 1)
+    light = light + light_above[0]
     top_left, top_right, bottom, keep, send = run_slots(
         card, (object_planes, right, below, corner_a, corner_b),
-        probe_planes, patterns[0, 0, 0], chunks, cards,
-    )
-
+        probe_planes, patterns[0, 0, 0], chunks, light_above,
+    )
+
+    light = lax.psum_scatter(light + light_left, "pos", scatter_dimension=0, tiled=True)
     from_above = moved(bottom, 1, 0)
     terms = keep + across_cores(send)
     terms = jnp.sum(exchanged(terms, plane), axis=0)
     terms, from_above = lax.optimization_barrier((terms, from_above))
     from_left = moved(top_right + from_above[1], 0, 1)
     terms = jnp.sum(shared(terms, "z_low"), axis=0)
-    light = run_light(cards, probe_planes)
-    terms, from_left, light = lax.optimization_barrier((terms, from_left, light))
     tile_sum = top_left + from_above[0] + from_left
-    pieces = [lax.dynamic_index_in_dim(tile_sum, post ^ k, 0, keepdims=False) for k in range(QUARTERS)]
-    pieces = [pieces[0], *(across_posts(pieces[k], k) for k in range(1, QUARTERS))]
+    tile_sum = lax.psum_scatter(tile_sum, "pos", scatter_dimension=0, tiled=True)[0]
     terms = jnp.sum(shared(terms, "z_high"), axis=0)
 
     rows = S // QUARTERS
     own_rows = lax.dynamic_slice_in_dim(object_planes, post * rows, rows, 1)
-    own_rows = own_rows + sum(pieces[1:], pieces[0]) / (light + 1.0)
+    own_rows = own_rows + tile_sum / (light + 1.0)
     object_new = jnp.zeros_like(object_planes)
     for k in range(QUARTERS):
         piece = across_posts(own_rows, k) if k else own_rows

time: 147 us -> 181 us (1.23)
  waiting for transfers between devices: 12.8 us -> 55.5 us
  blocking collectives: 26.8 us -> 0 us
  between operations: 1.73 us -> 15 us
  starting transfers between devices: 80.7 us -> 71.9 us
  Pallas kernels: 13.5 us -> 21.3 us
  other arithmetic: 3.25 us -> 8.47 us
    all_to_all x2 -> x0, blocking collectives: 26.8 us -> none  [exchanged(): return lax.all_to_all(block, axes, 0, 0)]
    all_to_all x3 -> x4, waiting for transfers between devices: 7.92 us -> 30.2 us  [exchanged(): return lax.all_to_all(block, axes, 0, 0)]
    reduce_scatter x0 -> x2, waiting for transfers between devices: none -> 14.7 us  [the longest x1 14.7 us: on_device(): lax.psum_scatter(tile_sum, 'pos', scatter_dimension=0, tiled=True)[0]]
    all_to_all x3 -> x4, starting transfers between devices: 23.5 us -> 36.2 us  [exchanged(): return lax.all_to_all(block, axes, 0, 0)]
    ppermute x2, starting transfers between devices: 14.4 us -> 3.83 us  [across_cores(): return lax.ppermute(block, 'core', [(0, 1), (1, 0)])]
    ppermute x6 -> x3, starting transfers between devices: 20.8 us -> 10.4 us  [across_posts(): return lax.ppermute(block, 'pos', [(p, p ^ bits) for p in range(QUARTERS)])]
    pallas_call x1, Pallas kernels: 9.55 us -> 18.5 us  [run_slots(): pl.pallas_call(slots_kernel, out_shape=(jax.ShapeDtypeStruct(quarter, f32...]
    ppermute x1, waiting for transfers between devices: 0.01 us -> 5.42 us  [corners(): lax.ppermute(right, 'core', [(1, 0)])]
  transfers between devices with their start and end apart: 20 -> 19, of which waited for: 4 -> 8; matrix products, arithmetic and copies ran while one was open for 4% -> 7% of each run, Pallas kernels for 3% -> 2%
where the time goes in v4:
time: 181 us; the launch traced here: 179 us
  starting transfers between devices  71.9 us (40%)
  waiting for transfers between devices  55.5 us (31%)
  Pallas kernels  21.3 us (12%)
  between operations  15 us (8%)
  other arithmetic  8.47 us (5%)
  local copies, waits for them, and re-layouts  7.25 us (4%)
    all_to_all x4, starting transfers between devices, exchanged(): return lax.all_to_all(block, axes, 0, 0)  36.2 us
    all_to_all x4, waiting for transfers between devices, exchanged(): return lax.all_to_all(block, axes, 0, 0)  30.2 us
    ppermute x6, starting transfers between devices, moved(): return lax.ppermute(block, (*TILE, 'band'), route)  19.4 us
    pallas_call x1, Pallas kernels, run_slots(): pl.pallas_call(slots_kernel, out_shape=(jax.ShapeDtypeStruct(quarter, f32...  18.5 us
    reduce_scatter x1, waiting for transfers between devices, on_device(): lax.psum_scatter(tile_sum, 'pos', scatter_dimension=0, tiled=True)[0]  14.7 us
    ppermute x3, starting transfers between devices, across_posts(): return lax.ppermute(block, 'pos', [(p, p ^ bits) for p in range(QUARTERS)])  10.4 us
    ppermute x1, waiting for transfers between devices, corners(): lax.ppermute(right, 'core', [(1, 0)])  5.42 us
    unnamed x27, local copies, waits for them, and re-layouts  4.14 us
  transfers between devices with their start and end apart: 19, of which 8 were waited for; matrix products, arithmetic and copies ran while one was open for 7% of the time, Pallas kernels for 2%

profile of v4, /device:TPU:2, one launch (start us, length us, event | category | flops | bytes accessed | tf_op | source)
XLA Modules:
  0.0 179.5 jit_solution(9745189302406294568)
XLA Ops:
  7.2 7.8 %collective-permute-start = (f32[2,256,256]{2,1,0:T(8,128)}, f32[2,256,256]{2,1,0:T(8,128)S(1)}, u32[]{:S(2)}, u32[]{:S(2)}) collective-permute-start(f32[2,256,256]{2,1,0:T(8,128)} %own.1), channel_id=1, source_target_pairs={{4,0},{8,4},{12,8},{20,16},{24,20},{28,24},{36,32},{40,36},{44,40}... | collective-permute-start | bytes 1572872 | tf_op jit(solution)/shard_map/ppermute | solution.py:225
  15.0 1.3 collective-permute-start.1
  16.3 0.8 copy.16
  17.1 0.1 reshape.20
  17.8 0.1 add_bitcast_fusion
  17.9 0.5 pad.4.card
  18.4 2.8 %light.1 = (f32[256,256]{1,0:T(8,128)}, f32[256,256]{1,0:T(8,128)}, f32[2,256,256]{2,1,0:T(8,128)}) custom-call(s32[1,128]{1,0:T(1,128)} %pad.4.card, f32[2,2,256,256]{3,2,1,0:T(8,128)} %probe.3), custom_call_target="tpu_custom_call" | custom-call | tf_op jit(solution)/shard_map/light/pallas_call | solution.py:206
  21.2 1.7 collective-permute-done.right
  22.9 1.3 collective-permute-start.4
  24.3 0.7 collective-permute-start.2
  25.0 1.3 collective-permute-start.3
  26.3 5.4 %collective-permute-done.3.corner_b = f32[2,256,256]{2,1,0:T(8,128)S(1)} collective-permute-done((f32[2,256,256]{2,1,0:T(8,128)S(1)}, f32[2,256,256]{2,1,0:T(8,128)S(1)}, u32[]{:S(2)}, u32[]{:S(2)}) %collective-permute-start.3) | collective-permute-done | bytes 524320 | tf_op jit(solution)/shard_map/ppermute | solution.py:247
  31.8 0.8 copy-done.6
  32.5 18.5 %slots.1 = (f32[4,2,64,256]{3,2,1,0:T(8,128)}, f32[4,2,64,256]{3,2,1,0:T(8,128)}, f32[2,4,2,64,256]{4,3,2,1,0:T(8,128)}, f32[16,5,8,256]{3,2,1,0:T(8,128)}, f32[16,5,8,256]{3,2,1,0:T(8,128)}) custom-call(s32[1,128]{1,0:T(1,128)} %pad.4.card, f32[2,256,256]{2,1,0:T(8,128)} %own.1, f32[2,256,256]{2,1,0:T(8,128)} %copy-done.3, f32[2,256,256]{2,1,0:T(8,128)} %copy-done.4, ...), custom_call_target="tpu_custom_call" | custom-call | tf_op jit(solution)/shard_map/slots/pallas_call | solution.py:159
  51.0 1.9 %collective-permute-start.5 = (f32[16,5,8,256]{3,2,1,0:T(8,128)}, f32[16,5,8,256]{3,2,1,0:T(8,128)S(1)}, u32[]{:S(2)}, u32[]{:S(2)}) collective-permute-start(f32[16,5,8,256]{3,2,1,0:T(8,128)} %get-tuple-element.21), channel_id=1, source_target_pairs={{0,16},{16,0},{1,17},{17,1},{2,18},{18,2},{3,19},{19,3},{4,20},{20... | collective-permute-start | bytes 1966088 | tf_op jit(solution)/shard_map/ppermute | solution.py:229
  52.9 2.5 %collective-permute-start.6 = (f32[2,4,2,64,256]{4,3,2,1,0:T(8,128)}, f32[2,4,2,64,256]{4,3,2,1,0:T(8,128)S(1)}, u32[]{:S(2)}, u32[]{:S(2)}) collective-permute-start(f32[2,4,2,64,256]{4,3,2,1,0:T(8,128)} %get-tuple-element.22), channel_id=1, source_target_pairs={{0,16},{4,20},{8,24},{12,28},{16,32},{20,36},{24,40},{28,44},{32,4... | collective-permute-start | bytes 3145736 | tf_op jit(solution)/shard_map/ppermute | solution.py:225
  55.4 2.0 %add.75 = f32[16,5,8,256]{3,2,1,0:T(8,128)} add(f32[16,5,8,256]{3,2,1,0:T(8,128)} %get-tuple-element.20, f32[16,5,8,256]{3,2,1,0:T(8,128)S(1)} %collective-permute-done.5) | non-fusion elementwise | flops 163840 | bytes 1966080 | tf_op jit(solution)/shard_map/add | solution.py:271
  57.5 10.7 %all-to-all-start = ((f32[16,5,8,256]{3,2,1,0:T(8,128)}), f32[16,5,8,256]{3,2,1,0:T(8,128)S(1)}, u32[]{:S(2)}, u32[]{:S(2)}) async-start(f32[16,5,8,256]{3,2,1,0:T(8,128)} %add.75), calls=%async_computation | async-start | bytes 1310720 | tf_op jit(solution)/shard_map/all_to_all | solution.py:237
  68.3 3.5 %collective-permute-start.8 = (f32[256,256]{1,0:T(8,128)S(1)}, f32[256,256]{1,0:T(8,128)}, u32[]{:S(2)}, u32[]{:S(2)}) collective-permute-start(f32[256,256]{1,0:T(8,128)S(1)} %fusion.1), channel_id=1, source_target_pairs={{0,4},{4,8},{8,12},{16,20},{20,24},{24,28},{32,36},{36,40},{40,44}... | collective-permute-start | bytes 786440 | tf_op jit(solution)/shard_map/ppermute | solution.py:225
  71.8 7.6 %all-to-all-done = f32[16,5,8,256]{3,2,1,0:T(8,128)S(1)} async-done(((f32[16,5,8,256]{3,2,1,0:T(8,128)}), f32[16,5,8,256]{3,2,1,0:T(8,128)S(1)}, u32[]{:S(2)}, u32[]{:S(2)}) %all-to-all-start) | async-done | bytes 655392 | tf_op jit(solution)/shard_map/all_to_all | solution.py:237
  79.5 0.7 broadcast_in_dim.23
  80.1 6.9 %all-to-all-start.1 = ((f32[4,5,8,256]{3,2,1,0:T(8,128)}), f32[4,5,8,256]{3,2,1,0:T(8,128)S(1)}, u32[]{:S(2)}, u32[]{:S(2)}) async-start(f32[4,5,8,256]{3,2,1,0:T(8,128)} %broadcast_in_dim.23), calls=%async_computation.3 | async-start | bytes 327680 | tf_op jit(solution)/shard_map/all_to_all | solution.py:237
  87.0 0.1 bitcast_add_fusion
  87.1 3.0 %collective-permute-start.7 = (f32[4,2,64,256]{3,2,1,0:T(8,128)S(1)}, f32[4,2,64,256]{3,2,1,0:T(8,128)}, u32[]{:S(2)}, u32[]{:S(2)}) collective-permute-start(f32[4,2,64,256]{3,2,1,0:T(8,128)S(1)} %bitcast_add_fusion), channel_id=1, source_target_pairs={{0,4},{4,8},{8,12},{16,20},{20,24},{24,28},{32,36},{36,40},{40,44}... | collective-permute-start | bytes 1572872 | tf_op jit(solution)/shard_map/ppermute | solution.py:225
  90.2 1.7 fusion.3
  91.9 0.0 reduce-scatter.5.cloned.1.call-update
  91.9 2.1 %all-to-all-done.1 = f32[4,5,8,256]{3,2,1,0:T(8,128)S(1)} async-done(((f32[4,5,8,256]{3,2,1,0:T(8,128)}), f32[4,5,8,256]{3,2,1,0:T(8,128)S(1)}, u32[]{:S(2)}, u32[]{:S(2)}) %all-to-all-start.1) | async-done | bytes 163872 | tf_op jit(solution)/shard_map/all_to_all | solution.py:237
  94.0 0.7 broadcast_in_dim.24
  94.7 12.7 %all-to-all-start.2 = ((f32[4,5,8,256]{3,2,1,0:T(8,128)}), f32[4,5,8,256]{3,2,1,0:T(8,128)S(1)}, u32[]{:S(2)}, u32[]{:S(2)}) async-start(f32[4,5,8,256]{3,2,1,0:T(8,128)} %broadcast_in_dim.24), calls=%async_computation.4 | async-start | bytes 327680 | tf_op jit(solution)/shard_map/all_to_all | solution.py:237
  107.4 1.9 %fusion = f32[4,2,64,256]{3,2,1,0:T(8,128)} fusion(f32[4,2,64,256]{3,2,1,0:T(8,128)} %collective-permute-done.7, f32[4,2,64,256]{3,2,1,0:T(8,128)S(1)} %copy-done.9, f32[2,4,2,64,256]{4,3,2,1,0:T(8,128)S(1)} %collective-permute-done.6), kind=kLoop, calls=%fused_computation.2 | loop fusion | flops 262144 | bytes 2097152 | tf_op jit(solution)/shard_map/add | solution.py:276
  109.3 0.0 reduce-scatter.3.cloned.1.call-update
  109.4 13.4 %all-to-all-done.2 = f32[4,5,8,256]{3,2,1,0:T(8,128)S(1)} async-done(((f32[4,5,8,256]{3,2,1,0:T(8,128)}), f32[4,5,8,256]{3,2,1,0:T(8,128)S(1)}, u32[]{:S(2)}, u32[]{:S(2)}) %all-to-all-start.2) | async-done | bytes 163872 | tf_op jit(solution)/shard_map/all_to_all | solution.py:237
  122.8 0.8 fusion.5
  123.6 0.8 broadcast_in_dim.25
  124.4 5.9 %all-to-all-start.3 = ((f32[16,4,8,256]{3,2,1,0:T(8,128)}), f32[16,4,8,256]{3,2,1,0:T(8,128)S(1)}, u32[]{:S(2)}, u32[]{:S(2)}) async-start(f32[16,4,8,256]{3,2,1,0:T(8,128)} %broadcast_in_dim.25), calls=%async_computation.5 | async-start | bytes 1048576 | tf_op jit(solution)/shard_map/all_to_all | solution.py:237
  130.4 0.8 broadcast_add_fusion
  131.2 7.0 %all-to-all-done.3 = f32[16,4,8,256]{3,2,1,0:T(8,128)S(1)} async-done(((f32[16,4,8,256]{3,2,1,0:T(8,128)}), f32[16,4,8,256]{3,2,1,0:T(8,128)S(1)}, u32[]{:S(2)}, u32[]{:S(2)}) %all-to-all-start.3) | async-done | bytes 524320 | tf_op jit(solution)/shard_map/all_to_all | solution.py:237
  138.3 1.9 %collective-permute-start.12 = (f32[4,128,256]{2,1,0:T(8,128)S(1)}, f32[4,128,256]{2,1,0:T(8,128)S(1)}, u32[]{:S(2)}, u32[]{:S(2)}) collective-permute-start(f32[4,128,256]{2,1,0:T(8,128)S(1)} %bitcast.40), channel_id=1, source_target_pairs={{0,16},{16,0},{1,17},{17,1},{2,18},{18,2},{3,19},{19,3},{4,20},{20... | collective-permute-start | bytes 1572872 | tf_op jit(solution)/shard_map/ppermute | solution.py:229
  140.2 14.7 %reduce-scatter.3.cloned.1.call-done = f32[1,2,64,256]{3,2,1,0:T(8,128)} async-done(((f32[4,2,64,256]{3,2,1,0:T(8,128)}), f32[1,2,64,256]{3,2,1,0:T(8,128)}) %reduce-scatter.3.cloned.1.call-update) | async-done | bytes 131088 | tf_op jit(solution)/shard_map/reduce_scatter | solution.py:277
  154.9 0.9 copy-done.12
  155.8 0.9 constant_dynamic-update-slice_fusion.5
  156.7 1.9 %collective-permute-start.9 = (f32[2,64,256]{2,1,0:T(8,128)S(1)}, f32[2,64,256]{2,1,0:T(8,128)S(1)}, u32[]{:S(2)}, u32[]{:S(2)}) collective-permute-start(f32[2,64,256]{2,1,0:T(8,128)S(1)} %get-tuple-element.29), channel_id=1, source_target_pairs={{0,1},{1,0},{2,3},{3,2},{4,5},{5,4},{6,7},{7,6},{8,9},{9,8},{10,11... | collective-permute-start | bytes 393224 | tf_op jit(solution)/shard_map/ppermute | solution.py:233
  158.7 4.0 %collective-permute-start.10 = (f32[2,64,256]{2,1,0:T(8,128)S(1)}, f32[2,64,256]{2,1,0:T(8,128)S(1)}, u32[]{:S(2)}, u32[]{:S(2)}) collective-permute-start(f32[2,64,256]{2,1,0:T(8,128)S(1)} %get-tuple-element.29), channel_id=1, source_target_pairs={{0,2},{1,3},{2,0},{3,1},{4,6},{5,7},{6,4},{7,5},{8,10},{9,11},{10,... | collective-permute-start | bytes 393224 | tf_op jit(solution)/shard_map/ppermute | solution.py:233
  162.7 0.1 broadcast_in_dim.22
  162.8 4.5 %collective-permute-start.11 = (f32[2,64,256]{2,1,0:T(8,128)S(1)}, f32[2,64,256]{2,1,0:T(8,128)S(1)}, u32[]{:S(2)}, u32[]{:S(2)}) collective-permute-start(f32[2,64,256]{2,1,0:T(8,128)S(1)} %get-tuple-element.29), channel_id=1, source_target_pairs={{0,3},{1,2},{2,1},{3,0},{4,7},{5,6},{6,5},{7,4},{8,11},{9,10},{10,... | collective-permute-start | bytes 393224 | tf_op jit(solution)/shard_map/ppermute | solution.py:233
  167.4 3.5 %collective-permute-done.11 = f32[2,64,256]{2,1,0:T(8,128)S(1)} collective-permute-done((f32[2,64,256]{2,1,0:T(8,128)S(1)}, f32[2,64,256]{2,1,0:T(8,128)S(1)}, u32[]{:S(2)}, u32[]{:S(2)}) %collective-permute-start.11) | collective-permute-done | bytes 131104 | tf_op jit(solution)/shard_map/ppermute | solution.py:233
  170.9 0.7 copy-done.8
  171.7 1.0 copy-done.2
  (47 shorter events, 0.4 us)
Async XLA Ops:
  7.2 15.8 %collective-permute-start = (f32[2,256,256]{2,1,0:T(8,128)}, f32[2,256,256]{2,1,0:T(8,128)S(1)}, u32[]{:S(2)}, u32[]{:S(2)}) collective-permute-start(f32[2,256,256]{2,1,0:T(8,128)} %own.1), channel_id=1, source_target_pairs={{4,0},{8,4},{12,8},{20,16},{24,20},{28,24},{36,32},{40,36},{44,40}... | collective-permute-start | bytes 1572872 | tf_op jit(solution)/shard_map/ppermute | solution.py:225
  15.0 7.9 %collective-permute-start.1 = (f32[2,256,256]{2,1,0:T(8,128)}, f32[2,256,256]{2,1,0:T(8,128)S(1)}, u32[]{:S(2)}, u32[]{:S(2)}) collective-permute-start(f32[2,256,256]{2,1,0:T(8,128)} %own.1), channel_id=1, source_target_pairs={{16,0},{20,4},{24,8},{28,12},{32,16},{36,20},{40,24},{44,28},{48,3... | collective-permute-start | bytes 1572872 | tf_op jit(solution)/shard_map/ppermute | solution.py:225
  22.9 8.8 %copy-start.3 = (f32[2,256,256]{2,1,0:T(8,128)}, f32[2,256,256]{2,1,0:T(8,128)S(1)}, u32[]{:S(2)}) copy-start(f32[2,256,256]{2,1,0:T(8,128)S(1)} %collective-permute-done.right) | copy-start | bytes 1572868
  22.9 8.8 %copy-start.4 = (f32[2,256,256]{2,1,0:T(8,128)}, f32[2,256,256]{2,1,0:T(8,128)S(1)}, u32[]{:S(2)}) copy-start(f32[2,256,256]{2,1,0:T(8,128)S(1)} %collective-permute-done.1.below) | copy-start | bytes 1572868
  22.9 3.3 %collective-permute-start.4 = (f32[2,256,256]{2,1,0:T(8,128)}, f32[2,256,256]{2,1,0:T(8,128)S(1)}, u32[]{:S(2)}, u32[]{:S(2)}) collective-permute-start(f32[2,256,256]{2,1,0:T(8,128)} %get-tuple-element.18), channel_id=1, source_target_pairs={{0,16},{4,20},{8,24},{12,28},{16,32},{20,36},{24,40},{28,44},{32,4... | collective-permute-start | bytes 1572872 | tf_op jit(solution)/shard_map/ppermute | solution.py:225
  24.3 2.0 %collective-permute-start.2 = (f32[2,256,256]{2,1,0:T(8,128)S(1)}, f32[2,256,256]{2,1,0:T(8,128)S(1)}, u32[]{:S(2)}, u32[]{:S(2)}) collective-permute-start(f32[2,256,256]{2,1,0:T(8,128)S(1)} %collective-permute-done.1.below), channel_id=1, source_target_pairs={{20,16},{24,20},{28,24},{52,48},{56,52},{60,56},{84,80},{88,84},{9... | collective-permute-start | bytes 1572872 | tf_op jit(solution)/shard_map/ppermute | solution.py:247
  25.0 6.8 %collective-permute-start.3 = (f32[2,256,256]{2,1,0:T(8,128)S(1)}, f32[2,256,256]{2,1,0:T(8,128)S(1)}, u32[]{:S(2)}, u32[]{:S(2)}) collective-permute-start(f32[2,256,256]{2,1,0:T(8,128)S(1)} %collective-permute-done.right), channel_id=1, source_target_pairs={{16,0},{17,1},{18,2},{19,3},{20,4},{21,5},{22,6},{23,7},{24,8},{25... | collective-permute-start | bytes 1572872 | tf_op jit(solution)/shard_map/ppermute | solution.py:247
  26.3 5.5 %copy-start = (f32[2,256,256]{2,1,0:T(8,128)}, f32[2,256,256]{2,1,0:T(8,128)S(1)}, u32[]{:S(2)}) copy-start(f32[2,256,256]{2,1,0:T(8,128)S(1)} %collective-permute-done.4.after) | copy-start | bytes 1572868
  26.3 5.5 %copy-start.5 = (f32[2,256,256]{2,1,0:T(8,128)}, f32[2,256,256]{2,1,0:T(8,128)S(1)}, u32[]{:S(2)}) copy-start(f32[2,256,256]{2,1,0:T(8,128)S(1)} %collective-permute-done.2.corner_a) | copy-start | bytes 1572868
  31.7 0.8 copy-start.6
  51.0 4.4 %collective-permute-start.5 = (f32[16,5,8,256]{3,2,1,0:T(8,128)}, f32[16,5,8,256]{3,2,1,0:T(8,128)S(1)}, u32[]{:S(2)}, u32[]{:S(2)}) collective-permute-start(f32[16,5,8,256]{3,2,1,0:T(8,128)} %get-tuple-element.21), channel_id=1, source_target_pairs={{0,16},{16,0},{1,17},{17,1},{2,18},{18,2},{3,19},{19,3},{4,20},{20... | collective-permute-start | bytes 1966088 | tf_op jit(solution)/shard_map/ppermute | solution.py:229
  52.9 26.5 %collective-permute-start.6 = (f32[2,4,2,64,256]{4,3,2,1,0:T(8,128)}, f32[2,4,2,64,256]{4,3,2,1,0:T(8,128)S(1)}, u32[]{:S(2)}, u32[]{:S(2)}) collective-permute-start(f32[2,4,2,64,256]{4,3,2,1,0:T(8,128)} %get-tuple-element.22), channel_id=1, source_target_pairs={{0,16},{4,20},{8,24},{12,28},{16,32},{20,36},{24,40},{28,44},{32,4... | collective-permute-start | bytes 3145736 | tf_op jit(solution)/shard_map/ppermute | solution.py:225
  57.5 10.8 %copy-start.1 = (f32[2,256,256]{2,1,0:T(8,128)S(1)}, f32[2,256,256]{2,1,0:T(8,128)}, u32[]{:S(2)}) copy-start(f32[2,256,256]{2,1,0:T(8,128)} %copy-done) | copy-start | bytes 1572868
  57.5 10.8 %copy-start.10 = (f32[256,256]{1,0:T(8,128)S(1)}, f32[256,256]{1,0:T(8,128)}, u32[]{:S(2)}) copy-start(f32[256,256]{1,0:T(8,128)} %get-tuple-element.26) | copy-start | bytes 786436
  57.5 21.9 %all-to-all-start = ((f32[16,5,8,256]{3,2,1,0:T(8,128)}), f32[16,5,8,256]{3,2,1,0:T(8,128)S(1)}, u32[]{:S(2)}, u32[]{:S(2)}) async-start(f32[16,5,8,256]{3,2,1,0:T(8,128)} %add.75), calls=%async_computation | async-start | bytes 1310720 | tf_op jit(solution)/shard_map/all_to_all | solution.py:237
  68.3 18.8 %copy-start.7 = (f32[4,2,64,256]{3,2,1,0:T(8,128)S(1)}, f32[4,2,64,256]{3,2,1,0:T(8,128)}, u32[]{:S(2)}) copy-start(f32[4,2,64,256]{3,2,1,0:T(8,128)} %get-tuple-element.24) | copy-start | bytes 1572868
  68.3 21.9 %collective-permute-start.8 = (f32[256,256]{1,0:T(8,128)S(1)}, f32[256,256]{1,0:T(8,128)}, u32[]{:S(2)}, u32[]{:S(2)}) collective-permute-start(f32[256,256]{1,0:T(8,128)S(1)} %fusion.1), channel_id=1, source_target_pairs={{0,4},{4,8},{8,12},{16,20},{20,24},{24,28},{32,36},{36,40},{40,44}... | collective-permute-start | bytes 786440 | tf_op jit(solution)/shard_map/ppermute | solution.py:225
  80.1 13.9 %all-to-all-start.1 = ((f32[4,5,8,256]{3,2,1,0:T(8,128)}), f32[4,5,8,256]{3,2,1,0:T(8,128)S(1)}, u32[]{:S(2)}, u32[]{:S(2)}) async-start(f32[4,5,8,256]{3,2,1,0:T(8,128)} %broadcast_in_dim.23), calls=%async_computation.3 | async-start | bytes 327680 | tf_op jit(solution)/shard_map/all_to_all | solution.py:237
  87.0 43.3 %reduce-scatter.5.cloned.1.call-start = ((), (), s32[]{:S(2)}) async-start(), calls=%async_computation.7 | async-start | bytes 327680 | tf_op jit(solution)/shard_map/reduce_scatter | solution.py:269
  87.0 3.1 %copy-start.11 = (f32[256,256]{1,0:T(8,128)S(1)}, f32[256,256]{1,0:T(8,128)}, u32[]{:S(2)}) copy-start(f32[256,256]{1,0:T(8,128)} %get-tuple-element.25) | copy-start | bytes 786436
  87.1 20.2 %collective-permute-start.7 = (f32[4,2,64,256]{3,2,1,0:T(8,128)S(1)}, f32[4,2,64,256]{3,2,1,0:T(8,128)}, u32[]{:S(2)}, u32[]{:S(2)}) collective-permute-start(f32[4,2,64,256]{3,2,1,0:T(8,128)S(1)} %bitcast_add_fusion), channel_id=1, source_target_pairs={{0,4},{4,8},{8,12},{16,20},{20,24},{24,28},{32,36},{36,40},{40,44}... | collective-permute-start | bytes 1572872 | tf_op jit(solution)/shard_map/ppermute | solution.py:225
  91.9 15.5 %copy-start.9 = (f32[4,2,64,256]{3,2,1,0:T(8,128)S(1)}, f32[4,2,64,256]{3,2,1,0:T(8,128)}, u32[]{:S(2)}) copy-start(f32[4,2,64,256]{3,2,1,0:T(8,128)} %get-tuple-element.19) | copy-start | bytes 1572868
  94.7 28.1 %all-to-all-start.2 = ((f32[4,5,8,256]{3,2,1,0:T(8,128)}), f32[4,5,8,256]{3,2,1,0:T(8,128)S(1)}, u32[]{:S(2)}, u32[]{:S(2)}) async-start(f32[4,5,8,256]{3,2,1,0:T(8,128)} %broadcast_in_dim.24), calls=%async_computation.4 | async-start | bytes 327680 | tf_op jit(solution)/shard_map/all_to_all | solution.py:237
  107.4 47.5 %reduce-scatter.3.cloned.1.call-start = ((), (), s32[]{:S(2)}) async-start(), calls=%async_computation.6 | async-start | bytes 655360 | tf_op jit(solution)/shard_map/reduce_scatter | solution.py:277
  124.4 13.8 %all-to-all-start.3 = ((f32[16,4,8,256]{3,2,1,0:T(8,128)}), f32[16,4,8,256]{3,2,1,0:T(8,128)S(1)}, u32[]{:S(2)}, u32[]{:S(2)}) async-start(f32[16,4,8,256]{3,2,1,0:T(8,128)} %broadcast_in_dim.25), calls=%async_computation.5 | async-start | bytes 1048576 | tf_op jit(solution)/shard_map/all_to_all | solution.py:237
  138.3 32.6 %collective-permute-start.12 = (f32[4,128,256]{2,1,0:T(8,128)S(1)}, f32[4,128,256]{2,1,0:T(8,128)S(1)}, u32[]{:S(2)}, u32[]{:S(2)}) collective-permute-start(f32[4,128,256]{2,1,0:T(8,128)S(1)} %bitcast.40), channel_id=1, source_target_pairs={{0,16},{16,0},{1,17},{17,1},{2,18},{18,2},{3,19},{19,3},{4,20},{20... | collective-permute-start | bytes 1572872 | tf_op jit(solution)/shard_map/ppermute | solution.py:229
  154.9 0.9 copy-start.12
  156.7 10.6 %collective-permute-start.9 = (f32[2,64,256]{2,1,0:T(8,128)S(1)}, f32[2,64,256]{2,1,0:T(8,128)S(1)}, u32[]{:S(2)}, u32[]{:S(2)}) collective-permute-start(f32[2,64,256]{2,1,0:T(8,128)S(1)} %get-tuple-element.29), channel_id=1, source_target_pairs={{0,1},{1,0},{2,3},{3,2},{4,5},{5,4},{6,7},{7,6},{8,9},{9,8},{10,11... | collective-permute-start | bytes 393224 | tf_op jit(solution)/shard_map/ppermute | solution.py:233
  158.7 8.7 %collective-permute-start.10 = (f32[2,64,256]{2,1,0:T(8,128)S(1)}, f32[2,64,256]{2,1,0:T(8,128)S(1)}, u32[]{:S(2)}, u32[]{:S(2)}) collective-permute-start(f32[2,64,256]{2,1,0:T(8,128)S(1)} %get-tuple-element.29), channel_id=1, source_target_pairs={{0,2},{1,3},{2,0},{3,1},{4,6},{5,7},{6,4},{7,5},{8,10},{9,11},{10,... | collective-permute-start | bytes 393224 | tf_op jit(solution)/shard_map/ppermute | solution.py:233
  162.8 8.1 %collective-permute-start.11 = (f32[2,64,256]{2,1,0:T(8,128)S(1)}, f32[2,64,256]{2,1,0:T(8,128)S(1)}, u32[]{:S(2)}, u32[]{:S(2)}) collective-permute-start(f32[2,64,256]{2,1,0:T(8,128)S(1)} %get-tuple-element.29), channel_id=1, source_target_pairs={{0,3},{1,2},{2,1},{3,0},{4,7},{5,6},{6,5},{7,4},{8,11},{9,10},{10,... | collective-permute-start | bytes 393224 | tf_op jit(solution)/shard_map/ppermute | solution.py:233
  170.9 0.8 copy-start.8
  171.7 1.0 copy-start.2
Sparse Core Ops, SparseCore 0:
  92.0 29.4 reduce-scatter.4
  125.1 29.7 reduce-scatter.2

commit v5 on v4

--- a/solution.py
+++ b/solution.py
@@ -11,7 +11,6 @@
 from jax.sharding import PartitionSpec as P
 
 S = 256
-QUARTERS = 4
 COUNT = 6
 TILE = ("z_high", "z_low", "core")
 
@@ -134,13 +133,10 @@
         return carry
 
     lax.fori_loop(0, card[0, COUNT], one_slot, 0)
-    rows = S // QUARTERS
-    for q in range(QUARTERS):
-        upper, lower = slice(q * rows, (q + 1) * rows), slice(S + q * rows, S + (q + 1) * rows)
-        top_left[q] = total[:, upper, :S]
-        top_right[q] = total[:, upper, S:]
-        bottom[0, q] = total[:, lower, :S]
-        bottom[1, q] = total[:, lower, S:]
+    top_left[...] = total[:, :S, :S]
+    top_right[...] = total[:, :S, S:]
+    bottom[0] = total[:, S:, :S]
+    bottom[1] = total[:, S:, S:]
     chunks, _, height, _ = keep.shape
     core = lax.axis_index("core")
     for chunk in range(chunks):
@@ -154,14 +150,14 @@
 def run_slots(card, blocks, probe, frames, chunks, after):
     height = S // 2 // chunks
     f32 = jnp.float32
-    quarter = (QUARTERS, 2, S // QUARTERS, S)
+    tile = (2, S, S)
     vmem = pl.BlockSpec(memory_space=pltpu.VMEM)
     return pl.pallas_call(
         slots_kernel,
         out_shape=(
-            jax.ShapeDtypeStruct(quarter, f32),
-            jax.ShapeDtypeStruct(quarter, f32),
-            jax.ShapeDtypeStruct((2, *quarter), f32),
+            jax.ShapeDtypeStruct(tile, f32),
+            jax.ShapeDtypeStruct(tile, f32),
+            jax.ShapeDtypeStruct((2, *tile), f32),
             jax.ShapeDtypeStruct((chunks, 5, height, S), f32),
             jax.ShapeDtypeStruct((chunks, 5, height, S), f32),
         ),
@@ -229,8 +225,10 @@
     return lax.ppermute(block, "core", [(0, 1), (1, 0)])
 
 
-def across_posts(block, bits):
-    return lax.ppermute(block, "pos", [(p, p ^ bits) for p in range(QUARTERS)])
+def sum_over_posts(block):
+    for bits in (1, 3):
+        block = block + lax.ppermute(block, "pos", [(p, p ^ bits) for p in range(4)])
+    return block
 
 
 def exchanged(block, axes):
@@ -266,24 +264,17 @@
         probe_planes, patterns[0, 0, 0], chunks, light_above,
     )
 
-    light = lax.psum_scatter(light + light_left, "pos", scatter_dimension=0, tiled=True)
+    light = sum_over_posts(light + light_left)
     from_above = moved(bottom, 1, 0)
     terms = keep + across_cores(send)
     terms = jnp.sum(exchanged(terms, plane), axis=0)
-    terms, from_above = lax.optimization_barrier((terms, from_above))
-    from_left = moved(top_right + from_above[1], 0, 1)
+    terms, right_sum = lax.optimization_barrier((terms, top_right + from_above[1]))
+    from_left = moved(right_sum, 0, 1)
     terms = jnp.sum(shared(terms, "z_low"), axis=0)
     tile_sum = top_left + from_above[0] + from_left
-    tile_sum = lax.psum_scatter(tile_sum, "pos", scatter_dimension=0, tiled=True)[0]
+    tile_sum = sum_over_posts(tile_sum)
+    object_new = object_planes + tile_sum / (light + 1.0)
     terms = jnp.sum(shared(terms, "z_high"), axis=0)
-
-    rows = S // QUARTERS
-    own_rows = lax.dynamic_slice_in_dim(object_planes, post * rows, rows, 1)
-    own_rows = own_rows + tile_sum / (light + 1.0)
-    object_new = jnp.zeros_like(object_planes)
-    for k in range(QUARTERS):
-        piece = across_posts(own_rows, k) if k else own_rows
-        object_new = lax.dynamic_update_slice_in_dim(object_new, piece, (post ^ k) * rows, 1)
 
     height = S // 2 // chunks
     place = core * (S // 2) + (band * posts + post) * height

time: 181 us -> 145 us (0.80)
  waiting for transfers between devices: 55.5 us -> 32.7 us
  between operations: 15 us -> 1.65 us
  starting transfers between devices: 71.9 us -> 84.2 us
  Pallas kernels: 21.3 us -> 12.1 us
    reduce_scatter x2 -> x0, waiting for transfers between devices: 14.7 us -> none  [the longest x1 14.7 us: on_device(): lax.psum_scatter(tile_sum, 'pos', scatter_dimension=0, tiled=True)[0]]
    ppermute x6, starting transfers between devices: 19.4 us -> 32.8 us  [moved(): return lax.ppermute(block, (*TILE, 'band'), route)]
    all_to_all x4, waiting for transfers between devices: 30.2 us -> 17.7 us  [exchanged(): return lax.all_to_all(block, axes, 0, 0)]
    pallas_call x1, Pallas kernels: 18.5 us -> 9.55 us  [run_slots(): pl.pallas_call(slots_kernel, out_shape=(jax.ShapeDtypeStruct(tile, f32),...]
    all_to_all x4, starting transfers between devices: 36.2 us -> 33.2 us  [exchanged(): return lax.all_to_all(block, axes, 0, 0)]
    ppermute x2, waiting for transfers between devices: 0.01 us -> 2.28 us  [across_cores(): return lax.ppermute(block, 'core', [(0, 1), (1, 0)])]
    ppermute x3 -> x4, waiting for transfers between devices: 3.49 us -> 5.45 us  [sum_over_posts(): lax.ppermute(block, 'pos', [(p, p ^ bits) for p in range(4)])]
    ppermute x3 -> x4, starting transfers between devices: 10.4 us -> 12.4 us  [sum_over_posts(): lax.ppermute(block, 'pos', [(p, p ^ bits) for p in range(4)])]
  transfers between devices with their start and end apart: 19 -> 18, of which waited for: 8 -> 7; matrix products, arithmetic and copies ran while one was open for 7% -> 8% of each run, Pallas kernels for 2% -> 2%
where the time goes in v5:
time: 145 us; the launch traced here: 144 us
  starting transfers between devices  84.2 us (58%)
  waiting for transfers between devices  32.7 us (23%)
  Pallas kernels  12.1 us (8%)
  other arithmetic  7.92 us (5%)
  local copies, waits for them, and re-layouts  5.62 us (4%)
  between operations  1.65 us (1%)
    all_to_all x4, starting transfers between devices, exchanged(): return lax.all_to_all(block, axes, 0, 0)  33.2 us
    ppermute x6, starting transfers between devices, moved(): return lax.ppermute(block, (*TILE, 'band'), route)  32.8 us
    all_to_all x4, waiting for transfers between devices, exchanged(): return lax.all_to_all(block, axes, 0, 0)  17.7 us
    ppermute x4, starting transfers between devices, sum_over_posts(): lax.ppermute(block, 'pos', [(p, p ^ bits) for p in range(4)])  12.4 us
    pallas_call x1, Pallas kernels, run_slots(): pl.pallas_call(slots_kernel, out_shape=(jax.ShapeDtypeStruct(tile, f32),...  9.55 us
    ppermute x4, waiting for transfers between devices, sum_over_posts(): lax.ppermute(block, 'pos', [(p, p ^ bits) for p in range(4)])  5.45 us
    ppermute x1, waiting for transfers between devices, corners(): lax.ppermute(right, 'core', [(1, 0)])  5.33 us
    ppermute x2, starting transfers between devices, across_cores(): return lax.ppermute(block, 'core', [(0, 1), (1, 0)])  3.84 us
  transfers between devices with their start and end apart: 18, of which 7 were waited for; matrix products, arithmetic and copies ran while one was open for 8% of the time, Pallas kernels for 2%

profile of v5, /device:TPU:2, one launch (start us, length us, event | category | flops | bytes accessed | tf_op | source)
XLA Modules:
  0.0 144.2 jit_solution(7418174652704034900)
XLA Ops:
  0.6 7.8 %collective-permute-start = (f32[2,256,256]{2,1,0:T(8,128)}, f32[2,256,256]{2,1,0:T(8,128)S(1)}, u32[]{:S(2)}, u32[]{:S(2)}) collective-permute-start(f32[2,256,256]{2,1,0:T(8,128)} %own.1), channel_id=1, source_target_pairs={{4,0},{8,4},{12,8},{20,16},{24,20},{28,24},{36,32},{40,36},{44,40}... | collective-permute-start | bytes 1572872 | tf_op jit(solution)/shard_map/ppermute | solution.py:221
  8.5 1.3 collective-permute-start.1
  9.8 0.8 copy.16
  10.5 0.1 reshape.20
  11.3 0.1 add_bitcast_fusion
  11.3 0.6 pad.4.card
  11.9 2.5 %light.1 = (f32[256,256]{1,0:T(8,128)}, f32[256,256]{1,0:T(8,128)}, f32[2,256,256]{2,1,0:T(8,128)}) custom-call(s32[1,128]{1,0:T(1,128)} %pad.4.card, f32[2,2,256,256]{3,2,1,0:T(8,128)} %probe.3), custom_call_target="tpu_custom_call" | custom-call | tf_op jit(solution)/shard_map/light/pallas_call | solution.py:202
  14.4 2.0 %collective-permute-done.right = f32[2,256,256]{2,1,0:T(8,128)S(1)} collective-permute-done((f32[2,256,256]{2,1,0:T(8,128)}, f32[2,256,256]{2,1,0:T(8,128)S(1)}, u32[]{:S(2)}, u32[]{:S(2)}) %collective-permute-start) | collective-permute-done | bytes 524320 | tf_op jit(solution)/shard_map/ppermute | solution.py:221
  16.4 1.4 collective-permute-start.4
  17.8 0.7 collective-permute-start.2
  18.5 1.3 collective-permute-start.3
  19.9 5.3 %collective-permute-done.3.corner_b = f32[2,256,256]{2,1,0:T(8,128)S(1)} collective-permute-done((f32[2,256,256]{2,1,0:T(8,128)S(1)}, f32[2,256,256]{2,1,0:T(8,128)S(1)}, u32[]{:S(2)}, u32[]{:S(2)}) %collective-permute-start.3) | collective-permute-done | bytes 524320 | tf_op jit(solution)/shard_map/ppermute | solution.py:245
  25.2 0.8 copy-done.7
  26.0 9.6 %slots.1 = (f32[2,256,256]{2,1,0:T(8,128)}, f32[2,256,256]{2,1,0:T(8,128)}, f32[2,2,256,256]{3,2,1,0:T(8,128)}, f32[16,5,8,256]{3,2,1,0:T(8,128)}, f32[16,5,8,256]{3,2,1,0:T(8,128)}) custom-call(s32[1,128]{1,0:T(1,128)} %pad.4.card, f32[2,256,256]{2,1,0:T(8,128)} %own.1, f32[2,256,256]{2,1,0:T(8,128)} %copy-done.4, f32[2,256,256]{2,1,0:T(8,128)} %copy-done.5, ...), custom_call_target="tpu_custom_call" | custom-call | tf_op jit(solution)/shard_map/slots/pallas_call | solution.py:155
  35.6 16.1 %collective-permute-start.5 = (f32[2,2,256,256]{3,2,1,0:T(8,128)}, f32[2,2,256,256]{3,2,1,0:T(8,128)S(1)}, u32[]{:S(2)}, u32[]{:S(2)}) collective-permute-start(f32[2,2,256,256]{3,2,1,0:T(8,128)} %get-tuple-element.20), channel_id=1, source_target_pairs={{0,16},{4,20},{8,24},{12,28},{16,32},{20,36},{24,40},{28,44},{32,4... | collective-permute-start | bytes 3145736 | tf_op jit(solution)/shard_map/ppermute | solution.py:221
  51.7 1.9 %collective-permute-start.6 = (f32[16,5,8,256]{3,2,1,0:T(8,128)}, f32[16,5,8,256]{3,2,1,0:T(8,128)S(1)}, u32[]{:S(2)}, u32[]{:S(2)}) collective-permute-start(f32[16,5,8,256]{3,2,1,0:T(8,128)} %get-tuple-element.22), channel_id=1, source_target_pairs={{0,16},{16,0},{1,17},{17,1},{2,18},{18,2},{3,19},{19,3},{4,20},{20... | collective-permute-start | bytes 1966088 | tf_op jit(solution)/shard_map/ppermute | solution.py:225
  53.6 2.3 %collective-permute-done.6 = f32[16,5,8,256]{3,2,1,0:T(8,128)S(1)} collective-permute-done((f32[16,5,8,256]{3,2,1,0:T(8,128)}, f32[16,5,8,256]{3,2,1,0:T(8,128)S(1)}, u32[]{:S(2)}, u32[]{:S(2)}) %collective-permute-start.6) | collective-permute-done | bytes 655392 | tf_op jit(solution)/shard_map/ppermute | solution.py:225
  55.9 2.0 %add.70 = f32[16,5,8,256]{3,2,1,0:T(8,128)} add(f32[16,5,8,256]{3,2,1,0:T(8,128)} %get-tuple-element.21, f32[16,5,8,256]{3,2,1,0:T(8,128)S(1)} %collective-permute-done.6) | non-fusion elementwise | flops 163840 | bytes 1966080 | tf_op jit(solution)/shard_map/add | solution.py:269
  57.9 7.6 %all-to-all-start = ((f32[16,5,8,256]{3,2,1,0:T(8,128)}), f32[16,5,8,256]{3,2,1,0:T(8,128)S(1)}, u32[]{:S(2)}, u32[]{:S(2)}) async-start(f32[16,5,8,256]{3,2,1,0:T(8,128)} %add.70), calls=%async_computation | async-start | bytes 1310720 | tf_op jit(solution)/shard_map/all_to_all | solution.py:235
  65.6 0.7 fusion.3
  66.3 3.4 %collective-permute-start.10 = (f32[256,256]{1,0:T(8,128)}, f32[256,256]{1,0:T(8,128)}, u32[]{:S(2)}, u32[]{:S(2)}) collective-permute-start(f32[256,256]{1,0:T(8,128)} %fusion.3), channel_id=1, source_target_pairs={{0,4},{4,8},{8,12},{16,20},{20,24},{24,28},{32,36},{36,40},{40,44}... | collective-permute-start | bytes 786440 | tf_op jit(solution)/shard_map/ppermute | solution.py:221
  69.7 0.1 fusion
  69.8 7.7 %all-to-all-done = f32[16,5,8,256]{3,2,1,0:T(8,128)S(1)} async-done(((f32[16,5,8,256]{3,2,1,0:T(8,128)}), f32[16,5,8,256]{3,2,1,0:T(8,128)S(1)}, u32[]{:S(2)}, u32[]{:S(2)}) %all-to-all-start) | async-done | bytes 655392 | tf_op jit(solution)/shard_map/all_to_all | solution.py:235
  77.6 0.7 broadcast_in_dim.19
  78.3 5.5 %all-to-all-start.1 = ((f32[4,5,8,256]{3,2,1,0:T(8,128)}), f32[4,5,8,256]{3,2,1,0:T(8,128)S(1)}, u32[]{:S(2)}, u32[]{:S(2)}) async-start(f32[4,5,8,256]{3,2,1,0:T(8,128)} %broadcast_in_dim.19), calls=%async_computation.1 | async-start | bytes 327680 | tf_op jit(solution)/shard_map/all_to_all | solution.py:235
  83.8 2.8 %collective-permute-start.7 = (f32[2,256,256]{2,1,0:T(8,128)S(1)}, f32[2,256,256]{2,1,0:T(8,128)}, u32[]{:S(2)}, u32[]{:S(2)}) collective-permute-start(f32[2,256,256]{2,1,0:T(8,128)S(1)} %fusion), channel_id=1, source_target_pairs={{0,4},{4,8},{8,12},{16,20},{20,24},{24,28},{32,36},{36,40},{40,44}... | collective-permute-start | bytes 1572872 | tf_op jit(solution)/shard_map/ppermute | solution.py:221
  86.6 1.0 fusion.5
  87.6 2.5 %collective-permute-start.11 = (f32[256,256]{1,0:T(8,128)S(1)}, f32[256,256]{1,0:T(8,128)S(1)}, u32[]{:S(2)}, u32[]{:S(2)}) collective-permute-start(f32[256,256]{1,0:T(8,128)S(1)} %fusion.5), channel_id=1, source_target_pairs={{0,1},{1,0},{2,3},{3,2},{4,5},{5,4},{6,7},{7,6},{8,9},{9,8},{10,11... | collective-permute-start | bytes 786440 | tf_op jit(solution)/shard_map/ppermute | solution.py:230
  90.1 0.7 broadcast_in_dim.20
  90.8 11.9 %all-to-all-start.2 = ((f32[4,5,8,256]{3,2,1,0:T(8,128)}), f32[4,5,8,256]{3,2,1,0:T(8,128)S(1)}, u32[]{:S(2)}, u32[]{:S(2)}) async-start(f32[4,5,8,256]{3,2,1,0:T(8,128)} %broadcast_in_dim.20), calls=%async_computation.2 | async-start | bytes 327680 | tf_op jit(solution)/shard_map/all_to_all | solution.py:235
  102.7 3.1 %collective-permute-start.12 = (f32[256,256]{1,0:T(8,128)S(1)}, f32[256,256]{1,0:T(8,128)}, u32[]{:S(2)}, u32[]{:S(2)}) collective-permute-start(f32[256,256]{1,0:T(8,128)S(1)} %add.78), channel_id=1, source_target_pairs={{0,3},{1,2},{2,1},{3,0},{4,7},{5,6},{6,5},{7,4},{8,11},{9,10},{10,... | collective-permute-start | bytes 786440 | tf_op jit(solution)/shard_map/ppermute | solution.py:230
  105.9 1.1 fusion.2
  107.1 2.2 %collective-permute-start.8 = (f32[2,256,256]{2,1,0:T(8,128)S(1)}, f32[2,256,256]{2,1,0:T(8,128)S(1)}, u32[]{:S(2)}, u32[]{:S(2)}) collective-permute-start(f32[2,256,256]{2,1,0:T(8,128)S(1)} %fusion.2), channel_id=1, source_target_pairs={{0,1},{1,0},{2,3},{3,2},{4,5},{5,4},{6,7},{7,6},{8,9},{9,8},{10,11... | collective-permute-start | bytes 1572872 | tf_op jit(solution)/shard_map/ppermute | solution.py:230
  109.2 7.7 %all-to-all-done.2 = f32[4,5,8,256]{3,2,1,0:T(8,128)S(1)} async-done(((f32[4,5,8,256]{3,2,1,0:T(8,128)}), f32[4,5,8,256]{3,2,1,0:T(8,128)S(1)}, u32[]{:S(2)}, u32[]{:S(2)}) %all-to-all-start.2) | async-done | bytes 163872 | tf_op jit(solution)/shard_map/all_to_all | solution.py:235
  117.0 0.8 fusion.6
  117.7 0.8 broadcast_in_dim.21
  118.6 8.1 %all-to-all-start.3 = ((f32[16,4,8,256]{3,2,1,0:T(8,128)}), f32[16,4,8,256]{3,2,1,0:T(8,128)S(1)}, u32[]{:S(2)}, u32[]{:S(2)}) async-start(f32[16,4,8,256]{3,2,1,0:T(8,128)} %broadcast_in_dim.21), calls=%async_computation.3 | async-start | bytes 1048576 | tf_op jit(solution)/shard_map/all_to_all | solution.py:235
  126.7 0.1 add.73
  126.8 4.6 %collective-permute-start.9 = (f32[2,256,256]{2,1,0:T(8,128)S(1)}, f32[2,256,256]{2,1,0:T(8,128)S(1)}, u32[]{:S(2)}, u32[]{:S(2)}) collective-permute-start(f32[2,256,256]{2,1,0:T(8,128)S(1)} %add.73), channel_id=1, source_target_pairs={{0,3},{1,2},{2,1},{3,0},{4,7},{5,6},{6,5},{7,4},{8,11},{9,10},{10,... | collective-permute-start | bytes 1572872 | tf_op jit(solution)/shard_map/ppermute | solution.py:230
  131.4 1.0 add_add_fusion
  132.4 2.2 %all-to-all-done.3 = f32[16,4,8,256]{3,2,1,0:T(8,128)S(1)} async-done(((f32[16,4,8,256]{3,2,1,0:T(8,128)}), f32[16,4,8,256]{3,2,1,0:T(8,128)S(1)}, u32[]{:S(2)}, u32[]{:S(2)}) %all-to-all-start.3) | async-done | bytes 524320 | tf_op jit(solution)/shard_map/all_to_all | solution.py:235
  134.7 1.9 %collective-permute-start.13 = (f32[4,128,256]{2,1,0:T(8,128)S(1)}, f32[4,128,256]{2,1,0:T(8,128)S(1)}, u32[]{:S(2)}, u32[]{:S(2)}) collective-permute-start(f32[4,128,256]{2,1,0:T(8,128)S(1)} %bitcast.39), channel_id=1, source_target_pairs={{0,16},{16,0},{1,17},{17,1},{2,18},{18,2},{3,19},{19,3},{4,20},{20... | collective-permute-start | bytes 1572872 | tf_op jit(solution)/shard_map/ppermute | solution.py:225
  136.6 0.1 broadcast_in_dim.18
  136.7 0.0 copy-start.2
  136.8 5.4 %collective-permute-done.9 = f32[2,256,256]{2,1,0:T(8,128)S(1)} collective-permute-done((f32[2,256,256]{2,1,0:T(8,128)S(1)}, f32[2,256,256]{2,1,0:T(8,128)S(1)}, u32[]{:S(2)}, u32[]{:S(2)}) %collective-permute-start.9) | collective-permute-done | bytes 524320 | tf_op jit(solution)/shard_map/ppermute | solution.py:230
  142.2 0.9 divide_add_fusion
  143.2 0.0 copy-start.3
  143.2 1.0 copy-done.3
  (39 shorter events, 0.3 us)
Async XLA Ops:
  0.6 15.8 %collective-permute-start = (f32[2,256,256]{2,1,0:T(8,128)}, f32[2,256,256]{2,1,0:T(8,128)S(1)}, u32[]{:S(2)}, u32[]{:S(2)}) collective-permute-start(f32[2,256,256]{2,1,0:T(8,128)} %own.1), channel_id=1, source_target_pairs={{4,0},{8,4},{12,8},{20,16},{24,20},{28,24},{36,32},{40,36},{44,40}... | collective-permute-start | bytes 1572872 | tf_op jit(solution)/shard_map/ppermute | solution.py:221
  8.5 7.9 %collective-permute-start.1 = (f32[2,256,256]{2,1,0:T(8,128)}, f32[2,256,256]{2,1,0:T(8,128)S(1)}, u32[]{:S(2)}, u32[]{:S(2)}) collective-permute-start(f32[2,256,256]{2,1,0:T(8,128)} %own.1), channel_id=1, source_target_pairs={{16,0},{20,4},{24,8},{28,12},{32,16},{36,20},{40,24},{44,28},{48,3... | collective-permute-start | bytes 1572872 | tf_op jit(solution)/shard_map/ppermute | solution.py:221
  16.4 8.8 %copy-start.4 = (f32[2,256,256]{2,1,0:T(8,128)}, f32[2,256,256]{2,1,0:T(8,128)S(1)}, u32[]{:S(2)}) copy-start(f32[2,256,256]{2,1,0:T(8,128)S(1)} %collective-permute-done.right) | copy-start | bytes 1572868
  16.4 8.8 %copy-start.5 = (f32[2,256,256]{2,1,0:T(8,128)}, f32[2,256,256]{2,1,0:T(8,128)S(1)}, u32[]{:S(2)}) copy-start(f32[2,256,256]{2,1,0:T(8,128)S(1)} %collective-permute-done.1.below) | copy-start | bytes 1572868
  16.4 3.4 %collective-permute-start.4 = (f32[2,256,256]{2,1,0:T(8,128)}, f32[2,256,256]{2,1,0:T(8,128)S(1)}, u32[]{:S(2)}, u32[]{:S(2)}) collective-permute-start(f32[2,256,256]{2,1,0:T(8,128)} %get-tuple-element.18), channel_id=1, source_target_pairs={{0,16},{4,20},{8,24},{12,28},{16,32},{20,36},{24,40},{28,44},{32,4... | collective-permute-start | bytes 1572872 | tf_op jit(solution)/shard_map/ppermute | solution.py:221
  17.8 2.0 %collective-permute-start.2 = (f32[2,256,256]{2,1,0:T(8,128)S(1)}, f32[2,256,256]{2,1,0:T(8,128)S(1)}, u32[]{:S(2)}, u32[]{:S(2)}) collective-permute-start(f32[2,256,256]{2,1,0:T(8,128)S(1)} %collective-permute-done.1.below), channel_id=1, source_target_pairs={{20,16},{24,20},{28,24},{52,48},{56,52},{60,56},{84,80},{88,84},{9... | collective-permute-start | bytes 1572872 | tf_op jit(solution)/shard_map/ppermute | solution.py:245
  18.5 6.7 %collective-permute-start.3 = (f32[2,256,256]{2,1,0:T(8,128)S(1)}, f32[2,256,256]{2,1,0:T(8,128)S(1)}, u32[]{:S(2)}, u32[]{:S(2)}) collective-permute-start(f32[2,256,256]{2,1,0:T(8,128)S(1)} %collective-permute-done.right), channel_id=1, source_target_pairs={{16,0},{17,1},{18,2},{19,3},{20,4},{21,5},{22,6},{23,7},{24,8},{25... | collective-permute-start | bytes 1572872 | tf_op jit(solution)/shard_map/ppermute | solution.py:245
  19.8 5.4 %copy-start = (f32[2,256,256]{2,1,0:T(8,128)}, f32[2,256,256]{2,1,0:T(8,128)S(1)}, u32[]{:S(2)}) copy-start(f32[2,256,256]{2,1,0:T(8,128)S(1)} %collective-permute-done.4.after) | copy-start | bytes 1572868
  19.9 5.4 %copy-start.6 = (f32[2,256,256]{2,1,0:T(8,128)}, f32[2,256,256]{2,1,0:T(8,128)S(1)}, u32[]{:S(2)}) copy-start(f32[2,256,256]{2,1,0:T(8,128)S(1)} %collective-permute-done.2.corner_a) | copy-start | bytes 1572868
  25.2 0.8 copy-start.7
  35.6 34.2 %collective-permute-start.5 = (f32[2,2,256,256]{3,2,1,0:T(8,128)}, f32[2,2,256,256]{3,2,1,0:T(8,128)S(1)}, u32[]{:S(2)}, u32[]{:S(2)}) collective-permute-start(f32[2,2,256,256]{3,2,1,0:T(8,128)} %get-tuple-element.20), channel_id=1, source_target_pairs={{0,16},{4,20},{8,24},{12,28},{16,32},{20,36},{24,40},{28,44},{32,4... | collective-permute-start | bytes 3145736 | tf_op jit(solution)/shard_map/ppermute | solution.py:221
  51.7 4.2 %collective-permute-start.6 = (f32[16,5,8,256]{3,2,1,0:T(8,128)}, f32[16,5,8,256]{3,2,1,0:T(8,128)S(1)}, u32[]{:S(2)}, u32[]{:S(2)}) collective-permute-start(f32[16,5,8,256]{3,2,1,0:T(8,128)} %get-tuple-element.22), channel_id=1, source_target_pairs={{0,16},{16,0},{1,17},{17,1},{2,18},{18,2},{3,19},{19,3},{4,20},{20... | collective-permute-start | bytes 1966088 | tf_op jit(solution)/shard_map/ppermute | solution.py:225
  57.9 7.6 %copy-start.1 = (f32[2,256,256]{2,1,0:T(8,128)S(1)}, f32[2,256,256]{2,1,0:T(8,128)}, u32[]{:S(2)}) copy-start(f32[2,256,256]{2,1,0:T(8,128)} %copy-done) | copy-start | bytes 1572868
  57.9 7.7 %copy-start.10 = (f32[256,256]{1,0:T(8,128)S(1)}, f32[256,256]{1,0:T(8,128)}, u32[]{:S(2)}) copy-start(f32[256,256]{1,0:T(8,128)} %get-tuple-element.26) | copy-start | bytes 786436
  57.9 19.6 %all-to-all-start = ((f32[16,5,8,256]{3,2,1,0:T(8,128)}), f32[16,5,8,256]{3,2,1,0:T(8,128)S(1)}, u32[]{:S(2)}, u32[]{:S(2)}) async-start(f32[16,5,8,256]{3,2,1,0:T(8,128)} %add.70), calls=%async_computation | async-start | bytes 1310720 | tf_op jit(solution)/shard_map/all_to_all | solution.py:235
  65.6 4.1 %copy-start.8 = (f32[2,256,256]{2,1,0:T(8,128)S(1)}, f32[2,256,256]{2,1,0:T(8,128)}, u32[]{:S(2)}) copy-start(f32[2,256,256]{2,1,0:T(8,128)} %get-tuple-element.23) | copy-start | bytes 1572868
  66.3 20.2 %collective-permute-start.10 = (f32[256,256]{1,0:T(8,128)}, f32[256,256]{1,0:T(8,128)}, u32[]{:S(2)}, u32[]{:S(2)}) collective-permute-start(f32[256,256]{1,0:T(8,128)} %fusion.3), channel_id=1, source_target_pairs={{0,4},{4,8},{8,12},{16,20},{20,24},{24,28},{32,36},{36,40},{40,44}... | collective-permute-start | bytes 786440 | tf_op jit(solution)/shard_map/ppermute | solution.py:221
  77.6 9.0 %copy-start.11 = (f32[256,256]{1,0:T(8,128)S(1)}, f32[256,256]{1,0:T(8,128)}, u32[]{:S(2)}) copy-start(f32[256,256]{1,0:T(8,128)} %get-tuple-element.25) | copy-start | bytes 786436
  78.3 11.8 %all-to-all-start.1 = ((f32[4,5,8,256]{3,2,1,0:T(8,128)}), f32[4,5,8,256]{3,2,1,0:T(8,128)S(1)}, u32[]{:S(2)}, u32[]{:S(2)}) async-start(f32[4,5,8,256]{3,2,1,0:T(8,128)} %broadcast_in_dim.19), calls=%async_computation.1 | async-start | bytes 327680 | tf_op jit(solution)/shard_map/all_to_all | solution.py:235
  83.8 22.1 %collective-permute-start.7 = (f32[2,256,256]{2,1,0:T(8,128)S(1)}, f32[2,256,256]{2,1,0:T(8,128)}, u32[]{:S(2)}, u32[]{:S(2)}) collective-permute-start(f32[2,256,256]{2,1,0:T(8,128)S(1)} %fusion), channel_id=1, source_target_pairs={{0,4},{4,8},{8,12},{16,20},{20,24},{24,28},{32,36},{36,40},{40,44}... | collective-permute-start | bytes 1572872 | tf_op jit(solution)/shard_map/ppermute | solution.py:221
  87.6 15.1 %collective-permute-start.11 = (f32[256,256]{1,0:T(8,128)S(1)}, f32[256,256]{1,0:T(8,128)S(1)}, u32[]{:S(2)}, u32[]{:S(2)}) collective-permute-start(f32[256,256]{1,0:T(8,128)S(1)} %fusion.5), channel_id=1, source_target_pairs={{0,1},{1,0},{2,3},{3,2},{4,5},{5,4},{6,7},{7,6},{8,9},{9,8},{10,11... | collective-permute-start | bytes 786440 | tf_op jit(solution)/shard_map/ppermute | solution.py:230
  90.8 15.1 %copy-start.9 = (f32[2,256,256]{2,1,0:T(8,128)S(1)}, f32[2,256,256]{2,1,0:T(8,128)}, u32[]{:S(2)}) copy-start(f32[2,256,256]{2,1,0:T(8,128)} %get-tuple-element.19) | copy-start | bytes 1572868
  90.8 26.2 %all-to-all-start.2 = ((f32[4,5,8,256]{3,2,1,0:T(8,128)}), f32[4,5,8,256]{3,2,1,0:T(8,128)S(1)}, u32[]{:S(2)}, u32[]{:S(2)}) async-start(f32[4,5,8,256]{3,2,1,0:T(8,128)} %broadcast_in_dim.20), calls=%async_computation.2 | async-start | bytes 327680 | tf_op jit(solution)/shard_map/all_to_all | solution.py:235
  102.7 28.7 %collective-permute-start.12 = (f32[256,256]{1,0:T(8,128)S(1)}, f32[256,256]{1,0:T(8,128)}, u32[]{:S(2)}, u32[]{:S(2)}) collective-permute-start(f32[256,256]{1,0:T(8,128)S(1)} %add.78), channel_id=1, source_target_pairs={{0,3},{1,2},{2,1},{3,0},{4,7},{5,6},{6,5},{7,4},{8,11},{9,10},{10,... | collective-permute-start | bytes 786440 | tf_op jit(solution)/shard_map/ppermute | solution.py:230
  107.1 19.7 %collective-permute-start.8 = (f32[2,256,256]{2,1,0:T(8,128)S(1)}, f32[2,256,256]{2,1,0:T(8,128)S(1)}, u32[]{:S(2)}, u32[]{:S(2)}) collective-permute-start(f32[2,256,256]{2,1,0:T(8,128)S(1)} %fusion.2), channel_id=1, source_target_pairs={{0,1},{1,0},{2,3},{3,2},{4,5},{5,4},{6,7},{7,6},{8,9},{9,8},{10,11... | collective-permute-start | bytes 1572872 | tf_op jit(solution)/shard_map/ppermute | solution.py:230
  118.6 16.1 %all-to-all-start.3 = ((f32[16,4,8,256]{3,2,1,0:T(8,128)}), f32[16,4,8,256]{3,2,1,0:T(8,128)S(1)}, u32[]{:S(2)}, u32[]{:S(2)}) async-start(f32[16,4,8,256]{3,2,1,0:T(8,128)} %broadcast_in_dim.21), calls=%async_computation.3 | async-start | bytes 1048576 | tf_op jit(solution)/shard_map/all_to_all | solution.py:235
  126.8 15.4 %collective-permute-start.9 = (f32[2,256,256]{2,1,0:T(8,128)S(1)}, f32[2,256,256]{2,1,0:T(8,128)S(1)}, u32[]{:S(2)}, u32[]{:S(2)}) collective-permute-start(f32[2,256,256]{2,1,0:T(8,128)S(1)} %add.73), channel_id=1, source_target_pairs={{0,3},{1,2},{2,1},{3,0},{4,7},{5,6},{6,5},{7,4},{8,11},{9,10},{10,... | collective-permute-start | bytes 1572872 | tf_op jit(solution)/shard_map/ppermute | solution.py:230
  134.7 8.4 %collective-permute-start.13 = (f32[4,128,256]{2,1,0:T(8,128)S(1)}, f32[4,128,256]{2,1,0:T(8,128)S(1)}, u32[]{:S(2)}, u32[]{:S(2)}) collective-permute-start(f32[4,128,256]{2,1,0:T(8,128)S(1)} %bitcast.39), channel_id=1, source_target_pairs={{0,16},{16,0},{1,17},{17,1},{2,18},{18,2},{3,19},{19,3},{4,20},{20... | collective-permute-start | bytes 1572872 | tf_op jit(solution)/shard_map/ppermute | solution.py:225
  136.7 5.5 %copy-start.2 = (f32[2,256,256]{2,1,0:T(8,128)S(1)}, f32[2,256,256]{2,1,0:T(8,128)}, u32[]{:S(2)}) copy-start(f32[2,256,256]{2,1,0:T(8,128)} %own.1) | copy-start | bytes 1572868
  143.2 1.0 copy-start.3

commit v6 on v5

--- a/solution.py
+++ b/solution.py
@@ -175,39 +175,40 @@
     )(card, *blocks, probe, frames, *(jnp.asarray(t) for t in tables()), after)
 
 
-def light_kernel(card, probe, top_left, top_right, bottom, total):
+def light_kernel(cards, probe, own, right, below, corner, total):
     power = jnp.zeros((S, S), jnp.float32)
     for m in range(2):
         power += probe[0, m] * probe[0, m] + probe[1, m] * probe[1, m]
     total[...] = jnp.zeros_like(total)
 
-    def one_slot(slot, carry):
-        row, column = card[0, 2 * slot], card[0, 2 * slot + 1]
-        inside, fine = lax.rem(row, 8), lax.rem(column, 128)
-        band_rows = pl.ds(pl.multiple_of(row - inside, 8), S + 8)
-        band_columns = pl.ds(pl.multiple_of(column - fine, 128), 384)
-        total[band_rows, band_columns] += placed(power, inside, fine)
-        return carry
-
-    lax.fori_loop(0, card[0, COUNT], one_slot, 0)
-    top_left[...] = total[:S, :S]
-    top_right[...] = total[:S, S:]
-    bottom[0] = total[S:, :S]
-    bottom[1] = total[S:, S:]
-
-
-def run_light(card, probe):
+    for post in range(cards.shape[0]):
+
+        def one_slot(slot, carry):
+            row, column = cards[post, 0, 2 * slot], cards[post, 0, 2 * slot + 1]
+            inside, fine = lax.rem(row, 8), lax.rem(column, 128)
+            band_rows = pl.ds(pl.multiple_of(row - inside, 8), S + 8)
+            band_columns = pl.ds(pl.multiple_of(column - fine, 128), 384)
+            total[band_rows, band_columns] += placed(power, inside, fine)
+            return carry
+
+        lax.fori_loop(0, cards[post, 0, COUNT], one_slot, 0)
+    own[...] = total[:S, :S]
+    right[...] = total[:S, S:]
+    below[...] = total[S:, :S]
+    corner[...] = total[S:, S:]
+
+
+def run_light(cards, probe):
     vmem = pl.BlockSpec(memory_space=pltpu.VMEM)
-    tile = jax.ShapeDtypeStruct((S, S), jnp.float32)
     return pl.pallas_call(
         light_kernel,
-        out_shape=(tile, tile, jax.ShapeDtypeStruct((2, S, S), jnp.float32)),
+        out_shape=(jax.ShapeDtypeStruct((S, S), jnp.float32),) * 4,
         in_specs=[pl.BlockSpec(memory_space=pltpu.SMEM), vmem],
-        out_specs=[vmem] * 3,
+        out_specs=[vmem] * 4,
         scratch_shapes=[pltpu.VMEM((2 * S, 2 * S), jnp.float32)],
         compiler_params=pltpu.CompilerParams(vmem_limit_bytes=54 * 1024 * 1024),
         name="light",
-    )(card, probe)
+    )(cards, probe)
 
 
 def moved(block, tiles_by, bands_by):
@@ -253,28 +254,26 @@
     right = moved(object_planes, 0, -1)
     below = moved(object_planes, -1, 0)
     card = jnp.pad(jnp.concatenate([offsets.reshape(6), counts.reshape(1)])[None], ((0, 0), (0, 121)))
-    light, light_right, light_bottom = run_light(card, probe_planes)
-    right, below, light_bottom = lax.optimization_barrier((right, below, light_bottom))
-    light_above = moved(light_bottom, 1, 0)
+    light, *spill = run_light(shared(card, "pos"), probe_planes)
+    right, below, spill = lax.optimization_barrier((right, below, spill))
     corner_a, corner_b = corners(right, below)
-    light_left = moved(light_right + light_above[1], 0, 1)
-    light = light + light_above[0]
+    light = light + moved(spill[0], 0, 1) + moved(spill[1], 1, 0) + moved(spill[2], 1, 1)
     top_left, top_right, bottom, keep, send = run_slots(
         card, (object_planes, right, below, corner_a, corner_b),
-        probe_planes, patterns[0, 0, 0], chunks, light_above,
-    )
-
-    light = sum_over_posts(light + light_left)
+        probe_planes, patterns[0, 0, 0], chunks, light,
+    )
+
     from_above = moved(bottom, 1, 0)
     terms = keep + across_cores(send)
     terms = jnp.sum(exchanged(terms, plane), axis=0)
-    terms, right_sum = lax.optimization_barrier((terms, top_right + from_above[1]))
-    from_left = moved(right_sum, 0, 1)
-    terms = jnp.sum(shared(terms, "z_low"), axis=0)
+    terms, from_above = lax.optimization_barrier((terms, from_above))
+    from_left = moved(top_right + from_above[1], 0, 1)
+    terms = jnp.sum(shared(terms, "z_high"), axis=0)
+    terms, from_left = lax.optimization_barrier((terms, from_left))
     tile_sum = top_left + from_above[0] + from_left
     tile_sum = sum_over_posts(tile_sum)
     object_new = object_planes + tile_sum / (light + 1.0)
-    terms = jnp.sum(shared(terms, "z_high"), axis=0)
+    terms = jnp.sum(shared(terms, "z_low"), axis=0)
 
     height = S // 2 // chunks
     place = core * (S // 2) + (band * posts + post) * height

time: 145 us -> 156 us (1.076)
  the two profiles are of different devices: /device:TPU:2 before, /device:TPU:1 now
where the time goes in v6:
time: 156 us; the launch traced here: 155 us
  starting transfers between devices  62.2 us (40%)
  blocking collectives  49.9 us (32%)
  waiting for transfers between devices  17.4 us (11%)
  Pallas kernels  13.1 us (8%)
  local copies, waits for them, and re-layouts  6.13 us (4%)
  other arithmetic  4.96 us (3%)
  between operations  1.56 us (1%)
    all_to_all x3, blocking collectives, exchanged(): return lax.all_to_all(block, axes, 0, 0)  49.9 us
    ppermute x7, starting transfers between devices, moved(): return lax.ppermute(block, (*TILE, 'band'), route)  33.2 us
    all_to_all x2, starting transfers between devices, exchanged(): return lax.all_to_all(block, axes, 0, 0)  11 us
    pallas_call x1, Pallas kernels, run_slots(): pl.pallas_call(slots_kernel, out_shape=(jax.ShapeDtypeStruct(tile, f32),...  9.53 us
    ppermute x2, starting transfers between devices, across_cores(): return lax.ppermute(block, 'core', [(0, 1), (1, 0)])  8.08 us
    all_to_all x2, waiting for transfers between devices, exchanged(): return lax.all_to_all(block, axes, 0, 0)  6.76 us
    ppermute x2, starting transfers between devices, sum_over_posts(): lax.ppermute(block, 'pos', [(p, p ^ bits) for p in range(4)])  6.54 us
    ppermute x2, waiting for transfers between devices, sum_over_posts(): lax.ppermute(block, 'pos', [(p, p ^ bits) for p in range(4)])  5.78 us
  transfers between devices with their start and end apart: 15, of which 6 were waited for; matrix products, arithmetic and copies ran while one was open for 5% of the time, Pallas kernels for 2%

profile of v6, /device:TPU:1, one launch (start us, length us, event | category | flops | bytes accessed | tf_op | source)
XLA Modules:
  0.0 155.3 jit_solution(5953357006459446015)
XLA Ops:
  0.6 1.3 collective-permute-start
  1.9 8.8 %collective-permute-start.1 = (f32[2,256,256]{2,1,0:T(8,128)}, f32[2,256,256]{2,1,0:T(8,128)S(1)}, u32[]{:S(2)}, u32[]{:S(2)}) collective-permute-start(f32[2,256,256]{2,1,0:T(8,128)} %own.1), channel_id=1, source_target_pairs={{16,0},{20,4},{24,8},{28,12},{32,16},{36,20},{40,24},{44,28},{48,3... | collective-permute-start | bytes 1572872 | tf_op jit(solution)/shard_map/ppermute | solution.py:222
  10.7 0.8 copy.16
  11.5 0.1 reshape.21
  12.2 0.1 add_bitcast_fusion
  12.3 0.6 pad_bitcast_fusion
  12.9 7.0 %all_to_all.25.cards = s32[4,1,128]{2,1,0:T(1,128)} all-to-all(s32[4,1,128]{2,1,0:T(1,128)S(1)} %broadcast_in_dim.21), channel_id=1, replica_groups=mesh['z_high'=4,'z_low'=4,'core'=2,'band'=4,'pos'=4] {'pos'}, dimensions={0} | all-to-all | bytes 4096 | tf_op jit(solution)/shard_map/all_to_all | solution.py:236
  19.9 3.5 %light.1 = (f32[256,256]{1,0:T(8,128)}, f32[256,256]{1,0:T(8,128)}, f32[256,256]{1,0:T(8,128)}, f32[256,256]{1,0:T(8,128)}) custom-call(s32[4,1,128]{2,1,0:T(1,128)} %all_to_all.25.cards, f32[2,2,256,256]{3,2,1,0:T(8,128)} %probe.3), custom_call_target="tpu_custom_call" | custom-call | tf_op jit(solution)/shard_map/light/pallas_call | solution.py:203
  23.4 4.3 %collective-permute-start.4 = (f32[256,256]{1,0:T(8,128)}, f32[256,256]{1,0:T(8,128)S(1)}, u32[]{:S(2)}, u32[]{:S(2)}) collective-permute-start(f32[256,256]{1,0:T(8,128)} %get-tuple-element.26), channel_id=1, source_target_pairs={{0,4},{4,8},{8,12},{16,20},{20,24},{24,28},{32,36},{36,40},{40,44}... | collective-permute-start | bytes 786440 | tf_op jit(solution)/shard_map/ppermute | solution.py:222
  27.7 1.9 %collective-permute-start.5 = (f32[256,256]{1,0:T(8,128)}, f32[256,256]{1,0:T(8,128)S(1)}, u32[]{:S(2)}, u32[]{:S(2)}) collective-permute-start(f32[256,256]{1,0:T(8,128)} %get-tuple-element.27), channel_id=1, source_target_pairs={{0,16},{4,20},{8,24},{12,28},{16,32},{20,36},{24,40},{28,44},{32,4... | collective-permute-start | bytes 786440 | tf_op jit(solution)/shard_map/ppermute | solution.py:222
  29.6 1.9 %collective-permute-start.6 = (f32[256,256]{1,0:T(8,128)}, f32[256,256]{1,0:T(8,128)S(1)}, u32[]{:S(2)}, u32[]{:S(2)}) collective-permute-start(f32[256,256]{1,0:T(8,128)} %get-tuple-element.28), channel_id=1, source_target_pairs={{0,20},{4,24},{8,28},{16,36},{20,40},{24,44},{32,52},{36,56},{40,6... | collective-permute-start | bytes 786440 | tf_op jit(solution)/shard_map/ppermute | solution.py:222
  31.6 1.3 collective-permute-start.2
  32.9 2.0 %collective-permute-start.3 = (f32[2,256,256]{2,1,0:T(8,128)S(1)}, f32[2,256,256]{2,1,0:T(8,128)S(1)}, u32[]{:S(2)}, u32[]{:S(2)}) collective-permute-start(f32[2,256,256]{2,1,0:T(8,128)S(1)} %collective-permute-done.right), channel_id=1, source_target_pairs={{16,0},{17,1},{18,2},{19,3},{20,4},{21,5},{22,6},{23,7},{24,8},{25... | collective-permute-start | bytes 1572872 | tf_op jit(solution)/shard_map/ppermute | solution.py:246
  34.9 0.0 collective-permute-done.4
  34.9 0.0 collective-permute-done.5
  34.9 1.2 collective-permute-done.6
  36.1 1.7 %broadcast_add_fusion = (f32[256,256]{1,0:T(8,128)S(1)}, f32[256,256]{1,0:T(8,128)}) fusion(f32[256,256]{1,0:T(8,128)S(1)} %collective-permute-done.6, f32[256,256]{1,0:T(8,128)S(1)} %collective-permute-done.5, f32[256,256]{1,0:T(8,128)} %get-tuple-element.25, f32[256,256]{1,0:T(8,128)S(1)} %collective-permute-done.4), kind=kLoop, calls=%fused_computation.6 | loop fusion | flops 262144 | bytes 1572864 | tf_op jit(solution)/shard_map/add | solution.py:275
  37.8 3.7 %collective-permute-done.2.corner_a = f32[2,256,256]{2,1,0:T(8,128)S(1)} collective-permute-done((f32[2,256,256]{2,1,0:T(8,128)S(1)}, f32[2,256,256]{2,1,0:T(8,128)S(1)}, u32[]{:S(2)}, u32[]{:S(2)}) %collective-permute-start.2) | collective-permute-done | bytes 524320 | tf_op jit(solution)/shard_map/ppermute | solution.py:246
  41.5 0.8 copy-done.6
  42.3 0.2 copy-done.7
  42.5 9.5 %slots.1 = (f32[2,256,256]{2,1,0:T(8,128)}, f32[2,256,256]{2,1,0:T(8,128)}, f32[2,2,256,256]{3,2,1,0:T(8,128)}, f32[16,5,8,256]{3,2,1,0:T(8,128)}, f32[16,5,8,256]{3,2,1,0:T(8,128)}) custom-call(s32[1,128]{1,0:T(1,128)} %get-tuple-element.41.card, f32[2,256,256]{2,1,0:T(8,128)} %own.1, f32[2,256,256]{2,1,0:T(8,128)} %copy-done.4, f32[2,256,256]{2,1,0:T(8,128)} %copy-done.5, ...), custom_call_target="tpu_custom_call" | custom-call | tf_op jit(solution)/shard_map/slots/pallas_call | solution.py:155
  52.0 1.9 %collective-permute-start.7 = (f32[16,5,8,256]{3,2,1,0:T(8,128)}, f32[16,5,8,256]{3,2,1,0:T(8,128)S(1)}, u32[]{:S(2)}, u32[]{:S(2)}) collective-permute-start(f32[16,5,8,256]{3,2,1,0:T(8,128)} %get-tuple-element.31), channel_id=1, source_target_pairs={{0,16},{16,0},{1,17},{17,1},{2,18},{18,2},{3,19},{19,3},{4,20},{20... | collective-permute-start | bytes 1966088 | tf_op jit(solution)/shard_map/ppermute | solution.py:226
  53.9 12.8 %collective-permute-start.8 = (f32[2,2,256,256]{3,2,1,0:T(8,128)}, f32[2,2,256,256]{3,2,1,0:T(8,128)S(1)}, u32[]{:S(2)}, u32[]{:S(2)}) collective-permute-start(f32[2,2,256,256]{3,2,1,0:T(8,128)} %get-tuple-element.32), channel_id=1, source_target_pairs={{0,16},{4,20},{8,24},{12,28},{16,32},{20,36},{24,40},{28,44},{32,4... | collective-permute-start | bytes 3145736 | tf_op jit(solution)/shard_map/ppermute | solution.py:222
  66.8 1.2 add.66
  68.0 15.4 %all_to_all.26 = f32[16,5,8,256]{3,2,1,0:T(8,128)S(1)} all-to-all(f32[16,5,8,256]{3,2,1,0:T(8,128)S(1)} %add.66), channel_id=1, replica_groups=mesh['z_high'=4,'z_low'=4,'core'=2,'band'=4,'pos'=4] {'band','pos'}, dimensions={0} | all-to-all | bytes 1310720 | tf_op jit(solution)/shard_map/all_to_all | solution.py:236
  83.4 1.0 copy-done.2
  84.4 0.1 bitcast_add_fusion
  84.4 2.2 %collective-permute-start.9 = (f32[2,256,256]{2,1,0:T(8,128)S(1)}, f32[2,256,256]{2,1,0:T(8,128)S(1)}, u32[]{:S(2)}, u32[]{:S(2)}) collective-permute-start(f32[2,256,256]{2,1,0:T(8,128)S(1)} %bitcast_add_fusion), channel_id=1, source_target_pairs={{0,4},{4,8},{8,12},{16,20},{20,24},{24,28},{32,36},{36,40},{40,44}... | collective-permute-start | bytes 1572872 | tf_op jit(solution)/shard_map/ppermute | solution.py:222
  86.7 27.6 %all_to_all.27 = f32[4,5,8,256]{3,2,1,0:T(8,128)S(1)} all-to-all(f32[4,5,8,256]{3,2,1,0:T(8,128)S(1)} %broadcast_in_dim.22), channel_id=1, replica_groups=mesh['z_high'=4,'z_low'=4,'core'=2,'band'=4,'pos'=4] {'z_high'}, dimensions={0} | all-to-all | bytes 327680 | tf_op jit(solution)/shard_map/all_to_all | solution.py:236
  114.3 0.7 broadcast_in_dim.24
  115.0 5.3 %all-to-all-start.3 = ((f32[4,5,8,256]{3,2,1,0:T(8,128)}), f32[4,5,8,256]{3,2,1,0:T(8,128)S(1)}, u32[]{:S(2)}, u32[]{:S(2)}) async-start(f32[4,5,8,256]{3,2,1,0:T(8,128)} %broadcast_in_dim.24), calls=%async_computation.3 | async-start | bytes 327680 | tf_op jit(solution)/shard_map/all_to_all | solution.py:236
  120.3 0.1 fusion
  120.4 1.9 %collective-permute-start.10 = (f32[2,256,256]{2,1,0:T(8,128)S(1)}, f32[2,256,256]{2,1,0:T(8,128)S(1)}, u32[]{:S(2)}, u32[]{:S(2)}) collective-permute-start(f32[2,256,256]{2,1,0:T(8,128)S(1)} %fusion), channel_id=1, source_target_pairs={{0,1},{1,0},{2,3},{3,2},{4,5},{5,4},{6,7},{7,6},{8,9},{9,8},{10,11... | collective-permute-start | bytes 1572872 | tf_op jit(solution)/shard_map/ppermute | solution.py:231
  122.4 2.8 %all-to-all-done.3 = f32[4,5,8,256]{3,2,1,0:T(8,128)S(1)} async-done(((f32[4,5,8,256]{3,2,1,0:T(8,128)}), f32[4,5,8,256]{3,2,1,0:T(8,128)S(1)}, u32[]{:S(2)}, u32[]{:S(2)}) %all-to-all-start.3) | async-done | bytes 163872 | tf_op jit(solution)/shard_map/all_to_all | solution.py:236
  125.2 0.8 fusion.1
  126.0 0.8 broadcast_in_dim.25
  126.8 5.7 %all-to-all-start.4 = ((f32[16,4,8,256]{3,2,1,0:T(8,128)}), f32[16,4,8,256]{3,2,1,0:T(8,128)S(1)}, u32[]{:S(2)}, u32[]{:S(2)}) async-start(f32[16,4,8,256]{3,2,1,0:T(8,128)} %broadcast_in_dim.25), calls=%async_computation.4 | async-start | bytes 1048576 | tf_op jit(solution)/shard_map/all_to_all | solution.py:236
  132.5 0.3 collective-permute-done.10
  132.8 0.1 add.70
  132.9 4.6 %collective-permute-start.11 = (f32[2,256,256]{2,1,0:T(8,128)S(1)}, f32[2,256,256]{2,1,0:T(8,128)S(1)}, u32[]{:S(2)}, u32[]{:S(2)}) collective-permute-start(f32[2,256,256]{2,1,0:T(8,128)S(1)} %add.70), channel_id=1, source_target_pairs={{0,3},{1,2},{2,1},{3,0},{4,7},{5,6},{6,5},{7,4},{8,11},{9,10},{10,... | collective-permute-start | bytes 1572872 | tf_op jit(solution)/shard_map/ppermute | solution.py:231
  137.5 3.9 %all-to-all-done.4 = f32[16,4,8,256]{3,2,1,0:T(8,128)S(1)} async-done(((f32[16,4,8,256]{3,2,1,0:T(8,128)}), f32[16,4,8,256]{3,2,1,0:T(8,128)S(1)}, u32[]{:S(2)}, u32[]{:S(2)}) %all-to-all-start.4) | async-done | bytes 524320 | tf_op jit(solution)/shard_map/all_to_all | solution.py:236
  141.5 6.2 %collective-permute-start.12 = (f32[4,128,256]{2,1,0:T(8,128)S(1)}, f32[4,128,256]{2,1,0:T(8,128)S(1)}, u32[]{:S(2)}, u32[]{:S(2)}) collective-permute-start(f32[4,128,256]{2,1,0:T(8,128)S(1)} %bitcast.27), channel_id=1, source_target_pairs={{0,16},{16,0},{1,17},{17,1},{2,18},{18,2},{3,19},{19,3},{4,20},{20... | collective-permute-start | bytes 1572872 | tf_op jit(solution)/shard_map/ppermute | solution.py:226
  147.7 0.1 broadcast_in_dim.23
  147.8 0.0 copy-start
  147.9 5.5 %collective-permute-done.11 = f32[2,256,256]{2,1,0:T(8,128)S(1)} collective-permute-done((f32[2,256,256]{2,1,0:T(8,128)S(1)}, f32[2,256,256]{2,1,0:T(8,128)S(1)}, u32[]{:S(2)}, u32[]{:S(2)}) %collective-permute-start.11) | collective-permute-done | bytes 524320 | tf_op jit(solution)/shard_map/ppermute | solution.py:231
  153.3 0.9 divide_add_fusion
  154.3 0.0 copy-start.1
  154.3 1.0 copy-done.1
  (26 shorter events, 0.2 us)
Async XLA Ops:
  0.6 22.8 %collective-permute-start = (f32[2,256,256]{2,1,0:T(8,128)}, f32[2,256,256]{2,1,0:T(8,128)S(1)}, u32[]{:S(2)}, u32[]{:S(2)}) collective-permute-start(f32[2,256,256]{2,1,0:T(8,128)} %own.1), channel_id=1, source_target_pairs={{4,0},{8,4},{12,8},{20,16},{24,20},{28,24},{36,32},{40,36},{44,40}... | collective-permute-start | bytes 1572872 | tf_op jit(solution)/shard_map/ppermute | solution.py:222
  1.9 21.5 %collective-permute-start.1 = (f32[2,256,256]{2,1,0:T(8,128)}, f32[2,256,256]{2,1,0:T(8,128)S(1)}, u32[]{:S(2)}, u32[]{:S(2)}) collective-permute-start(f32[2,256,256]{2,1,0:T(8,128)} %own.1), channel_id=1, source_target_pairs={{16,0},{20,4},{24,8},{28,12},{32,16},{36,20},{40,24},{44,28},{48,3... | collective-permute-start | bytes 1572872 | tf_op jit(solution)/shard_map/ppermute | solution.py:222
  23.4 14.4 %copy-start.4 = (f32[2,256,256]{2,1,0:T(8,128)}, f32[2,256,256]{2,1,0:T(8,128)S(1)}, u32[]{:S(2)}) copy-start(f32[2,256,256]{2,1,0:T(8,128)S(1)} %collective-permute-done.right) | copy-start | bytes 1572868
  23.4 14.4 %copy-start.5 = (f32[2,256,256]{2,1,0:T(8,128)}, f32[2,256,256]{2,1,0:T(8,128)S(1)}, u32[]{:S(2)}) copy-start(f32[2,256,256]{2,1,0:T(8,128)S(1)} %collective-permute-done.1.below) | copy-start | bytes 1572868
  23.4 11.5 %collective-permute-start.4 = (f32[256,256]{1,0:T(8,128)}, f32[256,256]{1,0:T(8,128)S(1)}, u32[]{:S(2)}, u32[]{:S(2)}) collective-permute-start(f32[256,256]{1,0:T(8,128)} %get-tuple-element.26), channel_id=1, source_target_pairs={{0,4},{4,8},{8,12},{16,20},{20,24},{24,28},{32,36},{36,40},{40,44}... | collective-permute-start | bytes 786440 | tf_op jit(solution)/shard_map/ppermute | solution.py:222
  27.7 7.2 %collective-permute-start.5 = (f32[256,256]{1,0:T(8,128)}, f32[256,256]{1,0:T(8,128)S(1)}, u32[]{:S(2)}, u32[]{:S(2)}) collective-permute-start(f32[256,256]{1,0:T(8,128)} %get-tuple-element.27), channel_id=1, source_target_pairs={{0,16},{4,20},{8,24},{12,28},{16,32},{20,36},{24,40},{28,44},{32,4... | collective-permute-start | bytes 786440 | tf_op jit(solution)/shard_map/ppermute | solution.py:222
  29.6 6.5 %collective-permute-start.6 = (f32[256,256]{1,0:T(8,128)}, f32[256,256]{1,0:T(8,128)S(1)}, u32[]{:S(2)}, u32[]{:S(2)}) collective-permute-start(f32[256,256]{1,0:T(8,128)} %get-tuple-element.28), channel_id=1, source_target_pairs={{0,20},{4,24},{8,28},{16,36},{20,40},{24,44},{32,52},{36,56},{40,6... | collective-permute-start | bytes 786440 | tf_op jit(solution)/shard_map/ppermute | solution.py:222
  31.6 9.9 %collective-permute-start.2 = (f32[2,256,256]{2,1,0:T(8,128)S(1)}, f32[2,256,256]{2,1,0:T(8,128)S(1)}, u32[]{:S(2)}, u32[]{:S(2)}) collective-permute-start(f32[2,256,256]{2,1,0:T(8,128)S(1)} %collective-permute-done.1.below), channel_id=1, source_target_pairs={{20,16},{24,20},{28,24},{52,48},{56,52},{60,56},{84,80},{88,84},{9... | collective-permute-start | bytes 1572872 | tf_op jit(solution)/shard_map/ppermute | solution.py:246
  32.9 8.6 %collective-permute-start.3 = (f32[2,256,256]{2,1,0:T(8,128)S(1)}, f32[2,256,256]{2,1,0:T(8,128)S(1)}, u32[]{:S(2)}, u32[]{:S(2)}) collective-permute-start(f32[2,256,256]{2,1,0:T(8,128)S(1)} %collective-permute-done.right), channel_id=1, source_target_pairs={{16,0},{17,1},{18,2},{19,3},{20,4},{21,5},{22,6},{23,7},{24,8},{25... | collective-permute-start | bytes 1572872 | tf_op jit(solution)/shard_map/ppermute | solution.py:246
  41.5 0.8 copy-start.6
  41.5 1.0 copy-start.7
  52.0 14.8 %collective-permute-start.7 = (f32[16,5,8,256]{3,2,1,0:T(8,128)}, f32[16,5,8,256]{3,2,1,0:T(8,128)S(1)}, u32[]{:S(2)}, u32[]{:S(2)}) collective-permute-start(f32[16,5,8,256]{3,2,1,0:T(8,128)} %get-tuple-element.31), channel_id=1, source_target_pairs={{0,16},{16,0},{1,17},{17,1},{2,18},{18,2},{3,19},{19,3},{4,20},{20... | collective-permute-start | bytes 1966088 | tf_op jit(solution)/shard_map/ppermute | solution.py:226
  53.9 29.4 %collective-permute-start.8 = (f32[2,2,256,256]{3,2,1,0:T(8,128)}, f32[2,2,256,256]{3,2,1,0:T(8,128)S(1)}, u32[]{:S(2)}, u32[]{:S(2)}) collective-permute-start(f32[2,2,256,256]{3,2,1,0:T(8,128)} %get-tuple-element.32), channel_id=1, source_target_pairs={{0,16},{4,20},{8,24},{12,28},{16,32},{20,36},{24,40},{28,44},{32,4... | collective-permute-start | bytes 3145736 | tf_op jit(solution)/shard_map/ppermute | solution.py:222
  83.3 1.0 copy-start.2
  84.4 29.9 %collective-permute-start.9 = (f32[2,256,256]{2,1,0:T(8,128)S(1)}, f32[2,256,256]{2,1,0:T(8,128)S(1)}, u32[]{:S(2)}, u32[]{:S(2)}) collective-permute-start(f32[2,256,256]{2,1,0:T(8,128)S(1)} %bitcast_add_fusion), channel_id=1, source_target_pairs={{0,4},{4,8},{8,12},{16,20},{20,24},{24,28},{32,36},{36,40},{40,44}... | collective-permute-start | bytes 1572872 | tf_op jit(solution)/shard_map/ppermute | solution.py:222
  86.6 33.7 %copy-start.3 = (f32[2,256,256]{2,1,0:T(8,128)S(1)}, f32[2,256,256]{2,1,0:T(8,128)}, u32[]{:S(2)}) copy-start(f32[2,256,256]{2,1,0:T(8,128)} %get-tuple-element.29) | copy-start | bytes 1572868
  115.0 10.2 %all-to-all-start.3 = ((f32[4,5,8,256]{3,2,1,0:T(8,128)}), f32[4,5,8,256]{3,2,1,0:T(8,128)S(1)}, u32[]{:S(2)}, u32[]{:S(2)}) async-start(f32[4,5,8,256]{3,2,1,0:T(8,128)} %broadcast_in_dim.24), calls=%async_computation.3 | async-start | bytes 327680 | tf_op jit(solution)/shard_map/all_to_all | solution.py:236
  120.4 12.4 %collective-permute-start.10 = (f32[2,256,256]{2,1,0:T(8,128)S(1)}, f32[2,256,256]{2,1,0:T(8,128)S(1)}, u32[]{:S(2)}, u32[]{:S(2)}) collective-permute-start(f32[2,256,256]{2,1,0:T(8,128)S(1)} %fusion), channel_id=1, source_target_pairs={{0,1},{1,0},{2,3},{3,2},{4,5},{5,4},{6,7},{7,6},{8,9},{9,8},{10,11... | collective-permute-start | bytes 1572872 | tf_op jit(solution)/shard_map/ppermute | solution.py:231
  126.8 14.7 %all-to-all-start.4 = ((f32[16,4,8,256]{3,2,1,0:T(8,128)}), f32[16,4,8,256]{3,2,1,0:T(8,128)S(1)}, u32[]{:S(2)}, u32[]{:S(2)}) async-start(f32[16,4,8,256]{3,2,1,0:T(8,128)} %broadcast_in_dim.25), calls=%async_computation.4 | async-start | bytes 1048576 | tf_op jit(solution)/shard_map/all_to_all | solution.py:236
  132.9 20.4 %collective-permute-start.11 = (f32[2,256,256]{2,1,0:T(8,128)S(1)}, f32[2,256,256]{2,1,0:T(8,128)S(1)}, u32[]{:S(2)}, u32[]{:S(2)}) collective-permute-start(f32[2,256,256]{2,1,0:T(8,128)S(1)} %add.70), channel_id=1, source_target_pairs={{0,3},{1,2},{2,1},{3,0},{4,7},{5,6},{6,5},{7,4},{8,11},{9,10},{10,... | collective-permute-start | bytes 1572872 | tf_op jit(solution)/shard_map/ppermute | solution.py:231
  141.5 12.7 %collective-permute-start.12 = (f32[4,128,256]{2,1,0:T(8,128)S(1)}, f32[4,128,256]{2,1,0:T(8,128)S(1)}, u32[]{:S(2)}, u32[]{:S(2)}) collective-permute-start(f32[4,128,256]{2,1,0:T(8,128)S(1)} %bitcast.27), channel_id=1, source_target_pairs={{0,16},{16,0},{1,17},{17,1},{2,18},{18,2},{3,19},{19,3},{4,20},{20... | collective-permute-start | bytes 1572872 | tf_op jit(solution)/shard_map/ppermute | solution.py:226
  147.8 5.5 %copy-start = (f32[2,256,256]{2,1,0:T(8,128)S(1)}, f32[2,256,256]{2,1,0:T(8,128)}, u32[]{:S(2)}) copy-start(f32[2,256,256]{2,1,0:T(8,128)} %own.1) | copy-start | bytes 1572868
  154.3 1.0 copy-start.1

commit v7 on v4

--- a/solution.py
+++ b/solution.py
@@ -78,7 +78,7 @@
 
 
 def slots_kernel(
-    card, own, right, below, corner_a, corner_b, probe, frames, lh, lr, rh, rr, after,
+    card, own, right, below, corner_a, corner_b, probe, frames, lh, lr, rh, rr,
     top_left, top_right, bottom, keep, send, extended, total, terms,
 ):
     extended[:, :S, :S] = own[...]
@@ -129,7 +129,10 @@
             terms[m] += patch_real * chi_real + patch_imag * chi_imag
             terms[2 + m] += patch_real * chi_imag - patch_imag * chi_real
         terms[4] += patch_real * patch_real + patch_imag * patch_imag
-        for plane, value in enumerate((object_real, object_imag)):
+        light = blank
+        for m in range(2):
+            light += probe[0, m] * probe[0, m] + probe[1, m] * probe[1, m]
+        for plane, value in enumerate((object_real, object_imag, light)):
             total[plane, band_rows, band_columns] += placed(value, inside, fine)
         return carry
 
@@ -151,10 +154,10 @@
             send[chunk, plane] = terms[plane, pl.ds(other, height), :]
 
 
-def run_slots(card, blocks, probe, frames, chunks, after):
+def run_slots(card, blocks, probe, frames, chunks):
     height = S // 2 // chunks
     f32 = jnp.float32
-    quarter = (QUARTERS, 2, S // QUARTERS, S)
+    quarter = (QUARTERS, 3, S // QUARTERS, S)
     vmem = pl.BlockSpec(memory_space=pltpu.VMEM)
     return pl.pallas_call(
         slots_kernel,
@@ -165,53 +168,16 @@
             jax.ShapeDtypeStruct((chunks, 5, height, S), f32),
             jax.ShapeDtypeStruct((chunks, 5, height, S), f32),
         ),
-        in_specs=[
-            pl.BlockSpec(memory_space=pltpu.SMEM), *[vmem] * 11, pl.BlockSpec(memory_space=pl.ANY)
-        ],
+        in_specs=[pl.BlockSpec(memory_space=pltpu.SMEM), *[vmem] * 11],
         out_specs=[vmem] * 5,
         scratch_shapes=[
             pltpu.VMEM((2, 2 * S, 2 * S), f32),
-            pltpu.VMEM((2, 2 * S, 2 * S), f32),
+            pltpu.VMEM((3, 2 * S, 2 * S), f32),
             pltpu.VMEM((5, S, S), f32),
         ],
         compiler_params=pltpu.CompilerParams(vmem_limit_bytes=54 * 1024 * 1024),
         name="slots",
-    )(card, *blocks, probe, frames, *(jnp.asarray(t) for t in tables()), after)
-
-
-def light_kernel(card, probe, top_left, top_right, bottom, total):
-    power = jnp.zeros((S, S), jnp.float32)
-    for m in range(2):
-        power += probe[0, m] * probe[0, m] + probe[1, m] * probe[1, m]
-    total[...] = jnp.zeros_like(total)
-
-    def one_slot(slot, carry):
-        row, column = card[0, 2 * slot], card[0, 2 * slot + 1]
-        inside, fine = lax.rem(row, 8), lax.rem(column, 128)
-        band_rows = pl.ds(pl.multiple_of(row - inside, 8), S + 8)
-        band_columns = pl.ds(pl.multiple_of(column - fine, 128), 384)
-        total[band_rows, band_columns] += placed(power, inside, fine)
-        return carry
-
-    lax.fori_loop(0, card[0, COUNT], one_slot, 0)
-    top_left[...] = total[:S, :S]
-    top_right[...] = total[:S, S:]
-    bottom[0] = total[S:, :S]
-    bottom[1] = total[S:, S:]
-
-
-def run_light(card, probe):
-    vmem = pl.BlockSpec(memory_space=pltpu.VMEM)
-    tile = jax.ShapeDtypeStruct((S, S), jnp.float32)
-    return pl.pallas_call(
-        light_kernel,
-        out_shape=(tile, tile, jax.ShapeDtypeStruct((2, S, S), jnp.float32)),
-        in_specs=[pl.BlockSpec(memory_space=pltpu.SMEM), vmem],
-        out_specs=[vmem] * 3,
-        scratch_shapes=[pltpu.VMEM((2 * S, 2 * S), jnp.float32)],
-        compiler_params=pltpu.CompilerParams(vmem_limit_bytes=54 * 1024 * 1024),
-        name="light",
-    )(card, probe)
+    )(card, *blocks, probe, frames, *(jnp.asarray(t) for t in tables()))
 
 
 def moved(block, tiles_by, bands_by):
@@ -255,18 +221,12 @@
     right = moved(object_planes, 0, -1)
     below = moved(object_planes, -1, 0)
     card = jnp.pad(jnp.concatenate([offsets.reshape(6), counts.reshape(1)])[None], ((0, 0), (0, 121)))
-    light, light_right, light_bottom = run_light(card, probe_planes)
-    right, below, light_bottom = lax.optimization_barrier((right, below, light_bottom))
-    light_above = moved(light_bottom, 1, 0)
     corner_a, corner_b = corners(right, below)
-    light_left = moved(light_right + light_above[1], 0, 1)
-    light = light + light_above[0]
     top_left, top_right, bottom, keep, send = run_slots(
         card, (object_planes, right, below, corner_a, corner_b),
-        probe_planes, patterns[0, 0, 0], chunks, light_above,
-    )
-
-    light = lax.psum_scatter(light + light_left, "pos", scatter_dimension=0, tiled=True)
+        probe_planes, patterns[0, 0, 0], chunks,
+    )
+
     from_above = moved(bottom, 1, 0)
     terms = keep + across_cores(send)
     terms = jnp.sum(exchanged(terms, plane), axis=0)
@@ -274,12 +234,14 @@
     from_left = moved(top_right + from_above[1], 0, 1)
     terms = jnp.sum(shared(terms, "z_low"), axis=0)
     tile_sum = top_left + from_above[0] + from_left
-    tile_sum = lax.psum_scatter(tile_sum, "pos", scatter_dimension=0, tiled=True)[0]
+    pieces = [lax.dynamic_index_in_dim(tile_sum, post ^ k, 0, keepdims=False) for k in range(QUARTERS)]
+    pieces = [pieces[0], *(across_posts(pieces[k], k) for k in range(1, QUARTERS))]
     terms = jnp.sum(shared(terms, "z_high"), axis=0)
 
     rows = S // QUARTERS
     own_rows = lax.dynamic_slice_in_dim(object_planes, post * rows, rows, 1)
-    own_rows = own_rows + tile_sum / (light + 1.0)
+    pieces = sum(pieces[1:], pieces[0])
+    own_rows = own_rows + pieces[:2] / (pieces[2] + 1.0)
     object_new = jnp.zeros_like(object_planes)
     for k in range(QUARTERS):
         piece = across_posts(own_rows, k) if k else own_rows

time: 181 us -> 142 us (0.78)
  waiting for transfers between devices: 55.5 us -> 18.8 us
  blocking collectives: 0 us -> 32.6 us
  between operations: 15 us -> 1.65 us
  starting transfers between devices: 71.9 us -> 61.9 us
  Pallas kernels: 21.3 us -> 14.6 us
  other arithmetic: 8.47 us -> 5.47 us
    all_to_all x0 -> x2, blocking collectives: none -> 32.6 us  [exchanged(): return lax.all_to_all(block, axes, 0, 0)]
    all_to_all x4 -> x2, waiting for transfers between devices: 30.2 us -> 1.21 us  [exchanged(): return lax.all_to_all(block, axes, 0, 0)]
    all_to_all x4 -> x2, starting transfers between devices: 36.2 us -> 17.8 us  [exchanged(): return lax.all_to_all(block, axes, 0, 0)]
    reduce_scatter x2 -> x0, waiting for transfers between devices: 14.7 us -> none  [the longest x1 14.7 us: on_device(): lax.psum_scatter(tile_sum, 'pos', scatter_dimension=0, tiled=True)[0]]
    ppermute x3 -> x6, starting transfers between devices: 10.4 us -> 20.8 us  [across_posts(): return lax.ppermute(block, 'pos', [(p, p ^ bits) for p in range(QUARTERS)])]
    ppermute x6 -> x4, waiting for transfers between devices: 1.72 us -> 11.7 us  [moved(): return lax.ppermute(block, (*TILE, 'band'), route)]
    ppermute x1, waiting for transfers between devices: 5.42 us -> 0.34 us  [corners(): lax.ppermute(right, 'core', [(1, 0)])]
    pallas_call x1, Pallas kernels: 18.5 us -> 14.6 us  [run_slots(): pl.pallas_call(slots_kernel, out_shape=(jax.ShapeDtypeStruct(quarter, f32...]
  transfers between devices with their start and end apart: 19 -> 16, of which waited for: 8 -> 5; matrix products, arithmetic and copies ran while one was open for 7% -> 5% of each run, Pallas kernels for 2% -> 0%
where the time goes in v7:
time: 142 us; the launch traced here: 141 us
  starting transfers between devices  61.9 us (44%)
  blocking collectives  32.6 us (23%)
  waiting for transfers between devices  18.8 us (13%)
  Pallas kernels  14.6 us (10%)
  local copies, waits for them, and re-layouts  6.53 us (5%)
  other arithmetic  5.47 us (4%)
  between operations  1.65 us (1%)
    all_to_all x2, blocking collectives, exchanged(): return lax.all_to_all(block, axes, 0, 0)  32.6 us
    ppermute x6, starting transfers between devices, across_posts(): return lax.ppermute(block, 'pos', [(p, p ^ bits) for p in range(QUARTERS)])  20.8 us
    all_to_all x2, starting transfers between devices, exchanged(): return lax.all_to_all(block, axes, 0, 0)  17.8 us
    ppermute x4, starting transfers between devices, moved(): return lax.ppermute(block, (*TILE, 'band'), route)  16 us
    pallas_call x1, Pallas kernels, run_slots(): pl.pallas_call(slots_kernel, out_shape=(jax.ShapeDtypeStruct(quarter, f32...  14.6 us
    ppermute x4, waiting for transfers between devices, moved(): return lax.ppermute(block, (*TILE, 'band'), route)  11.7 us
    ppermute x2, starting transfers between devices, across_cores(): return lax.ppermute(block, 'core', [(0, 1), (1, 0)])  5.28 us
    unnamed x19, local copies, waits for them, and re-layouts  4 us
  transfers between devices with their start and end apart: 16, of which 5 were waited for; matrix products, arithmetic and copies ran while one was open for 5% of the time, Pallas kernels for 0%

profile of v7, /device:TPU:2, one launch (start us, length us, event | category | flops | bytes accessed | tf_op | source)
XLA Modules:
  0.0 141.5 jit_solution(4273824659511660392)
XLA Ops:
  0.6 1.3 collective-permute-start.1
  1.9 7.8 %collective-permute-start = (f32[2,256,256]{2,1,0:T(8,128)}, f32[2,256,256]{2,1,0:T(8,128)S(1)}, u32[]{:S(2)}, u32[]{:S(2)}) collective-permute-start(f32[2,256,256]{2,1,0:T(8,128)} %own.1), channel_id=1, source_target_pairs={{4,0},{8,4},{12,8},{20,16},{24,20},{28,24},{36,32},{40,36},{44,40}... | collective-permute-start | bytes 1572872 | tf_op jit(solution)/shard_map/ppermute | solution.py:191
  9.8 0.7 collective-permute-start.2
  10.5 11.7 %collective-permute-done.right = f32[2,256,256]{2,1,0:T(8,128)S(1)} collective-permute-done((f32[2,256,256]{2,1,0:T(8,128)}, f32[2,256,256]{2,1,0:T(8,128)S(1)}, u32[]{:S(2)}, u32[]{:S(2)}) %collective-permute-start) | collective-permute-done | bytes 524320 | tf_op jit(solution)/shard_map/ppermute | solution.py:191
  22.2 1.3 collective-permute-start.3
  23.5 0.8 copy.16
  24.3 0.1 reshape.19
  25.0 0.1 add_bitcast_fusion
  25.1 0.6 pad.4.card
  25.7 0.3 collective-permute-done.3.corner_b
  26.0 0.4 copy-done.7
  26.5 0.3 copy-done.8
  26.8 14.6 %slots.1 = (f32[4,3,64,256]{3,2,1,0:T(8,128)}, f32[4,3,64,256]{3,2,1,0:T(8,128)}, f32[2,4,3,64,256]{4,3,2,1,0:T(8,128)}, f32[16,5,8,256]{3,2,1,0:T(8,128)}, f32[16,5,8,256]{3,2,1,0:T(8,128)}) custom-call(s32[1,128]{1,0:T(1,128)} %pad.4.card, f32[2,256,256]{2,1,0:T(8,128)} %own.1, f32[2,256,256]{2,1,0:T(8,128)} %copy-done.6, f32[2,256,256]{2,1,0:T(8,128)} %copy-done.5, ...), custom_call_target="tpu_custom_call" | custom-call | tf_op jit(solution)/shard_map/slots/pallas_call | solution.py:162
  41.4 4.1 %collective-permute-start.5 = (f32[2,4,3,64,256]{4,3,2,1,0:T(8,128)}, f32[2,4,3,64,256]{4,3,2,1,0:T(8,128)S(1)}, u32[]{:S(2)}, u32[]{:S(2)}) collective-permute-start(f32[2,4,3,64,256]{4,3,2,1,0:T(8,128)} %get-tuple-element.12), channel_id=1, source_target_pairs={{0,16},{4,20},{8,24},{12,28},{16,32},{20,36},{24,40},{28,44},{32,4... | collective-permute-start | bytes 4718600 | tf_op jit(solution)/shard_map/ppermute | solution.py:191
  45.5 3.4 %collective-permute-start.4 = (f32[16,5,8,256]{3,2,1,0:T(8,128)}, f32[16,5,8,256]{3,2,1,0:T(8,128)S(1)}, u32[]{:S(2)}, u32[]{:S(2)}) collective-permute-start(f32[16,5,8,256]{3,2,1,0:T(8,128)} %get-tuple-element.11), channel_id=1, source_target_pairs={{0,16},{16,0},{1,17},{17,1},{2,18},{18,2},{3,19},{19,3},{4,20},{20... | collective-permute-start | bytes 1966088 | tf_op jit(solution)/shard_map/ppermute | solution.py:195
  48.9 1.9 %collective-permute-done.4 = f32[16,5,8,256]{3,2,1,0:T(8,128)S(1)} collective-permute-done((f32[16,5,8,256]{3,2,1,0:T(8,128)}, f32[16,5,8,256]{3,2,1,0:T(8,128)S(1)}, u32[]{:S(2)}, u32[]{:S(2)}) %collective-permute-start.4) | collective-permute-done | bytes 655392 | tf_op jit(solution)/shard_map/ppermute | solution.py:195
  50.8 1.2 add.85
  52.0 19.0 %all_to_all.20 = f32[16,5,8,256]{3,2,1,0:T(8,128)S(1)} all-to-all(f32[16,5,8,256]{3,2,1,0:T(8,128)S(1)} %add.85), channel_id=1, replica_groups=mesh['z_high'=4,'z_low'=4,'core'=2,'band'=4,'pos'=4] {'band','pos'}, dimensions={0} | all-to-all | bytes 1310720 | tf_op jit(solution)/shard_map/all_to_all | solution.py:203
  71.1 0.0 copy-start.1
  71.1 1.0 bitcast_add_fusion
  72.1 2.7 %collective-permute-start.6 = (f32[4,3,64,256]{3,2,1,0:T(8,128)}, f32[4,3,64,256]{3,2,1,0:T(8,128)S(1)}, u32[]{:S(2)}, u32[]{:S(2)}) collective-permute-start(f32[4,3,64,256]{3,2,1,0:T(8,128)} %bitcast_add_fusion), channel_id=1, source_target_pairs={{0,4},{4,8},{8,12},{16,20},{20,24},{24,28},{32,36},{36,40},{40,44}... | collective-permute-start | bytes 2359304 | tf_op jit(solution)/shard_map/ppermute | solution.py:191
  74.8 13.6 %all_to_all.21 = f32[4,5,8,256]{3,2,1,0:T(8,128)S(1)} all-to-all(f32[4,5,8,256]{3,2,1,0:T(8,128)S(1)} %broadcast_in_dim.23), channel_id=1, replica_groups=mesh['z_high'=4,'z_low'=4,'core'=2,'band'=4,'pos'=4] {'z_low'}, dimensions={0} | all-to-all | bytes 327680 | tf_op jit(solution)/shard_map/all_to_all | solution.py:203
  88.5 0.7 broadcast_in_dim.24
  89.1 12.3 %all-to-all-start.2 = ((f32[4,5,8,256]{3,2,1,0:T(8,128)}), f32[4,5,8,256]{3,2,1,0:T(8,128)S(1)}, u32[]{:S(2)}, u32[]{:S(2)}) async-start(f32[4,5,8,256]{3,2,1,0:T(8,128)} %broadcast_in_dim.24), calls=%async_computation.2 | async-start | bytes 327680 | tf_op jit(solution)/shard_map/all_to_all | solution.py:203
  101.4 0.9 copy-done.2
  102.3 1.3 fusion
  103.7 2.4 %collective-permute-start.7 = (f32[3,64,256]{2,1,0:T(8,128)S(1)}, f32[3,64,256]{2,1,0:T(8,128)S(1)}, u32[]{:S(2)}, u32[]{:S(2)}) collective-permute-start(f32[3,64,256]{2,1,0:T(8,128)S(1)} %get-tuple-element.18), channel_id=1, source_target_pairs={{0,1},{1,0},{2,3},{3,2},{4,5},{5,4},{6,7},{7,6},{8,9},{9,8},{10,11... | collective-permute-start | bytes 589832 | tf_op jit(solution)/shard_map/ppermute | solution.py:199
  106.0 4.0 %collective-permute-start.8 = (f32[3,64,256]{2,1,0:T(8,128)S(1)}, f32[3,64,256]{2,1,0:T(8,128)S(1)}, u32[]{:S(2)}, u32[]{:S(2)}) collective-permute-start(f32[3,64,256]{2,1,0:T(8,128)S(1)} %get-tuple-element.20), channel_id=1, source_target_pairs={{0,2},{1,3},{2,0},{3,1},{4,6},{5,7},{6,4},{7,5},{8,10},{9,11},{10,... | collective-permute-start | bytes 589832 | tf_op jit(solution)/shard_map/ppermute | solution.py:199
  110.0 4.1 %collective-permute-start.9 = (f32[3,64,256]{2,1,0:T(8,128)S(1)}, f32[3,64,256]{2,1,0:T(8,128)S(1)}, u32[]{:S(2)}, u32[]{:S(2)}) collective-permute-start(f32[3,64,256]{2,1,0:T(8,128)S(1)} %get-tuple-element.19), channel_id=1, source_target_pairs={{0,3},{1,2},{2,1},{3,0},{4,7},{5,6},{6,5},{7,4},{8,11},{9,10},{10,... | collective-permute-start | bytes 589832 | tf_op jit(solution)/shard_map/ppermute | solution.py:199
  114.1 1.2 all-to-all-done.2
  115.3 0.8 fusion.5
  116.1 0.8 broadcast_in_dim.25
  117.0 5.6 %all-to-all-start.3 = ((f32[16,4,8,256]{3,2,1,0:T(8,128)}), f32[16,4,8,256]{3,2,1,0:T(8,128)S(1)}, u32[]{:S(2)}, u32[]{:S(2)}) async-start(f32[16,4,8,256]{3,2,1,0:T(8,128)} %broadcast_in_dim.25), calls=%async_computation.3 | async-start | bytes 1048576 | tf_op jit(solution)/shard_map/all_to_all | solution.py:203
  122.5 0.0 collective-permute-done.7
  122.5 0.0 collective-permute-done.9
  122.5 0.1 fusion.2
  122.7 0.9 constant_dynamic-update-slice_fusion.5
  123.6 3.4 %collective-permute-start.10 = (f32[2,64,256]{2,1,0:T(8,128)S(1)}, f32[2,64,256]{2,1,0:T(8,128)S(1)}, u32[]{:S(2)}, u32[]{:S(2)}) collective-permute-start(f32[2,64,256]{2,1,0:T(8,128)S(1)} %get-tuple-element.17), channel_id=1, source_target_pairs={{0,1},{1,0},{2,3},{3,2},{4,5},{5,4},{6,7},{7,6},{8,9},{9,8},{10,11... | collective-permute-start | bytes 393224 | tf_op jit(solution)/shard_map/ppermute | solution.py:199
  127.0 4.6 %collective-permute-start.11 = (f32[2,64,256]{2,1,0:T(8,128)S(1)}, f32[2,64,256]{2,1,0:T(8,128)S(1)}, u32[]{:S(2)}, u32[]{:S(2)}) collective-permute-start(f32[2,64,256]{2,1,0:T(8,128)S(1)} %get-tuple-element.17), channel_id=1, source_target_pairs={{0,2},{1,3},{2,0},{3,1},{4,6},{5,7},{6,4},{7,5},{8,10},{9,11},{10,... | collective-permute-start | bytes 393224 | tf_op jit(solution)/shard_map/ppermute | solution.py:199
  131.6 2.5 %collective-permute-start.12 = (f32[2,64,256]{2,1,0:T(8,128)S(1)}, f32[2,64,256]{2,1,0:T(8,128)S(1)}, u32[]{:S(2)}, u32[]{:S(2)}) collective-permute-start(f32[2,64,256]{2,1,0:T(8,128)S(1)} %get-tuple-element.17), channel_id=1, source_target_pairs={{0,3},{1,2},{2,1},{3,0},{4,7},{5,6},{6,5},{7,4},{8,11},{9,10},{10,... | collective-permute-start | bytes 393224 | tf_op jit(solution)/shard_map/ppermute | solution.py:199
  134.1 0.0 all-to-all-done.3
  134.1 1.9 %collective-permute-start.13 = (f32[4,128,256]{2,1,0:T(8,128)S(1)}, f32[4,128,256]{2,1,0:T(8,128)S(1)}, u32[]{:S(2)}, u32[]{:S(2)}) collective-permute-start(f32[4,128,256]{2,1,0:T(8,128)S(1)} %bitcast.39), channel_id=1, source_target_pairs={{0,16},{16,0},{1,17},{17,1},{2,18},{18,2},{3,19},{19,3},{4,20},{20... | collective-permute-start | bytes 1572872 | tf_op jit(solution)/shard_map/ppermute | solution.py:195
  136.1 0.0 collective-permute-done.10
  136.1 3.5 %collective-permute-done.12 = f32[2,64,256]{2,1,0:T(8,128)S(1)} collective-permute-done((f32[2,64,256]{2,1,0:T(8,128)S(1)}, f32[2,64,256]{2,1,0:T(8,128)S(1)}, u32[]{:S(2)}, u32[]{:S(2)}) %collective-permute-start.12) | collective-permute-done | bytes 131104 | tf_op jit(solution)/shard_map/ppermute | solution.py:199
  139.7 0.0 copy-start.4
  139.7 0.1 broadcast_in_dim.22
  139.9 0.6 copy-done.4
  140.5 1.0 copy-done
  (32 shorter events, 0.4 us)
Async XLA Ops:
  0.6 9.1 %collective-permute-start.1 = (f32[2,256,256]{2,1,0:T(8,128)}, f32[2,256,256]{2,1,0:T(8,128)S(1)}, u32[]{:S(2)}, u32[]{:S(2)}) collective-permute-start(f32[2,256,256]{2,1,0:T(8,128)} %own.1), channel_id=1, source_target_pairs={{16,0},{20,4},{24,8},{28,12},{32,16},{36,20},{40,24},{44,28},{48,3... | collective-permute-start | bytes 1572872 | tf_op jit(solution)/shard_map/ppermute | solution.py:191
  1.9 20.3 %collective-permute-start = (f32[2,256,256]{2,1,0:T(8,128)}, f32[2,256,256]{2,1,0:T(8,128)S(1)}, u32[]{:S(2)}, u32[]{:S(2)}) collective-permute-start(f32[2,256,256]{2,1,0:T(8,128)} %own.1), channel_id=1, source_target_pairs={{4,0},{8,4},{12,8},{20,16},{24,20},{28,24},{36,32},{40,36},{44,40}... | collective-permute-start | bytes 1572872 | tf_op jit(solution)/shard_map/ppermute | solution.py:191
  9.8 16.2 %copy-start.5 = (f32[2,256,256]{2,1,0:T(8,128)}, f32[2,256,256]{2,1,0:T(8,128)S(1)}, u32[]{:S(2)}) copy-start(f32[2,256,256]{2,1,0:T(8,128)S(1)} %collective-permute-done.1.below) | copy-start | bytes 1572868
  9.8 15.9 %collective-permute-start.2 = (f32[2,256,256]{2,1,0:T(8,128)S(1)}, f32[2,256,256]{2,1,0:T(8,128)S(1)}, u32[]{:S(2)}, u32[]{:S(2)}) collective-permute-start(f32[2,256,256]{2,1,0:T(8,128)S(1)} %collective-permute-done.1.below), channel_id=1, source_target_pairs={{20,16},{24,20},{28,24},{52,48},{56,52},{60,56},{84,80},{88,84},{9... | collective-permute-start | bytes 1572872 | tf_op jit(solution)/shard_map/ppermute | solution.py:213
  22.2 3.8 %copy-start.6 = (f32[2,256,256]{2,1,0:T(8,128)}, f32[2,256,256]{2,1,0:T(8,128)S(1)}, u32[]{:S(2)}) copy-start(f32[2,256,256]{2,1,0:T(8,128)S(1)} %collective-permute-done.right) | copy-start | bytes 1572868
  22.2 3.8 %collective-permute-start.3 = (f32[2,256,256]{2,1,0:T(8,128)S(1)}, f32[2,256,256]{2,1,0:T(8,128)S(1)}, u32[]{:S(2)}, u32[]{:S(2)}) collective-permute-start(f32[2,256,256]{2,1,0:T(8,128)S(1)} %collective-permute-done.right), channel_id=1, source_target_pairs={{16,0},{17,1},{18,2},{19,3},{20,4},{21,5},{22,6},{23,7},{24,8},{25... | collective-permute-start | bytes 1572872 | tf_op jit(solution)/shard_map/ppermute | solution.py:213
  25.7 0.8 copy-start.7
  26.0 0.8 copy-start.8
  41.4 29.7 %collective-permute-start.5 = (f32[2,4,3,64,256]{4,3,2,1,0:T(8,128)}, f32[2,4,3,64,256]{4,3,2,1,0:T(8,128)S(1)}, u32[]{:S(2)}, u32[]{:S(2)}) collective-permute-start(f32[2,4,3,64,256]{4,3,2,1,0:T(8,128)} %get-tuple-element.12), channel_id=1, source_target_pairs={{0,16},{4,20},{8,24},{12,28},{16,32},{20,36},{24,40},{28,44},{32,4... | collective-permute-start | bytes 4718600 | tf_op jit(solution)/shard_map/ppermute | solution.py:191
  45.5 5.3 %collective-permute-start.4 = (f32[16,5,8,256]{3,2,1,0:T(8,128)}, f32[16,5,8,256]{3,2,1,0:T(8,128)S(1)}, u32[]{:S(2)}, u32[]{:S(2)}) collective-permute-start(f32[16,5,8,256]{3,2,1,0:T(8,128)} %get-tuple-element.11), channel_id=1, source_target_pairs={{0,16},{16,0},{1,17},{17,1},{2,18},{18,2},{3,19},{19,3},{4,20},{20... | collective-permute-start | bytes 1966088 | tf_op jit(solution)/shard_map/ppermute | solution.py:195
  50.8 20.3 %copy-start.3 = (f32[4,3,64,256]{3,2,1,0:T(8,128)S(1)}, f32[4,3,64,256]{3,2,1,0:T(8,128)}, u32[]{:S(2)}) copy-start(f32[4,3,64,256]{3,2,1,0:T(8,128)} %get-tuple-element.14) | copy-start | bytes 2359300
  71.1 31.2 %copy-start.1 = (f32[4,3,64,256]{3,2,1,0:T(8,128)S(1)}, f32[4,3,64,256]{3,2,1,0:T(8,128)}, u32[]{:S(2)}) copy-start(f32[4,3,64,256]{3,2,1,0:T(8,128)} %get-tuple-element.9) | copy-start | bytes 2359300
  72.1 29.3 %collective-permute-start.6 = (f32[4,3,64,256]{3,2,1,0:T(8,128)}, f32[4,3,64,256]{3,2,1,0:T(8,128)S(1)}, u32[]{:S(2)}, u32[]{:S(2)}) collective-permute-start(f32[4,3,64,256]{3,2,1,0:T(8,128)} %bitcast_add_fusion), channel_id=1, source_target_pairs={{0,4},{4,8},{8,12},{16,20},{20,24},{24,28},{32,36},{36,40},{40,44}... | collective-permute-start | bytes 2359304 | tf_op jit(solution)/shard_map/ppermute | solution.py:191
  89.1 26.2 %all-to-all-start.2 = ((f32[4,5,8,256]{3,2,1,0:T(8,128)}), f32[4,5,8,256]{3,2,1,0:T(8,128)S(1)}, u32[]{:S(2)}, u32[]{:S(2)}) async-start(f32[4,5,8,256]{3,2,1,0:T(8,128)} %broadcast_in_dim.24), calls=%async_computation.2 | async-start | bytes 327680 | tf_op jit(solution)/shard_map/all_to_all | solution.py:203
  101.4 0.9 copy-start.2
  103.7 18.9 %collective-permute-start.7 = (f32[3,64,256]{2,1,0:T(8,128)S(1)}, f32[3,64,256]{2,1,0:T(8,128)S(1)}, u32[]{:S(2)}, u32[]{:S(2)}) collective-permute-start(f32[3,64,256]{2,1,0:T(8,128)S(1)} %get-tuple-element.18), channel_id=1, source_target_pairs={{0,1},{1,0},{2,3},{3,2},{4,5},{5,4},{6,7},{7,6},{8,9},{9,8},{10,11... | collective-permute-start | bytes 589832 | tf_op jit(solution)/shard_map/ppermute | solution.py:199
  106.0 16.5 %collective-permute-start.8 = (f32[3,64,256]{2,1,0:T(8,128)S(1)}, f32[3,64,256]{2,1,0:T(8,128)S(1)}, u32[]{:S(2)}, u32[]{:S(2)}) collective-permute-start(f32[3,64,256]{2,1,0:T(8,128)S(1)} %get-tuple-element.20), channel_id=1, source_target_pairs={{0,2},{1,3},{2,0},{3,1},{4,6},{5,7},{6,4},{7,5},{8,10},{9,11},{10,... | collective-permute-start | bytes 589832 | tf_op jit(solution)/shard_map/ppermute | solution.py:199
  110.0 12.5 %collective-permute-start.9 = (f32[3,64,256]{2,1,0:T(8,128)S(1)}, f32[3,64,256]{2,1,0:T(8,128)S(1)}, u32[]{:S(2)}, u32[]{:S(2)}) collective-permute-start(f32[3,64,256]{2,1,0:T(8,128)S(1)} %get-tuple-element.19), channel_id=1, source_target_pairs={{0,3},{1,2},{2,1},{3,0},{4,7},{5,6},{6,5},{7,4},{8,11},{9,10},{10,... | collective-permute-start | bytes 589832 | tf_op jit(solution)/shard_map/ppermute | solution.py:199
  117.0 17.1 %all-to-all-start.3 = ((f32[16,4,8,256]{3,2,1,0:T(8,128)}), f32[16,4,8,256]{3,2,1,0:T(8,128)S(1)}, u32[]{:S(2)}, u32[]{:S(2)}) async-start(f32[16,4,8,256]{3,2,1,0:T(8,128)} %broadcast_in_dim.25), calls=%async_computation.3 | async-start | bytes 1048576 | tf_op jit(solution)/shard_map/all_to_all | solution.py:203
  123.6 12.5 %collective-permute-start.10 = (f32[2,64,256]{2,1,0:T(8,128)S(1)}, f32[2,64,256]{2,1,0:T(8,128)S(1)}, u32[]{:S(2)}, u32[]{:S(2)}) collective-permute-start(f32[2,64,256]{2,1,0:T(8,128)S(1)} %get-tuple-element.17), channel_id=1, source_target_pairs={{0,1},{1,0},{2,3},{3,2},{4,5},{5,4},{6,7},{7,6},{8,9},{9,8},{10,11... | collective-permute-start | bytes 393224 | tf_op jit(solution)/shard_map/ppermute | solution.py:199
  127.0 9.1 %collective-permute-start.11 = (f32[2,64,256]{2,1,0:T(8,128)S(1)}, f32[2,64,256]{2,1,0:T(8,128)S(1)}, u32[]{:S(2)}, u32[]{:S(2)}) collective-permute-start(f32[2,64,256]{2,1,0:T(8,128)S(1)} %get-tuple-element.17), channel_id=1, source_target_pairs={{0,2},{1,3},{2,0},{3,1},{4,6},{5,7},{6,4},{7,5},{8,10},{9,11},{10,... | collective-permute-start | bytes 393224 | tf_op jit(solution)/shard_map/ppermute | solution.py:199
  131.6 8.1 %collective-permute-start.12 = (f32[2,64,256]{2,1,0:T(8,128)S(1)}, f32[2,64,256]{2,1,0:T(8,128)S(1)}, u32[]{:S(2)}, u32[]{:S(2)}) collective-permute-start(f32[2,64,256]{2,1,0:T(8,128)S(1)} %get-tuple-element.17), channel_id=1, source_target_pairs={{0,3},{1,2},{2,1},{3,0},{4,7},{5,6},{6,5},{7,4},{8,11},{9,10},{10,... | collective-permute-start | bytes 393224 | tf_op jit(solution)/shard_map/ppermute | solution.py:199
  134.1 5.7 %collective-permute-start.13 = (f32[4,128,256]{2,1,0:T(8,128)S(1)}, f32[4,128,256]{2,1,0:T(8,128)S(1)}, u32[]{:S(2)}, u32[]{:S(2)}) collective-permute-start(f32[4,128,256]{2,1,0:T(8,128)S(1)} %bitcast.39), channel_id=1, source_target_pairs={{0,16},{16,0},{1,17},{17,1},{2,18},{18,2},{3,19},{19,3},{4,20},{20... | collective-permute-start | bytes 1572872 | tf_op jit(solution)/shard_map/ppermute | solution.py:195
  139.7 0.8 copy-start.4
  140.5 1.0 copy-start

commit v8 on v7

--- a/solution.py
+++ b/solution.py
@@ -16,14 +16,18 @@
 TILE = ("z_high", "z_low", "core")
 
 
-def tables():
+def waves():
     index = np.arange(S)
     angle = (index[:, None] * index[None, :] % S) * (2.0 * math.pi / S)
-    cosine, sine = np.cos(angle) / 16.0, np.sin(angle) / 16.0
-    left = np.block([[cosine, sine], [-sine, cosine]]).astype(np.float32)
-    head = left.astype(ml_dtypes.bfloat16)
-    rest = (left - head.astype(np.float32)).astype(ml_dtypes.bfloat16)
-    return (head, rest, np.ascontiguousarray(head.T), np.ascontiguousarray(rest.T))
+    both = np.stack([np.cos(angle), np.sin(angle)]).astype(np.float32) / 16.0
+    head = both.astype(ml_dtypes.bfloat16)
+    return np.stack([head, (both - head.astype(np.float32)).astype(ml_dtypes.bfloat16)])
+
+
+def table(cosine, sine):
+    return jnp.concatenate(
+        [jnp.concatenate([cosine, sine], axis=1), jnp.concatenate([-sine, cosine], axis=1)], axis=0
+    )
 
 
 def split(value):
@@ -78,8 +82,8 @@
 
 
 def slots_kernel(
-    card, own, right, below, corner_a, corner_b, probe, frames, lh, lr, rh, rr,
-    top_left, top_right, bottom, keep, send, extended, total, terms,
+    card, own, right, below, corner_a, corner_b, probe, roots, lh, lr,
+    top_left, top_right, bottom, keep, send, extended, total, terms, rh, rr,
 ):
     extended[:, :S, :S] = own[...]
     extended[:, :S, S:] = right[...]
@@ -87,6 +91,7 @@
     extended[:, S:, S:] = corner_a[...] + corner_b[...]
     total[...] = jnp.zeros_like(total)
     terms[...] = jnp.zeros_like(terms)
+    rh[...], rr[...] = regroup(lh[...]), regroup(lr[...])
     blank = jnp.zeros((S, S), jnp.float32)
 
     def one_slot(slot, carry):
@@ -100,8 +105,8 @@
         RC = 256
         wave = []
         for m in range(2):
-            real = probe[0, m] * patch_real - probe[1, m] * patch_imag
-            imag = probe[0, m] * patch_imag + probe[1, m] * patch_real
+            real = probe[m] * patch_real - probe[2 + m] * patch_imag
+            imag = probe[m] * patch_imag + probe[2 + m] * patch_real
             wave.append(product(left_table, split(jnp.concatenate([real, imag], axis=0))))
         back = [[], []]
         for at in range(0, S, RC):
@@ -113,7 +118,7 @@
             far = product(split(jnp.concatenate(far, axis=0)), right_table)
             power = far[:RC] * far[:RC] + far[RC:] * far[RC:]
             power = power[:, :S] + power[:, S:]
-            change = jnp.sqrt(frames[slot, part]) / jnp.sqrt(power + 1.0) - 1.0
+            change = roots[slot, part] / jnp.sqrt(power + 1.0) - 1.0
             change = jnp.concatenate([change, change], axis=0)
             swapped = jnp.concatenate([far[:, S:] * change, far[:, :S] * change], axis=1)
             chunk = product(split(swapped), right_table)
@@ -124,15 +129,12 @@
             whole = jnp.concatenate([c[:, :S] for c in back[m]] + [c[:, S:] for c in back[m]], axis=0)
             chi = product(left_table, split(whole))
             chi_imag, chi_real = chi[:S], chi[S:]
-            object_real += probe[0, m] * chi_real + probe[1, m] * chi_imag
-            object_imag += probe[0, m] * chi_imag - probe[1, m] * chi_real
+            object_real += probe[m] * chi_real + probe[2 + m] * chi_imag
+            object_imag += probe[m] * chi_imag - probe[2 + m] * chi_real
             terms[m] += patch_real * chi_real + patch_imag * chi_imag
             terms[2 + m] += patch_real * chi_imag - patch_imag * chi_real
         terms[4] += patch_real * patch_real + patch_imag * patch_imag
-        light = blank
-        for m in range(2):
-            light += probe[0, m] * probe[0, m] + probe[1, m] * probe[1, m]
-        for plane, value in enumerate((object_real, object_imag, light)):
+        for plane, value in enumerate((object_real, object_imag, probe[4])):
             total[plane, band_rows, band_columns] += placed(value, inside, fine)
         return carry
 
@@ -154,7 +156,7 @@
             send[chunk, plane] = terms[plane, pl.ds(other, height), :]
 
 
-def run_slots(card, blocks, probe, frames, chunks):
+def run_slots(card, blocks, probe, roots, tables, chunks):
     height = S // 2 // chunks
     f32 = jnp.float32
     quarter = (QUARTERS, 3, S // QUARTERS, S)
@@ -168,16 +170,18 @@
             jax.ShapeDtypeStruct((chunks, 5, height, S), f32),
             jax.ShapeDtypeStruct((chunks, 5, height, S), f32),
         ),
-        in_specs=[pl.BlockSpec(memory_space=pltpu.SMEM), *[vmem] * 11],
+        in_specs=[pl.BlockSpec(memory_space=pltpu.SMEM), *[vmem] * 9],
         out_specs=[vmem] * 5,
         scratch_shapes=[
             pltpu.VMEM((2, 2 * S, 2 * S), f32),
             pltpu.VMEM((3, 2 * S, 2 * S), f32),
             pltpu.VMEM((5, S, S), f32),
+            pltpu.VMEM((2 * S, 2 * S), jnp.bfloat16),
+            pltpu.VMEM((2 * S, 2 * S), jnp.bfloat16),
         ],
-        compiler_params=pltpu.CompilerParams(vmem_limit_bytes=54 * 1024 * 1024),
+        compiler_params=pltpu.CompilerParams(vmem_limit_bytes=40 * 1024 * 1024),
         name="slots",
-    )(card, *blocks, probe, frames, *(jnp.asarray(t) for t in tables()))
+    )(card, *blocks, probe, roots, *tables)
 
 
 def moved(block, tiles_by, bands_by):
@@ -221,10 +225,16 @@
     right = moved(object_planes, 0, -1)
     below = moved(object_planes, -1, 0)
     card = jnp.pad(jnp.concatenate([offsets.reshape(6), counts.reshape(1)])[None], ((0, 0), (0, 121)))
+    power = jnp.sum(probe_planes[0] ** 2 + probe_planes[1] ** 2, axis=0)
+    probe = jnp.concatenate([probe_planes.reshape(4, S, S), power[None]])
+    roots = jnp.sqrt(patterns[0, 0, 0])
+    parts = lax.optimization_barrier(jnp.asarray(waves()))
+    tables = (table(*parts[0]), table(*parts[1]))
+    below, card, probe, roots, tables = lax.optimization_barrier((below, card, probe, roots, tables))
     corner_a, corner_b = corners(right, below)
     top_left, top_right, bottom, keep, send = run_slots(
         card, (object_planes, right, below, corner_a, corner_b),
-        probe_planes, patterns[0, 0, 0], chunks,
+        probe, roots, tables, chunks,
     )
 
     from_above = moved(bottom, 1, 0)

time: 142 us -> 136 us (0.958)
  Pallas kernels: 14.6 us -> 2.42 us
  blocking collectives: 32.6 us -> 40.7 us
    pallas_call x1, Pallas kernels: 14.6 us -> 2.42 us  [run_slots(): pl.pallas_call(slots_kernel, out_shape=(jax.ShapeDtypeStruct(quarter, f32...]
    all_to_all x2, blocking collectives: 32.6 us -> 40.7 us  [exchanged(): return lax.all_to_all(block, axes, 0, 0)]
    ppermute x4, waiting for transfers between devices: 11.7 us -> 7.2 us  [moved(): return lax.ppermute(block, (*TILE, 'band'), route)]
    ppermute x1, waiting for transfers between devices: 0.34 us -> 2.49 us  [corners(): lax.ppermute(right, 'core', [(1, 0)])]
    ppermute x2, starting transfers between devices: 5.28 us -> 3.83 us  [across_cores(): return lax.ppermute(block, 'core', [(0, 1), (1, 0)])]
    unnamed x19 -> x13, local copies, waits for them, and re-layouts: 4 us -> 2.69 us
where the time goes in v8:
time: 136 us; the launch traced here: 135 us
  starting transfers between devices  61.3 us (45%)
  blocking collectives  40.7 us (30%)
  waiting for transfers between devices  17.4 us (13%)
  local copies, waits for them, and re-layouts  5.97 us (4%)
  other arithmetic  5.74 us (4%)
  Pallas kernels  2.42 us (2%)
  between operations  1.7 us (1%)
    all_to_all x2, blocking collectives, exchanged(): return lax.all_to_all(block, axes, 0, 0)  40.7 us
    ppermute x6, starting transfers between devices, across_posts(): return lax.ppermute(block, 'pos', [(p, p ^ bits) for p in range(QUARTERS)])  20.8 us
    all_to_all x2, starting transfers between devices, exchanged(): return lax.all_to_all(block, axes, 0, 0)  17.6 us
    ppermute x4, starting transfers between devices, moved(): return lax.ppermute(block, (*TILE, 'band'), route)  17 us
    ppermute x4, waiting for transfers between devices, moved(): return lax.ppermute(block, (*TILE, 'band'), route)  7.2 us
    ppermute x2, starting transfers between devices, across_cores(): return lax.ppermute(block, 'core', [(0, 1), (1, 0)])  3.83 us
    ppermute x6, waiting for transfers between devices, across_posts(): return lax.ppermute(block, 'pos', [(p, p ^ bits) for p in range(QUARTERS)])  3.56 us
  transfers between devices with their start and end apart: 16, of which 5 were waited for; matrix products, arithmetic and copies ran while one was open for 5% of the time, Pallas kernels for 0%

profile of v8, /device:TPU:2, one launch (start us, length us, event | category | flops | bytes accessed | tf_op | source)
XLA Modules:
  0.0 135.2 jit_solution(16140254217725868786)
XLA Ops:
  0.6 0.0 copy-start.1
  0.7 1.4 %collective-permute-start = (f32[2,256,256]{2,1,0:T(8,128)}, f32[2,256,256]{2,1,0:T(8,128)S(1)}, u32[]{:S(2)}, u32[]{:S(2)}) collective-permute-start(f32[2,256,256]{2,1,0:T(8,128)} %own.1), channel_id=1, source_target_pairs={{16,0},{20,4},{24,8},{28,12},{32,16},{36,20},{40,24},{44,28},{48,3... | collective-permute-start | bytes 1572872 | tf_op jit(solution)/shard_map/ppermute | solution.py:195
  2.1 7.8 %collective-permute-start.1 = (f32[2,256,256]{2,1,0:T(8,128)}, f32[2,256,256]{2,1,0:T(8,128)S(1)}, u32[]{:S(2)}, u32[]{:S(2)}) collective-permute-start(f32[2,256,256]{2,1,0:T(8,128)} %own.1), channel_id=1, source_target_pairs={{4,0},{8,4},{12,8},{20,16},{24,20},{28,24},{36,32},{40,36},{44,40}... | collective-permute-start | bytes 1572872 | tf_op jit(solution)/shard_map/ppermute | solution.py:195
  9.9 1.1 slice_bitcast_fusion
  11.0 1.0 fusion.8
  12.1 0.1 add_reduce_fusion
  12.1 0.1 copy.13
  12.2 0.1 reshape.32
  13.0 0.1 add_bitcast_fusion
  13.1 0.1 maximum_maximum_fusion
  13.1 0.0 copy-start.3
  13.2 0.0 copy-start
  13.2 0.1 pad_maximum_fusion.probe
  13.3 1.0 copy-done.3
  14.3 0.2 sqrt_bitcast_fusion.roots
  14.5 0.7 collective-permute-start.2
  15.2 7.2 %collective-permute-done.1.right = f32[2,256,256]{2,1,0:T(8,128)S(1)} collective-permute-done((f32[2,256,256]{2,1,0:T(8,128)}, f32[2,256,256]{2,1,0:T(8,128)S(1)}, u32[]{:S(2)}, u32[]{:S(2)}) %collective-permute-start.1) | collective-permute-done | bytes 524320 | tf_op jit(solution)/shard_map/ppermute | solution.py:195
  22.4 1.3 collective-permute-start.3
  23.7 2.5 %collective-permute-done.3.corner_b = f32[2,256,256]{2,1,0:T(8,128)S(1)} collective-permute-done((f32[2,256,256]{2,1,0:T(8,128)S(1)}, f32[2,256,256]{2,1,0:T(8,128)S(1)}, u32[]{:S(2)}, u32[]{:S(2)}) %collective-permute-start.3) | collective-permute-done | bytes 524320 | tf_op jit(solution)/shard_map/ppermute | solution.py:217
  26.2 2.4 %slots.1 = (f32[4,3,64,256]{3,2,1,0:T(8,128)S(1)}, f32[4,3,64,256]{3,2,1,0:T(8,128)S(1)}, f32[2,4,3,64,256]{4,3,2,1,0:T(8,128)}, f32[16,5,8,256]{3,2,1,0:T(8,128)S(1)}, f32[16,5,8,256]{3,2,1,0:T(8,128)S(1)}) custom-call(s32[1,128]{1,0:T(1,128)S(1)} %pad.4.card, f32[2,256,256]{2,1,0:T(8,128)S(1)} %copy-done, f32[2,256,256]{2,1,0:T(8,128)S(1)} %collective-permute-done.1.right, ...), custom_call_target="tpu_custom_call" | custom-call | tf_op jit(solution)/shard_map/slots/pallas_call | solution.py:164
  28.6 5.0 %collective-permute-start.5 = (f32[2,4,3,64,256]{4,3,2,1,0:T(8,128)}, f32[2,4,3,64,256]{4,3,2,1,0:T(8,128)}, u32[]{:S(2)}, u32[]{:S(2)}) collective-permute-start(f32[2,4,3,64,256]{4,3,2,1,0:T(8,128)} %get-tuple-element.24), channel_id=1, source_target_pairs={{0,16},{4,20},{8,24},{12,28},{16,32},{20,36},{24,40},{28,44},{32,4... | collective-permute-start | bytes 4718600 | tf_op jit(solution)/shard_map/ppermute | solution.py:195
  33.6 1.9 %collective-permute-start.4 = (f32[16,5,8,256]{3,2,1,0:T(8,128)S(1)}, f32[16,5,8,256]{3,2,1,0:T(8,128)S(1)}, u32[]{:S(2)}, u32[]{:S(2)}) collective-permute-start(f32[16,5,8,256]{3,2,1,0:T(8,128)S(1)} %get-tuple-element.23), channel_id=1, source_target_pairs={{0,16},{16,0},{1,17},{17,1},{2,18},{18,2},{3,19},{19,3},{4,20},{20... | collective-permute-start | bytes 1966088 | tf_op jit(solution)/shard_map/ppermute | solution.py:199
  35.5 2.1 %collective-permute-done.4 = f32[16,5,8,256]{3,2,1,0:T(8,128)S(1)} collective-permute-done((f32[16,5,8,256]{3,2,1,0:T(8,128)S(1)}, f32[16,5,8,256]{3,2,1,0:T(8,128)S(1)}, u32[]{:S(2)}, u32[]{:S(2)}) %collective-permute-start.4) | collective-permute-done | bytes 655392 | tf_op jit(solution)/shard_map/ppermute | solution.py:199
  37.6 0.1 add.90
  37.7 29.0 %all_to_all.20 = f32[16,5,8,256]{3,2,1,0:T(8,128)S(1)} all-to-all(f32[16,5,8,256]{3,2,1,0:T(8,128)S(1)} %add.90), channel_id=1, replica_groups=mesh['z_high'=4,'z_low'=4,'core'=2,'band'=4,'pos'=4] {'band','pos'}, dimensions={0} | all-to-all | bytes 1310720 | tf_op jit(solution)/shard_map/all_to_all | solution.py:207
  66.8 2.1 %bitcast_add_fusion = f32[4,3,64,256]{3,2,1,0:T(8,128)} fusion(f32[4,3,64,256]{3,2,1,0:T(8,128)S(1)} %get-tuple-element.26, f32[2,4,3,64,256]{4,3,2,1,0:T(8,128)} %collective-permute-done.5), kind=kLoop, calls=%fused_computation.1 | loop fusion | flops 196608 | bytes 2359296 | tf_op jit(solution)/shard_map/add | solution.py:244
  68.9 2.7 %collective-permute-start.6 = (f32[4,3,64,256]{3,2,1,0:T(8,128)}, f32[4,3,64,256]{3,2,1,0:T(8,128)S(1)}, u32[]{:S(2)}, u32[]{:S(2)}) collective-permute-start(f32[4,3,64,256]{3,2,1,0:T(8,128)} %bitcast_add_fusion), channel_id=1, source_target_pairs={{0,4},{4,8},{8,12},{16,20},{20,24},{24,28},{32,36},{36,40},{40,44}... | collective-permute-start | bytes 2359304 | tf_op jit(solution)/shard_map/ppermute | solution.py:195
  71.6 11.7 %all_to_all.21 = f32[4,5,8,256]{3,2,1,0:T(8,128)S(1)} all-to-all(f32[4,5,8,256]{3,2,1,0:T(8,128)S(1)} %broadcast_in_dim.27), channel_id=1, replica_groups=mesh['z_high'=4,'z_low'=4,'core'=2,'band'=4,'pos'=4] {'z_low'}, dimensions={0} | all-to-all | bytes 327680 | tf_op jit(solution)/shard_map/all_to_all | solution.py:207
  83.3 0.7 broadcast_in_dim.28
  84.0 12.1 %all-to-all-start.2 = ((f32[4,5,8,256]{3,2,1,0:T(8,128)}), f32[4,5,8,256]{3,2,1,0:T(8,128)S(1)}, u32[]{:S(2)}, u32[]{:S(2)}) async-start(f32[4,5,8,256]{3,2,1,0:T(8,128)} %broadcast_in_dim.28), calls=%async_computation.2 | async-start | bytes 327680 | tf_op jit(solution)/shard_map/all_to_all | solution.py:207
  96.1 1.3 fusion
  97.4 2.4 %collective-permute-start.7 = (f32[3,64,256]{2,1,0:T(8,128)S(1)}, f32[3,64,256]{2,1,0:T(8,128)S(1)}, u32[]{:S(2)}, u32[]{:S(2)}) collective-permute-start(f32[3,64,256]{2,1,0:T(8,128)S(1)} %get-tuple-element.30), channel_id=1, source_target_pairs={{0,1},{1,0},{2,3},{3,2},{4,5},{5,4},{6,7},{7,6},{8,9},{9,8},{10,11... | collective-permute-start | bytes 589832 | tf_op jit(solution)/shard_map/ppermute | solution.py:203
  99.8 4.0 %collective-permute-start.8 = (f32[3,64,256]{2,1,0:T(8,128)S(1)}, f32[3,64,256]{2,1,0:T(8,128)S(1)}, u32[]{:S(2)}, u32[]{:S(2)}) collective-permute-start(f32[3,64,256]{2,1,0:T(8,128)S(1)} %get-tuple-element.32), channel_id=1, source_target_pairs={{0,2},{1,3},{2,0},{3,1},{4,6},{5,7},{6,4},{7,5},{8,10},{9,11},{10,... | collective-permute-start | bytes 589832 | tf_op jit(solution)/shard_map/ppermute | solution.py:203
  103.8 4.1 %collective-permute-start.9 = (f32[3,64,256]{2,1,0:T(8,128)S(1)}, f32[3,64,256]{2,1,0:T(8,128)S(1)}, u32[]{:S(2)}, u32[]{:S(2)}) collective-permute-start(f32[3,64,256]{2,1,0:T(8,128)S(1)} %get-tuple-element.31), channel_id=1, source_target_pairs={{0,3},{1,2},{2,1},{3,0},{4,7},{5,6},{6,5},{7,4},{8,11},{9,10},{10,... | collective-permute-start | bytes 589832 | tf_op jit(solution)/shard_map/ppermute | solution.py:203
  107.9 2.1 %all-to-all-done.2 = f32[4,5,8,256]{3,2,1,0:T(8,128)S(1)} async-done(((f32[4,5,8,256]{3,2,1,0:T(8,128)}), f32[4,5,8,256]{3,2,1,0:T(8,128)S(1)}, u32[]{:S(2)}, u32[]{:S(2)}) %all-to-all-start.2) | async-done | bytes 163872 | tf_op jit(solution)/shard_map/all_to_all | solution.py:207
  110.0 0.8 fusion.5
  110.8 0.8 broadcast_in_dim.29
  111.6 5.6 %all-to-all-start.3 = ((f32[16,4,8,256]{3,2,1,0:T(8,128)}), f32[16,4,8,256]{3,2,1,0:T(8,128)S(1)}, u32[]{:S(2)}, u32[]{:S(2)}) async-start(f32[16,4,8,256]{3,2,1,0:T(8,128)} %broadcast_in_dim.29), calls=%async_computation.3 | async-start | bytes 1048576 | tf_op jit(solution)/shard_map/all_to_all | solution.py:207
  117.2 0.1 fusion.2
  117.4 3.4 %collective-permute-start.10 = (f32[2,64,256]{2,1,0:T(8,128)S(1)}, f32[2,64,256]{2,1,0:T(8,128)S(1)}, u32[]{:S(2)}, u32[]{:S(2)}) collective-permute-start(f32[2,64,256]{2,1,0:T(8,128)S(1)} %get-tuple-element.29), channel_id=1, source_target_pairs={{0,1},{1,0},{2,3},{3,2},{4,5},{5,4},{6,7},{7,6},{8,9},{9,8},{10,11... | collective-permute-start | bytes 393224 | tf_op jit(solution)/shard_map/ppermute | solution.py:203
  120.7 4.6 %collective-permute-start.11 = (f32[2,64,256]{2,1,0:T(8,128)S(1)}, f32[2,64,256]{2,1,0:T(8,128)S(1)}, u32[]{:S(2)}, u32[]{:S(2)}) collective-permute-start(f32[2,64,256]{2,1,0:T(8,128)S(1)} %get-tuple-element.29), channel_id=1, source_target_pairs={{0,2},{1,3},{2,0},{3,1},{4,6},{5,7},{6,4},{7,5},{8,10},{9,11},{10,... | collective-permute-start | bytes 393224 | tf_op jit(solution)/shard_map/ppermute | solution.py:203
  125.4 2.5 %collective-permute-start.12 = (f32[2,64,256]{2,1,0:T(8,128)S(1)}, f32[2,64,256]{2,1,0:T(8,128)S(1)}, u32[]{:S(2)}, u32[]{:S(2)}) collective-permute-start(f32[2,64,256]{2,1,0:T(8,128)S(1)} %get-tuple-element.29), channel_id=1, source_target_pairs={{0,3},{1,2},{2,1},{3,0},{4,7},{5,6},{6,5},{7,4},{8,11},{9,10},{10,... | collective-permute-start | bytes 393224 | tf_op jit(solution)/shard_map/ppermute | solution.py:203
  127.9 1.9 %collective-permute-start.13 = (f32[4,128,256]{2,1,0:T(8,128)S(1)}, f32[4,128,256]{2,1,0:T(8,128)S(1)}, u32[]{:S(2)}, u32[]{:S(2)}) collective-permute-start(f32[4,128,256]{2,1,0:T(8,128)S(1)} %bitcast.54), channel_id=1, source_target_pairs={{0,16},{16,0},{1,17},{17,1},{2,18},{18,2},{3,19},{19,3},{4,20},{20... | collective-permute-start | bytes 1572872 | tf_op jit(solution)/shard_map/ppermute | solution.py:199
  129.9 3.5 %collective-permute-done.12 = f32[2,64,256]{2,1,0:T(8,128)S(1)} collective-permute-done((f32[2,64,256]{2,1,0:T(8,128)S(1)}, f32[2,64,256]{2,1,0:T(8,128)S(1)}, u32[]{:S(2)}, u32[]{:S(2)}) %collective-permute-start.12) | collective-permute-done | bytes 131104 | tf_op jit(solution)/shard_map/ppermute | solution.py:203
  133.5 0.0 copy-start.4
  133.5 0.1 broadcast_in_dim.26
  133.7 0.6 copy-done.4
  134.3 1.0 copy-done.2
  (32 shorter events, 0.4 us)
Async XLA Ops:
  0.6 11.4 %copy-start.1 = (f32[2,2,256,256]{3,2,1,0:T(8,128)S(1)}, f32[2,2,256,256]{3,2,1,0:T(8,128)}, u32[]{:S(2)}) copy-start(f32[2,2,256,256]{3,2,1,0:T(8,128)} %param.7) | copy-start | bytes 3145732
  0.6 11.5 %copy-start.5 = (s32[1,1,1,3,2]{3,4,2,1,0:T(2,128)S(1)}, s32[1,1,1,3,2]{3,4,2,1,0:T(2,128)}, u32[]{:S(2)}) copy-start(s32[1,1,1,3,2]{3,4,2,1,0:T(2,128)} %param.9) | copy-start | bytes 76
  0.7 13.8 %collective-permute-start = (f32[2,256,256]{2,1,0:T(8,128)}, f32[2,256,256]{2,1,0:T(8,128)S(1)}, u32[]{:S(2)}, u32[]{:S(2)}) collective-permute-start(f32[2,256,256]{2,1,0:T(8,128)} %own.1), channel_id=1, source_target_pairs={{16,0},{20,4},{24,8},{28,12},{32,16},{36,20},{40,24},{44,28},{48,3... | collective-permute-start | bytes 1572872 | tf_op jit(solution)/shard_map/ppermute | solution.py:195
  2.1 20.3 %collective-permute-start.1 = (f32[2,256,256]{2,1,0:T(8,128)}, f32[2,256,256]{2,1,0:T(8,128)S(1)}, u32[]{:S(2)}, u32[]{:S(2)}) collective-permute-start(f32[2,256,256]{2,1,0:T(8,128)} %own.1), channel_id=1, source_target_pairs={{4,0},{8,4},{12,8},{20,16},{24,20},{28,24},{36,32},{40,36},{44,40}... | collective-permute-start | bytes 1572872 | tf_op jit(solution)/shard_map/ppermute | solution.py:195
  13.1 1.1 copy-start.3
  13.2 13.0 %copy-start = (f32[2,256,256]{2,1,0:T(8,128)S(1)}, f32[2,256,256]{2,1,0:T(8,128)}, u32[]{:S(2)}) copy-start(f32[2,256,256]{2,1,0:T(8,128)} %own.1) | copy-start | bytes 1572868
  14.5 9.2 %collective-permute-start.2 = (f32[2,256,256]{2,1,0:T(8,128)S(1)}, f32[2,256,256]{2,1,0:T(8,128)S(1)}, u32[]{:S(2)}, u32[]{:S(2)}) collective-permute-start(f32[2,256,256]{2,1,0:T(8,128)S(1)} %collective-permute-done.below), channel_id=1, source_target_pairs={{20,16},{24,20},{28,24},{52,48},{56,52},{60,56},{84,80},{88,84},{9... | collective-permute-start | bytes 1572872 | tf_op jit(solution)/shard_map/ppermute | solution.py:217
  22.4 3.8 %collective-permute-start.3 = (f32[2,256,256]{2,1,0:T(8,128)S(1)}, f32[2,256,256]{2,1,0:T(8,128)S(1)}, u32[]{:S(2)}, u32[]{:S(2)}) collective-permute-start(f32[2,256,256]{2,1,0:T(8,128)S(1)} %collective-permute-done.1.right), channel_id=1, source_target_pairs={{16,0},{17,1},{18,2},{19,3},{20,4},{21,5},{22,6},{23,7},{24,8},{25... | collective-permute-start | bytes 1572872 | tf_op jit(solution)/shard_map/ppermute | solution.py:217
  28.6 38.2 %collective-permute-start.5 = (f32[2,4,3,64,256]{4,3,2,1,0:T(8,128)}, f32[2,4,3,64,256]{4,3,2,1,0:T(8,128)}, u32[]{:S(2)}, u32[]{:S(2)}) collective-permute-start(f32[2,4,3,64,256]{4,3,2,1,0:T(8,128)} %get-tuple-element.24), channel_id=1, source_target_pairs={{0,16},{4,20},{8,24},{12,28},{16,32},{20,36},{24,40},{28,44},{32,4... | collective-permute-start | bytes 4718600 | tf_op jit(solution)/shard_map/ppermute | solution.py:195
  33.6 4.0 %collective-permute-start.4 = (f32[16,5,8,256]{3,2,1,0:T(8,128)S(1)}, f32[16,5,8,256]{3,2,1,0:T(8,128)S(1)}, u32[]{:S(2)}, u32[]{:S(2)}) collective-permute-start(f32[16,5,8,256]{3,2,1,0:T(8,128)S(1)} %get-tuple-element.23), channel_id=1, source_target_pairs={{0,16},{16,0},{1,17},{17,1},{2,18},{18,2},{3,19},{19,3},{4,20},{20... | collective-permute-start | bytes 1966088 | tf_op jit(solution)/shard_map/ppermute | solution.py:199
  68.9 27.2 %collective-permute-start.6 = (f32[4,3,64,256]{3,2,1,0:T(8,128)}, f32[4,3,64,256]{3,2,1,0:T(8,128)S(1)}, u32[]{:S(2)}, u32[]{:S(2)}) collective-permute-start(f32[4,3,64,256]{3,2,1,0:T(8,128)} %bitcast_add_fusion), channel_id=1, source_target_pairs={{0,4},{4,8},{8,12},{16,20},{20,24},{24,28},{32,36},{36,40},{40,44}... | collective-permute-start | bytes 2359304 | tf_op jit(solution)/shard_map/ppermute | solution.py:195
  84.0 26.0 %all-to-all-start.2 = ((f32[4,5,8,256]{3,2,1,0:T(8,128)}), f32[4,5,8,256]{3,2,1,0:T(8,128)S(1)}, u32[]{:S(2)}, u32[]{:S(2)}) async-start(f32[4,5,8,256]{3,2,1,0:T(8,128)} %broadcast_in_dim.28), calls=%async_computation.2 | async-start | bytes 327680 | tf_op jit(solution)/shard_map/all_to_all | solution.py:207
  97.4 19.7 %collective-permute-start.7 = (f32[3,64,256]{2,1,0:T(8,128)S(1)}, f32[3,64,256]{2,1,0:T(8,128)S(1)}, u32[]{:S(2)}, u32[]{:S(2)}) collective-permute-start(f32[3,64,256]{2,1,0:T(8,128)S(1)} %get-tuple-element.30), channel_id=1, source_target_pairs={{0,1},{1,0},{2,3},{3,2},{4,5},{5,4},{6,7},{7,6},{8,9},{9,8},{10,11... | collective-permute-start | bytes 589832 | tf_op jit(solution)/shard_map/ppermute | solution.py:203
  99.8 17.4 %collective-permute-start.8 = (f32[3,64,256]{2,1,0:T(8,128)S(1)}, f32[3,64,256]{2,1,0:T(8,128)S(1)}, u32[]{:S(2)}, u32[]{:S(2)}) collective-permute-start(f32[3,64,256]{2,1,0:T(8,128)S(1)} %get-tuple-element.32), channel_id=1, source_target_pairs={{0,2},{1,3},{2,0},{3,1},{4,6},{5,7},{6,4},{7,5},{8,10},{9,11},{10,... | collective-permute-start | bytes 589832 | tf_op jit(solution)/shard_map/ppermute | solution.py:203
  103.8 13.4 %collective-permute-start.9 = (f32[3,64,256]{2,1,0:T(8,128)S(1)}, f32[3,64,256]{2,1,0:T(8,128)S(1)}, u32[]{:S(2)}, u32[]{:S(2)}) collective-permute-start(f32[3,64,256]{2,1,0:T(8,128)S(1)} %get-tuple-element.31), channel_id=1, source_target_pairs={{0,3},{1,2},{2,1},{3,0},{4,7},{5,6},{6,5},{7,4},{8,11},{9,10},{10,... | collective-permute-start | bytes 589832 | tf_op jit(solution)/shard_map/ppermute | solution.py:203
  111.6 16.2 %all-to-all-start.3 = ((f32[16,4,8,256]{3,2,1,0:T(8,128)}), f32[16,4,8,256]{3,2,1,0:T(8,128)S(1)}, u32[]{:S(2)}, u32[]{:S(2)}) async-start(f32[16,4,8,256]{3,2,1,0:T(8,128)} %broadcast_in_dim.29), calls=%async_computation.3 | async-start | bytes 1048576 | tf_op jit(solution)/shard_map/all_to_all | solution.py:207
  117.4 12.5 %collective-permute-start.10 = (f32[2,64,256]{2,1,0:T(8,128)S(1)}, f32[2,64,256]{2,1,0:T(8,128)S(1)}, u32[]{:S(2)}, u32[]{:S(2)}) collective-permute-start(f32[2,64,256]{2,1,0:T(8,128)S(1)} %get-tuple-element.29), channel_id=1, source_target_pairs={{0,1},{1,0},{2,3},{3,2},{4,5},{5,4},{6,7},{7,6},{8,9},{9,8},{10,11... | collective-permute-start | bytes 393224 | tf_op jit(solution)/shard_map/ppermute | solution.py:203
  120.7 9.1 %collective-permute-start.11 = (f32[2,64,256]{2,1,0:T(8,128)S(1)}, f32[2,64,256]{2,1,0:T(8,128)S(1)}, u32[]{:S(2)}, u32[]{:S(2)}) collective-permute-start(f32[2,64,256]{2,1,0:T(8,128)S(1)} %get-tuple-element.29), channel_id=1, source_target_pairs={{0,2},{1,3},{2,0},{3,1},{4,6},{5,7},{6,4},{7,5},{8,10},{9,11},{10,... | collective-permute-start | bytes 393224 | tf_op jit(solution)/shard_map/ppermute | solution.py:203
  125.4 8.1 %collective-permute-start.12 = (f32[2,64,256]{2,1,0:T(8,128)S(1)}, f32[2,64,256]{2,1,0:T(8,128)S(1)}, u32[]{:S(2)}, u32[]{:S(2)}) collective-permute-start(f32[2,64,256]{2,1,0:T(8,128)S(1)} %get-tuple-element.29), channel_id=1, source_target_pairs={{0,3},{1,2},{2,1},{3,0},{4,7},{5,6},{6,5},{7,4},{8,11},{9,10},{10,... | collective-permute-start | bytes 393224 | tf_op jit(solution)/shard_map/ppermute | solution.py:203
  127.9 5.7 %collective-permute-start.13 = (f32[4,128,256]{2,1,0:T(8,128)S(1)}, f32[4,128,256]{2,1,0:T(8,128)S(1)}, u32[]{:S(2)}, u32[]{:S(2)}) collective-permute-start(f32[4,128,256]{2,1,0:T(8,128)S(1)} %bitcast.54), channel_id=1, source_target_pairs={{0,16},{16,0},{1,17},{17,1},{2,18},{18,2},{3,19},{19,3},{4,20},{20... | collective-permute-start | bytes 1572872 | tf_op jit(solution)/shard_map/ppermute | solution.py:199
  133.5 0.8 copy-start.4
  134.2 1.0 copy-start.2

commit v9 on v8

--- a/solution.py
+++ b/solution.py
@@ -16,18 +16,13 @@
 TILE = ("z_high", "z_low", "core")
 
 
-def waves():
+def tables():
     index = np.arange(S)
     angle = (index[:, None] * index[None, :] % S) * (2.0 * math.pi / S)
-    both = np.stack([np.cos(angle), np.sin(angle)]).astype(np.float32) / 16.0
-    head = both.astype(ml_dtypes.bfloat16)
-    return np.stack([head, (both - head.astype(np.float32)).astype(ml_dtypes.bfloat16)])
-
-
-def table(cosine, sine):
-    return jnp.concatenate(
-        [jnp.concatenate([cosine, sine], axis=1), jnp.concatenate([-sine, cosine], axis=1)], axis=0
-    )
+    cosine, sine = np.cos(angle) / 16.0, np.sin(angle) / 16.0
+    three = np.stack([cosine, sine - cosine, cosine + sine]).astype(np.float32)
+    head = three.astype(ml_dtypes.bfloat16)
+    return head, (three - head.astype(np.float32)).astype(ml_dtypes.bfloat16)
 
 
 def split(value):
@@ -38,16 +33,6 @@
 def product(first, second):
     dot = functools.partial(jnp.dot, preferred_element_type=jnp.float32)
     return dot(first[0], second[0]) + dot(first[0], second[1]) + dot(first[1], second[0])
-
-
-def regroup(value):
-    return jnp.concatenate(
-        [
-            jnp.concatenate([value[:S, :S], value[S:, :S]], axis=1),
-            jnp.concatenate([value[:S, S:], value[S:, S:]], axis=1),
-        ],
-        axis=0,
-    )
 
 
 def cut(block, row, column):
@@ -82,8 +67,8 @@
 
 
 def slots_kernel(
-    card, own, right, below, corner_a, corner_b, probe, roots, lh, lr,
-    top_left, top_right, bottom, keep, send, extended, total, terms, rh, rr,
+    card, own, right, below, corner_a, corner_b, probe, roots, head, rest,
+    top_left, top_right, bottom, keep, send, extended, total, terms,
 ):
     extended[:, :S, :S] = own[...]
     extended[:, :S, S:] = right[...]
@@ -91,7 +76,6 @@
     extended[:, S:, S:] = corner_a[...] + corner_b[...]
     total[...] = jnp.zeros_like(total)
     terms[...] = jnp.zeros_like(terms)
-    rh[...], rr[...] = regroup(lh[...]), regroup(lr[...])
     blank = jnp.zeros((S, S), jnp.float32)
 
     def one_slot(slot, carry):
@@ -101,34 +85,31 @@
         fine = lax.rem(column, 128)
         band_columns = pl.ds(pl.multiple_of(column - fine, 128), 384)
         patch_real, patch_imag = (cut(extended[p, band_rows, band_columns], inside, fine) for p in range(2))
-        left_table, right_table = (lh[...], lr[...]), (rh[...], rr[...])
-        RC = 256
-        wave = []
-        for m in range(2):
-            real = probe[m] * patch_real - probe[2 + m] * patch_imag
-            imag = probe[m] * patch_imag + probe[2 + m] * patch_real
-            wave.append(product(left_table, split(jnp.concatenate([real, imag], axis=0))))
-        back = [[], []]
-        for at in range(0, S, RC):
-            part = slice(at, at + RC)
-            far = [
-                jnp.concatenate([wave[m][at : at + RC], wave[m][S + at : S + at + RC]], axis=1)
-                for m in range(2)
-            ]
-            far = product(split(jnp.concatenate(far, axis=0)), right_table)
-            power = far[:RC] * far[:RC] + far[RC:] * far[RC:]
-            power = power[:, :S] + power[:, S:]
-            change = roots[slot, part] / jnp.sqrt(power + 1.0) - 1.0
-            change = jnp.concatenate([change, change], axis=0)
-            swapped = jnp.concatenate([far[:, S:] * change, far[:, :S] * change], axis=1)
-            chunk = product(split(swapped), right_table)
-            for m in range(2):
-                back[m].append(chunk[m * RC : m * RC + RC])
+
+        def down(real, imag):
+            both, second, first = (
+                product((head[k], rest[k]), split(v)) for k, v in enumerate((real + imag, imag, real))
+            )
+            return both + second, both - first
+
+        def along(real, imag):
+            both, second, first = (
+                product(split(v), (head[k], rest[k])) for k, v in enumerate((real + imag, imag, real))
+            )
+            return both + second, both - first
+
+        wave = [
+            down(probe[m] * patch_real - probe[2 + m] * patch_imag, probe[m] * patch_imag + probe[2 + m] * patch_real)
+            for m in range(2)
+        ]
+        real, imag = along(*(jnp.concatenate([wave[0][k], wave[1][k]], axis=0) for k in range(2)))
+        power = real * real + imag * imag
+        change = roots[slot] / jnp.sqrt(power[:S] + power[S:] + 1.0) - 1.0
+        change = jnp.concatenate([change, change], axis=0)
+        back = along(imag * change, real * change)
         object_real, object_imag = blank, blank
         for m in range(2):
-            whole = jnp.concatenate([c[:, :S] for c in back[m]] + [c[:, S:] for c in back[m]], axis=0)
-            chi = product(left_table, split(whole))
-            chi_imag, chi_real = chi[:S], chi[S:]
+            chi_imag, chi_real = down(back[0][m * S : m * S + S], back[1][m * S : m * S + S])
             object_real += probe[m] * chi_real + probe[2 + m] * chi_imag
             object_imag += probe[m] * chi_imag - probe[2 + m] * chi_real
             terms[m] += patch_real * chi_real + patch_imag * chi_imag
@@ -156,7 +137,7 @@
             send[chunk, plane] = terms[plane, pl.ds(other, height), :]
 
 
-def run_slots(card, blocks, probe, roots, tables, chunks):
+def run_slots(card, blocks, probe, roots, parts, chunks):
     height = S // 2 // chunks
     f32 = jnp.float32
     quarter = (QUARTERS, 3, S // QUARTERS, S)
@@ -176,12 +157,10 @@
             pltpu.VMEM((2, 2 * S, 2 * S), f32),
             pltpu.VMEM((3, 2 * S, 2 * S), f32),
             pltpu.VMEM((5, S, S), f32),
-            pltpu.VMEM((2 * S, 2 * S), jnp.bfloat16),
-            pltpu.VMEM((2 * S, 2 * S), jnp.bfloat16),
         ],
         compiler_params=pltpu.CompilerParams(vmem_limit_bytes=40 * 1024 * 1024),
         name="slots",
-    )(card, *blocks, probe, roots, *tables)
+    )(card, *blocks, probe, roots, *parts)
 
 
 def moved(block, tiles_by, bands_by):
@@ -228,13 +207,12 @@
     power = jnp.sum(probe_planes[0] ** 2 + probe_planes[1] ** 2, axis=0)
     probe = jnp.concatenate([probe_planes.reshape(4, S, S), power[None]])
     roots = jnp.sqrt(patterns[0, 0, 0])
-    parts = lax.optimization_barrier(jnp.asarray(waves()))
-    tables = (table(*parts[0]), table(*parts[1]))
-    below, card, probe, roots, tables = lax.optimization_barrier((below, card, probe, roots, tables))
+    parts = tuple(jnp.asarray(part) for part in tables())
+    below, card, probe, roots = lax.optimization_barrier((below, card, probe, roots))
     corner_a, corner_b = corners(right, below)
     top_left, top_right, bottom, keep, send = run_slots(
         card, (object_planes, right, below, corner_a, corner_b),
-        probe, roots, tables, chunks,
+        probe, roots, parts, chunks,
     )
 
     from_above = moved(bottom, 1, 0)

time: 136 us -> 137 us (level)
  blocking collectives: 40.7 us -> 32.8 us
  starting transfers between devices: 61.3 us -> 65.8 us
  Pallas kernels: 2.42 us -> 6.68 us
    all_to_all x2, blocking collectives: 40.7 us -> 32.8 us  [exchanged(): return lax.all_to_all(block, axes, 0, 0)]
    ppermute x2, starting transfers between devices: 3.83 us -> 11.1 us  [across_cores(): return lax.ppermute(block, 'core', [(0, 1), (1, 0)])]
    pallas_call x1, Pallas kernels: 2.42 us -> 6.68 us  [run_slots(): pl.pallas_call(slots_kernel, out_shape=(jax.ShapeDtypeStruct(quarter, f32...]
    ppermute x4, starting transfers between devices: 17 us -> 14.4 us  [moved(): return lax.ppermute(block, (*TILE, 'band'), route)]
    unnamed x13 -> x15, local copies, waits for them, and re-layouts: 2.69 us -> 3.34 us
where the time goes in v9:
time: 137 us; the launch traced here: 136 us
  starting transfers between devices  65.8 us (48%)
  blocking collectives  32.8 us (24%)
  waiting for transfers between devices  17.4 us (13%)
  Pallas kernels  6.68 us (5%)
  other arithmetic  5.9 us (4%)
  local copies, waits for them, and re-layouts  5.48 us (4%)
  between operations  1.69 us (1%)
    all_to_all x2, blocking collectives, exchanged(): return lax.all_to_all(block, axes, 0, 0)  32.8 us
    ppermute x6, starting transfers between devices, across_posts(): return lax.ppermute(block, 'pos', [(p, p ^ bits) for p in range(QUARTERS)])  20.8 us
    all_to_all x2, starting transfers between devices, exchanged(): return lax.all_to_all(block, axes, 0, 0)  17.6 us
    ppermute x4, starting transfers between devices, moved(): return lax.ppermute(block, (*TILE, 'band'), route)  14.4 us
    ppermute x2, starting transfers between devices, across_cores(): return lax.ppermute(block, 'core', [(0, 1), (1, 0)])  11.1 us
    ppermute x4, waiting for transfers between devices, moved(): return lax.ppermute(block, (*TILE, 'band'), route)  7.53 us
    pallas_call x1, Pallas kernels, run_slots(): pl.pallas_call(slots_kernel, out_shape=(jax.ShapeDtypeStruct(quarter, f32...  6.68 us
    ppermute x6, waiting for transfers between devices, across_posts(): return lax.ppermute(block, 'pos', [(p, p ^ bits) for p in range(QUARTERS)])  3.56 us
  transfers between devices with their start and end apart: 16, of which 5 were waited for; matrix products, arithmetic and copies ran while one was open for 5% of the time, Pallas kernels for 0%

profile of v9, /device:TPU:2, one launch (start us, length us, event | category | flops | bytes accessed | tf_op | source)
XLA Modules:
  0.0 135.8 jit_solution(11766582796377111615)
XLA Ops:
  0.6 0.0 copy-start.3
  0.6 1.4 %collective-permute-start = (f32[2,256,256]{2,1,0:T(8,128)}, f32[2,256,256]{2,1,0:T(8,128)S(1)}, u32[]{:S(2)}, u32[]{:S(2)}) collective-permute-start(f32[2,256,256]{2,1,0:T(8,128)} %own.1), channel_id=1, source_target_pairs={{16,0},{20,4},{24,8},{28,12},{32,16},{36,20},{40,24},{44,28},{48,3... | collective-permute-start | bytes 1572872 | tf_op jit(solution)/shard_map/ppermute | solution.py:174
  2.1 7.8 %collective-permute-start.1 = (f32[2,256,256]{2,1,0:T(8,128)}, f32[2,256,256]{2,1,0:T(8,128)S(1)}, u32[]{:S(2)}, u32[]{:S(2)}) collective-permute-start(f32[2,256,256]{2,1,0:T(8,128)} %own.1), channel_id=1, source_target_pairs={{4,0},{8,4},{12,8},{20,16},{24,20},{28,24},{36,32},{40,36},{44,40}... | collective-permute-start | bytes 1572872 | tf_op jit(solution)/shard_map/ppermute | solution.py:174
  9.9 0.8 copy.14
  10.7 0.1 reshape.24
  11.4 0.1 add_bitcast_fusion
  11.5 1.3 add_reduce_fusion
  12.8 0.0 copy-start.5
  12.8 0.0 copy-start
  12.8 0.0 copy-start.1
  12.8 0.0 copy-start.2
  12.9 0.1 pad_maximum_fusion.probe
  12.9 1.0 copy-done.5
  13.9 0.2 sqrt_bitcast_fusion.roots
  14.1 0.0 collective-permute-done.below
  14.1 0.7 collective-permute-start.2
  14.8 7.5 %collective-permute-done.1.right = f32[2,256,256]{2,1,0:T(8,128)S(1)} collective-permute-done((f32[2,256,256]{2,1,0:T(8,128)}, f32[2,256,256]{2,1,0:T(8,128)S(1)}, u32[]{:S(2)}, u32[]{:S(2)}) %collective-permute-start.1) | collective-permute-done | bytes 524320 | tf_op jit(solution)/shard_map/ppermute | solution.py:174
  22.4 1.3 collective-permute-start.3
  23.6 2.5 %collective-permute-done.3.corner_b = f32[2,256,256]{2,1,0:T(8,128)S(1)} collective-permute-done((f32[2,256,256]{2,1,0:T(8,128)S(1)}, f32[2,256,256]{2,1,0:T(8,128)S(1)}, u32[]{:S(2)}, u32[]{:S(2)}) %collective-permute-start.3) | collective-permute-done | bytes 524320 | tf_op jit(solution)/shard_map/ppermute | solution.py:196
  26.2 6.7 %slots.1 = (f32[4,3,64,256]{3,2,1,0:T(8,128)S(1)}, f32[4,3,64,256]{3,2,1,0:T(8,128)S(1)}, f32[2,4,3,64,256]{4,3,2,1,0:T(8,128)}, f32[16,5,8,256]{3,2,1,0:T(8,128)S(1)}, f32[16,5,8,256]{3,2,1,0:T(8,128)S(1)}) custom-call(s32[1,128]{1,0:T(1,128)S(1)} %pad.4.card, f32[2,256,256]{2,1,0:T(8,128)S(1)} %copy-done, f32[2,256,256]{2,1,0:T(8,128)S(1)} %collective-permute-done.1.right, ...), custom_call_target="tpu_custom_call" | custom-call | tf_op jit(solution)/shard_map/slots/pallas_call | solution.py:145
  32.8 2.4 %collective-permute-start.5 = (f32[2,4,3,64,256]{4,3,2,1,0:T(8,128)}, f32[2,4,3,64,256]{4,3,2,1,0:T(8,128)}, u32[]{:S(2)}, u32[]{:S(2)}) collective-permute-start(f32[2,4,3,64,256]{4,3,2,1,0:T(8,128)} %get-tuple-element.20), channel_id=1, source_target_pairs={{0,16},{4,20},{8,24},{12,28},{16,32},{20,36},{24,40},{28,44},{32,4... | collective-permute-start | bytes 4718600 | tf_op jit(solution)/shard_map/ppermute | solution.py:174
  35.3 9.1 %collective-permute-start.4 = (f32[16,5,8,256]{3,2,1,0:T(8,128)S(1)}, f32[16,5,8,256]{3,2,1,0:T(8,128)S(1)}, u32[]{:S(2)}, u32[]{:S(2)}) collective-permute-start(f32[16,5,8,256]{3,2,1,0:T(8,128)S(1)} %get-tuple-element.19), channel_id=1, source_target_pairs={{0,16},{16,0},{1,17},{17,1},{2,18},{18,2},{3,19},{19,3},{4,20},{20... | collective-permute-start | bytes 1966088 | tf_op jit(solution)/shard_map/ppermute | solution.py:178
  44.4 1.7 %collective-permute-done.4 = f32[16,5,8,256]{3,2,1,0:T(8,128)S(1)} collective-permute-done((f32[16,5,8,256]{3,2,1,0:T(8,128)S(1)}, f32[16,5,8,256]{3,2,1,0:T(8,128)S(1)}, u32[]{:S(2)}, u32[]{:S(2)}) %collective-permute-start.4) | collective-permute-done | bytes 655392 | tf_op jit(solution)/shard_map/ppermute | solution.py:178
  46.1 0.1 add.90
  46.2 20.9 %all_to_all.20 = f32[16,5,8,256]{3,2,1,0:T(8,128)S(1)} all-to-all(f32[16,5,8,256]{3,2,1,0:T(8,128)S(1)} %add.90), channel_id=1, replica_groups=mesh['z_high'=4,'z_low'=4,'core'=2,'band'=4,'pos'=4] {'band','pos'}, dimensions={0} | all-to-all | bytes 1310720 | tf_op jit(solution)/shard_map/all_to_all | solution.py:186
  67.1 2.1 %bitcast_add_fusion = f32[4,3,64,256]{3,2,1,0:T(8,128)} fusion(f32[4,3,64,256]{3,2,1,0:T(8,128)S(1)} %get-tuple-element.22, f32[2,4,3,64,256]{4,3,2,1,0:T(8,128)} %collective-permute-done.5), kind=kLoop, calls=%fused_computation.1 | loop fusion | flops 196608 | bytes 2359296 | tf_op jit(solution)/shard_map/add | solution.py:222
  69.3 2.7 %collective-permute-start.6 = (f32[4,3,64,256]{3,2,1,0:T(8,128)}, f32[4,3,64,256]{3,2,1,0:T(8,128)S(1)}, u32[]{:S(2)}, u32[]{:S(2)}) collective-permute-start(f32[4,3,64,256]{3,2,1,0:T(8,128)} %bitcast_add_fusion), channel_id=1, source_target_pairs={{0,4},{4,8},{8,12},{16,20},{20,24},{24,28},{32,36},{36,40},{40,44}... | collective-permute-start | bytes 2359304 | tf_op jit(solution)/shard_map/ppermute | solution.py:174
  72.0 11.9 %all_to_all.21 = f32[4,5,8,256]{3,2,1,0:T(8,128)S(1)} all-to-all(f32[4,5,8,256]{3,2,1,0:T(8,128)S(1)} %broadcast_in_dim.27), channel_id=1, replica_groups=mesh['z_high'=4,'z_low'=4,'core'=2,'band'=4,'pos'=4] {'z_low'}, dimensions={0} | all-to-all | bytes 327680 | tf_op jit(solution)/shard_map/all_to_all | solution.py:186
  83.9 0.7 broadcast_in_dim.28
  84.6 12.0 %all-to-all-start.2 = ((f32[4,5,8,256]{3,2,1,0:T(8,128)}), f32[4,5,8,256]{3,2,1,0:T(8,128)S(1)}, u32[]{:S(2)}, u32[]{:S(2)}) async-start(f32[4,5,8,256]{3,2,1,0:T(8,128)} %broadcast_in_dim.28), calls=%async_computation.2 | async-start | bytes 327680 | tf_op jit(solution)/shard_map/all_to_all | solution.py:186
  96.6 1.3 fusion
  98.0 2.4 %collective-permute-start.7 = (f32[3,64,256]{2,1,0:T(8,128)S(1)}, f32[3,64,256]{2,1,0:T(8,128)S(1)}, u32[]{:S(2)}, u32[]{:S(2)}) collective-permute-start(f32[3,64,256]{2,1,0:T(8,128)S(1)} %get-tuple-element.26), channel_id=1, source_target_pairs={{0,1},{1,0},{2,3},{3,2},{4,5},{5,4},{6,7},{7,6},{8,9},{9,8},{10,11... | collective-permute-start | bytes 589832 | tf_op jit(solution)/shard_map/ppermute | solution.py:182
  100.4 4.0 %collective-permute-start.8 = (f32[3,64,256]{2,1,0:T(8,128)S(1)}, f32[3,64,256]{2,1,0:T(8,128)S(1)}, u32[]{:S(2)}, u32[]{:S(2)}) collective-permute-start(f32[3,64,256]{2,1,0:T(8,128)S(1)} %get-tuple-element.28), channel_id=1, source_target_pairs={{0,2},{1,3},{2,0},{3,1},{4,6},{5,7},{6,4},{7,5},{8,10},{9,11},{10,... | collective-permute-start | bytes 589832 | tf_op jit(solution)/shard_map/ppermute | solution.py:182
  104.4 4.1 %collective-permute-start.9 = (f32[3,64,256]{2,1,0:T(8,128)S(1)}, f32[3,64,256]{2,1,0:T(8,128)S(1)}, u32[]{:S(2)}, u32[]{:S(2)}) collective-permute-start(f32[3,64,256]{2,1,0:T(8,128)S(1)} %get-tuple-element.27), channel_id=1, source_target_pairs={{0,3},{1,2},{2,1},{3,0},{4,7},{5,6},{6,5},{7,4},{8,11},{9,10},{10,... | collective-permute-start | bytes 589832 | tf_op jit(solution)/shard_map/ppermute | solution.py:182
  108.4 2.1 %all-to-all-done.2 = f32[4,5,8,256]{3,2,1,0:T(8,128)S(1)} async-done(((f32[4,5,8,256]{3,2,1,0:T(8,128)}), f32[4,5,8,256]{3,2,1,0:T(8,128)S(1)}, u32[]{:S(2)}, u32[]{:S(2)}) %all-to-all-start.2) | async-done | bytes 163872 | tf_op jit(solution)/shard_map/all_to_all | solution.py:186
  110.6 0.8 fusion.5
  111.3 0.8 broadcast_in_dim.29
  112.2 5.6 %all-to-all-start.3 = ((f32[16,4,8,256]{3,2,1,0:T(8,128)}), f32[16,4,8,256]{3,2,1,0:T(8,128)S(1)}, u32[]{:S(2)}, u32[]{:S(2)}) async-start(f32[16,4,8,256]{3,2,1,0:T(8,128)} %broadcast_in_dim.29), calls=%async_computation.3 | async-start | bytes 1048576 | tf_op jit(solution)/shard_map/all_to_all | solution.py:186
  117.8 0.1 fusion.2
  117.9 3.4 %collective-permute-start.10 = (f32[2,64,256]{2,1,0:T(8,128)S(1)}, f32[2,64,256]{2,1,0:T(8,128)S(1)}, u32[]{:S(2)}, u32[]{:S(2)}) collective-permute-start(f32[2,64,256]{2,1,0:T(8,128)S(1)} %get-tuple-element.25), channel_id=1, source_target_pairs={{0,1},{1,0},{2,3},{3,2},{4,5},{5,4},{6,7},{7,6},{8,9},{9,8},{10,11... | collective-permute-start | bytes 393224 | tf_op jit(solution)/shard_map/ppermute | solution.py:182
  121.3 4.6 %collective-permute-start.11 = (f32[2,64,256]{2,1,0:T(8,128)S(1)}, f32[2,64,256]{2,1,0:T(8,128)S(1)}, u32[]{:S(2)}, u32[]{:S(2)}) collective-permute-start(f32[2,64,256]{2,1,0:T(8,128)S(1)} %get-tuple-element.25), channel_id=1, source_target_pairs={{0,2},{1,3},{2,0},{3,1},{4,6},{5,7},{6,4},{7,5},{8,10},{9,11},{10,... | collective-permute-start | bytes 393224 | tf_op jit(solution)/shard_map/ppermute | solution.py:182
  125.9 2.5 %collective-permute-start.12 = (f32[2,64,256]{2,1,0:T(8,128)S(1)}, f32[2,64,256]{2,1,0:T(8,128)S(1)}, u32[]{:S(2)}, u32[]{:S(2)}) collective-permute-start(f32[2,64,256]{2,1,0:T(8,128)S(1)} %get-tuple-element.25), channel_id=1, source_target_pairs={{0,3},{1,2},{2,1},{3,0},{4,7},{5,6},{6,5},{7,4},{8,11},{9,10},{10,... | collective-permute-start | bytes 393224 | tf_op jit(solution)/shard_map/ppermute | solution.py:182
  128.5 1.9 %collective-permute-start.13 = (f32[4,128,256]{2,1,0:T(8,128)S(1)}, f32[4,128,256]{2,1,0:T(8,128)S(1)}, u32[]{:S(2)}, u32[]{:S(2)}) collective-permute-start(f32[4,128,256]{2,1,0:T(8,128)S(1)} %bitcast.42), channel_id=1, source_target_pairs={{0,16},{16,0},{1,17},{17,1},{2,18},{18,2},{3,19},{19,3},{4,20},{20... | collective-permute-start | bytes 1572872 | tf_op jit(solution)/shard_map/ppermute | solution.py:178
  130.5 3.5 %collective-permute-done.12 = f32[2,64,256]{2,1,0:T(8,128)S(1)} collective-permute-done((f32[2,64,256]{2,1,0:T(8,128)S(1)}, f32[2,64,256]{2,1,0:T(8,128)S(1)}, u32[]{:S(2)}, u32[]{:S(2)}) %collective-permute-start.12) | collective-permute-done | bytes 131104 | tf_op jit(solution)/shard_map/ppermute | solution.py:182
  134.0 0.0 copy-start.6
  134.0 0.1 broadcast_in_dim.26
  134.2 0.6 copy-done.6
  134.8 1.0 copy-done.4
  (31 shorter events, 0.4 us)
Async XLA Ops:
  0.6 12.2 %copy-start.3 = (f32[2,2,256,256]{3,2,1,0:T(8,128)S(1)}, f32[2,2,256,256]{3,2,1,0:T(8,128)}, u32[]{:S(2)}) copy-start(f32[2,2,256,256]{3,2,1,0:T(8,128)} %param.8) | copy-start | bytes 3145732
  0.6 13.5 %collective-permute-start = (f32[2,256,256]{2,1,0:T(8,128)}, f32[2,256,256]{2,1,0:T(8,128)S(1)}, u32[]{:S(2)}, u32[]{:S(2)}) collective-permute-start(f32[2,256,256]{2,1,0:T(8,128)} %own.1), channel_id=1, source_target_pairs={{16,0},{20,4},{24,8},{28,12},{32,16},{36,20},{40,24},{44,28},{48,3... | collective-permute-start | bytes 1572872 | tf_op jit(solution)/shard_map/ppermute | solution.py:174
  2.1 20.3 %collective-permute-start.1 = (f32[2,256,256]{2,1,0:T(8,128)}, f32[2,256,256]{2,1,0:T(8,128)S(1)}, u32[]{:S(2)}, u32[]{:S(2)}) collective-permute-start(f32[2,256,256]{2,1,0:T(8,128)} %own.1), channel_id=1, source_target_pairs={{4,0},{8,4},{12,8},{20,16},{24,20},{28,24},{36,32},{40,36},{44,40}... | collective-permute-start | bytes 1572872 | tf_op jit(solution)/shard_map/ppermute | solution.py:174
  12.8 1.1 copy-start.5
  12.8 13.3 %copy-start = (f32[2,256,256]{2,1,0:T(8,128)S(1)}, f32[2,256,256]{2,1,0:T(8,128)}, u32[]{:S(2)}) copy-start(f32[2,256,256]{2,1,0:T(8,128)} %own.1) | copy-start | bytes 1572868
  12.8 13.3 %copy-start.1 = (bf16[3,256,256]{2,1,0:T(8,128)(2,1)S(1)}, bf16[3,256,256]{2,1,0:T(8,128)(2,1)}, u32[]{:S(2)}) copy-start(bf16[3,256,256]{2,1,0:T(8,128)(2,1)} %constant.52.clone.head) | copy-start | bytes 1179652
  12.8 13.3 %copy-start.2 = (bf16[3,256,256]{2,1,0:T(8,128)(2,1)S(1)}, bf16[3,256,256]{2,1,0:T(8,128)(2,1)}, u32[]{:S(2)}) copy-start(bf16[3,256,256]{2,1,0:T(8,128)(2,1)} %constant.53.clone.rest) | copy-start | bytes 1179652
  14.1 9.5 %collective-permute-start.2 = (f32[2,256,256]{2,1,0:T(8,128)S(1)}, f32[2,256,256]{2,1,0:T(8,128)S(1)}, u32[]{:S(2)}, u32[]{:S(2)}) collective-permute-start(f32[2,256,256]{2,1,0:T(8,128)S(1)} %collective-permute-done.below), channel_id=1, source_target_pairs={{20,16},{24,20},{28,24},{52,48},{56,52},{60,56},{84,80},{88,84},{9... | collective-permute-start | bytes 1572872 | tf_op jit(solution)/shard_map/ppermute | solution.py:196
  22.4 3.8 %collective-permute-start.3 = (f32[2,256,256]{2,1,0:T(8,128)S(1)}, f32[2,256,256]{2,1,0:T(8,128)S(1)}, u32[]{:S(2)}, u32[]{:S(2)}) collective-permute-start(f32[2,256,256]{2,1,0:T(8,128)S(1)} %collective-permute-done.1.right), channel_id=1, source_target_pairs={{16,0},{17,1},{18,2},{19,3},{20,4},{21,5},{22,6},{23,7},{24,8},{25... | collective-permute-start | bytes 1572872 | tf_op jit(solution)/shard_map/ppermute | solution.py:196
  32.8 34.3 %collective-permute-start.5 = (f32[2,4,3,64,256]{4,3,2,1,0:T(8,128)}, f32[2,4,3,64,256]{4,3,2,1,0:T(8,128)}, u32[]{:S(2)}, u32[]{:S(2)}) collective-permute-start(f32[2,4,3,64,256]{4,3,2,1,0:T(8,128)} %get-tuple-element.20), channel_id=1, source_target_pairs={{0,16},{4,20},{8,24},{12,28},{16,32},{20,36},{24,40},{28,44},{32,4... | collective-permute-start | bytes 4718600 | tf_op jit(solution)/shard_map/ppermute | solution.py:174
  35.3 10.9 %collective-permute-start.4 = (f32[16,5,8,256]{3,2,1,0:T(8,128)S(1)}, f32[16,5,8,256]{3,2,1,0:T(8,128)S(1)}, u32[]{:S(2)}, u32[]{:S(2)}) collective-permute-start(f32[16,5,8,256]{3,2,1,0:T(8,128)S(1)} %get-tuple-element.19), channel_id=1, source_target_pairs={{0,16},{16,0},{1,17},{17,1},{2,18},{18,2},{3,19},{19,3},{4,20},{20... | collective-permute-start | bytes 1966088 | tf_op jit(solution)/shard_map/ppermute | solution.py:178
  69.3 27.4 %collective-permute-start.6 = (f32[4,3,64,256]{3,2,1,0:T(8,128)}, f32[4,3,64,256]{3,2,1,0:T(8,128)S(1)}, u32[]{:S(2)}, u32[]{:S(2)}) collective-permute-start(f32[4,3,64,256]{3,2,1,0:T(8,128)} %bitcast_add_fusion), channel_id=1, source_target_pairs={{0,4},{4,8},{8,12},{16,20},{20,24},{24,28},{32,36},{36,40},{40,44}... | collective-permute-start | bytes 2359304 | tf_op jit(solution)/shard_map/ppermute | solution.py:174
  84.6 25.9 %all-to-all-start.2 = ((f32[4,5,8,256]{3,2,1,0:T(8,128)}), f32[4,5,8,256]{3,2,1,0:T(8,128)S(1)}, u32[]{:S(2)}, u32[]{:S(2)}) async-start(f32[4,5,8,256]{3,2,1,0:T(8,128)} %broadcast_in_dim.28), calls=%async_computation.2 | async-start | bytes 327680 | tf_op jit(solution)/shard_map/all_to_all | solution.py:186
  98.0 19.7 %collective-permute-start.7 = (f32[3,64,256]{2,1,0:T(8,128)S(1)}, f32[3,64,256]{2,1,0:T(8,128)S(1)}, u32[]{:S(2)}, u32[]{:S(2)}) collective-permute-start(f32[3,64,256]{2,1,0:T(8,128)S(1)} %get-tuple-element.26), channel_id=1, source_target_pairs={{0,1},{1,0},{2,3},{3,2},{4,5},{5,4},{6,7},{7,6},{8,9},{9,8},{10,11... | collective-permute-start | bytes 589832 | tf_op jit(solution)/shard_map/ppermute | solution.py:182
  100.4 17.4 %collective-permute-start.8 = (f32[3,64,256]{2,1,0:T(8,128)S(1)}, f32[3,64,256]{2,1,0:T(8,128)S(1)}, u32[]{:S(2)}, u32[]{:S(2)}) collective-permute-start(f32[3,64,256]{2,1,0:T(8,128)S(1)} %get-tuple-element.28), channel_id=1, source_target_pairs={{0,2},{1,3},{2,0},{3,1},{4,6},{5,7},{6,4},{7,5},{8,10},{9,11},{10,... | collective-permute-start | bytes 589832 | tf_op jit(solution)/shard_map/ppermute | solution.py:182
  104.4 13.4 %collective-permute-start.9 = (f32[3,64,256]{2,1,0:T(8,128)S(1)}, f32[3,64,256]{2,1,0:T(8,128)S(1)}, u32[]{:S(2)}, u32[]{:S(2)}) collective-permute-start(f32[3,64,256]{2,1,0:T(8,128)S(1)} %get-tuple-element.27), channel_id=1, source_target_pairs={{0,3},{1,2},{2,1},{3,0},{4,7},{5,6},{6,5},{7,4},{8,11},{9,10},{10,... | collective-permute-start | bytes 589832 | tf_op jit(solution)/shard_map/ppermute | solution.py:182
  112.2 16.2 %all-to-all-start.3 = ((f32[16,4,8,256]{3,2,1,0:T(8,128)}), f32[16,4,8,256]{3,2,1,0:T(8,128)S(1)}, u32[]{:S(2)}, u32[]{:S(2)}) async-start(f32[16,4,8,256]{3,2,1,0:T(8,128)} %broadcast_in_dim.29), calls=%async_computation.3 | async-start | bytes 1048576 | tf_op jit(solution)/shard_map/all_to_all | solution.py:186
  117.9 12.5 %collective-permute-start.10 = (f32[2,64,256]{2,1,0:T(8,128)S(1)}, f32[2,64,256]{2,1,0:T(8,128)S(1)}, u32[]{:S(2)}, u32[]{:S(2)}) collective-permute-start(f32[2,64,256]{2,1,0:T(8,128)S(1)} %get-tuple-element.25), channel_id=1, source_target_pairs={{0,1},{1,0},{2,3},{3,2},{4,5},{5,4},{6,7},{7,6},{8,9},{9,8},{10,11... | collective-permute-start | bytes 393224 | tf_op jit(solution)/shard_map/ppermute | solution.py:182
  121.3 9.1 %collective-permute-start.11 = (f32[2,64,256]{2,1,0:T(8,128)S(1)}, f32[2,64,256]{2,1,0:T(8,128)S(1)}, u32[]{:S(2)}, u32[]{:S(2)}) collective-permute-start(f32[2,64,256]{2,1,0:T(8,128)S(1)} %get-tuple-element.25), channel_id=1, source_target_pairs={{0,2},{1,3},{2,0},{3,1},{4,6},{5,7},{6,4},{7,5},{8,10},{9,11},{10,... | collective-permute-start | bytes 393224 | tf_op jit(solution)/shard_map/ppermute | solution.py:182
  125.9 8.1 %collective-permute-start.12 = (f32[2,64,256]{2,1,0:T(8,128)S(1)}, f32[2,64,256]{2,1,0:T(8,128)S(1)}, u32[]{:S(2)}, u32[]{:S(2)}) collective-permute-start(f32[2,64,256]{2,1,0:T(8,128)S(1)} %get-tuple-element.25), channel_id=1, source_target_pairs={{0,3},{1,2},{2,1},{3,0},{4,7},{5,6},{6,5},{7,4},{8,11},{9,10},{10,... | collective-permute-start | bytes 393224 | tf_op jit(solution)/shard_map/ppermute | solution.py:182
  128.5 5.7 %collective-permute-start.13 = (f32[4,128,256]{2,1,0:T(8,128)S(1)}, f32[4,128,256]{2,1,0:T(8,128)S(1)}, u32[]{:S(2)}, u32[]{:S(2)}) collective-permute-start(f32[4,128,256]{2,1,0:T(8,128)S(1)} %bitcast.42), channel_id=1, source_target_pairs={{0,16},{16,0},{1,17},{17,1},{2,18},{18,2},{3,19},{19,3},{4,20},{20... | collective-permute-start | bytes 1572872 | tf_op jit(solution)/shard_map/ppermute | solution.py:178
  134.0 0.8 copy-start.6
  134.8 1.0 copy-start.4

commit v10 on v9

--- a/solution.py
+++ b/solution.py
@@ -12,6 +12,7 @@
 
 S = 256
 QUARTERS = 4
+PARTNERS = (0, 1, 3, 2)
 COUNT = 6
 TILE = ("z_high", "z_low", "core")
 
@@ -222,8 +223,8 @@
     from_left = moved(top_right + from_above[1], 0, 1)
     terms = jnp.sum(shared(terms, "z_low"), axis=0)
     tile_sum = top_left + from_above[0] + from_left
-    pieces = [lax.dynamic_index_in_dim(tile_sum, post ^ k, 0, keepdims=False) for k in range(QUARTERS)]
-    pieces = [pieces[0], *(across_posts(pieces[k], k) for k in range(1, QUARTERS))]
+    pieces = [lax.dynamic_index_in_dim(tile_sum, post ^ k, 0, keepdims=False) for k in PARTNERS]
+    pieces = [pieces[0], *(across_posts(piece, k) for piece, k in zip(pieces[1:], PARTNERS[1:]))]
     terms = jnp.sum(shared(terms, "z_high"), axis=0)
 
     rows = S // QUARTERS
@@ -231,7 +232,7 @@
     pieces = sum(pieces[1:], pieces[0])
     own_rows = own_rows + pieces[:2] / (pieces[2] + 1.0)
     object_new = jnp.zeros_like(object_planes)
-    for k in range(QUARTERS):
+    for k in PARTNERS:
         piece = across_posts(own_rows, k) if k else own_rows
         object_new = lax.dynamic_update_slice_in_dim(object_new, piece, (post ^ k) * rows, 1)
 

time: 137 us -> 136 us (level)
  Pallas kernels: 6.68 us -> 2.37 us
  starting transfers between devices: 65.8 us -> 68.6 us
    ppermute x4, starting transfers between devices: 14.4 us -> 25.6 us  [moved(): return lax.ppermute(block, (*TILE, 'band'), route)]
    ppermute x2, starting transfers between devices: 11.1 us -> 3.83 us  [across_cores(): return lax.ppermute(block, 'core', [(0, 1), (1, 0)])]
    pallas_call x1, Pallas kernels: 6.68 us -> 2.37 us  [run_slots(): pl.pallas_call(slots_kernel, out_shape=(jax.ShapeDtypeStruct(quarter, f32...]
where the time goes in v10:
time: 136 us; the launch traced here: 135 us
  starting transfers between devices  68.6 us (50%)
  blocking collectives  32.7 us (24%)
  waiting for transfers between devices  18.6 us (14%)
  other arithmetic  5.9 us (4%)
  local copies, waits for them, and re-layouts  5.48 us (4%)
  Pallas kernels  2.37 us (2%)
  between operations  1.69 us (1%)
    all_to_all x2, blocking collectives, exchanged(): return lax.all_to_all(block, axes, 0, 0)  32.7 us
    ppermute x4, starting transfers between devices, moved(): return lax.ppermute(block, (*TILE, 'band'), route)  25.6 us
    ppermute x6, starting transfers between devices, across_posts(): return lax.ppermute(block, 'pos', [(p, p ^ bits) for p in range(QUARTERS)])  19.7 us
    all_to_all x2, starting transfers between devices, exchanged(): return lax.all_to_all(block, axes, 0, 0)  17.5 us
    ppermute x4, waiting for transfers between devices, moved(): return lax.ppermute(block, (*TILE, 'band'), route)  7.53 us
    ppermute x2, starting transfers between devices, across_cores(): return lax.ppermute(block, 'core', [(0, 1), (1, 0)])  3.83 us
    ppermute x6, waiting for transfers between devices, across_posts(): return lax.ppermute(block, 'pos', [(p, p ^ bits) for p in range(QUARTERS)])  3.79 us
    unnamed x15, local copies, waits for them, and re-layouts  3.34 us
  transfers between devices with their start and end apart: 16, of which 5 were waited for; matrix products, arithmetic and copies ran while one was open for 5% of the time, Pallas kernels for 0%

profile of v10, /device:TPU:2, one launch (start us, length us, event | category | flops | bytes accessed | tf_op | source)
XLA Modules:
  0.0 135.3 jit_solution(8898297218046066969)
XLA Ops:
  0.6 0.0 copy-start.3
  0.6 1.4 %collective-permute-start = (f32[2,256,256]{2,1,0:T(8,128)}, f32[2,256,256]{2,1,0:T(8,128)S(1)}, u32[]{:S(2)}, u32[]{:S(2)}) collective-permute-start(f32[2,256,256]{2,1,0:T(8,128)} %own.1), channel_id=1, source_target_pairs={{16,0},{20,4},{24,8},{28,12},{32,16},{36,20},{40,24},{44,28},{48,3... | collective-permute-start | bytes 1572872 | tf_op jit(solution)/shard_map/ppermute | solution.py:175
  2.1 7.8 %collective-permute-start.1 = (f32[2,256,256]{2,1,0:T(8,128)}, f32[2,256,256]{2,1,0:T(8,128)S(1)}, u32[]{:S(2)}, u32[]{:S(2)}) collective-permute-start(f32[2,256,256]{2,1,0:T(8,128)} %own.1), channel_id=1, source_target_pairs={{4,0},{8,4},{12,8},{20,16},{24,20},{28,24},{36,32},{40,36},{44,40}... | collective-permute-start | bytes 1572872 | tf_op jit(solution)/shard_map/ppermute | solution.py:175
  9.9 0.8 copy.14
  10.7 0.1 reshape.24
  11.4 0.1 add_bitcast_fusion
  11.5 1.3 add_reduce_fusion
  12.8 0.0 copy-start.5
  12.8 0.0 copy-start
  12.8 0.0 copy-start.1
  12.8 0.0 copy-start.2
  12.9 0.1 pad_maximum_fusion.probe
  12.9 1.0 copy-done.5
  13.9 0.2 sqrt_bitcast_fusion.roots
  14.1 0.7 collective-permute-start.2
  14.8 7.5 %collective-permute-done.1.right = f32[2,256,256]{2,1,0:T(8,128)S(1)} collective-permute-done((f32[2,256,256]{2,1,0:T(8,128)}, f32[2,256,256]{2,1,0:T(8,128)S(1)}, u32[]{:S(2)}, u32[]{:S(2)}) %collective-permute-start.1) | collective-permute-done | bytes 524320 | tf_op jit(solution)/shard_map/ppermute | solution.py:175
  22.4 1.3 collective-permute-start.3
  23.6 2.5 %collective-permute-done.3.corner_b = f32[2,256,256]{2,1,0:T(8,128)S(1)} collective-permute-done((f32[2,256,256]{2,1,0:T(8,128)S(1)}, f32[2,256,256]{2,1,0:T(8,128)S(1)}, u32[]{:S(2)}, u32[]{:S(2)}) %collective-permute-start.3) | collective-permute-done | bytes 524320 | tf_op jit(solution)/shard_map/ppermute | solution.py:197
  26.2 2.4 %slots.1 = (f32[4,3,64,256]{3,2,1,0:T(8,128)S(1)}, f32[4,3,64,256]{3,2,1,0:T(8,128)S(1)}, f32[2,4,3,64,256]{4,3,2,1,0:T(8,128)}, f32[16,5,8,256]{3,2,1,0:T(8,128)S(1)}, f32[16,5,8,256]{3,2,1,0:T(8,128)S(1)}) custom-call(s32[1,128]{1,0:T(1,128)S(1)} %pad.4.card, f32[2,256,256]{2,1,0:T(8,128)S(1)} %copy-done, f32[2,256,256]{2,1,0:T(8,128)S(1)} %collective-permute-done.1.right, ...), custom_call_target="tpu_custom_call" | custom-call | tf_op jit(solution)/shard_map/slots/pallas_call | solution.py:146
  28.5 13.7 %collective-permute-start.5 = (f32[2,4,3,64,256]{4,3,2,1,0:T(8,128)}, f32[2,4,3,64,256]{4,3,2,1,0:T(8,128)}, u32[]{:S(2)}, u32[]{:S(2)}) collective-permute-start(f32[2,4,3,64,256]{4,3,2,1,0:T(8,128)} %get-tuple-element.20), channel_id=1, source_target_pairs={{0,16},{4,20},{8,24},{12,28},{16,32},{20,36},{24,40},{28,44},{32,4... | collective-permute-start | bytes 4718600 | tf_op jit(solution)/shard_map/ppermute | solution.py:175
  42.2 1.9 %collective-permute-start.4 = (f32[16,5,8,256]{3,2,1,0:T(8,128)S(1)}, f32[16,5,8,256]{3,2,1,0:T(8,128)S(1)}, u32[]{:S(2)}, u32[]{:S(2)}) collective-permute-start(f32[16,5,8,256]{3,2,1,0:T(8,128)S(1)} %get-tuple-element.19), channel_id=1, source_target_pairs={{0,16},{16,0},{1,17},{17,1},{2,18},{18,2},{3,19},{19,3},{4,20},{20... | collective-permute-start | bytes 1966088 | tf_op jit(solution)/shard_map/ppermute | solution.py:179
  44.1 2.1 %collective-permute-done.4 = f32[16,5,8,256]{3,2,1,0:T(8,128)S(1)} collective-permute-done((f32[16,5,8,256]{3,2,1,0:T(8,128)S(1)}, f32[16,5,8,256]{3,2,1,0:T(8,128)S(1)}, u32[]{:S(2)}, u32[]{:S(2)}) %collective-permute-start.4) | collective-permute-done | bytes 655392 | tf_op jit(solution)/shard_map/ppermute | solution.py:179
  46.2 0.1 add.90
  46.2 19.1 %all_to_all.20 = f32[16,5,8,256]{3,2,1,0:T(8,128)S(1)} all-to-all(f32[16,5,8,256]{3,2,1,0:T(8,128)S(1)} %add.90), channel_id=1, replica_groups=mesh['z_high'=4,'z_low'=4,'core'=2,'band'=4,'pos'=4] {'band','pos'}, dimensions={0} | all-to-all | bytes 1310720 | tf_op jit(solution)/shard_map/all_to_all | solution.py:187
  65.4 0.0 collective-permute-done.5
  65.4 2.1 %bitcast_add_fusion = f32[4,3,64,256]{3,2,1,0:T(8,128)} fusion(f32[4,3,64,256]{3,2,1,0:T(8,128)S(1)} %get-tuple-element.22, f32[2,4,3,64,256]{4,3,2,1,0:T(8,128)} %collective-permute-done.5), kind=kLoop, calls=%fused_computation.1 | loop fusion | flops 196608 | bytes 2359296 | tf_op jit(solution)/shard_map/add | solution.py:223
  67.5 2.7 %collective-permute-start.6 = (f32[4,3,64,256]{3,2,1,0:T(8,128)}, f32[4,3,64,256]{3,2,1,0:T(8,128)S(1)}, u32[]{:S(2)}, u32[]{:S(2)}) collective-permute-start(f32[4,3,64,256]{3,2,1,0:T(8,128)} %bitcast_add_fusion), channel_id=1, source_target_pairs={{0,4},{4,8},{8,12},{16,20},{20,24},{24,28},{32,36},{36,40},{40,44}... | collective-permute-start | bytes 2359304 | tf_op jit(solution)/shard_map/ppermute | solution.py:175
  70.3 13.6 %all_to_all.21 = f32[4,5,8,256]{3,2,1,0:T(8,128)S(1)} all-to-all(f32[4,5,8,256]{3,2,1,0:T(8,128)S(1)} %broadcast_in_dim.27), channel_id=1, replica_groups=mesh['z_high'=4,'z_low'=4,'core'=2,'band'=4,'pos'=4] {'z_low'}, dimensions={0} | all-to-all | bytes 327680 | tf_op jit(solution)/shard_map/all_to_all | solution.py:187
  83.9 0.7 broadcast_in_dim.28
  84.6 11.9 %all-to-all-start.2 = ((f32[4,5,8,256]{3,2,1,0:T(8,128)}), f32[4,5,8,256]{3,2,1,0:T(8,128)S(1)}, u32[]{:S(2)}, u32[]{:S(2)}) async-start(f32[4,5,8,256]{3,2,1,0:T(8,128)} %broadcast_in_dim.28), calls=%async_computation.2 | async-start | bytes 327680 | tf_op jit(solution)/shard_map/all_to_all | solution.py:187
  96.5 1.3 fusion
  97.8 2.4 %collective-permute-start.7 = (f32[3,64,256]{2,1,0:T(8,128)S(1)}, f32[3,64,256]{2,1,0:T(8,128)S(1)}, u32[]{:S(2)}, u32[]{:S(2)}) collective-permute-start(f32[3,64,256]{2,1,0:T(8,128)S(1)} %get-tuple-element.26), channel_id=1, source_target_pairs={{0,1},{1,0},{2,3},{3,2},{4,5},{5,4},{6,7},{7,6},{8,9},{9,8},{10,11... | collective-permute-start | bytes 589832 | tf_op jit(solution)/shard_map/ppermute | solution.py:183
  100.2 3.4 %collective-permute-start.8 = (f32[3,64,256]{2,1,0:T(8,128)S(1)}, f32[3,64,256]{2,1,0:T(8,128)S(1)}, u32[]{:S(2)}, u32[]{:S(2)}) collective-permute-start(f32[3,64,256]{2,1,0:T(8,128)S(1)} %get-tuple-element.28), channel_id=1, source_target_pairs={{0,3},{1,2},{2,1},{3,0},{4,7},{5,6},{6,5},{7,4},{8,11},{9,10},{10,... | collective-permute-start | bytes 589832 | tf_op jit(solution)/shard_map/ppermute | solution.py:183
  103.7 4.0 %collective-permute-start.9 = (f32[3,64,256]{2,1,0:T(8,128)S(1)}, f32[3,64,256]{2,1,0:T(8,128)S(1)}, u32[]{:S(2)}, u32[]{:S(2)}) collective-permute-start(f32[3,64,256]{2,1,0:T(8,128)S(1)} %get-tuple-element.27), channel_id=1, source_target_pairs={{0,2},{1,3},{2,0},{3,1},{4,6},{5,7},{6,4},{7,5},{8,10},{9,11},{10,... | collective-permute-start | bytes 589832 | tf_op jit(solution)/shard_map/ppermute | solution.py:183
  107.7 2.7 %all-to-all-done.2 = f32[4,5,8,256]{3,2,1,0:T(8,128)S(1)} async-done(((f32[4,5,8,256]{3,2,1,0:T(8,128)}), f32[4,5,8,256]{3,2,1,0:T(8,128)S(1)}, u32[]{:S(2)}, u32[]{:S(2)}) %all-to-all-start.2) | async-done | bytes 163872 | tf_op jit(solution)/shard_map/all_to_all | solution.py:187
  110.4 0.8 fusion.5
  111.2 0.8 broadcast_in_dim.29
  112.0 5.6 %all-to-all-start.3 = ((f32[16,4,8,256]{3,2,1,0:T(8,128)}), f32[16,4,8,256]{3,2,1,0:T(8,128)S(1)}, u32[]{:S(2)}, u32[]{:S(2)}) async-start(f32[16,4,8,256]{3,2,1,0:T(8,128)} %broadcast_in_dim.29), calls=%async_computation.3 | async-start | bytes 1048576 | tf_op jit(solution)/shard_map/all_to_all | solution.py:187
  117.6 0.1 fusion.2
  117.8 3.4 %collective-permute-start.10 = (f32[2,64,256]{2,1,0:T(8,128)S(1)}, f32[2,64,256]{2,1,0:T(8,128)S(1)}, u32[]{:S(2)}, u32[]{:S(2)}) collective-permute-start(f32[2,64,256]{2,1,0:T(8,128)S(1)} %get-tuple-element.25), channel_id=1, source_target_pairs={{0,1},{1,0},{2,3},{3,2},{4,5},{5,4},{6,7},{7,6},{8,9},{9,8},{10,11... | collective-permute-start | bytes 393224 | tf_op jit(solution)/shard_map/ppermute | solution.py:183
  121.1 4.0 %collective-permute-start.11 = (f32[2,64,256]{2,1,0:T(8,128)S(1)}, f32[2,64,256]{2,1,0:T(8,128)S(1)}, u32[]{:S(2)}, u32[]{:S(2)}) collective-permute-start(f32[2,64,256]{2,1,0:T(8,128)S(1)} %get-tuple-element.25), channel_id=1, source_target_pairs={{0,3},{1,2},{2,1},{3,0},{4,7},{5,6},{6,5},{7,4},{8,11},{9,10},{10,... | collective-permute-start | bytes 393224 | tf_op jit(solution)/shard_map/ppermute | solution.py:183
  125.1 2.5 %collective-permute-start.12 = (f32[2,64,256]{2,1,0:T(8,128)S(1)}, f32[2,64,256]{2,1,0:T(8,128)S(1)}, u32[]{:S(2)}, u32[]{:S(2)}) collective-permute-start(f32[2,64,256]{2,1,0:T(8,128)S(1)} %get-tuple-element.25), channel_id=1, source_target_pairs={{0,2},{1,3},{2,0},{3,1},{4,6},{5,7},{6,4},{7,5},{8,10},{9,11},{10,... | collective-permute-start | bytes 393224 | tf_op jit(solution)/shard_map/ppermute | solution.py:183
  127.7 1.9 %collective-permute-start.13 = (f32[4,128,256]{2,1,0:T(8,128)S(1)}, f32[4,128,256]{2,1,0:T(8,128)S(1)}, u32[]{:S(2)}, u32[]{:S(2)}) collective-permute-start(f32[4,128,256]{2,1,0:T(8,128)S(1)} %bitcast.42), channel_id=1, source_target_pairs={{0,16},{16,0},{1,17},{17,1},{2,18},{18,2},{3,19},{19,3},{4,20},{20... | collective-permute-start | bytes 1572872 | tf_op jit(solution)/shard_map/ppermute | solution.py:179
  129.7 3.8 %collective-permute-done.12 = f32[2,64,256]{2,1,0:T(8,128)S(1)} collective-permute-done((f32[2,64,256]{2,1,0:T(8,128)S(1)}, f32[2,64,256]{2,1,0:T(8,128)S(1)}, u32[]{:S(2)}, u32[]{:S(2)}) %collective-permute-start.12) | collective-permute-done | bytes 131104 | tf_op jit(solution)/shard_map/ppermute | solution.py:183
  133.5 0.0 copy-start.6
  133.5 0.1 broadcast_in_dim.26
  133.7 0.6 copy-done.6
  134.3 1.0 copy-done.4
  (31 shorter events, 0.4 us)
Async XLA Ops:
  0.6 12.2 %copy-start.3 = (f32[2,2,256,256]{3,2,1,0:T(8,128)S(1)}, f32[2,2,256,256]{3,2,1,0:T(8,128)}, u32[]{:S(2)}) copy-start(f32[2,2,256,256]{3,2,1,0:T(8,128)} %param.8) | copy-start | bytes 3145732
  0.6 13.5 %collective-permute-start = (f32[2,256,256]{2,1,0:T(8,128)}, f32[2,256,256]{2,1,0:T(8,128)S(1)}, u32[]{:S(2)}, u32[]{:S(2)}) collective-permute-start(f32[2,256,256]{2,1,0:T(8,128)} %own.1), channel_id=1, source_target_pairs={{16,0},{20,4},{24,8},{28,12},{32,16},{36,20},{40,24},{44,28},{48,3... | collective-permute-start | bytes 1572872 | tf_op jit(solution)/shard_map/ppermute | solution.py:175
  2.1 20.3 %collective-permute-start.1 = (f32[2,256,256]{2,1,0:T(8,128)}, f32[2,256,256]{2,1,0:T(8,128)S(1)}, u32[]{:S(2)}, u32[]{:S(2)}) collective-permute-start(f32[2,256,256]{2,1,0:T(8,128)} %own.1), channel_id=1, source_target_pairs={{4,0},{8,4},{12,8},{20,16},{24,20},{28,24},{36,32},{40,36},{44,40}... | collective-permute-start | bytes 1572872 | tf_op jit(solution)/shard_map/ppermute | solution.py:175
  12.8 1.1 copy-start.5
  12.8 13.3 %copy-start = (f32[2,256,256]{2,1,0:T(8,128)S(1)}, f32[2,256,256]{2,1,0:T(8,128)}, u32[]{:S(2)}) copy-start(f32[2,256,256]{2,1,0:T(8,128)} %own.1) | copy-start | bytes 1572868
  12.8 13.3 %copy-start.1 = (bf16[3,256,256]{2,1,0:T(8,128)(2,1)S(1)}, bf16[3,256,256]{2,1,0:T(8,128)(2,1)}, u32[]{:S(2)}) copy-start(bf16[3,256,256]{2,1,0:T(8,128)(2,1)} %constant.52.clone.head) | copy-start | bytes 1179652
  12.8 13.3 %copy-start.2 = (bf16[3,256,256]{2,1,0:T(8,128)(2,1)S(1)}, bf16[3,256,256]{2,1,0:T(8,128)(2,1)}, u32[]{:S(2)}) copy-start(bf16[3,256,256]{2,1,0:T(8,128)(2,1)} %constant.53.clone.rest) | copy-start | bytes 1179652
  14.1 9.5 %collective-permute-start.2 = (f32[2,256,256]{2,1,0:T(8,128)S(1)}, f32[2,256,256]{2,1,0:T(8,128)S(1)}, u32[]{:S(2)}, u32[]{:S(2)}) collective-permute-start(f32[2,256,256]{2,1,0:T(8,128)S(1)} %collective-permute-done.below), channel_id=1, source_target_pairs={{20,16},{24,20},{28,24},{52,48},{56,52},{60,56},{84,80},{88,84},{9... | collective-permute-start | bytes 1572872 | tf_op jit(solution)/shard_map/ppermute | solution.py:197
  22.4 3.8 %collective-permute-start.3 = (f32[2,256,256]{2,1,0:T(8,128)S(1)}, f32[2,256,256]{2,1,0:T(8,128)S(1)}, u32[]{:S(2)}, u32[]{:S(2)}) collective-permute-start(f32[2,256,256]{2,1,0:T(8,128)S(1)} %collective-permute-done.1.right), channel_id=1, source_target_pairs={{16,0},{17,1},{18,2},{19,3},{20,4},{21,5},{22,6},{23,7},{24,8},{25... | collective-permute-start | bytes 1572872 | tf_op jit(solution)/shard_map/ppermute | solution.py:197
  28.5 36.9 %collective-permute-start.5 = (f32[2,4,3,64,256]{4,3,2,1,0:T(8,128)}, f32[2,4,3,64,256]{4,3,2,1,0:T(8,128)}, u32[]{:S(2)}, u32[]{:S(2)}) collective-permute-start(f32[2,4,3,64,256]{4,3,2,1,0:T(8,128)} %get-tuple-element.20), channel_id=1, source_target_pairs={{0,16},{4,20},{8,24},{12,28},{16,32},{20,36},{24,40},{28,44},{32,4... | collective-permute-start | bytes 4718600 | tf_op jit(solution)/shard_map/ppermute | solution.py:175
  42.2 4.0 %collective-permute-start.4 = (f32[16,5,8,256]{3,2,1,0:T(8,128)S(1)}, f32[16,5,8,256]{3,2,1,0:T(8,128)S(1)}, u32[]{:S(2)}, u32[]{:S(2)}) collective-permute-start(f32[16,5,8,256]{3,2,1,0:T(8,128)S(1)} %get-tuple-element.19), channel_id=1, source_target_pairs={{0,16},{16,0},{1,17},{17,1},{2,18},{18,2},{3,19},{19,3},{4,20},{20... | collective-permute-start | bytes 1966088 | tf_op jit(solution)/shard_map/ppermute | solution.py:179
  67.5 28.9 %collective-permute-start.6 = (f32[4,3,64,256]{3,2,1,0:T(8,128)}, f32[4,3,64,256]{3,2,1,0:T(8,128)S(1)}, u32[]{:S(2)}, u32[]{:S(2)}) collective-permute-start(f32[4,3,64,256]{3,2,1,0:T(8,128)} %bitcast_add_fusion), channel_id=1, source_target_pairs={{0,4},{4,8},{8,12},{16,20},{20,24},{24,28},{32,36},{36,40},{40,44}... | collective-permute-start | bytes 2359304 | tf_op jit(solution)/shard_map/ppermute | solution.py:175
  84.6 25.8 %all-to-all-start.2 = ((f32[4,5,8,256]{3,2,1,0:T(8,128)}), f32[4,5,8,256]{3,2,1,0:T(8,128)S(1)}, u32[]{:S(2)}, u32[]{:S(2)}) async-start(f32[4,5,8,256]{3,2,1,0:T(8,128)} %broadcast_in_dim.28), calls=%async_computation.2 | async-start | bytes 327680 | tf_op jit(solution)/shard_map/all_to_all | solution.py:187
  97.8 19.7 %collective-permute-start.7 = (f32[3,64,256]{2,1,0:T(8,128)S(1)}, f32[3,64,256]{2,1,0:T(8,128)S(1)}, u32[]{:S(2)}, u32[]{:S(2)}) collective-permute-start(f32[3,64,256]{2,1,0:T(8,128)S(1)} %get-tuple-element.26), channel_id=1, source_target_pairs={{0,1},{1,0},{2,3},{3,2},{4,5},{5,4},{6,7},{7,6},{8,9},{9,8},{10,11... | collective-permute-start | bytes 589832 | tf_op jit(solution)/shard_map/ppermute | solution.py:183
  100.2 17.4 %collective-permute-start.8 = (f32[3,64,256]{2,1,0:T(8,128)S(1)}, f32[3,64,256]{2,1,0:T(8,128)S(1)}, u32[]{:S(2)}, u32[]{:S(2)}) collective-permute-start(f32[3,64,256]{2,1,0:T(8,128)S(1)} %get-tuple-element.28), channel_id=1, source_target_pairs={{0,3},{1,2},{2,1},{3,0},{4,7},{5,6},{6,5},{7,4},{8,11},{9,10},{10,... | collective-permute-start | bytes 589832 | tf_op jit(solution)/shard_map/ppermute | solution.py:183
  103.7 13.9 %collective-permute-start.9 = (f32[3,64,256]{2,1,0:T(8,128)S(1)}, f32[3,64,256]{2,1,0:T(8,128)S(1)}, u32[]{:S(2)}, u32[]{:S(2)}) collective-permute-start(f32[3,64,256]{2,1,0:T(8,128)S(1)} %get-tuple-element.27), channel_id=1, source_target_pairs={{0,2},{1,3},{2,0},{3,1},{4,6},{5,7},{6,4},{7,5},{8,10},{9,11},{10,... | collective-permute-start | bytes 589832 | tf_op jit(solution)/shard_map/ppermute | solution.py:183
  112.0 15.7 %all-to-all-start.3 = ((f32[16,4,8,256]{3,2,1,0:T(8,128)}), f32[16,4,8,256]{3,2,1,0:T(8,128)S(1)}, u32[]{:S(2)}, u32[]{:S(2)}) async-start(f32[16,4,8,256]{3,2,1,0:T(8,128)} %broadcast_in_dim.29), calls=%async_computation.3 | async-start | bytes 1048576 | tf_op jit(solution)/shard_map/all_to_all | solution.py:187
  117.8 11.9 %collective-permute-start.10 = (f32[2,64,256]{2,1,0:T(8,128)S(1)}, f32[2,64,256]{2,1,0:T(8,128)S(1)}, u32[]{:S(2)}, u32[]{:S(2)}) collective-permute-start(f32[2,64,256]{2,1,0:T(8,128)S(1)} %get-tuple-element.25), channel_id=1, source_target_pairs={{0,1},{1,0},{2,3},{3,2},{4,5},{5,4},{6,7},{7,6},{8,9},{9,8},{10,11... | collective-permute-start | bytes 393224 | tf_op jit(solution)/shard_map/ppermute | solution.py:183
  121.1 8.6 %collective-permute-start.11 = (f32[2,64,256]{2,1,0:T(8,128)S(1)}, f32[2,64,256]{2,1,0:T(8,128)S(1)}, u32[]{:S(2)}, u32[]{:S(2)}) collective-permute-start(f32[2,64,256]{2,1,0:T(8,128)S(1)} %get-tuple-element.25), channel_id=1, source_target_pairs={{0,3},{1,2},{2,1},{3,0},{4,7},{5,6},{6,5},{7,4},{8,11},{9,10},{10,... | collective-permute-start | bytes 393224 | tf_op jit(solution)/shard_map/ppermute | solution.py:183
  125.1 8.4 %collective-permute-start.12 = (f32[2,64,256]{2,1,0:T(8,128)S(1)}, f32[2,64,256]{2,1,0:T(8,128)S(1)}, u32[]{:S(2)}, u32[]{:S(2)}) collective-permute-start(f32[2,64,256]{2,1,0:T(8,128)S(1)} %get-tuple-element.25), channel_id=1, source_target_pairs={{0,2},{1,3},{2,0},{3,1},{4,6},{5,7},{6,4},{7,5},{8,10},{9,11},{10,... | collective-permute-start | bytes 393224 | tf_op jit(solution)/shard_map/ppermute | solution.py:183
  127.7 5.9 %collective-permute-start.13 = (f32[4,128,256]{2,1,0:T(8,128)S(1)}, f32[4,128,256]{2,1,0:T(8,128)S(1)}, u32[]{:S(2)}, u32[]{:S(2)}) collective-permute-start(f32[4,128,256]{2,1,0:T(8,128)S(1)} %bitcast.42), channel_id=1, source_target_pairs={{0,16},{16,0},{1,17},{17,1},{2,18},{18,2},{3,19},{19,3},{4,20},{20... | collective-permute-start | bytes 1572872 | tf_op jit(solution)/shard_map/ppermute | solution.py:179
  133.5 0.8 copy-start.6
  134.3 1.0 copy-start.4

commit v11 on v10

--- a/solution.py
+++ b/solution.py
@@ -231,10 +231,7 @@
     own_rows = lax.dynamic_slice_in_dim(object_planes, post * rows, rows, 1)
     pieces = sum(pieces[1:], pieces[0])
     own_rows = own_rows + pieces[:2] / (pieces[2] + 1.0)
-    object_new = jnp.zeros_like(object_planes)
-    for k in PARTNERS:
-        piece = across_posts(own_rows, k) if k else own_rows
-        object_new = lax.dynamic_update_slice_in_dim(object_new, piece, (post ^ k) * rows, 1)
+    gathered = [own_rows, *(across_posts(own_rows, k) for k in PARTNERS[1:])]
 
     height = S // 2 // chunks
     place = core * (S // 2) + (band * posts + post) * height
@@ -244,6 +241,10 @@
     probe_new = jnp.zeros((4, S, S), jnp.float32)
     for half, at in ((mine, core), (across_cores(mine), 1 - core)):
         probe_new = lax.dynamic_update_slice_in_dim(probe_new, half, at * (S // 2), 1)
+    gathered[-1] = lax.optimization_barrier((gathered[-1], probe_new))[0]
+    object_new = jnp.zeros_like(object_planes)
+    for piece, k in zip(gathered, PARTNERS):
+        object_new = lax.dynamic_update_slice_in_dim(object_new, piece, (post ^ k) * rows, 1)
     return (object_new, probe_new.reshape(probe_planes.shape))
 
 

time: 136 us -> 143 us (1.051)
  the two profiles are of different devices: /device:TPU:2 before, /device:TPU:1 now
where the time goes in v11:
time: 143 us; the launch traced here: 142 us
  starting transfers between devices  65.8 us (46%)
  blocking collectives  27.6 us (19%)
  waiting for transfers between devices  25.5 us (18%)
  Pallas kernels  11 us (8%)
  other arithmetic  5.9 us (4%)
  local copies, waits for them, and re-layouts  4.7 us (3%)
  between operations  1.7 us (1%)
    all_to_all x2, blocking collectives, exchanged(): return lax.all_to_all(block, axes, 0, 0)  27.6 us
    ppermute x6, starting transfers between devices, across_posts(): return lax.ppermute(block, 'pos', [(p, p ^ bits) for p in range(QUARTERS)])  18.1 us
    all_to_all x2, starting transfers between devices, exchanged(): return lax.all_to_all(block, axes, 0, 0)  16.3 us
    ppermute x4, starting transfers between devices, moved(): return lax.ppermute(block, (*TILE, 'band'), route)  13.9 us
    ppermute x2, starting transfers between devices, across_cores(): return lax.ppermute(block, 'core', [(0, 1), (1, 0)])  13.8 us
    pallas_call x1, Pallas kernels, run_slots(): pl.pallas_call(slots_kernel, out_shape=(jax.ShapeDtypeStruct(quarter, f32...  11 us
    ppermute x4, waiting for transfers between devices, moved(): return lax.ppermute(block, (*TILE, 'band'), route)  8.91 us
    all_to_all x2, waiting for transfers between devices, exchanged(): return lax.all_to_all(block, axes, 0, 0)  7.44 us
  transfers between devices with their start and end apart: 16, of which 7 were waited for; matrix products, arithmetic and copies ran while one was open for 5% of the time, Pallas kernels for 0%

profile of v11, /device:TPU:1, one launch (start us, length us, event | category | flops | bytes accessed | tf_op | source)
XLA Modules:
  0.0 142.2 jit_solution(13209640992078132786)
XLA Ops:
  0.6 0.0 copy-start.3
  0.6 8.9 %collective-permute-start = (f32[2,256,256]{2,1,0:T(8,128)}, f32[2,256,256]{2,1,0:T(8,128)S(1)}, u32[]{:S(2)}, u32[]{:S(2)}) collective-permute-start(f32[2,256,256]{2,1,0:T(8,128)} %own.1), channel_id=1, source_target_pairs={{16,0},{20,4},{24,8},{28,12},{32,16},{36,20},{40,24},{44,28},{48,3... | collective-permute-start | bytes 1572872 | tf_op jit(solution)/shard_map/ppermute | solution.py:175
  9.6 1.3 collective-permute-start.1
  10.9 0.8 copy.14
  11.6 0.1 reshape.24
  12.4 0.1 add_bitcast_fusion
  12.5 1.3 add_reduce_fusion
  13.8 0.0 copy-start.5
  13.8 0.0 copy-start
  13.8 0.0 copy-start.1
  13.8 0.0 copy-start.2
  13.8 0.1 pad_maximum_fusion.probe
  13.9 1.0 copy-done.5
  14.9 0.2 sqrt_bitcast_fusion.roots
  15.1 1.3 collective-permute-start.2
  16.4 8.9 %collective-permute-done.1.right = f32[2,256,256]{2,1,0:T(8,128)S(1)} collective-permute-done((f32[2,256,256]{2,1,0:T(8,128)}, f32[2,256,256]{2,1,0:T(8,128)S(1)}, u32[]{:S(2)}, u32[]{:S(2)}) %collective-permute-start.1) | collective-permute-done | bytes 524320 | tf_op jit(solution)/shard_map/ppermute | solution.py:175
  25.3 2.3 %collective-permute-start.3 = (f32[2,256,256]{2,1,0:T(8,128)S(1)}, f32[2,256,256]{2,1,0:T(8,128)S(1)}, u32[]{:S(2)}, u32[]{:S(2)}) collective-permute-start(f32[2,256,256]{2,1,0:T(8,128)S(1)} %collective-permute-done.1.right), channel_id=1, source_target_pairs={{16,0},{17,1},{18,2},{19,3},{20,4},{21,5},{22,6},{23,7},{24,8},{25... | collective-permute-start | bytes 1572872 | tf_op jit(solution)/shard_map/ppermute | solution.py:197
  27.6 3.2 %collective-permute-done.2.corner_a = f32[2,256,256]{2,1,0:T(8,128)S(1)} collective-permute-done((f32[2,256,256]{2,1,0:T(8,128)S(1)}, f32[2,256,256]{2,1,0:T(8,128)S(1)}, u32[]{:S(2)}, u32[]{:S(2)}) %collective-permute-start.2) | collective-permute-done | bytes 524320 | tf_op jit(solution)/shard_map/ppermute | solution.py:197
  30.8 11.0 %slots.1 = (f32[4,3,64,256]{3,2,1,0:T(8,128)S(1)}, f32[4,3,64,256]{3,2,1,0:T(8,128)S(1)}, f32[2,4,3,64,256]{4,3,2,1,0:T(8,128)}, f32[16,5,8,256]{3,2,1,0:T(8,128)S(1)}, f32[16,5,8,256]{3,2,1,0:T(8,128)S(1)}) custom-call(s32[1,128]{1,0:T(1,128)S(1)} %pad.4.card, f32[2,256,256]{2,1,0:T(8,128)S(1)} %copy-done, f32[2,256,256]{2,1,0:T(8,128)S(1)} %collective-permute-done.1.right, ...), custom_call_target="tpu_custom_call" | custom-call | tf_op jit(solution)/shard_map/slots/pallas_call | solution.py:146
  41.8 1.9 %collective-permute-start.5 = (f32[2,4,3,64,256]{4,3,2,1,0:T(8,128)}, f32[2,4,3,64,256]{4,3,2,1,0:T(8,128)}, u32[]{:S(2)}, u32[]{:S(2)}) collective-permute-start(f32[2,4,3,64,256]{4,3,2,1,0:T(8,128)} %get-tuple-element.21), channel_id=1, source_target_pairs={{0,16},{4,20},{8,24},{12,28},{16,32},{20,36},{24,40},{28,44},{32,4... | collective-permute-start | bytes 4718600 | tf_op jit(solution)/shard_map/ppermute | solution.py:175
  43.7 5.4 %collective-permute-start.4 = (f32[16,5,8,256]{3,2,1,0:T(8,128)S(1)}, f32[16,5,8,256]{3,2,1,0:T(8,128)S(1)}, u32[]{:S(2)}, u32[]{:S(2)}) collective-permute-start(f32[16,5,8,256]{3,2,1,0:T(8,128)S(1)} %get-tuple-element.20), channel_id=1, source_target_pairs={{0,16},{16,0},{1,17},{17,1},{2,18},{18,2},{3,19},{19,3},{4,20},{20... | collective-permute-start | bytes 1966088 | tf_op jit(solution)/shard_map/ppermute | solution.py:179
  49.1 1.7 %collective-permute-done.4 = f32[16,5,8,256]{3,2,1,0:T(8,128)S(1)} collective-permute-done((f32[16,5,8,256]{3,2,1,0:T(8,128)S(1)}, f32[16,5,8,256]{3,2,1,0:T(8,128)S(1)}, u32[]{:S(2)}, u32[]{:S(2)}) %collective-permute-start.4) | collective-permute-done | bytes 655392 | tf_op jit(solution)/shard_map/ppermute | solution.py:179
  50.8 0.1 add.90
  50.9 15.4 %all_to_all.20 = f32[16,5,8,256]{3,2,1,0:T(8,128)S(1)} all-to-all(f32[16,5,8,256]{3,2,1,0:T(8,128)S(1)} %add.90), channel_id=1, replica_groups=mesh['z_high'=4,'z_low'=4,'core'=2,'band'=4,'pos'=4] {'band','pos'}, dimensions={0} | all-to-all | bytes 1310720 | tf_op jit(solution)/shard_map/all_to_all | solution.py:187
  66.3 2.1 %bitcast_add_fusion = f32[4,3,64,256]{3,2,1,0:T(8,128)} fusion(f32[4,3,64,256]{3,2,1,0:T(8,128)S(1)} %get-tuple-element.23, f32[2,4,3,64,256]{4,3,2,1,0:T(8,128)} %collective-permute-done.5), kind=kLoop, calls=%fused_computation.1 | loop fusion | flops 196608 | bytes 2359296 | tf_op jit(solution)/shard_map/add | solution.py:223
  68.5 1.8 %collective-permute-start.6 = (f32[4,3,64,256]{3,2,1,0:T(8,128)}, f32[4,3,64,256]{3,2,1,0:T(8,128)S(1)}, u32[]{:S(2)}, u32[]{:S(2)}) collective-permute-start(f32[4,3,64,256]{3,2,1,0:T(8,128)} %bitcast_add_fusion), channel_id=1, source_target_pairs={{0,4},{4,8},{8,12},{16,20},{20,24},{24,28},{32,36},{36,40},{40,44}... | collective-permute-start | bytes 2359304 | tf_op jit(solution)/shard_map/ppermute | solution.py:175
  70.3 12.2 %all_to_all.21 = f32[4,5,8,256]{3,2,1,0:T(8,128)S(1)} all-to-all(f32[4,5,8,256]{3,2,1,0:T(8,128)S(1)} %broadcast_in_dim.27), channel_id=1, replica_groups=mesh['z_high'=4,'z_low'=4,'core'=2,'band'=4,'pos'=4] {'z_low'}, dimensions={0} | all-to-all | bytes 327680 | tf_op jit(solution)/shard_map/all_to_all | solution.py:187
  82.5 0.7 broadcast_in_dim.28
  83.2 11.8 %all-to-all-start.2 = ((f32[4,5,8,256]{3,2,1,0:T(8,128)}), f32[4,5,8,256]{3,2,1,0:T(8,128)S(1)}, u32[]{:S(2)}, u32[]{:S(2)}) async-start(f32[4,5,8,256]{3,2,1,0:T(8,128)} %broadcast_in_dim.28), calls=%async_computation.2 | async-start | bytes 327680 | tf_op jit(solution)/shard_map/all_to_all | solution.py:187
  95.0 1.3 fusion
  96.4 2.0 %collective-permute-start.7 = (f32[3,64,256]{2,1,0:T(8,128)S(1)}, f32[3,64,256]{2,1,0:T(8,128)S(1)}, u32[]{:S(2)}, u32[]{:S(2)}) collective-permute-start(f32[3,64,256]{2,1,0:T(8,128)S(1)} %get-tuple-element.28), channel_id=1, source_target_pairs={{0,1},{1,0},{2,3},{3,2},{4,5},{5,4},{6,7},{7,6},{8,9},{9,8},{10,11... | collective-permute-start | bytes 589832 | tf_op jit(solution)/shard_map/ppermute | solution.py:183
  98.4 3.8 %collective-permute-start.8 = (f32[3,64,256]{2,1,0:T(8,128)S(1)}, f32[3,64,256]{2,1,0:T(8,128)S(1)}, u32[]{:S(2)}, u32[]{:S(2)}) collective-permute-start(f32[3,64,256]{2,1,0:T(8,128)S(1)} %get-tuple-element.30), channel_id=1, source_target_pairs={{0,3},{1,2},{2,1},{3,0},{4,7},{5,6},{6,5},{7,4},{8,11},{9,10},{10,... | collective-permute-start | bytes 589832 | tf_op jit(solution)/shard_map/ppermute | solution.py:183
  102.2 3.2 %collective-permute-start.9 = (f32[3,64,256]{2,1,0:T(8,128)S(1)}, f32[3,64,256]{2,1,0:T(8,128)S(1)}, u32[]{:S(2)}, u32[]{:S(2)}) collective-permute-start(f32[3,64,256]{2,1,0:T(8,128)S(1)} %get-tuple-element.29), channel_id=1, source_target_pairs={{0,2},{1,3},{2,0},{3,1},{4,6},{5,7},{6,4},{7,5},{8,10},{9,11},{10,... | collective-permute-start | bytes 589832 | tf_op jit(solution)/shard_map/ppermute | solution.py:183
  105.4 1.9 %all-to-all-done.2 = f32[4,5,8,256]{3,2,1,0:T(8,128)S(1)} async-done(((f32[4,5,8,256]{3,2,1,0:T(8,128)}), f32[4,5,8,256]{3,2,1,0:T(8,128)S(1)}, u32[]{:S(2)}, u32[]{:S(2)}) %all-to-all-start.2) | async-done | bytes 163872 | tf_op jit(solution)/shard_map/all_to_all | solution.py:187
  107.3 0.8 fusion.5
  108.1 0.8 broadcast_in_dim.29
  109.0 4.5 %all-to-all-start.3 = ((f32[16,4,8,256]{3,2,1,0:T(8,128)}), f32[16,4,8,256]{3,2,1,0:T(8,128)S(1)}, u32[]{:S(2)}, u32[]{:S(2)}) async-start(f32[16,4,8,256]{3,2,1,0:T(8,128)} %broadcast_in_dim.29), calls=%async_computation.3 | async-start | bytes 1048576 | tf_op jit(solution)/shard_map/all_to_all | solution.py:187
  113.5 0.1 fusion.2
  113.6 3.3 %collective-permute-start.10 = (f32[2,64,256]{2,1,0:T(8,128)S(1)}, f32[2,64,256]{2,1,0:T(8,128)S(1)}, u32[]{:S(2)}, u32[]{:S(2)}) collective-permute-start(f32[2,64,256]{2,1,0:T(8,128)S(1)} %get-tuple-element.27), channel_id=1, source_target_pairs={{0,1},{1,0},{2,3},{3,2},{4,5},{5,4},{6,7},{7,6},{8,9},{9,8},{10,11... | collective-permute-start | bytes 393224 | tf_op jit(solution)/shard_map/ppermute | solution.py:183
  116.9 5.5 %all-to-all-done.3 = f32[16,4,8,256]{3,2,1,0:T(8,128)S(1)} async-done(((f32[16,4,8,256]{3,2,1,0:T(8,128)}), f32[16,4,8,256]{3,2,1,0:T(8,128)S(1)}, u32[]{:S(2)}, u32[]{:S(2)}) %all-to-all-start.3) | async-done | bytes 524320 | tf_op jit(solution)/shard_map/all_to_all | solution.py:187
  122.5 8.4 %collective-permute-start.13 = (f32[4,128,256]{2,1,0:T(8,128)S(1)}, f32[4,128,256]{2,1,0:T(8,128)S(1)}, u32[]{:S(2)}, u32[]{:S(2)}) collective-permute-start(f32[4,128,256]{2,1,0:T(8,128)S(1)} %bitcast.42), channel_id=1, source_target_pairs={{0,16},{16,0},{1,17},{17,1},{2,18},{18,2},{3,19},{19,3},{4,20},{20... | collective-permute-start | bytes 1572872 | tf_op jit(solution)/shard_map/ppermute | solution.py:179
  130.9 2.1 %collective-permute-start.11 = (f32[2,64,256]{2,1,0:T(8,128)S(1)}, f32[2,64,256]{2,1,0:T(8,128)S(1)}, u32[]{:S(2)}, u32[]{:S(2)}) collective-permute-start(f32[2,64,256]{2,1,0:T(8,128)S(1)} %get-tuple-element.27), channel_id=1, source_target_pairs={{0,3},{1,2},{2,1},{3,0},{4,7},{5,6},{6,5},{7,4},{8,11},{9,10},{10,... | collective-permute-start | bytes 393224 | tf_op jit(solution)/shard_map/ppermute | solution.py:183
  133.1 3.7 %collective-permute-start.12 = (f32[2,64,256]{2,1,0:T(8,128)S(1)}, f32[2,64,256]{2,1,0:T(8,128)S(1)}, u32[]{:S(2)}, u32[]{:S(2)}) collective-permute-start(f32[2,64,256]{2,1,0:T(8,128)S(1)} %get-tuple-element.27), channel_id=1, source_target_pairs={{0,2},{1,3},{2,0},{3,1},{4,6},{5,7},{6,4},{7,5},{8,10},{9,11},{10,... | collective-permute-start | bytes 393224 | tf_op jit(solution)/shard_map/ppermute | solution.py:183
  136.9 2.3 %collective-permute-done.11 = f32[2,64,256]{2,1,0:T(8,128)S(1)} collective-permute-done((f32[2,64,256]{2,1,0:T(8,128)S(1)}, f32[2,64,256]{2,1,0:T(8,128)S(1)}, u32[]{:S(2)}, u32[]{:S(2)}) %collective-permute-start.11) | collective-permute-done | bytes 131104 | tf_op jit(solution)/shard_map/ppermute | solution.py:183
  139.2 0.1 broadcast_in_dim.26
  139.4 0.0 copy-start.4
  139.4 2.0 %collective-permute-done.12 = f32[2,64,256]{2,1,0:T(8,128)S(1)} collective-permute-done((f32[2,64,256]{2,1,0:T(8,128)S(1)}, f32[2,64,256]{2,1,0:T(8,128)S(1)}, u32[]{:S(2)}, u32[]{:S(2)}) %collective-permute-start.12) | collective-permute-done | bytes 131104 | tf_op jit(solution)/shard_map/ppermute | solution.py:183
  141.4 0.8 copy-done.6
  (31 shorter events, 0.4 us)
Async XLA Ops:
  0.6 13.1 %copy-start.3 = (f32[2,2,256,256]{3,2,1,0:T(8,128)S(1)}, f32[2,2,256,256]{3,2,1,0:T(8,128)}, u32[]{:S(2)}) copy-start(f32[2,2,256,256]{3,2,1,0:T(8,128)} %param.8) | copy-start | bytes 3145732
  0.6 14.4 %collective-permute-start = (f32[2,256,256]{2,1,0:T(8,128)}, f32[2,256,256]{2,1,0:T(8,128)S(1)}, u32[]{:S(2)}, u32[]{:S(2)}) collective-permute-start(f32[2,256,256]{2,1,0:T(8,128)} %own.1), channel_id=1, source_target_pairs={{16,0},{20,4},{24,8},{28,12},{32,16},{36,20},{40,24},{44,28},{48,3... | collective-permute-start | bytes 1572872 | tf_op jit(solution)/shard_map/ppermute | solution.py:175
  9.6 15.7 %collective-permute-start.1 = (f32[2,256,256]{2,1,0:T(8,128)}, f32[2,256,256]{2,1,0:T(8,128)S(1)}, u32[]{:S(2)}, u32[]{:S(2)}) collective-permute-start(f32[2,256,256]{2,1,0:T(8,128)} %own.1), channel_id=1, source_target_pairs={{4,0},{8,4},{12,8},{20,16},{24,20},{28,24},{36,32},{40,36},{44,40}... | collective-permute-start | bytes 1572872 | tf_op jit(solution)/shard_map/ppermute | solution.py:175
  13.8 1.1 copy-start.5
  13.8 17.0 %copy-start = (f32[2,256,256]{2,1,0:T(8,128)S(1)}, f32[2,256,256]{2,1,0:T(8,128)}, u32[]{:S(2)}) copy-start(f32[2,256,256]{2,1,0:T(8,128)} %own.1) | copy-start | bytes 1572868
  13.8 17.0 %copy-start.1 = (bf16[3,256,256]{2,1,0:T(8,128)(2,1)S(1)}, bf16[3,256,256]{2,1,0:T(8,128)(2,1)}, u32[]{:S(2)}) copy-start(bf16[3,256,256]{2,1,0:T(8,128)(2,1)} %constant.52.clone.head) | copy-start | bytes 1179652
  13.8 17.0 %copy-start.2 = (bf16[3,256,256]{2,1,0:T(8,128)(2,1)S(1)}, bf16[3,256,256]{2,1,0:T(8,128)(2,1)}, u32[]{:S(2)}) copy-start(bf16[3,256,256]{2,1,0:T(8,128)(2,1)} %constant.53.clone.rest) | copy-start | bytes 1179652
  15.1 15.7 %collective-permute-start.2 = (f32[2,256,256]{2,1,0:T(8,128)S(1)}, f32[2,256,256]{2,1,0:T(8,128)S(1)}, u32[]{:S(2)}, u32[]{:S(2)}) collective-permute-start(f32[2,256,256]{2,1,0:T(8,128)S(1)} %collective-permute-done.below), channel_id=1, source_target_pairs={{20,16},{24,20},{28,24},{52,48},{56,52},{60,56},{84,80},{88,84},{9... | collective-permute-start | bytes 1572872 | tf_op jit(solution)/shard_map/ppermute | solution.py:197
  25.3 5.5 %collective-permute-start.3 = (f32[2,256,256]{2,1,0:T(8,128)S(1)}, f32[2,256,256]{2,1,0:T(8,128)S(1)}, u32[]{:S(2)}, u32[]{:S(2)}) collective-permute-start(f32[2,256,256]{2,1,0:T(8,128)S(1)} %collective-permute-done.1.right), channel_id=1, source_target_pairs={{16,0},{17,1},{18,2},{19,3},{20,4},{21,5},{22,6},{23,7},{24,8},{25... | collective-permute-start | bytes 1572872 | tf_op jit(solution)/shard_map/ppermute | solution.py:197
  41.8 24.6 %collective-permute-start.5 = (f32[2,4,3,64,256]{4,3,2,1,0:T(8,128)}, f32[2,4,3,64,256]{4,3,2,1,0:T(8,128)}, u32[]{:S(2)}, u32[]{:S(2)}) collective-permute-start(f32[2,4,3,64,256]{4,3,2,1,0:T(8,128)} %get-tuple-element.21), channel_id=1, source_target_pairs={{0,16},{4,20},{8,24},{12,28},{16,32},{20,36},{24,40},{28,44},{32,4... | collective-permute-start | bytes 4718600 | tf_op jit(solution)/shard_map/ppermute | solution.py:175
  43.7 7.1 %collective-permute-start.4 = (f32[16,5,8,256]{3,2,1,0:T(8,128)S(1)}, f32[16,5,8,256]{3,2,1,0:T(8,128)S(1)}, u32[]{:S(2)}, u32[]{:S(2)}) collective-permute-start(f32[16,5,8,256]{3,2,1,0:T(8,128)S(1)} %get-tuple-element.20), channel_id=1, source_target_pairs={{0,16},{16,0},{1,17},{17,1},{2,18},{18,2},{3,19},{19,3},{4,20},{20... | collective-permute-start | bytes 1966088 | tf_op jit(solution)/shard_map/ppermute | solution.py:179
  68.5 26.6 %collective-permute-start.6 = (f32[4,3,64,256]{3,2,1,0:T(8,128)}, f32[4,3,64,256]{3,2,1,0:T(8,128)S(1)}, u32[]{:S(2)}, u32[]{:S(2)}) collective-permute-start(f32[4,3,64,256]{3,2,1,0:T(8,128)} %bitcast_add_fusion), channel_id=1, source_target_pairs={{0,4},{4,8},{8,12},{16,20},{20,24},{24,28},{32,36},{36,40},{40,44}... | collective-permute-start | bytes 2359304 | tf_op jit(solution)/shard_map/ppermute | solution.py:175
  83.2 24.1 %all-to-all-start.2 = ((f32[4,5,8,256]{3,2,1,0:T(8,128)}), f32[4,5,8,256]{3,2,1,0:T(8,128)S(1)}, u32[]{:S(2)}, u32[]{:S(2)}) async-start(f32[4,5,8,256]{3,2,1,0:T(8,128)} %broadcast_in_dim.28), calls=%async_computation.2 | async-start | bytes 327680 | tf_op jit(solution)/shard_map/all_to_all | solution.py:187
  96.4 17.1 %collective-permute-start.7 = (f32[3,64,256]{2,1,0:T(8,128)S(1)}, f32[3,64,256]{2,1,0:T(8,128)S(1)}, u32[]{:S(2)}, u32[]{:S(2)}) collective-permute-start(f32[3,64,256]{2,1,0:T(8,128)S(1)} %get-tuple-element.28), channel_id=1, source_target_pairs={{0,1},{1,0},{2,3},{3,2},{4,5},{5,4},{6,7},{7,6},{8,9},{9,8},{10,11... | collective-permute-start | bytes 589832 | tf_op jit(solution)/shard_map/ppermute | solution.py:183
  98.4 15.0 %collective-permute-start.8 = (f32[3,64,256]{2,1,0:T(8,128)S(1)}, f32[3,64,256]{2,1,0:T(8,128)S(1)}, u32[]{:S(2)}, u32[]{:S(2)}) collective-permute-start(f32[3,64,256]{2,1,0:T(8,128)S(1)} %get-tuple-element.30), channel_id=1, source_target_pairs={{0,3},{1,2},{2,1},{3,0},{4,7},{5,6},{6,5},{7,4},{8,11},{9,10},{10,... | collective-permute-start | bytes 589832 | tf_op jit(solution)/shard_map/ppermute | solution.py:183
  102.2 11.3 %collective-permute-start.9 = (f32[3,64,256]{2,1,0:T(8,128)S(1)}, f32[3,64,256]{2,1,0:T(8,128)S(1)}, u32[]{:S(2)}, u32[]{:S(2)}) collective-permute-start(f32[3,64,256]{2,1,0:T(8,128)S(1)} %get-tuple-element.29), channel_id=1, source_target_pairs={{0,2},{1,3},{2,0},{3,1},{4,6},{5,7},{6,4},{7,5},{8,10},{9,11},{10,... | collective-permute-start | bytes 589832 | tf_op jit(solution)/shard_map/ppermute | solution.py:183
  109.0 13.5 %all-to-all-start.3 = ((f32[16,4,8,256]{3,2,1,0:T(8,128)}), f32[16,4,8,256]{3,2,1,0:T(8,128)S(1)}, u32[]{:S(2)}, u32[]{:S(2)}) async-start(f32[16,4,8,256]{3,2,1,0:T(8,128)} %broadcast_in_dim.29), calls=%async_computation.3 | async-start | bytes 1048576 | tf_op jit(solution)/shard_map/all_to_all | solution.py:187
  113.6 23.2 %collective-permute-start.10 = (f32[2,64,256]{2,1,0:T(8,128)S(1)}, f32[2,64,256]{2,1,0:T(8,128)S(1)}, u32[]{:S(2)}, u32[]{:S(2)}) collective-permute-start(f32[2,64,256]{2,1,0:T(8,128)S(1)} %get-tuple-element.27), channel_id=1, source_target_pairs={{0,1},{1,0},{2,3},{3,2},{4,5},{5,4},{6,7},{7,6},{8,9},{9,8},{10,11... | collective-permute-start | bytes 393224 | tf_op jit(solution)/shard_map/ppermute | solution.py:183
  122.5 16.8 %collective-permute-start.13 = (f32[4,128,256]{2,1,0:T(8,128)S(1)}, f32[4,128,256]{2,1,0:T(8,128)S(1)}, u32[]{:S(2)}, u32[]{:S(2)}) collective-permute-start(f32[4,128,256]{2,1,0:T(8,128)S(1)} %bitcast.42), channel_id=1, source_target_pairs={{0,16},{16,0},{1,17},{17,1},{2,18},{18,2},{3,19},{19,3},{4,20},{20... | collective-permute-start | bytes 1572872 | tf_op jit(solution)/shard_map/ppermute | solution.py:179
  130.9 8.2 %collective-permute-start.11 = (f32[2,64,256]{2,1,0:T(8,128)S(1)}, f32[2,64,256]{2,1,0:T(8,128)S(1)}, u32[]{:S(2)}, u32[]{:S(2)}) collective-permute-start(f32[2,64,256]{2,1,0:T(8,128)S(1)} %get-tuple-element.27), channel_id=1, source_target_pairs={{0,3},{1,2},{2,1},{3,0},{4,7},{5,6},{6,5},{7,4},{8,11},{9,10},{10,... | collective-permute-start | bytes 393224 | tf_op jit(solution)/shard_map/ppermute | solution.py:183
  133.1 8.2 %collective-permute-start.12 = (f32[2,64,256]{2,1,0:T(8,128)S(1)}, f32[2,64,256]{2,1,0:T(8,128)S(1)}, u32[]{:S(2)}, u32[]{:S(2)}) collective-permute-start(f32[2,64,256]{2,1,0:T(8,128)S(1)} %get-tuple-element.27), channel_id=1, source_target_pairs={{0,2},{1,3},{2,0},{3,1},{4,6},{5,7},{6,4},{7,5},{8,10},{9,11},{10,... | collective-permute-start | bytes 393224 | tf_op jit(solution)/shard_map/ppermute | solution.py:183
  139.4 2.0 %copy-start.4 = (f32[4,256,256]{2,1,0:T(8,128)}, f32[4,256,256]{2,1,0:T(8,128)S(1)}, u32[]{:S(2)}) copy-start(f32[4,256,256]{2,1,0:T(8,128)S(1)} %constant_dynamic-update-slice_fusion.1) | copy-start | bytes 3145732
  141.4 0.8 copy-start.6
